TPU v7x, 32 devices: a whole 2x2x4 slice. The times are simulated.
32 devices in a mesh: fsdp: 8 (over y, x, core), ctx: 4 (over z).
Axes of the slice: x: 2, y: 2, z: 4, core: 2. Of those that a mesh axis runs over, the one named last changes fastest.
Arguments:
- tokens: bfloat16 [8, 512, 1024], P('fsdp', 'ctx'), may hold values from -6 to 6
- segment_ids: int32 [8, 512], P('fsdp'), may hold values from 0 to 2, as said below
- group_order: int32 [4], replicated, may hold values from 0 to 3, each once
- ln1_gain: bfloat16 [2, 1024], P(None, ('fsdp', 'ctx')), may hold values from 0.5 to 1.5
- ln1_bias: bfloat16 [2, 1024], P(None, ('fsdp', 'ctx')), may hold values from -2 to 2
- qkv_weight: bfloat16 [2, 1024, 3072], P(None, ('fsdp', 'ctx')), may hold values from -0.1875 to 0.1875
- qv_bias: bfloat16 [2, 2048], P(None, ('fsdp', 'ctx')), may hold values from -3 to 3
- out_weight: bfloat16 [2, 1024, 1024], P(None, ('fsdp', 'ctx')), may hold values from -0.5 to 0.5
- out_bias: bfloat16 [2, 1024], P(None, ('fsdp', 'ctx')), may hold values from -2 to 2
- ln2_gain: bfloat16 [2, 1024], P(None, ('fsdp', 'ctx')), may hold values from 0.5 to 1.5
- ln2_bias: bfloat16 [2, 1024], P(None, ('fsdp', 'ctx')), may hold values from -2 to 2
- up_weight: bfloat16 [2, 1024, 4096], P(None, ('fsdp', 'ctx')), may hold values from -0.1875 to 0.1875
- up_bias: bfloat16 [2, 4096], P(None, ('fsdp', 'ctx')), may hold values from -3 to 3
- down_weight: bfloat16 [2, 4096, 1024], P(None, ('fsdp', 'ctx')), may hold values from -0.09375 to 0.09375
- down_bias: bfloat16 [2, 1024], P(None, ('fsdp', 'ctx')), may hold values from -2 to 2
- cotangent: bfloat16 [8, 512, 1024], P('fsdp', 'ctx'), may hold values from -6 to 6
Outputs:
- output: bfloat16 [8, 512, 1024], P('fsdp', 'ctx')
- tokens_grad: float32 [8, 512, 1024], P('fsdp', 'ctx')
- grad_ln1_gain: float32 [2, 1024], P(None, ('fsdp', 'ctx'))
- grad_ln1_bias: float32 [2, 1024], P(None, ('fsdp', 'ctx'))
- grad_qkv_weight: float32 [2, 1024, 3072], P(None, ('fsdp', 'ctx'))
- grad_qv_bias: float32 [2, 2048], P(None, ('fsdp', 'ctx'))
- grad_out_weight: float32 [2, 1024, 1024], P(None, ('fsdp', 'ctx'))
- grad_out_bias: float32 [2, 1024], P(None, ('fsdp', 'ctx'))
- grad_ln2_gain: float32 [2, 1024], P(None, ('fsdp', 'ctx'))
- grad_ln2_bias: float32 [2, 1024], P(None, ('fsdp', 'ctx'))
- grad_up_weight: float32 [2, 1024, 4096], P(None, ('fsdp', 'ctx'))
- grad_up_bias: float32 [2, 4096], P(None, ('fsdp', 'ctx'))
- grad_down_weight: float32 [2, 4096, 1024], P(None, ('fsdp', 'ctx'))
- grad_down_bias: float32 [2, 1024], P(None, ('fsdp', 'ctx'))
Inputs may be any that keep to these rules, and one draw needn't show every extreme that they name: `segment_ids`: in each stream the ids never fall with position; document 0 ends before position 64, document 2 begins after position 448 and is never empty. A permutation; index c of ctx holds the position blocks group_order[c] and 7 - group_order[c].
All inputs are finite; a program needn't handle non-finite values.
Results may differ from a plain program's by a relative error of at most 0.02.
Values may be sent and summed in bfloat16 or wider, within the bound.
No kernel may reach another device: no remote copies, remote signals or barrier semaphores. Data moves between devices by JAX's collectives and lax.ppermute only.
A program may use at most 320 MiB of HBM per device.

v0:
```python
import jax
import jax.numpy as jnp
from jax import lax
from jax.sharding import PartitionSpec as P

HEADS = 16


EPSILON = 1e-05


def shifted(value, axis, by):
    count = lax.axis_size(axis)
    return lax.ppermute(value, axis, [(i, (i + by) % count) for i in range(count)])


def norm_rows(values, gain, shift):
    row_mean = jnp.mean(values, axis=-1, keepdims=True)
    centred = values - row_mean
    row_var = jnp.mean(centred * centred, axis=-1, keepdims=True)
    return centred * lax.rsqrt(row_var + EPSILON) * gain + shift


def gelu_tanh(values):
    return jax.nn.gelu(values, approximate=True)


def times_transposed(left, matrix):
    return lax.dot_general(
        left, matrix, (((1,), (1,)), ((), ())), preferred_element_type=jnp.float32
    )


def outer_sum(left, right):
    return jnp.einsum("td,te->de", left, right, preferred_element_type=jnp.float32)


def fetch_forward(shards):
    return (
        lax.all_gather(shards[0], ("fsdp", "ctx"), axis=0, tiled=True),
        lax.all_gather(shards[1], ("fsdp", "ctx"), axis=0, tiled=True),
        lax.all_gather(shards[2], ("fsdp", "ctx"), axis=0, tiled=True),
        lax.all_gather(shards[3], ("fsdp", "ctx"), axis=0, tiled=True),
        lax.all_gather(shards[4], ("fsdp", "ctx"), axis=0, tiled=True),
        lax.all_gather(shards[5], ("fsdp", "ctx"), axis=0, tiled=True),
        lax.all_gather(shards[6], ("fsdp", "ctx"), axis=0, tiled=True),
        lax.all_gather(shards[7], ("fsdp", "ctx"), axis=0, tiled=True),
        lax.all_gather(shards[8], ("fsdp", "ctx"), axis=0, tiled=True),
        lax.all_gather(shards[9], ("fsdp", "ctx"), axis=0, tiled=True),
        lax.all_gather(shards[10], ("fsdp", "ctx"), axis=0, tiled=True),
        lax.all_gather(shards[11], ("fsdp", "ctx"), axis=0, tiled=True),
    )


def fetch_backward(shards):
    return (
        lax.all_gather(shards[0], ("fsdp", "ctx"), axis=0, tiled=True),
        lax.all_gather(shards[1], ("fsdp", "ctx"), axis=0, tiled=True),
        lax.all_gather(shards[2], ("fsdp", "ctx"), axis=0, tiled=True),
        lax.all_gather(shards[3], ("fsdp", "ctx"), axis=0, tiled=True),
        lax.all_gather(shards[4], ("fsdp", "ctx"), axis=0, tiled=True),
        lax.all_gather(shards[5], ("fsdp", "ctx"), axis=0, tiled=True),
        lax.all_gather(shards[6], ("fsdp", "ctx"), axis=0, tiled=True),
        lax.all_gather(shards[7], ("fsdp", "ctx"), axis=0, tiled=True),
        lax.all_gather(shards[8], ("fsdp", "ctx"), axis=0, tiled=True),
        lax.all_gather(shards[9], ("fsdp", "ctx"), axis=0, tiled=True),
        lax.all_gather(shards[10], ("fsdp", "ctx"), axis=0, tiled=True),
        lax.all_gather(shards[11], ("fsdp", "ctx"), axis=0, tiled=True),
    )


def send_layer(grads):
    return (
        lax.psum_scatter(grads[0], ("fsdp", "ctx"), scatter_dimension=0, tiled=True),
        lax.psum_scatter(grads[1], ("fsdp", "ctx"), scatter_dimension=0, tiled=True),
        lax.psum_scatter(grads[2], ("fsdp", "ctx"), scatter_dimension=0, tiled=True),
        lax.psum_scatter(grads[3], ("fsdp", "ctx"), scatter_dimension=0, tiled=True),
        lax.psum_scatter(grads[4], ("fsdp", "ctx"), scatter_dimension=0, tiled=True),
        lax.psum_scatter(grads[5], ("fsdp", "ctx"), scatter_dimension=0, tiled=True),
        lax.psum_scatter(grads[6], ("fsdp", "ctx"), scatter_dimension=0, tiled=True),
        lax.psum_scatter(grads[7], ("fsdp", "ctx"), scatter_dimension=0, tiled=True),
        lax.psum_scatter(grads[8], ("fsdp", "ctx"), scatter_dimension=0, tiled=True),
        lax.psum_scatter(grads[9], ("fsdp", "ctx"), scatter_dimension=0, tiled=True),
        lax.psum_scatter(grads[10], ("fsdp", "ctx"), scatter_dimension=0, tiled=True),
        lax.psum_scatter(grads[11], ("fsdp", "ctx"), scatter_dimension=0, tiled=True),
    )


def row_places(start, count, order, group_len):
    rows = start + jnp.arange(count, dtype=jnp.int32)
    half = group_len // 2
    owner = rows // group_len
    within = rows % group_len
    ctx_count = order.shape[0]
    picks = (owner[:, None] == jnp.arange(ctx_count, dtype=jnp.int32)[None, :]).astype(jnp.int32)
    lead = jnp.sum(picks * order[None, :], axis=1)
    block = jnp.where(within < half, lead, 2 * ctx_count - 1 - lead)
    return block * half + within % half


def score_block(queries, key_piece, offset, query_pos, query_seg, seg_stream, order, slopes):
    key_count = key_piece.shape[0]
    head_count = slopes.shape[0]
    head_size = queries.shape[2]
    key_h = key_piece.reshape(key_count, head_count, head_size)
    scores = jnp.einsum(
        "qhd,khd->hqk", queries, key_h, preferred_element_type=jnp.float32
    ) * head_size ** (-0.5)
    key_pos = row_places(offset, key_count, order, queries.shape[0])
    key_seg = jnp.take(seg_stream, key_pos)
    distance = query_pos[:, None] - key_pos[None, :]
    allowed = (distance >= 0) & (query_seg[:, None] == key_seg[None, :])
    scores = scores - slopes[:, None, None] * distance.astype(jnp.float32)[None]
    return (scores, allowed[None], key_h)


def attend_forward(qkv_rows, seg_stream, order, my_start, slopes):
    row_count = qkv_rows.shape[0]
    model_width = qkv_rows.shape[1] // 3
    head_count = slopes.shape[0]
    head_size = model_width // head_count
    queries = qkv_rows[:, :model_width].reshape(row_count, head_count, head_size)
    key_rows = qkv_rows[:, model_width : 2 * model_width]
    value_rows = qkv_rows[:, 2 * model_width :]
    query_pos = row_places(my_start, row_count, order, row_count)
    query_seg = jnp.take(seg_stream, query_pos)
    running_max = jnp.full((head_count, row_count), -1e30, jnp.float32)
    key_piece = lax.all_gather(key_rows, "ctx", axis=0, tiled=True)
    value_piece = lax.all_gather(value_rows, "ctx", axis=0, tiled=True)
    key_count = key_piece.shape[0]
    scores, allowed, key_h = score_block(
        queries, key_piece, jnp.int32(0), query_pos, query_seg, seg_stream, order, slopes
    )
    new_max = jnp.maximum(running_max, jnp.max(jnp.where(allowed, scores, -1e30), axis=-1))
    softmax_w = jnp.where(allowed, jnp.exp(scores - new_max[:, :, None]), 0.0)
    running_sum = jnp.sum(softmax_w, axis=-1)
    value_h = value_piece.reshape(key_count, head_count, head_size)
    weighted = jnp.einsum(
        "hqk,khd->qhd", softmax_w.astype(jnp.bfloat16), value_h, preferred_element_type=jnp.float32
    )
    running_max, running_sum, weighted = (new_max, running_sum, weighted)
    out_f = weighted / jnp.transpose(running_sum)[:, :, None]
    log_total = running_max + jnp.log(running_sum)
    return (out_f.reshape(row_count, model_width), log_total)


def piece_grads(
    queries,
    grad_out_h,
    row_dots,
    log_total,
    key_piece,
    value_piece,
    offset,
    query_pos,
    query_seg,
    seg_stream,
    order,
    slopes,
):
    key_count = key_piece.shape[0]
    head_count = slopes.shape[0]
    head_size = queries.shape[2]
    scale = head_size ** (-0.5)
    scores, allowed, key_h = score_block(
        queries, key_piece, offset, query_pos, query_seg, seg_stream, order, slopes
    )
    softmax_w = jnp.where(allowed, jnp.exp(scores - log_total[:, :, None]), 0.0)
    value_h = value_piece.reshape(key_count, head_count, head_size)
    grad_value = jnp.einsum(
        "hqk,qhd->khd",
        softmax_w.astype(jnp.bfloat16),
        grad_out_h,
        preferred_element_type=jnp.float32,
    )
    grad_weight = jnp.einsum(
        "qhd,khd->hqk", grad_out_h, value_h, preferred_element_type=jnp.float32
    )
    grad_scores = (softmax_w * (grad_weight - row_dots[:, :, None])).astype(jnp.bfloat16)
    grad_query = scale * jnp.einsum(
        "hqk,khd->qhd", grad_scores, key_h, preferred_element_type=jnp.float32
    )
    grad_key = scale * jnp.einsum(
        "hqk,qhd->khd", grad_scores, queries, preferred_element_type=jnp.float32
    )
    return (
        grad_query,
        grad_key.reshape(key_count, head_count * head_size),
        grad_value.reshape(key_count, head_count * head_size),
    )


def attend_backward(qkv_rows, out_f, log_total, grad_out, seg_stream, order, my_start, slopes):
    row_count = qkv_rows.shape[0]
    model_width = qkv_rows.shape[1] // 3
    head_count = slopes.shape[0]
    head_size = model_width // head_count
    queries = qkv_rows[:, :model_width].reshape(row_count, head_count, head_size)
    key_rows = qkv_rows[:, model_width : 2 * model_width]
    value_rows = qkv_rows[:, 2 * model_width :]
    query_pos = row_places(my_start, row_count, order, row_count)
    query_seg = jnp.take(seg_stream, query_pos)
    grad_out_h = grad_out.reshape(row_count, head_count, head_size)
    row_dots = jnp.transpose(
        jnp.sum(
            (grad_out.astype(jnp.float32) * out_f).reshape(row_count, head_count, head_size),
            axis=-1,
        )
    )
    ctx_count = lax.axis_size("ctx")
    my_index = lax.axis_index("ctx")

    def turn(step, state_in):
        grad_query, key_piece, value_piece, grad_key, grad_value = state_in
        anchor = (my_index - step + ctx_count) % ctx_count
        offset = anchor * row_count
        part_q, part_k, part_v = piece_grads(
            queries,
            grad_out_h,
            row_dots,
            log_total,
            key_piece,
            value_piece,
            offset,
            query_pos,
            query_seg,
            seg_stream,
            order,
            slopes,
        )
        key_piece, value_piece = shifted((key_piece, value_piece), "ctx", 1)
        grad_key, grad_value = (
            shifted((grad_key + part_k).astype(jnp.bfloat16), "ctx", 1).astype(jnp.float32),
            shifted((grad_value + part_v).astype(jnp.bfloat16), "ctx", 1).astype(jnp.float32),
        )
        return (grad_query + part_q, key_piece, value_piece, grad_key, grad_value)

    initial = (
        jnp.zeros((row_count, head_count, head_size), jnp.float32),
        key_rows,
        value_rows,
        jnp.zeros((row_count, model_width), jnp.float32),
        jnp.zeros((row_count, model_width), jnp.float32),
    )
    grad_query, unused_keys, unused_values, grad_key_mine, grad_value_mine = lax.fori_loop(
        0, ctx_count, turn, initial
    )
    return jnp.concatenate(
        [grad_query.reshape(row_count, model_width), grad_key_mine, grad_value_mine], axis=1
    )


def layer_forward(residual, weights, seg_stream, order, my_start, slopes):
    (
        gain_one,
        shift_one,
        w_qkv,
        bias_qv,
        w_out,
        bias_out,
        gain_two,
        shift_two,
        w_up,
        bias_up,
        w_down,
        bias_down,
    ) = weights
    model_width = residual.shape[1]
    normed = norm_rows(
        residual, gain_one.astype(jnp.float32), shift_one.astype(jnp.float32)
    ).astype(jnp.bfloat16)
    bias_qv_f = bias_qv.astype(jnp.float32)
    bias_full = jnp.concatenate(
        [bias_qv_f[:model_width], jnp.zeros((model_width,), jnp.float32), bias_qv_f[model_width:]]
    )
    qkv_rows = (jnp.dot(normed, w_qkv, preferred_element_type=jnp.float32) + bias_full).astype(
        jnp.bfloat16
    )
    out_f, log_total = attend_forward(qkv_rows, seg_stream, order, my_start, slopes)
    out_rows = out_f.astype(jnp.bfloat16)
    middle = (
        residual
        + jnp.dot(out_rows, w_out, preferred_element_type=jnp.float32)
        + bias_out.astype(jnp.float32)
    )
    normed_two = norm_rows(
        middle, gain_two.astype(jnp.float32), shift_two.astype(jnp.float32)
    ).astype(jnp.bfloat16)
    pre_act = jnp.dot(normed_two, w_up, preferred_element_type=jnp.float32) + bias_up.astype(
        jnp.float32
    )
    hidden = gelu_tanh(pre_act).astype(jnp.bfloat16)
    result = (
        middle
        + jnp.dot(hidden, w_down, preferred_element_type=jnp.float32)
        + bias_down.astype(jnp.float32)
    )
    return (result, (residual, qkv_rows, out_f, log_total, middle, pre_act))


def layer_backward(upstream, stored, weights, seg_stream, order, my_start, slopes):
    (
        gain_one,
        shift_one,
        w_qkv,
        bias_qv,
        w_out,
        bias_out,
        gain_two,
        shift_two,
        w_up,
        bias_up,
        w_down,
        bias_down,
    ) = weights
    residual, qkv_rows, out_f, log_total, middle, pre_act = stored
    model_width = residual.shape[1]
    normed_f, norm_back_one = jax.vjp(
        norm_rows, residual, gain_one.astype(jnp.float32), shift_one.astype(jnp.float32)
    )
    normed = normed_f.astype(jnp.bfloat16)
    normed_two_f, norm_back_two = jax.vjp(
        norm_rows, middle, gain_two.astype(jnp.float32), shift_two.astype(jnp.float32)
    )
    normed_two = normed_two_f.astype(jnp.bfloat16)
    gelu_out, gelu_back = jax.vjp(gelu_tanh, pre_act)
    hidden = gelu_out.astype(jnp.bfloat16)
    out_rows = out_f.astype(jnp.bfloat16)
    grad_branch = upstream.astype(jnp.bfloat16)
    grad_w_down = outer_sum(hidden, grad_branch)
    grad_b_down = jnp.sum(grad_branch.astype(jnp.float32), axis=0)
    grad_hidden = times_transposed(grad_branch, w_down)
    grad_pre = gelu_back(grad_hidden)[0].astype(jnp.bfloat16)
    grad_w_up = outer_sum(normed_two, grad_pre)
    grad_b_up = jnp.sum(grad_pre.astype(jnp.float32), axis=0)
    grad_middle_n, grad_gain_two, grad_shift_two = norm_back_two(times_transposed(grad_pre, w_up))
    grad_middle = upstream + grad_middle_n
    grad_attn = grad_middle.astype(jnp.bfloat16)
    grad_w_out = outer_sum(out_rows, grad_attn)
    grad_b_out = jnp.sum(grad_attn.astype(jnp.float32), axis=0)
    grad_out = times_transposed(grad_attn, w_out).astype(jnp.bfloat16)
    grad_qkv = attend_backward(
        qkv_rows, out_f, log_total, grad_out, seg_stream, order, my_start, slopes
    ).astype(jnp.bfloat16)
    grad_w_qkv = outer_sum(normed, grad_qkv)
    grad_qkv_f = grad_qkv.astype(jnp.float32)
    grad_b_qv = jnp.concatenate(
        [
            jnp.sum(grad_qkv_f[:, :model_width], axis=0),
            jnp.sum(grad_qkv_f[:, 2 * model_width :], axis=0),
        ]
    )
    grad_input_n, grad_gain_one, grad_shift_one = norm_back_one(times_transposed(grad_qkv, w_qkv))
    grad_input = grad_middle + grad_input_n
    grads = (
        grad_gain_one,
        grad_shift_one,
        grad_w_qkv,
        grad_b_qv,
        grad_w_out,
        grad_b_out,
        grad_gain_two,
        grad_shift_two,
        grad_w_up,
        grad_b_up,
        grad_w_down,
        grad_b_down,
    )
    return (grad_input, grads)


def body(
    tokens,
    segment_ids,
    group_order,
    ln1_gain,
    ln1_bias,
    qkv_weight,
    qv_bias,
    out_weight,
    out_bias,
    ln2_gain,
    ln2_bias,
    up_weight,
    up_bias,
    down_weight,
    down_bias,
    cotangent,
):
    shard_list = (
        ln1_gain,
        ln1_bias,
        qkv_weight,
        qv_bias,
        out_weight,
        out_bias,
        ln2_gain,
        ln2_bias,
        up_weight,
        up_bias,
        down_weight,
        down_bias,
    )
    layer_count = ln1_gain.shape[0]
    group_len = tokens.shape[1]
    my_start = lax.axis_index("ctx") * group_len
    seg_stream = segment_ids[0]
    slopes = jnp.exp2(-8.0 * (jnp.arange(HEADS, dtype=jnp.float32) + 1.0) / HEADS)
    residual = tokens[0].astype(jnp.float32)
    fetched = []
    stored_all = []
    for layer_no in range(layer_count):
        weights = fetch_forward([shard[layer_no] for shard in shard_list])
        fetched.append(weights)
        residual, stored = layer_forward(
            residual, weights, seg_stream, group_order, my_start, slopes
        )
        stored_all.append(stored)
    final_rows = residual.astype(jnp.bfloat16)[None]
    upstream = cotangent[0].astype(jnp.float32)
    layer_grads = [None] * layer_count
    for layer_no in reversed(range(layer_count)):
        weights = fetch_backward([shard[layer_no] for shard in shard_list])
        upstream, grads = layer_backward(
            upstream, stored_all[layer_no], weights, seg_stream, group_order, my_start, slopes
        )
        layer_grads[layer_no] = send_layer(grads)
    stacked = [
        jnp.stack([layer_grads[layer_no][item] for layer_no in range(layer_count)])
        for item in range(12)
    ]
    return (final_rows, upstream[None]) + tuple(stacked)


def solution(mesh):
    in_specs = (
        P("fsdp", "ctx", None),
        P("fsdp", None),
        P(),
        P(None, ("fsdp", "ctx")),
        P(None, ("fsdp", "ctx")),
        P(None, ("fsdp", "ctx"), None),
        P(None, ("fsdp", "ctx")),
        P(None, ("fsdp", "ctx"), None),
        P(None, ("fsdp", "ctx")),
        P(None, ("fsdp", "ctx")),
        P(None, ("fsdp", "ctx")),
        P(None, ("fsdp", "ctx"), None),
        P(None, ("fsdp", "ctx")),
        P(None, ("fsdp", "ctx"), None),
        P(None, ("fsdp", "ctx")),
        P("fsdp", "ctx", None),
    )
    out_specs = (
        P("fsdp", "ctx", None),
        P("fsdp", "ctx", None),
        P(None, ("fsdp", "ctx")),
        P(None, ("fsdp", "ctx")),
        P(None, ("fsdp", "ctx"), None),
        P(None, ("fsdp", "ctx")),
        P(None, ("fsdp", "ctx"), None),
        P(None, ("fsdp", "ctx")),
        P(None, ("fsdp", "ctx")),
        P(None, ("fsdp", "ctx")),
        P(None, ("fsdp", "ctx"), None),
        P(None, ("fsdp", "ctx")),
        P(None, ("fsdp", "ctx"), None),
        P(None, ("fsdp", "ctx")),
    )
    return jax.shard_map(body, mesh=mesh, in_specs=in_specs, out_specs=out_specs, check_vma=False)
```

profile of v0, /device:TPU:4, one launch (start us, length us, event | category | flops | bytes accessed | tf_op | source)
XLA Modules:
  0.0 3201.2 jit_solution(2230867785773764650)
XLA Ops:
  27.2 42.4 %all-reduce.31 = (bf16[1024]{0:T(1024)(128)(2,1)S(1)}, bf16[2048]{0:T(1024)(128)(2,1)S(1)}, bf16[1024]{0:T(1024)(128)(2,1)S(1)}, bf16[1024]{0:T(1024)(128)(2,1)S...) all-reduce(bf16[1024]{0:T(1024)(128)(2,1)S(1)} %dynamic-update-slic, ...), channel_id=7, replica_groups=mesh['fsdp'=8,'ctx'=4] {'fsdp','ctx'}, use_global_device_ids=true, to_apply=%add.3 | all-reduce | flops 16384 | bytes 65536
  71.9 11.1 all-gather.45.cloned.1.call-done
  83.1 4.0 fusion.73
  93.6 3.5 gather_fusion.3
  97.7 65.7 %all-gather.9 = bf16[1,4096]{1,0:T(2,128)(2,1)S(1)} all-gather(bf16[1,128]{1,0:T(2,128)(2,1)S(1)} %get-tuple-element.1251), channel_id=11, replica_groups=mesh['fsdp'=8,'ctx'=4] {'fsdp','ctx'}, dimensions={1}, use_global_device_ids=true | all-gather | bytes 8448 | tf_op jit(solution)/shard_map/all_gather | solution.py:49
  173.6 30.1 all-gather.47.cloned.1.call-done
  206.1 77.2 %all-gather.49.cloned.1.call-done = bf16[1,1024,4096]{2,1,0:T(8,128)(2,1)} async-done(((bf16[1,32,4096]{2,1,0:T(8,128)(2,1)}), bf16[1,1024,4096]{2,1,0:T(8,128)(2,1)}) %all-gather.49.cloned.1.call-update) | async-done | bytes 8388624 | tf_op jit(solution)/shard_map/all_gather | solution.py:48
  283.4 6.1 fusion.58
  289.4 73.3 %all-gather.51.cloned.1.call-done = bf16[1,4096,1024]{2,1,0:T(8,128)(2,1)} async-done(((bf16[1,128,1024]{2,1,0:T(8,128)(2,1)}), bf16[1,4096,1024]{2,1,0:T(8,128)(2,1)}) %all-gather.51.cloned.1.call-update) | async-done | bytes 8388624 | tf_op jit(solution)/shard_map/all_gather | solution.py:50
  362.7 5.7 fusion.237
  368.7 65.7 %all-gather.53.cloned.1.call-done = bf16[1,1024,3072]{2,1,0:T(8,128)(2,1)} async-done(((bf16[1,32,3072]{2,1,0:T(8,128)(2,1)}), bf16[1,1024,3072]{2,1,0:T(8,128)(2,1)}) %all-gather.53.cloned.1.call-update) | async-done | bytes 6291472 | tf_op jit(solution)/shard_map/all_gather | solution.py:42
  434.4 3.9 fusion.70
  442.6 65.5 %all-gather.21 = bf16[1,4096]{1,0:T(2,128)(2,1)S(1)} all-gather(bf16[1,128]{1,0:T(2,128)(2,1)S(1)} %copy-done.73), channel_id=23, replica_groups=mesh['fsdp'=8,'ctx'=4] {'fsdp','ctx'}, dimensions={1}, use_global_device_ids=true | all-gather | bytes 8448 | tf_op jit(solution)/shard_map/all_gather | solution.py:49
  516.8 2.7 copy.83
  521.8 2.7 select_reduce_fusion.2
  528.5 25.3 all-gather.55.cloned.1.call-done
  556.2 76.8 %all-gather.57.cloned.1.call-done = bf16[1,1024,4096]{2,1,0:T(8,128)(2,1)} async-done(((bf16[1,32,4096]{2,1,0:T(8,128)(2,1)}), bf16[1,1024,4096]{2,1,0:T(8,128)(2,1)}) %all-gather.57.cloned.1.call-update) | async-done | bytes 8388624 | tf_op jit(solution)/shard_map/all_gather | solution.py:48
  633.1 6.1 fusion.61
  639.1 72.7 %all-gather.59.cloned.1.call-done = bf16[1,4096,1024]{2,1,0:T(8,128)(2,1)} async-done(((bf16[1,128,1024]{2,1,0:T(8,128)(2,1)}), bf16[1,4096,1024]{2,1,0:T(8,128)(2,1)}) %all-gather.59.cloned.1.call-update) | async-done | bytes 8388624 | tf_op jit(solution)/shard_map/all_gather | solution.py:50
  711.9 8.4 convert_reduce_fusion
  720.3 3.6 multiply_reduce_fusion
  727.0 114.9 %while.50 = (s32[]{:T(128)}, f32[128,16,64]{0,2,1:T(8,128)}, bf16[128,1024]{0,1:T(8,128)(2,1)}, bf16[128,1024]{0,1:T(8,128)(2,1)}, f32[128,1024]{0,1:T(8,128)}, ...) while((s32[]{:T(128)}, f32[128,16,64]{0,2,1:T(8,128)}, ...), condition=%wide.region_19.22_spmd.clone, body=%wide.region_17.21_spmd.clone.sunk | while | flops 171812016 | bytes 22476992 | solution.py:245
  742.1 8.3 collective-permute-done.2
  752.2 3.2 collective-permute-done.3
  767.1 3.7 collective-permute-start.3
  770.8 2.3 fusion.318
  773.1 7.4 collective-permute-done.2
  795.7 4.3 collective-permute-start.3
  800.0 2.3 fusion.318
  802.3 7.4 collective-permute-done.2
  823.9 4.3 collective-permute-start.3
  828.2 2.3 fusion.318
  830.5 6.7 collective-permute-done.2
  846.7 5.8 multiply_reduce_fusion.2
  854.1 8.1 convert_reduce_fusion.1
  863.1 3.6 multiply_reduce_fusion.1
  869.9 100.0 %while.51 = (s32[]{:T(128)}, f32[128,16,64]{0,2,1:T(8,128)}, bf16[128,1024]{0,1:T(8,128)(2,1)}, bf16[128,1024]{0,1:T(8,128)(2,1)}, f32[128,1024]{0,1:T(8,128)S(1...) while((s32[]{:T(128)}, f32[128,16,64]{0,2,1:T(8,128)}, ...), condition=%wide.region_27.30_spmd.clone, body=%wide.region_25.29_spmd.clone.sunk | while | flops 171812016 | bytes 18282632 | solution.py:245
  879.4 4.3 collective-permute-start.7
  884.9 7.0 collective-permute-done.6
  905.0 4.3 collective-permute-start.7
  911.6 5.0 collective-permute-done.6
  930.1 3.9 collective-permute-start.7
  936.3 5.0 collective-permute-done.6
  954.9 3.9 collective-permute-start.7
  961.0 5.0 collective-permute-done.6
  972.9 5.8 fusion.217
  980.8 2.7 fusion.177
  984.6 2.7 fusion.180
  987.4 6.6 fusion.208
  995.2 6.5 fusion.213
  1003.0 8.2 fusion.216
  1012.4 8.2 fusion.215
  1022.4 8.2 fusion.201
  1032.1 9.1 fusion.173
  1044.1 5.7 fusion.151
  1049.8 60.4 %all-reduce.34.cloned.1.call-done = (f32[1024]{0:T(1024)}, f32[1024]{0:T(1024)}, f32[1024]{0:T(1024)}, f32[1024]{0:T(1024)}, f32[2048]{0:T(1024)}, /*index=5*/f3...) async-done(((f32[1024]{0:T(1024)}, f32[1024]{0:T(1024)}, ...) | async-done | bytes 98320
  1120.9 141.4 %reduce-scatter.15.cloned.1.call-done = f32[32,1024]{1,0:T(8,128)} async-done(((f32[1024,1024]{1,0:T(8,128)}), f32[32,1024]{1,0:T(8,128)}) %reduce-scatter.15.cloned.1.call-update) | async-done | bytes 131088 | tf_op jit(solution)/shard_map/reduce_scatter | solution.py:78
  1262.4 149.4 %reduce-scatter.13.cloned.1.call-done = f32[32,1024]{1,0:T(8,128)} async-done(((f32[1024,1024]{1,0:T(8,128)}), f32[32,1024]{1,0:T(8,128)}) %reduce-scatter.13.cloned.1.call-update) | async-done | bytes 131088 | tf_op jit(solution)/shard_map/reduce_scatter | solution.py:78
  1413.5 158.4 %reduce-scatter.9.cloned.1.call-done = f32[32,3072]{1,0:T(8,128)} async-done(((f32[1024,3072]{1,0:T(8,128)}), f32[32,3072]{1,0:T(8,128)}) %reduce-scatter.9.cloned.1.call-update) | async-done | bytes 393232 | tf_op jit(solution)/shard_map/reduce_scatter | solution.py:76
  1571.9 161.7 %reduce-scatter.11.cloned.1.call-done = f32[32,3072]{1,0:T(8,128)} async-done(((f32[1024,3072]{1,0:T(8,128)}), f32[32,3072]{1,0:T(8,128)}) %reduce-scatter.11.cloned.1.call-update) | async-done | bytes 393232 | tf_op jit(solution)/shard_map/reduce_scatter | solution.py:76
  1735.7 362.6 %reduce-scatter.19.cloned.1.call-done = f32[32,4096]{1,0:T(8,128)} async-done(((f32[1024,4096]{1,0:T(8,128)}), f32[32,4096]{1,0:T(8,128)}) %reduce-scatter.19.cloned.1.call-update) | async-done | bytes 524304 | tf_op jit(solution)/shard_map/reduce_scatter | solution.py:82
  2098.3 364.4 %reduce-scatter.17.cloned.1.call-done = f32[32,4096]{1,0:T(8,128)} async-done(((f32[1024,4096]{1,0:T(8,128)}), f32[32,4096]{1,0:T(8,128)}) %reduce-scatter.17.cloned.1.call-update) | async-done | bytes 524304 | tf_op jit(solution)/shard_map/reduce_scatter | solution.py:82
  2465.0 362.1 %reduce-scatter.21.cloned.1.call-done = f32[128,1024]{1,0:T(8,128)} async-done(((f32[4096,1024]{1,0:T(8,128)}), f32[128,1024]{1,0:T(8,128)}) %reduce-scatter.21.cloned.1.call-update) | async-done | bytes 524304 | tf_op jit(solution)/shard_map/reduce_scatter | solution.py:84
  2827.1 364.5 %reduce-scatter.23.cloned.1.call-done = f32[128,1024]{1,0:T(8,128)} async-done(((f32[4096,1024]{1,0:T(8,128)}), f32[128,1024]{1,0:T(8,128)}) %reduce-scatter.23.cloned.1.call-update) | async-done | bytes 524304 | tf_op jit(solution)/shard_map/reduce_scatter | solution.py:84
  (605 shorter events, 234.7 us)
Async XLA Ops:
  7.2 75.9 %all-gather.45.cloned.1.call-start = ((), (), s32[]{:S(2)}) async-start(), calls=%async_computation.20 | async-start | bytes 6488064 | tf_op jit(solution)/shard_map/all_gather | solution.py:42
  9.0 156.2 %all-gather.39.cloned.1.call-start = ((), (), s32[]{:S(2)}) async-start(), calls=%async_computation.9 | async-start | bytes 1310720 | tf_op jit(solution)/shard_map/all_gather | solution.py:128
  88.0 78.7 %all-gather.37.cloned.1.call-start = ((), (), s32[]{:S(2)}) async-start(), calls=%async_computation.8 | async-start | bytes 1310720 | tf_op jit(solution)/shard_map/all_gather | solution.py:129
  88.7 115.0 %all-gather.47.cloned.1.call-start = ((), (), s32[]{:S(2)}) async-start(), calls=%async_computation.21 | async-start | bytes 2162688 | tf_op jit(solution)/shard_map/all_gather | solution.py:44
  89.5 193.9 %all-gather.49.cloned.1.call-start = ((), (), s32[]{:S(2)}) async-start(), calls=%async_computation.22 | async-start | bytes 8650752 | tf_op jit(solution)/shard_map/all_gather | solution.py:48
  90.4 272.3 %all-gather.51.cloned.1.call-start = ((), (), s32[]{:S(2)}) async-start(), calls=%async_computation.23 | async-start | bytes 8650752 | tf_op jit(solution)/shard_map/all_gather | solution.py:50
  91.3 343.1 %all-gather.53.cloned.1.call-start = ((), (), s32[]{:S(2)}) async-start(), calls=%async_computation.24 | async-start | bytes 6488064 | tf_op jit(solution)/shard_map/all_gather | solution.py:42
  92.0 424.8 %all-gather.43.cloned.1.call-start = ((), (), s32[]{:S(2)}) async-start(), calls=%async_computation.11 | async-start | bytes 1310720 | tf_op jit(solution)/shard_map/all_gather | solution.py:128
  173.6 338.1 %copy-start.20 = (f32[128,16,64]{0,2,1:T(8,128)}, f32[128,16,64]{0,2,1:T(8,128)S(1)}, u32[]{:S(2)}) copy-start(f32[128,16,64]{0,2,1:T(8,128)S(1)} %fusion.157) | copy-start | bytes 1572868
  205.9 83.5 %copy-start.53 = (f32[128]{0:T(128)}, f32[128]{0:T(128)S(1)}, u32[]{:S(2)}) copy-start(f32[128]{0:T(128)S(1)} %broadcast_multiply_fusion.2) | copy-start | bytes 1540
  206.1 77.3 %copy-start.78 = (f32[128]{0:T(128)}, f32[128]{0:T(128)S(1)}, u32[]{:S(2)}) copy-start(f32[128]{0:T(128)S(1)} %multiply_reduce_fusion.8) | copy-start | bytes 1540
  206.1 83.3 %copy-start.57 = (f32[128]{0:T(128)}, f32[128]{0:T(128)S(1)}, u32[]{:S(2)}) copy-start(f32[128]{0:T(128)S(1)} %fusion.198) | copy-start | bytes 1540
  283.4 79.4 %copy-start.65 = (f32[1024]{0:T(1024)S(1)}, f32[1024]{0:T(1024)}, u32[]{:S(2)}) copy-start(f32[1024]{0:T(1024)} %convert_element_type.417) | copy-start | bytes 12292
  368.4 185.4 %copy-start.6 = (f32[128,1024]{1,0:T(8,128)}, f32[128,1024]{1,0:T(8,128)S(1)}, u32[]{:S(2)}) copy-start(f32[128,1024]{1,0:T(8,128)S(1)} %get-tuple-element.1271) | copy-start | bytes 1572868
  368.4 69.8 %copy-start.60 = (f32[128]{0:T(128)}, f32[128]{0:T(128)S(1)}, u32[]{:S(2)}) copy-start(f32[128]{0:T(128)S(1)} %broadcast_multiply_fusion.1) | copy-start | bytes 1540
  438.3 74.4 %copy-start.50 = (f32[16,128]{1,0:T(8,128)S(1)}, f32[16,128]{1,0:T(8,128)}, u32[]{:S(2)}) copy-start(f32[16,128]{1,0:T(8,128)} %copy-done.49) | copy-start | bytes 24580
  439.2 74.1 %copy-start.41 = (bf16[128,1024]{1,0:T(8,128)(2,1)S(1)}, bf16[128,1024]{1,0:T(8,128)(2,1)}, u32[]{:S(2)}) copy-start(bf16[128,1024]{1,0:T(8,128)(2,1)} %get-tuple-element.1229) | copy-start | bytes 786436
  439.2 75.0 %copy-start.40 = (bf16[128,1024]{1,0:T(8,128)(2,1)S(1)}, bf16[128,1024]{1,0:T(8,128)(2,1)}, u32[]{:S(2)}) copy-start(bf16[128,1024]{1,0:T(8,128)(2,1)} %get-tuple-element.1231) | copy-start | bytes 786436
  439.2 80.2 %all-gather.41.cloned.1.call-start = ((), (), s32[]{:S(2)}) async-start(), calls=%async_computation.10 | async-start | bytes 1310720 | tf_op jit(solution)/shard_map/all_gather | solution.py:129
  440.0 113.9 %all-gather.55.cloned.1.call-start = ((), (), s32[]{:S(2)}) async-start(), calls=%async_computation.25 | async-start | bytes 2162688 | tf_op jit(solution)/shard_map/all_gather | solution.py:44
  440.6 192.5 %all-gather.57.cloned.1.call-start = ((), (), s32[]{:S(2)}) async-start(), calls=%async_computation.26 | async-start | bytes 8650752 | tf_op jit(solution)/shard_map/all_gather | solution.py:48
  441.3 270.6 %all-gather.59.cloned.1.call-start = ((), (), s32[]{:S(2)}) async-start(), calls=%async_computation.27 | async-start | bytes 8650752 | tf_op jit(solution)/shard_map/all_gather | solution.py:50
  441.9 668.4 %all-reduce.34.cloned.1.call-start = ((), (), s32[]{:S(2)}) async-start(), calls=%async_computation.28 | async-start | bytes 196608
  633.0 78.8 %copy-start.28 = (bf16[1,128,1024]{2,1,0:T(8,128)(2,1)S(1)}, bf16[1,128,1024]{2,1,0:T(8,128)(2,1)}, u32[]{:S(2)}) copy-start(bf16[1,128,1024]{2,1,0:T(8,128)(2,1)} %param.39) | copy-start | bytes 786436
  728.1 29.0 collective-permute-start
  730.6 26.6 collective-permute-start.1
  737.3 13.1 collective-permute-start.2
  738.9 16.4 collective-permute-start.3
  758.1 28.2 collective-permute-start
  759.0 27.2 collective-permute-start.1
  765.5 15.0 collective-permute-start.2
  767.1 17.4 collective-permute-start.3
  787.2 27.3 collective-permute-start
  788.2 26.3 collective-permute-start.1
  794.0 15.6 collective-permute-start.2
  795.7 17.1 collective-permute-start.3
  815.5 26.4 collective-permute-start
  816.4 25.4 collective-permute-start.1
  822.2 15.0 collective-permute-start.2
  823.9 16.1 collective-permute-start.3
  871.0 24.6 collective-permute-start.4
  872.0 23.7 collective-permute-start.5
  877.7 14.2 collective-permute-start.6
  879.4 15.3 collective-permute-start.7
  896.7 23.7 collective-permute-start.4
  897.6 22.8 collective-permute-start.5
  903.3 13.3 collective-permute-start.6
  905.0 14.4 collective-permute-start.7
  921.4 23.8 collective-permute-start.4
  922.3 22.8 collective-permute-start.5
  928.0 13.3 collective-permute-start.6
  930.1 14.1 collective-permute-start.7
  946.1 23.8 collective-permute-start.4
  947.1 22.8 collective-permute-start.5
  952.8 13.3 collective-permute-start.6
  954.9 14.0 collective-permute-start.7
  980.7 281.6 %reduce-scatter.15.cloned.1.call-start = ((), (), s32[]{:S(2)}) async-start(), calls=%async_computation.15 | async-start | bytes 4325376 | tf_op jit(solution)/shard_map/reduce_scatter | solution.py:78
  983.5 428.3 %reduce-scatter.13.cloned.1.call-start = ((), (), s32[]{:S(2)}) async-start(), calls=%async_computation.14 | async-start | bytes 4325376 | tf_op jit(solution)/shard_map/reduce_scatter | solution.py:78
  987.4 584.6 %reduce-scatter.9.cloned.1.call-start = ((), (), s32[]{:S(2)}) async-start(), calls=%async_computation.12 | async-start | bytes 12976128 | tf_op jit(solution)/shard_map/reduce_scatter | solution.py:76
  994.0 739.7 %reduce-scatter.11.cloned.1.call-start = ((), (), s32[]{:S(2)}) async-start(), calls=%async_computation.13 | async-start | bytes 12976128 | tf_op jit(solution)/shard_map/reduce_scatter | solution.py:76
  1001.8 1096.5 %reduce-scatter.19.cloned.1.call-start = ((), (), s32[]{:S(2)}) async-start(), calls=%async_computation.17 | async-start | bytes 17301504 | tf_op jit(solution)/shard_map/reduce_scatter | solution.py:82
  1011.2 1451.5 %reduce-scatter.17.cloned.1.call-start = ((), (), s32[]{:S(2)}) async-start(), calls=%async_computation.16 | async-start | bytes 17301504 | tf_op jit(solution)/shard_map/reduce_scatter | solution.py:82
  1020.7 1806.4 %reduce-scatter.21.cloned.1.call-start = ((), (), s32[]{:S(2)}) async-start(), calls=%async_computation.18 | async-start | bytes 17301504 | tf_op jit(solution)/shard_map/reduce_scatter | solution.py:84
  1030.6 2161.0 %reduce-scatter.23.cloned.1.call-start = ((), (), s32[]{:S(2)}) async-start(), calls=%async_computation.19 | async-start | bytes 17301504 | tf_op jit(solution)/shard_map/reduce_scatter | solution.py:84
  (79 other events, 533.4 us)
Sparse Core Ops, SparseCore 0:
  11.5 71.5 all-gather.44
  88.1 26.5 all-gather.38
  116.8 27.5 all-gather.36
  147.7 55.9 all-gather.46
  207.1 76.2 all-gather.48
  286.7 75.9 all-gather.50
  366.2 68.1 all-gather.52
  439.3 26.5 all-gather.42
  467.5 27.5 all-gather.40
  497.8 55.9 all-gather.54
  556.8 76.2 all-gather.56
  635.8 75.9 all-gather.58
  980.9 129.3 all-reduce.33
  1113.9 148.4 reduce-scatter.14
  1264.5 147.2 reduce-scatter.12
  1417.7 154.1 reduce-scatter.8
  1578.8 154.7 reduce-scatter.10
  1735.8 362.4 reduce-scatter.18
  2100.6 362.1 reduce-scatter.16
  2464.9 362.1 reduce-scatter.20
  2829.4 362.1 reduce-scatter.22
where the time goes:
time: 3210 us; the launch traced here: 3200 us
  waiting for transfers between devices  2630 us (82%)
  matrix products  177 us (6%)
  blocking collectives  174 us (5%)
  local copies, waits for them, and re-layouts  91.2 us (3%)
  other arithmetic  72.6 us (2%)
  starting transfers between devices  40.9 us (1%)
    reduce_scatter x2, waiting for transfers between devices, send_layer(): lax.psum_scatter(grads[8], ('fsdp', 'ctx'), scatter_dimension=0, tiled=True)  727 us
    reduce_scatter x2, waiting for transfers between devices, send_layer(): lax.psum_scatter(grads[10], ('fsdp', 'ctx'), scatter_dimension=0, tiled=T...  727 us
    reduce_scatter x2, waiting for transfers between devices, send_layer(): lax.psum_scatter(grads[2], ('fsdp', 'ctx'), scatter_dimension=0, tiled=True)  320 us
    reduce_scatter x2, waiting for transfers between devices, send_layer(): lax.psum_scatter(grads[4], ('fsdp', 'ctx'), scatter_dimension=0, tiled=True)  291 us
    all_gather x2, waiting for transfers between devices, fetch_forward(): lax.all_gather(shards[8], ('fsdp', 'ctx'), axis=0, tiled=True)  154 us
    all_gather x2, waiting for transfers between devices, fetch_forward(): lax.all_gather(shards[10], ('fsdp', 'ctx'), axis=0, tiled=True)  146 us
    all_gather x2, blocking collectives, fetch_forward(): lax.all_gather(shards[9], ('fsdp', 'ctx'), axis=0, tiled=True)  131 us
    all_gather x2, waiting for transfers between devices, fetch_forward(): lax.all_gather(shards[2], ('fsdp', 'ctx'), axis=0, tiled=True)  76.9 us
  transfers between devices with their start and end apart: 53, of which 33 were waited for; matrix products, arithmetic and copies ran while one was open for 8% of the time, Pallas kernels for 0%

commit v1 on v0

v1 whole, which is shorter than its diff:
```python
import jax
import jax.numpy as jnp
from jax import lax
from jax.sharding import Mesh, PartitionSpec as P

HEADS = 16
EPSILON = 1e-05
BF = jnp.bfloat16
F32 = jnp.float32
AXES = ("y", "x", "core", "zh", "zl")


def here(axis):
    return lax.axis_index(axis)


def swap(value, axis):
    return lax.ppermute(value, axis, [(0, 1), (1, 0)])


def ordered(mine, other, axis):
    first = here(axis) == 0
    return jnp.stack([jnp.where(first, mine, other), jnp.where(first, other, mine)])


def pick(value, axis):
    return lax.dynamic_index_in_dim(value, here(axis), 0, keepdims=False)


def pick_other(value, axis):
    return lax.dynamic_index_in_dim(value, 1 - here(axis), 0, keepdims=False)


def trade(value, axis):
    if lax.axis_size(axis) == 2:
        return ordered(pick(value, axis), swap(pick_other(value, axis), axis), axis)
    return lax.all_to_all(value, axis, 0, 0, tiled=True)


def collect(value, axis):
    if lax.axis_size(axis) == 2:
        return ordered(value, swap(value, axis), axis)
    return lax.all_gather(value, axis, axis=0, tiled=False)


def reduce_to(value, axis):
    if lax.axis_size(axis) == 2:
        return pick(value, axis) + swap(pick_other(value, axis), axis)
    return lax.psum_scatter(value, axis, scatter_dimension=0, tiled=False)


def flipped(value, axis, dim):
    return jnp.where(here(axis) == 0, value, jnp.flip(value, dim))


def gather_shards(shard):
    if lax.axis_size("y") != 2:
        return lax.all_gather(shard, ("y", "x", "zh"), axis=0, tiled=False)
    far = swap(shard, "zh")
    near_x = swap(shard, "x")
    far_y = swap(far, "y")
    near_y = swap(shard, "y")
    near_xy = swap(near_x, "y")
    far_x = swap(far, "x")
    far_yx = swap(far_y, "x")
    rel = jnp.stack([shard, far, near_x, far_x, near_y, far_y, near_xy, far_yx])
    rel = rel.reshape((2, 2, 2) + shard.shape)
    rel = flipped(flipped(flipped(rel, "y", 0), "x", 1), "zh", 2)
    return rel.reshape((8,) + shard.shape)


def scatter_shards(grads):
    shape = grads.shape[1:]
    if lax.axis_size("y") != 2:
        return lax.psum_scatter(
            grads, ("y", "x", "zh"), scatter_dimension=0, tiled=False
        )
    rel = grads.reshape((2, 2, 2) + shape)
    rel = flipped(flipped(flipped(rel, "y", 0), "x", 1), "zh", 2)
    near, far = rel[:, :, 0], rel[:, :, 1]
    far = far[:, 0] + swap(far[:, 1].astype(BF), "x").astype(F32)
    near = near[0] + swap(near[1].astype(BF), "y").astype(F32)
    far = far[0] + swap(far[1].astype(BF), "y").astype(F32)
    near = near[0] + swap(near[1].astype(BF), "x").astype(F32)
    return near + swap(far.astype(BF), "zh").astype(F32)


def corner_turn(value):
    return lax.ppermute(value, ("core", "zh"), [(0, 0), (1, 2), (2, 1), (3, 3)])


def norm_rows(values, gain, shift):
    row_mean = jnp.mean(values, axis=-1, keepdims=True)
    centred = values - row_mean
    row_var = jnp.mean(centred * centred, axis=-1, keepdims=True)
    return centred * lax.rsqrt(row_var + EPSILON) * gain + shift


def gelu_tanh(values):
    return jax.nn.gelu(values, approximate=True)


def dot(left, right):
    return jnp.dot(left, right, preferred_element_type=F32)


def dot_t(left, matrix):
    return lax.dot_general(
        left, matrix, (((1,), (1,)), ((), ())), preferred_element_type=F32
    )


def outer_sum(left, right):
    return jnp.einsum("td,te->de", left, right, preferred_element_type=F32)


def body(
    tokens,
    segment_ids,
    group_order,
    ln1_gain,
    ln1_bias,
    qkv_weight,
    qv_bias,
    out_weight,
    out_bias,
    ln2_gain,
    ln2_bias,
    up_weight,
    up_bias,
    down_weight,
    down_bias,
    cotangent,
):
    ny, nx, nc, nzh, nzl = (lax.axis_size(a) for a in AXES)
    chips = ny * nx
    span = chips // nzl
    layers, width = ln1_gain.shape[0], tokens.shape[2]
    hidden = up_weight.shape[2]
    group = tokens.shape[1]
    ctx_count = nzh * nzl
    rank_width = width // (nc * nzl)
    rank_hidden = hidden // (nc * nzl)
    head_size = width // HEADS
    rank_heads = rank_width // head_size
    quarter = width // (chips * nc)
    unit = width // (chips * nc * nzh)
    core_rows = nzl * group
    rows = nc * core_rows
    scale = head_size ** (-0.5)

    def inner(value):
        shape = value.shape
        value = value.reshape(shape[:-1] + (chips, 2, 2, unit))
        return jnp.swapaxes(value, -3, -2).reshape(shape)

    small = (ln1_gain, ln1_bias, out_bias, ln2_gain, ln2_bias, down_bias)
    small_all = small + (qv_bias, up_bias)
    packed = jnp.concatenate([v.reshape(-1) for v in small_all])
    for axis in reversed(AXES):
        packed = collect(packed, axis)
    vectors = []
    at = 0
    for v in small_all:
        size = v.shape[0] * v.shape[1]
        part = packed[..., at : at + size].reshape((ny, nx, nc, nzh, nzl) + v.shape)
        part = jnp.moveaxis(part, 5, 0)
        vectors.append(part.reshape(layers, -1).astype(F32))
        at += size
    vec = [inner(v) for v in vectors[:6]]
    full_qv, full_up = vectors[6], vectors[7]

    def rank_columns(value):
        shape = value.shape[:-1]
        value = value.reshape(shape + (nzl, span, nc, quarter))
        value = lax.dynamic_index_in_dim(value, here("zl"), len(shape), keepdims=False)
        value = lax.dynamic_index_in_dim(value, here("core"), len(shape) + 1, keepdims=False)
        return value.reshape(shape + (rank_width,))

    q_bias = rank_columns(full_qv[:, :width])
    v_bias = rank_columns(full_qv[:, width:])
    qkv_bias = jnp.concatenate([q_bias, jnp.zeros_like(q_bias), v_bias], axis=1)
    up_b = full_up.reshape(layers, chips, nc, nzh, nzl, -1)
    up_b = lax.dynamic_index_in_dim(up_b, here("zl"), 4, keepdims=False)
    up_b = lax.dynamic_index_in_dim(up_b, here("core"), 2, keepdims=False)
    up_b = up_b.reshape(layers, rank_hidden)

    def to_ranks(value):
        value = trade(value, "core")
        return jnp.swapaxes(trade(jnp.swapaxes(value, 0, 1), "zl"), 0, 1)

    def fetch(layer):
        w = qkv_weight[layer]
        n = w.shape[0]
        w = w.reshape(n, 3, nzl, span, nc, quarter)
        w = jnp.transpose(w, (4, 2, 0, 1, 3, 5)).reshape(nc, nzl, n, 3 * rank_width)
        w_qkv = gather_shards(to_ranks(w).reshape(-1, 3 * rank_width))
        w = gather_shards(inner(out_weight[layer]))
        w = trade(w.reshape(nzl, span, nzh, n, width), "zl")
        w_out = jnp.transpose(w, (1, 2, 0, 3, 4)).reshape(rank_width, width)
        w = up_weight[layer].reshape(n, chips, nc, nzh, nzl, -1)
        w = jnp.transpose(w, (2, 4, 0, 1, 3, 5)).reshape(nc, nzl, n, rank_hidden)
        w_up = gather_shards(to_ranks(w).reshape(-1, rank_hidden))
        w_down = gather_shards(inner(down_weight[layer]))
        return (
            w_qkv.reshape(width, 3 * rank_width),
            w_out,
            w_up.reshape(width, rank_hidden),
            w_down.reshape(rank_hidden, width),
        )

    def from_ranks(value):
        value = jnp.swapaxes(trade(jnp.swapaxes(value, 0, 1), "zl"), 0, 1)
        return trade(value, "core")

    def send(grads):
        g_qkv, g_out, g_up, g_down = grads
        n = width // (chips * 2 * ctx_count)
        g = scatter_shards(g_qkv.reshape(chips * nzh, -1, 3 * rank_width))
        g = from_ranks(g.astype(BF).reshape(nc, nzl, n, 3 * rank_width)).astype(F32)
        g = g.reshape(nc, nzl, n, 3, span, quarter)
        d_qkv = jnp.transpose(g, (2, 3, 1, 4, 0, 5)).reshape(n, 3 * width)
        g = g_out.astype(BF).reshape(span, nzh, nzl, n, width)
        g = trade(jnp.transpose(g, (2, 0, 1, 3, 4)), "zl").astype(F32)
        d_out = inner(scatter_shards(g.reshape(chips * nzh, n, width)))
        g = scatter_shards(g_up.reshape(chips * nzh, -1, rank_hidden))
        g = from_ranks(g.astype(BF).reshape(nc, nzl, n, rank_hidden)).astype(F32)
        g = g.reshape(nc, nzl, n, chips, nzh, -1)
        d_up = jnp.transpose(g, (2, 3, 0, 4, 1, 5)).reshape(n, hidden)
        d_down = inner(scatter_shards(g_down.reshape(chips * nzh, -1, width)))
        return d_qkv, d_out, d_up, d_down

    def own_columns(value, mine):
        value = inner(value).reshape(ny, nx, nc, nzh, nzl, -1)
        keep = jnp.arange(nzl)[:, None] == here("zl")
        return jnp.where(keep, value, 0.0)

    def send_small(sums):
        g1, b1, gqv, bo, g2, b2, bu, bd = sums
        parts = [own_columns(v, None) for v in (g1, b1, bo, g2, b2, bd)]

        def placed(value):
            value = value.reshape(1, span, 1, quarter)
            keep = (jnp.arange(nzl)[:, None, None, None] == here("zl")) & (
                jnp.arange(nc)[None, None, :, None] == here("core")
            )
            return jnp.where(keep, value, 0.0).reshape(width)

        qv = jnp.concatenate([placed(gqv[0]), placed(gqv[1])])
        parts.append(qv.reshape(ny, nx, nc, nzh, nzl, -1))
        up = bu.reshape(ny, nx, 1, nzh, 1, -1)
        keep = (jnp.arange(nzl)[:, None] == here("zl")) & (
            jnp.arange(nc)[:, None, None, None] == here("core")
        )
        parts.append(jnp.where(keep, up, 0.0))
        value = jnp.concatenate(parts, axis=-1)
        for axis in AXES:
            value = reduce_to(value, axis)
        sizes = [p.shape[-1] for p in parts]
        cut, at = [], 0
        for s in sizes:
            cut.append(value[at : at + s])
            at += s
        g1, b1, bo, g2, b2, bd, qv, up = cut
        return g1, b1, qv, bo, g2, b2, up, bd

    def place(value):
        return collect(inner(corner_turn(value)), "zl").reshape(core_rows, width)

    def both_cores(value):
        return collect(value, "core").reshape(rows, -1)

    def total(partial):
        part = partial.reshape(nc, core_rows, width)
        part = pick(part, "core") + swap(pick_other(part, "core").astype(BF), "core").astype(F32)
        if nzl == 2:
            return part + swap(part.astype(BF), "zl").astype(F32)
        return lax.psum(part, "zl")

    seg = collect(segment_ids[0], "core")
    seg = lax.dynamic_index_in_dim(seg, here("zh"), 0, keepdims=False)
    half = group // 2
    block = jnp.stack([group_order, 2 * ctx_count - 1 - group_order], axis=1)
    pos = (block[:, :, None] * half + jnp.arange(half, dtype=jnp.int32)).reshape(rows)
    row_seg = jnp.take(seg, pos)
    distance = pos[:, None] - pos[None, :]
    allowed = (distance >= 0) & (row_seg[:, None] == row_seg[None, :])
    distance = distance.astype(F32)
    head_no = jnp.arange(rank_heads)
    head_no = (
        (here("zl") * span + head_no // (quarter // head_size)) * nc + here("core")
    ) * (quarter // head_size) + head_no % (quarter // head_size)
    slopes = jnp.exp2(-8.0 * (head_no.astype(F32) + 1.0) / HEADS)

    def scores_of(q, k):
        s = jnp.einsum("qhd,khd->hqk", q, k, preferred_element_type=F32) * scale
        return s - slopes[:, None, None] * distance[None]

    def split(qkv):
        return [
            v.reshape(rows, rank_heads, head_size) for v in jnp.split(qkv, 3, axis=1)
        ]

    weights = [fetch(layer) for layer in range(layers)]
    x = place(tokens[0]).astype(F32)
    kept = []
    for layer in range(layers):
        w_qkv, w_out, w_up, w_down = weights[layer]
        g1, b1, bo, g2, b2, bd = (v[layer] for v in vec)
        h1 = both_cores(norm_rows(x, g1, b1).astype(BF))
        qkv = (dot(h1, w_qkv) + qkv_bias[layer]).astype(BF)
        q, k, v = split(qkv)
        s = jnp.where(allowed, scores_of(q, k), -1e30)
        top = jnp.max(s, axis=-1, keepdims=True)
        p = jnp.where(allowed, jnp.exp(s - top), 0.0)
        den = jnp.sum(p, axis=-1, keepdims=True)
        p = p / den
        o = jnp.einsum("hqk,khd->qhd", p.astype(BF), v, preferred_element_type=F32)
        log_total = top + jnp.log(den)
        o = o.reshape(rows, rank_width).astype(BF)
        x1 = x + total(dot(o, w_out)) + bo
        h2 = both_cores(norm_rows(x1, g2, b2).astype(BF))
        u = dot(h2, w_up) + up_b[layer]
        a = gelu_tanh(u).astype(BF)
        x2 = x1 + total(dot(a, w_down)) + bd
        kept.append((x, h1, qkv, log_total, o, x1, h2, u, a))
        x = x2

    def leave(value):
        mine = lax.dynamic_index_in_dim(
            value.reshape(nzl, group, width), here("zl"), 0, keepdims=False
        )
        return corner_turn(inner(mine))[None]

    final_rows = leave(x.astype(BF))

    gx = place(cotangent[0]).astype(F32)
    result = [None] * layers
    for layer in reversed(range(layers)):
        w_qkv, w_out, w_up, w_down = weights[layer]
        g1, b1, bo, g2, b2, bd = (v[layer] for v in vec)
        x, h1, qkv, log_total, o, x1, h2, u, a = kept[layer]
        gy2_mine = gx.astype(BF)
        gy2 = both_cores(gy2_mine)
        d_down = outer_sum(a, gy2)
        d_bd = jnp.sum(gy2_mine.astype(F32), axis=0)
        _, gelu_back = jax.vjp(gelu_tanh, u)
        gu = gelu_back(dot_t(gy2, w_down))[0].astype(BF)
        d_up = outer_sum(h2, gu)
        d_bu = jnp.sum(gu.astype(F32), axis=0)
        _, back = jax.vjp(norm_rows, x1, g2, b2)
        gn, d_g2, d_b2 = back(total(dot_t(gu, w_up)))
        gm = gx + gn
        gy1_mine = gm.astype(BF)
        gy1 = both_cores(gy1_mine)
        d_out = outer_sum(o, gy1)
        d_bo = jnp.sum(gy1_mine.astype(F32), axis=0)
        go_f = dot_t(gy1, w_out)
        go = go_f.astype(BF).reshape(rows, rank_heads, head_size)
        q, k, v = split(qkv)
        p = jnp.where(allowed, jnp.exp(scores_of(q, k) - log_total), 0.0)
        dp = jnp.einsum("qhd,khd->hqk", go, v, preferred_element_type=F32)
        ds = (p * (dp - jnp.sum(dp * p, axis=-1, keepdims=True))).astype(BF)
        gq = scale * jnp.einsum("hqk,khd->qhd", ds, k, preferred_element_type=F32)
        gk = scale * jnp.einsum("hqk,qhd->khd", ds, q, preferred_element_type=F32)
        gv = jnp.einsum("hqk,qhd->khd", p.astype(BF), go, preferred_element_type=F32)
        gqkv = jnp.concatenate(
            [g.reshape(rows, rank_width) for g in (gq, gk, gv)], axis=1
        ).astype(BF)
        d_qkv = outer_sum(h1, gqkv)
        sums = jnp.sum(gqkv.astype(F32), axis=0)
        _, back = jax.vjp(norm_rows, x, g1, b1)
        gn, d_g1, d_b1 = back(total(dot_t(gqkv, w_qkv)))
        gx = gm + gn
        d_qv = (sums[:rank_width], sums[2 * rank_width :])
        big = send((d_qkv, d_out, d_up, d_down))
        tiny = send_small((d_g1, d_b1, d_qv, d_bo, d_g2, d_b2, d_bu, d_bd))
        result[layer] = (
            tiny[0], tiny[1], big[0], tiny[2], big[1], tiny[3],
            tiny[4], tiny[5], big[2], tiny[6], big[3], tiny[7],
        )
    stacked = [jnp.stack([result[layer][i] for layer in range(layers)]) for i in range(12)]
    return (final_rows, leave(gx)) + tuple(stacked)


def solution(mesh):
    fsdp, ctx = mesh.shape["fsdp"], mesh.shape["ctx"]
    fine = Mesh(mesh.devices.reshape(fsdp // 4, 2, 2, 2, ctx // 2), AXES)
    stream, place = ("y", "x", "core"), ("zh", "zl")
    rows = P(stream, place, None)
    flat, deep = P(None, AXES), P(None, AXES, None)
    params = (flat, flat, deep, flat, deep, flat, flat, flat, deep, flat, deep, flat)
    in_specs = (rows, P(stream, None), P()) + params + (rows,)
    out_specs = (rows, rows) + params
    return jax.shard_map(body, mesh=fine, in_specs=in_specs, out_specs=out_specs, check_vma=False)
```

time: 3210 us -> 896 us (0.28)
  waiting for transfers between devices: 2630 us -> 302 us
  blocking collectives: 174 us -> 0 us
  local copies, waits for them, and re-layouts: 91.2 us -> 227 us
  starting transfers between devices: 40.9 us -> 170 us
  matrix products: 177 us -> 60.5 us
  other arithmetic: 72.6 us -> 119 us
    reduce_scatter x8 -> x0, waiting for transfers between devices: 2060 us -> none  [the longest x2 727 us: send_layer(): lax.psum_scatter(grads[8], ('fsdp', 'ctx'), scatter_dimension=0, tiled=True)]
    all_gather x12 -> x0, waiting for transfers between devices: 432 us -> none  [the longest x2 154 us: fetch_forward(): lax.all_gather(shards[8], ('fsdp', 'ctx'), axis=0, tiled=True)]
    ppermute x32 -> x162, waiting for transfers between devices: 66.9 us -> 302 us  [the longest x158 302 us: swap(): return lax.ppermute(value, axis, [(0, 1), (1, 0)])]
    all_gather x2 -> x0, blocking collectives: 131 us -> none  [fetch_forward(): lax.all_gather(shards[9], ('fsdp', 'ctx'), axis=0, tiled=True)]
    ppermute x32 -> x162, starting transfers between devices: 39.5 us -> 170 us  [the longest x158 163 us: swap(): return lax.ppermute(value, axis, [(0, 1), (1, 0)])]
    dot_general x68 -> x36, matrix products: 177 us -> 60.5 us  [the longest x8 15.8 us: dot_t(): lax.dot_general(left, matrix, (((1,), (1,)), ((), ())), preferred_element...]
    unnamed x22 -> x0, waiting for transfers between devices: 64.5 us -> none
    unnamed x203 -> x427, local copies, waits for them, and re-layouts: 35.3 us -> 79.3 us
  transfers between devices with their start and end apart: 53 -> 162, of which waited for: 33 -> 78; matrix products, arithmetic and copies ran while one was open for 8% -> 32% of each run, Pallas kernels for 0% -> 0%
where the time goes in v1:
time: 896 us; the launch traced here: 884 us
  waiting for transfers between devices  302 us (34%)
  local copies, waits for them, and re-layouts  227 us (25%)
  starting transfers between devices  170 us (19%)
  other arithmetic  119 us (13%)
  matrix products  60.5 us (7%)
    ppermute x158, waiting for transfers between devices, swap(): return lax.ppermute(value, axis, [(0, 1), (1, 0)])  302 us
    ppermute x158, starting transfers between devices, swap(): return lax.ppermute(value, axis, [(0, 1), (1, 0)])  163 us
    unnamed x427, local copies, waits for them, and re-layouts  79.3 us
    select_n x48, other arithmetic, flipped(): return jnp.where(here(axis) == 0, value, jnp.flip(value, dim))  37.7 us
    concatenate x12, local copies, waits for them, and re-layouts, body(): jnp.concatenate([g.reshape(rows, rank_width) for g in (gq, gk, gv)], axis=1)  19.5 us
  transfers between devices with their start and end apart: 162, of which 78 were waited for; matrix products, arithmetic and copies ran while one was open for 32% of the time, Pallas kernels for 0%

profile of v1, /device:TPU:4, one launch (start us, length us, event | category | flops | bytes accessed | tf_op | source)
XLA Modules:
  0.0 883.6 jit_solution(15282970446115807720)
XLA Ops:
  33.8 3.5 collective-permute-done.3
  37.4 3.5 gather_fusion
  41.6 3.2 collective-permute-done.5
  45.7 3.0 collective-permute-done.6
  62.2 3.5 collective-permute-done.19
  74.4 3.0 collective-permute-done.20
  90.3 3.6 collective-permute-done.59
  105.0 3.7 collective-permute-done.24
  109.6 3.3 collective-permute-done.63
  113.8 3.7 collective-permute-done.9
  126.0 3.4 collective-permute-done.69
  129.4 4.9 collective-permute-done.30
  144.4 5.1 collective-permute-done.77
  150.3 7.2 collective-permute-start.10
  159.2 4.0 collective-permute-done.10
  164.9 4.1 collective-permute-done.11
  169.1 4.3 collective-permute-start.50
  174.0 6.9 collective-permute-done.50
  182.7 5.8 collective-permute-done.51
  188.5 3.0 collective-permute-start.13
  194.0 5.7 collective-permute-done.40
  203.6 2.7 collective-permute-done.42
  209.0 2.8 collective-permute-start.88
  214.1 5.0 collective-permute-done.79
  223.7 7.8 collective-permute-done.81
  235.1 3.0 collective-permute-done.82
  254.2 3.2 collective-permute-done.71
  267.4 4.1 collective-permute-done.14
  275.1 3.6 collective-permute-done.52
  288.2 2.8 collective-permute-done.44
  293.1 3.9 copy.278
  297.0 3.2 reverse_select_fusion.26
  305.1 4.2 copy.302
  309.3 3.2 reverse_select_fusion.20
  320.5 3.0 collective-permute-done.35
  328.9 2.8 collective-permute-done.72
  332.8 4.7 collective-permute-done.16
  361.5 3.9 collective-permute-start.27
  367.2 9.3 %collective-permute-done.27 = bf16[256,1024]{1,0:T(8,128)(2,1)S(1)} collective-permute-done((bf16[256,1024]{1,0:T(8,128)(2,1)S(1)}, bf16[256,1024]{1,0:T(8,128)(2,1)S(1)}, u32[]{:S(2)}, u32[]{:S(2)}) %collective-permute-start.27) | collective-permute-done | bytes 524320 | tf_op jit(solution)/shard_map/ppermute | solution.py:18
  380.5 3.0 multiply_convert_fusion.3
  392.1 11.5 %collective-permute-done.46 = bf16[256,1024]{1,0:T(8,128)(2,1)S(1)} collective-permute-done((bf16[256,1024]{1,0:T(8,128)(2,1)S(1)}, bf16[256,1024]{1,0:T(8,128)(2,1)S(1)}, u32[]{:S(2)}, u32[]{:S(2)}) %collective-permute-start.46) | collective-permute-done | bytes 524320 | tf_op jit(solution)/shard_map/ppermute | solution.py:18
  439.8 9.1 %collective-permute-done.66 = bf16[256,1024]{1,0:T(8,128)(2,1)} collective-permute-done((bf16[256,1024]{1,0:T(8,128)(2,1)}, bf16[256,1024]{1,0:T(8,128)(2,1)}, u32[]{:S(2)}, u32[]{:S(2)}) %collective-permute-start.66) | collective-permute-done | bytes 524320 | tf_op jit(solution)/shard_map/ppermute | solution.py:18
  464.2 4.7 fusion.37
  468.9 4.2 convert_reduce_fusion
  483.2 2.8 fusion.338
  500.7 8.3 collective-permute-done.145
  514.6 6.7 collective-permute-done.159
  524.7 5.4 collective-permute-done.148
  543.6 4.0 collective-permute-start.86
  547.6 6.9 collective-permute-done.149
  557.0 7.4 collective-permute-done.150
  639.1 7.0 collective-permute-done.133
  655.5 3.3 collective-permute-start.123
  659.1 7.8 collective-permute-done.123
  668.8 9.0 %collective-permute-done.124 = bf16[2,32,768]{2,1,0:T(8,128)(2,1)S(1)} collective-permute-done((bf16[2,32,768]{2,1,0:T(8,128)(2,1)S(1)}, bf16[2,32,768]{2,1,0:T(8,128)(2,1)S(1)}, u32[]{:S(2)}, u32[]{:S(2)}) %collective-permute-start.124) | collective-permute-done | bytes 98336 | tf_op jit(solution)/shard_map/ppermute | solution.py:18
  710.8 8.8 %collective-permute-done.138 = bf16[2,128,1024]{2,1,0:T(8,128)(2,1)S(1)} collective-permute-done((bf16[2,128,1024]{2,1,0:T(8,128)(2,1)S(1)}, bf16[2,128,1024]{2,1,0:T(8,128)(2,1)S(1)}, u32[]{:S(2)}, u32[]{:S(2)}) %collective-permute-start.138) | collective-permute-done | bytes 524320 | tf_op jit(solution)/shard_map/ppermute | solution.py:18
  723.1 8.6 collective-permute-done.154
  737.9 3.8 collective-permute-done.155
  747.6 9.8 %collective-permute-done.142 = bf16[128,1024]{1,0:T(8,128)(2,1)} collective-permute-done((bf16[128,1024]{1,0:T(8,128)(2,1)}, bf16[128,1024]{1,0:T(8,128)(2,1)}, u32[]{:S(2)}, u32[]{:S(2)}) %collective-permute-start.142) | collective-permute-done | bytes 262176 | tf_op jit(solution)/shard_map/ppermute | solution.py:18
  759.4 3.6 collective-permute-done.156
  806.1 6.8 collective-permute-done.127
  825.4 8.5 collective-permute-done.116
  846.6 3.2 collective-permute-done.100
  867.8 5.8 collective-permute-done.110
  (1279 shorter events, 556.7 us)
Async XLA Ops:
  2.6 92.8 %collective-permute-start.60 = (bf16[32,1024]{1,0:T(8,128)(2,1)}, bf16[32,1024]{1,0:T(8,128)(2,1)}, u32[]{:S(2)}, u32[]{:S(2)}) collective-permute-start(bf16[32,1024]{1,0:T(8,128)(2,1)} %reshape.1150), channel_id=1, source_target_pairs={{0,16},{16,0},{1,17},{17,1},{2,18},{18,2},{3,19},{19,3},{4,20},{20... | collective-permute-start | bytes 196616 | tf_op jit(solution)/shard_map/ppermute | solution.py:18
  2.6 64.7 %collective-permute-start.58 = (bf16[32,1024]{1,0:T(8,128)(2,1)}, bf16[32,1024]{1,0:T(8,128)(2,1)}, u32[]{:S(2)}, u32[]{:S(2)}) collective-permute-start(bf16[32,1024]{1,0:T(8,128)(2,1)} %reshape.1150), channel_id=1, source_target_pairs={{0,8},{8,0},{1,9},{9,1},{2,10},{10,2},{3,11},{11,3},{4,12},{12,4},... | collective-permute-start | bytes 196616 | tf_op jit(solution)/shard_map/ppermute | solution.py:18
  4.6 61.2 %collective-permute-start.57 = (bf16[32,1024]{1,0:T(8,128)(2,1)}, bf16[32,1024]{1,0:T(8,128)(2,1)}, u32[]{:S(2)}, u32[]{:S(2)}) collective-permute-start(bf16[32,1024]{1,0:T(8,128)(2,1)} %reshape.1150), channel_id=1, source_target_pairs={{0,2},{2,0},{1,3},{3,1},{4,6},{6,4},{5,7},{7,5},{8,10},{10,8},{9,1... | collective-permute-start | bytes 196616 | tf_op jit(solution)/shard_map/ppermute | solution.py:18
  13.1 17.4 %collective-permute-start.2 = (bf16[768]{0:T(1024)(128)(2,1)S(1)}, bf16[768]{0:T(1024)(128)(2,1)}, u32[]{:S(2)}, u32[]{:S(2)}) collective-permute-start(bf16[768]{0:T(1024)(128)(2,1)S(1)} %concatenate.56), channel_id=1, source_target_pairs={{0,1},{1,0},{2,3},{3,2},{4,5},{5,4},{6,7},{7,6},{8,9},{9,8},{10,11... | collective-permute-start | bytes 4616 | tf_op jit(solution)/shard_map/ppermute | solution.py:18
  14.7 18.0 %collective-permute-start.17 = (s32[512]{0:T(512)}, s32[512]{0:T(512)}, u32[]{:S(2)}, u32[]{:S(2)}) collective-permute-start(s32[512]{0:T(512)} %bitcast.1403), channel_id=1, source_target_pairs={{0,4},{4,0},{1,5},{5,1},{2,6},{6,2},{3,7},{7,3},{8,12},{12,8},{9,1... | collective-permute-start | bytes 6152 | tf_op jit(solution)/shard_map/ppermute | solution.py:18
  30.4 49.5 %collective-permute-start.21 = (bf16[32,1024]{1,0:T(8,128)(2,1)}, bf16[32,1024]{1,0:T(8,128)(2,1)}, u32[]{:S(2)}, u32[]{:S(2)}) collective-permute-start(bf16[32,1024]{1,0:T(8,128)(2,1)} %reshape.1134), channel_id=1, source_target_pairs={{0,16},{16,0},{1,17},{17,1},{2,18},{18,2},{3,19},{19,3},{4,20},{20... | collective-permute-start | bytes 196616 | tf_op jit(solution)/shard_map/ppermute | solution.py:18
  65.7 136.3 %collective-permute-start.41 = (bf16[128,1024]{0,1:T(8,128)(2,1)S(1)}, bf16[128,1024]{0,1:T(8,128)(2,1)S(1)}, u32[]{:S(2)}, u32[]{:S(2)}) collective-permute-start(bf16[128,1024]{0,1:T(8,128)(2,1)S(1)} %bitcast.1323), channel_id=1, source_target_pairs={{0,16},{16,0},{1,17},{17,1},{2,18},{18,2},{3,19},{19,3},{4,20},{20... | collective-permute-start | bytes 786440 | tf_op jit(solution)/shard_map/ppermute | solution.py:18
  65.8 70.0 %collective-permute-start.39 = (bf16[128,1024]{0,1:T(8,128)(2,1)S(1)}, bf16[128,1024]{0,1:T(8,128)(2,1)S(1)}, u32[]{:S(2)}, u32[]{:S(2)}) collective-permute-start(bf16[128,1024]{0,1:T(8,128)(2,1)S(1)} %bitcast.1324), channel_id=1, source_target_pairs={{0,8},{8,0},{1,9},{9,1},{2,10},{10,2},{3,11},{11,3},{4,12},{12,4},... | collective-permute-start | bytes 786440 | tf_op jit(solution)/shard_map/ppermute | solution.py:18
  77.3 57.0 %collective-permute-start.38 = (bf16[128,1024]{0,1:T(8,128)(2,1)S(1)}, bf16[128,1024]{0,1:T(8,128)(2,1)S(1)}, u32[]{:S(2)}, u32[]{:S(2)}) collective-permute-start(bf16[128,1024]{0,1:T(8,128)(2,1)S(1)} %bitcast.1325), channel_id=1, source_target_pairs={{0,2},{2,0},{1,3},{3,1},{4,6},{6,4},{5,7},{7,5},{8,10},{10,8},{9,1... | collective-permute-start | bytes 786440 | tf_op jit(solution)/shard_map/ppermute | solution.py:18
  93.9 56.4 %collective-permute-start.78 = (bf16[128,1024]{0,1:T(8,128)(2,1)S(1)}, bf16[128,1024]{0,1:T(8,128)(2,1)}, u32[]{:S(2)}, u32[]{:S(2)}) collective-permute-start(bf16[128,1024]{0,1:T(8,128)(2,1)S(1)} %bitcast.1319), channel_id=1, source_target_pairs={{0,8},{8,0},{1,9},{9,1},{2,10},{10,2},{3,11},{11,3},{4,12},{12,4},... | collective-permute-start | bytes 786440 | tf_op jit(solution)/shard_map/ppermute | solution.py:18
  134.3 15.2 %collective-permute-start.77 = (bf16[128,1024]{0,1:T(8,128)(2,1)S(1)}, bf16[128,1024]{0,1:T(8,128)(2,1)S(1)}, u32[]{:S(2)}, u32[]{:S(2)}) collective-permute-start(bf16[128,1024]{0,1:T(8,128)(2,1)S(1)} %bitcast.1320), channel_id=1, source_target_pairs={{0,2},{2,0},{1,3},{3,1},{4,6},{6,4},{5,7},{7,5},{8,10},{10,8},{9,1... | collective-permute-start | bytes 786440 | tf_op jit(solution)/shard_map/ppermute | solution.py:18
  140.6 80.9 %collective-permute-start.80 = (bf16[128,1024]{0,1:T(8,128)(2,1)S(1)}, bf16[128,1024]{0,1:T(8,128)(2,1)S(1)}, u32[]{:S(2)}, u32[]{:S(2)}) collective-permute-start(bf16[128,1024]{0,1:T(8,128)(2,1)S(1)} %bitcast.1321), channel_id=1, source_target_pairs={{0,16},{16,0},{1,17},{17,1},{2,18},{18,2},{3,19},{19,3},{4,20},{20... | collective-permute-start | bytes 786440 | tf_op jit(solution)/shard_map/ppermute | solution.py:18
  143.0 49.2 %collective-permute-start.25 = (bf16[2,2,32,1024]{3,2,1,0:T(8,128)(2,1)S(1)}, bf16[2,2,32,1024]{3,2,1,0:T(8,128)(2,1)S(1)}, u32[]{:S(2)}, u32[]{:S(2)}) collective-permute-start(bf16[2,2,32,1024]{3,2,1,0:T(8,128)(2,1)S(1)} %dynamic-slice_bitcast_fusion.3), channel_id=1, source_target_pairs={{0,1},{1,0},{2,3},{3,2},{4,5},{5,4},{6,7},{7,6},{8,9},{9,8},{10,11... | collective-permute-start | bytes 786440 | tf_op jit(solution)/shard_map/ppermute | solution.py:18
  149.5 42.8 %collective-permute-start.64 = (bf16[2,2,32,1024]{3,2,1,0:T(8,128)(2,1)S(1)}, bf16[2,2,32,1024]{3,2,1,0:T(8,128)(2,1)S(1)}, u32[]{:S(2)}, u32[]{:S(2)}) collective-permute-start(bf16[2,2,32,1024]{3,2,1,0:T(8,128)(2,1)S(1)} %dynamic-slice_bitcast_fusion.2), channel_id=1, source_target_pairs={{0,1},{1,0},{2,3},{3,2},{4,5},{5,4},{6,7},{7,6},{8,9},{9,8},{10,11... | collective-permute-start | bytes 786440 | tf_op jit(solution)/shard_map/ppermute | solution.py:18
  188.5 75.2 %collective-permute-start.13 = (bf16[128,768]{1,0:T(8,128)(2,1)}, bf16[128,768]{1,0:T(8,128)(2,1)}, u32[]{:S(2)}, u32[]{:S(2)}) collective-permute-start(bf16[128,768]{1,0:T(8,128)(2,1)} %bitcast.36), channel_id=1, source_target_pairs={{0,16},{16,0},{1,17},{17,1},{2,18},{18,2},{3,19},{19,3},{4,20},{20... | collective-permute-start | bytes 589832 | tf_op jit(solution)/shard_map/ppermute | solution.py:18
  192.2 88.3 %collective-permute-start.53 = (bf16[128,768]{1,0:T(8,128)(2,1)}, bf16[128,768]{1,0:T(8,128)(2,1)}, u32[]{:S(2)}, u32[]{:S(2)}) collective-permute-start(bf16[128,768]{1,0:T(8,128)(2,1)} %bitcast.144), channel_id=1, source_target_pairs={{0,16},{16,0},{1,17},{17,1},{2,18},{18,2},{3,19},{19,3},{4,20},{20... | collective-permute-start | bytes 589832 | tf_op jit(solution)/shard_map/ppermute | solution.py:18
  219.1 98.7 %collective-permute-start.34 = (bf16[128,1024]{1,0:T(8,128)(2,1)}, bf16[128,1024]{1,0:T(8,128)(2,1)}, u32[]{:S(2)}, u32[]{:S(2)}) collective-permute-start(bf16[128,1024]{1,0:T(8,128)(2,1)} %bitcast.97), channel_id=1, source_target_pairs={{0,16},{16,0},{1,17},{17,1},{2,18},{18,2},{3,19},{19,3},{4,20},{20... | collective-permute-start | bytes 786440 | tf_op jit(solution)/shard_map/ppermute | solution.py:18
  222.8 17.4 %collective-permute-start.31 = (bf16[128,1024]{1,0:T(8,128)(2,1)}, bf16[128,1024]{1,0:T(8,128)(2,1)}, u32[]{:S(2)}, u32[]{:S(2)}) collective-permute-start(bf16[128,1024]{1,0:T(8,128)(2,1)} %bitcast.97), channel_id=1, source_target_pairs={{0,2},{2,0},{1,3},{3,1},{4,6},{6,4},{5,7},{7,5},{8,10},{10,8},{9,1... | collective-permute-start | bytes 786440 | tf_op jit(solution)/shard_map/ppermute | solution.py:18
  244.8 110.4 %collective-permute-start.73 = (bf16[128,1024]{1,0:T(8,128)(2,1)}, bf16[128,1024]{1,0:T(8,128)(2,1)}, u32[]{:S(2)}, u32[]{:S(2)}) collective-permute-start(bf16[128,1024]{1,0:T(8,128)(2,1)} %bitcast.1328), channel_id=1, source_target_pairs={{0,16},{16,0},{1,17},{17,1},{2,18},{18,2},{3,19},{19,3},{4,20},{20... | collective-permute-start | bytes 786440 | tf_op jit(solution)/shard_map/ppermute | solution.py:18
  271.5 16.1 %collective-permute-start.55 = (bf16[128,768]{1,0:T(8,128)(2,1)S(1)}, bf16[128,768]{1,0:T(8,128)(2,1)S(1)}, u32[]{:S(2)}, u32[]{:S(2)}) collective-permute-start(bf16[128,768]{1,0:T(8,128)(2,1)S(1)} %copy-done.105), channel_id=1, source_target_pairs={{0,16},{16,0},{1,17},{17,1},{2,18},{18,2},{3,19},{19,3},{4,20},{20... | collective-permute-start | bytes 589832 | tf_op jit(solution)/shard_map/ppermute | solution.py:18
  280.6 61.3 %collective-permute-start.7 = (bf16[256,1024]{1,0:T(8,128)(2,1)S(1)}, bf16[256,1024]{1,0:T(8,128)(2,1)S(1)}, u32[]{:S(2)}, u32[]{:S(2)}) collective-permute-start(bf16[256,1024]{1,0:T(8,128)(2,1)S(1)} %add_convert_fusion.6), channel_id=1, source_target_pairs={{0,4},{4,0},{1,5},{5,1},{2,6},{6,2},{3,7},{7,3},{8,12},{12,8},{9,1... | collective-permute-start | bytes 1572872 | tf_op jit(solution)/shard_map/ppermute | solution.py:18
  287.5 137.2 %collective-permute-start.89 = (bf16[256,1024]{1,0:T(8,128)(2,1)S(1)}, bf16[256,1024]{1,0:T(8,128)(2,1)}, u32[]{:S(2)}, u32[]{:S(2)}) collective-permute-start(bf16[256,1024]{1,0:T(8,128)(2,1)S(1)} %bitcast.1232), channel_id=1, source_target_pairs={{0,4},{4,0},{1,5},{5,1},{2,6},{6,2},{3,7},{7,3},{8,12},{12,8},{9,1... | collective-permute-start | bytes 1572872 | tf_op jit(solution)/shard_map/ppermute | solution.py:18
  327.2 32.6 %collective-permute-start.75 = (bf16[128,1024]{1,0:T(8,128)(2,1)}, bf16[128,1024]{1,0:T(8,128)(2,1)}, u32[]{:S(2)}, u32[]{:S(2)}) collective-permute-start(bf16[128,1024]{1,0:T(8,128)(2,1)} %collective-permute-done.71), channel_id=1, source_target_pairs={{0,16},{16,0},{1,17},{17,1},{2,18},{18,2},{3,19},{19,3},{4,20},{20... | collective-permute-start | bytes 786440 | tf_op jit(solution)/shard_map/ppermute | solution.py:18
  337.4 19.8 %collective-permute-start.74 = (bf16[128,1024]{1,0:T(8,128)(2,1)}, bf16[128,1024]{1,0:T(8,128)(2,1)}, u32[]{:S(2)}, u32[]{:S(2)}) collective-permute-start(bf16[128,1024]{1,0:T(8,128)(2,1)} %collective-permute-done.70), channel_id=1, source_target_pairs={{0,16},{16,0},{1,17},{17,1},{2,18},{18,2},{3,19},{19,3},{4,20},{20... | collective-permute-start | bytes 786440 | tf_op jit(solution)/shard_map/ppermute | solution.py:18
  341.9 43.6 %collective-permute-start.56 = (bf16[128,768]{1,0:T(8,128)(2,1)}, bf16[128,768]{1,0:T(8,128)(2,1)}, u32[]{:S(2)}, u32[]{:S(2)}) collective-permute-start(bf16[128,768]{1,0:T(8,128)(2,1)} %collective-permute-done.54), channel_id=1, source_target_pairs={{0,8},{8,0},{1,9},{9,1},{2,10},{10,2},{3,11},{11,3},{4,12},{12,4},... | collective-permute-start | bytes 589832 | tf_op jit(solution)/shard_map/ppermute | solution.py:18
  359.8 44.8 %collective-permute-start.76 = (bf16[128,1024]{1,0:T(8,128)(2,1)}, bf16[128,1024]{1,0:T(8,128)(2,1)S(1)}, u32[]{:S(2)}, u32[]{:S(2)}) collective-permute-start(bf16[128,1024]{1,0:T(8,128)(2,1)} %collective-permute-done.74), channel_id=1, source_target_pairs={{0,8},{8,0},{1,9},{9,1},{2,10},{10,2},{3,11},{11,3},{4,12},{12,4},... | collective-permute-start | bytes 786440 | tf_op jit(solution)/shard_map/ppermute | solution.py:18
  361.5 15.0 %collective-permute-start.27 = (bf16[256,1024]{1,0:T(8,128)(2,1)S(1)}, bf16[256,1024]{1,0:T(8,128)(2,1)S(1)}, u32[]{:S(2)}, u32[]{:S(2)}) collective-permute-start(bf16[256,1024]{1,0:T(8,128)(2,1)S(1)} %fusion.93), channel_id=1, source_target_pairs={{0,1},{1,0},{2,3},{3,2},{4,5},{5,4},{6,7},{7,6},{8,9},{9,8},{10,11... | collective-permute-start | bytes 1572872 | tf_op jit(solution)/shard_map/ppermute | solution.py:18
  494.2 14.8 %collective-permute-start.145 = (bf16[2,128,1024]{2,1,0:T(8,128)(2,1)S(1)}, bf16[2,128,1024]{2,1,0:T(8,128)(2,1)S(1)}, u32[]{:S(2)}, u32[]{:S(2)}) collective-permute-start(bf16[2,128,1024]{2,1,0:T(8,128)(2,1)S(1)} %copy-done.94), channel_id=1, source_target_pairs={{0,16},{16,0},{1,17},{17,1},{2,18},{18,2},{3,19},{19,3},{4,20},{20... | collective-permute-start | bytes 1572872 | tf_op jit(solution)/shard_map/ppermute | solution.py:18
  495.2 17.7 %collective-permute-start.147 = (bf16[2,128,1024]{2,1,0:T(8,128)(2,1)S(1)}, bf16[2,128,1024]{2,1,0:T(8,128)(2,1)S(1)}, u32[]{:S(2)}, u32[]{:S(2)}) collective-permute-start(bf16[2,128,1024]{2,1,0:T(8,128)(2,1)S(1)} %fusion.110), channel_id=1, source_target_pairs={{0,8},{8,0},{1,9},{9,1},{2,10},{10,2},{3,11},{11,3},{4,12},{12,4},... | collective-permute-start | bytes 1572872 | tf_op jit(solution)/shard_map/ppermute | solution.py:18
  496.4 26.4 %collective-permute-start.157 = (bf16[2,128,1024]{2,1,0:T(8,128)(2,1)S(1)}, bf16[2,128,1024]{2,1,0:T(8,128)(2,1)S(1)}, u32[]{:S(2)}, u32[]{:S(2)}) collective-permute-start(bf16[2,128,1024]{2,1,0:T(8,128)(2,1)S(1)} %fusion.116), channel_id=1, source_target_pairs={{0,16},{16,0},{1,17},{17,1},{2,18},{18,2},{3,19},{19,3},{4,20},{20... | collective-permute-start | bytes 1572872 | tf_op jit(solution)/shard_map/ppermute | solution.py:18
  498.0 23.4 %collective-permute-start.159 = (bf16[2,128,1024]{2,1,0:T(8,128)(2,1)S(1)}, bf16[2,128,1024]{2,1,0:T(8,128)(2,1)S(1)}, u32[]{:S(2)}, u32[]{:S(2)}) collective-permute-start(bf16[2,128,1024]{2,1,0:T(8,128)(2,1)S(1)} %fusion.112), channel_id=1, source_target_pairs={{0,8},{8,0},{1,9},{9,1},{2,10},{10,2},{3,11},{11,3},{4,12},{12,4},... | collective-permute-start | bytes 1572872 | tf_op jit(solution)/shard_map/ppermute | solution.py:18
  498.8 36.4 %collective-permute-start.91 = (bf16[256,1024]{1,0:T(8,128)(2,1)S(1)}, bf16[256,1024]{1,0:T(8,128)(2,1)S(1)}, u32[]{:S(2)}, u32[]{:S(2)}) collective-permute-start(bf16[256,1024]{1,0:T(8,128)(2,1)S(1)} %fusion.97), channel_id=1, source_target_pairs={{0,1},{1,0},{2,3},{3,2},{4,5},{5,4},{6,7},{7,6},{8,9},{9,8},{10,11... | collective-permute-start | bytes 1572872 | tf_op jit(solution)/shard_map/ppermute | solution.py:18
  509.0 28.8 %collective-permute-start.85 = (bf16[256,1024]{1,0:T(8,128)(2,1)S(1)}, bf16[256,1024]{1,0:T(8,128)(2,1)S(1)}, u32[]{:S(2)}, u32[]{:S(2)}) collective-permute-start(bf16[256,1024]{1,0:T(8,128)(2,1)S(1)} %fusion.96), channel_id=1, source_target_pairs={{0,1},{1,0},{2,3},{3,2},{4,5},{5,4},{6,7},{7,6},{8,9},{9,8},{10,11... | collective-permute-start | bytes 1572872 | tf_op jit(solution)/shard_map/ppermute | solution.py:18
  513.0 34.7 %collective-permute-start.146 = (bf16[128,1024]{1,0:T(8,128)(2,1)}, bf16[128,1024]{1,0:T(8,128)(2,1)}, u32[]{:S(2)}, u32[]{:S(2)}) collective-permute-start(bf16[128,1024]{1,0:T(8,128)(2,1)} %fusion.151), channel_id=1, source_target_pairs={{0,8},{8,0},{1,9},{9,1},{2,10},{10,2},{3,11},{11,3},{4,12},{12,4},... | collective-permute-start | bytes 786440 | tf_op jit(solution)/shard_map/ppermute | solution.py:18
  530.1 35.6 %collective-permute-start.158 = (bf16[128,1024]{1,0:T(8,128)(2,1)}, bf16[128,1024]{1,0:T(8,128)(2,1)}, u32[]{:S(2)}, u32[]{:S(2)}) collective-permute-start(bf16[128,1024]{1,0:T(8,128)(2,1)} %fusion.155), channel_id=1, source_target_pairs={{0,8},{8,0},{1,9},{9,1},{2,10},{10,2},{3,11},{11,3},{4,12},{12,4},... | collective-permute-start | bytes 786440 | tf_op jit(solution)/shard_map/ppermute | solution.py:18
  532.9 21.6 %collective-permute-start.149 = (bf16[128,1024]{1,0:T(8,128)(2,1)}, bf16[128,1024]{1,0:T(8,128)(2,1)}, u32[]{:S(2)}, u32[]{:S(2)}) collective-permute-start(bf16[128,1024]{1,0:T(8,128)(2,1)} %fusion.126), channel_id=1, source_target_pairs={{0,2},{2,0},{1,3},{3,1},{4,6},{6,4},{5,7},{7,5},{8,10},{10,8},{9,1... | collective-permute-start | bytes 786440 | tf_op jit(solution)/shard_map/ppermute | solution.py:18
  535.2 30.5 %collective-permute-start.161 = (bf16[128,1024]{1,0:T(8,128)(2,1)}, bf16[128,1024]{1,0:T(8,128)(2,1)}, u32[]{:S(2)}, u32[]{:S(2)}) collective-permute-start(bf16[128,1024]{1,0:T(8,128)(2,1)} %fusion.118), channel_id=1, source_target_pairs={{0,2},{2,0},{1,3},{3,1},{4,6},{6,4},{5,7},{7,5},{8,10},{10,8},{9,1... | collective-permute-start | bytes 786440 | tf_op jit(solution)/shard_map/ppermute | solution.py:18
  543.6 35.5 %collective-permute-start.86 = (bf16[128,1024]{0,1:T(8,128)(2,1)}, bf16[128,1024]{0,1:T(8,128)(2,1)}, u32[]{:S(2)}, u32[]{:S(2)}) collective-permute-start(bf16[128,1024]{0,1:T(8,128)(2,1)} %bitcast.222), channel_id=1, source_target_pairs={{0,0},{2,4},{4,2},{6,6},{1,1},{3,5},{5,3},{7,7},{8,8},{10,12},{12,... | collective-permute-start | bytes 786440 | tf_op jit(solution)/shard_map/ppermute | solution.py:89
  557.0 32.4 %collective-permute-start.92 = (bf16[256,1024]{1,0:T(8,128)(2,1)}, bf16[256,1024]{1,0:T(8,128)(2,1)}, u32[]{:S(2)}, u32[]{:S(2)}) collective-permute-start(bf16[256,1024]{1,0:T(8,128)(2,1)} %get-tuple-element.70), channel_id=1, source_target_pairs={{0,4},{4,0},{1,5},{5,1},{2,6},{6,2},{3,7},{7,3},{8,12},{12,8},{9,1... | collective-permute-start | bytes 1572872 | tf_op jit(solution)/shard_map/ppermute | solution.py:18
  565.7 15.2 %collective-permute-start.151 = (bf16[2,32,1024]{2,1,0:T(8,128)(2,1)}, bf16[2,32,1024]{2,1,0:T(8,128)(2,1)}, u32[]{:S(2)}, u32[]{:S(2)}) collective-permute-start(bf16[2,32,1024]{2,1,0:T(8,128)(2,1)} %fusion.184), channel_id=1, source_target_pairs={{0,4},{4,0},{1,5},{5,1},{2,6},{6,2},{3,7},{7,3},{8,12},{12,8},{9,1... | collective-permute-start | bytes 393224 | tf_op jit(solution)/shard_map/ppermute | solution.py:18
  618.2 17.7 %collective-permute-start.132 = (bf16[2,2,32,1024]{3,2,1,0:T(8,128)(2,1)}, bf16[2,2,32,1024]{3,2,1,0:T(8,128)(2,1)}, u32[]{:S(2)}, u32[]{:S(2)}) collective-permute-start(bf16[2,2,32,1024]{3,2,1,0:T(8,128)(2,1)} %dynamic-slice_bitcast_fusion), channel_id=1, source_target_pairs={{0,1},{1,0},{2,3},{3,2},{4,5},{5,4},{6,7},{7,6},{8,9},{9,8},{10,11... | collective-permute-start | bytes 786440 | tf_op jit(solution)/shard_map/ppermute | solution.py:18
  631.6 27.3 %collective-permute-start.93 = (bf16[256,1024]{1,0:T(8,128)(2,1)}, bf16[256,1024]{1,0:T(8,128)(2,1)S(1)}, u32[]{:S(2)}, u32[]{:S(2)}) collective-permute-start(bf16[256,1024]{1,0:T(8,128)(2,1)} %fusion.106), channel_id=1, source_target_pairs={{0,4},{4,0},{1,5},{5,1},{2,6},{6,2},{3,7},{7,3},{8,12},{12,8},{9,1... | collective-permute-start | bytes 1572872 | tf_op jit(solution)/shard_map/ppermute | solution.py:18
  632.0 18.4 %collective-permute-start.119 = (bf16[2,128,768]{2,1,0:T(8,128)(2,1)}, bf16[2,128,768]{2,1,0:T(8,128)(2,1)S(1)}, u32[]{:S(2)}, u32[]{:S(2)}) collective-permute-start(bf16[2,128,768]{2,1,0:T(8,128)(2,1)} %fusion.138), channel_id=1, source_target_pairs={{0,16},{16,0},{1,17},{17,1},{2,18},{18,2},{3,19},{19,3},{4,20},{20... | collective-permute-start | bytes 1179656 | tf_op jit(solution)/shard_map/ppermute | solution.py:18
  634.3 14.7 %collective-permute-start.121 = (bf16[2,128,768]{2,1,0:T(8,128)(2,1)S(1)}, bf16[2,128,768]{2,1,0:T(8,128)(2,1)S(1)}, u32[]{:S(2)}, u32[]{:S(2)}) collective-permute-start(bf16[2,128,768]{2,1,0:T(8,128)(2,1)S(1)} %fusion.136), channel_id=1, source_target_pairs={{0,8},{8,0},{1,9},{9,1},{2,10},{10,2},{3,11},{11,3},{4,12},{12,4},... | collective-permute-start | bytes 1179656 | tf_op jit(solution)/shard_map/ppermute | solution.py:18
  646.2 35.5 %collective-permute-start.134 = (bf16[32,1024]{1,0:T(8,128)(2,1)S(1)}, bf16[32,1024]{1,0:T(8,128)(2,1)S(1)}, u32[]{:S(2)}, u32[]{:S(2)}) collective-permute-start(bf16[32,1024]{1,0:T(8,128)(2,1)S(1)} %fusion.241), channel_id=1, source_target_pairs={{0,8},{8,0},{1,9},{9,1},{2,10},{10,2},{3,11},{11,3},{4,12},{12,4},... | collective-permute-start | bytes 196616 | tf_op jit(solution)/shard_map/ppermute | solution.py:18
  648.0 19.0 %collective-permute-start.136 = (bf16[32,1024]{1,0:T(8,128)(2,1)S(1)}, bf16[32,1024]{1,0:T(8,128)(2,1)S(1)}, u32[]{:S(2)}, u32[]{:S(2)}) collective-permute-start(bf16[32,1024]{1,0:T(8,128)(2,1)S(1)} %fusion.242), channel_id=1, source_target_pairs={{0,16},{16,0},{1,17},{17,1},{2,18},{18,2},{3,19},{19,3},{4,20},{20... | collective-permute-start | bytes 196616 | tf_op jit(solution)/shard_map/ppermute | solution.py:18
  659.0 19.5 %collective-permute-start.94 = (bf16[256,1024]{1,0:T(8,128)(2,1)S(1)}, bf16[256,1024]{1,0:T(8,128)(2,1)S(1)}, u32[]{:S(2)}, u32[]{:S(2)}) collective-permute-start(bf16[256,1024]{1,0:T(8,128)(2,1)S(1)} %fusion.98), channel_id=1, source_target_pairs={{0,1},{1,0},{2,3},{3,2},{4,5},{5,4},{6,7},{7,6},{8,9},{9,8},{10,11... | collective-permute-start | bytes 1572872 | tf_op jit(solution)/shard_map/ppermute | solution.py:18
  667.0 14.6 %collective-permute-start.137 = (bf16[32,1024]{1,0:T(8,128)(2,1)S(1)}, bf16[32,1024]{1,0:T(8,128)(2,1)S(1)}, u32[]{:S(2)}, u32[]{:S(2)}) collective-permute-start(bf16[32,1024]{1,0:T(8,128)(2,1)S(1)} %fusion.200), channel_id=1, source_target_pairs={{0,2},{2,0},{1,3},{3,1},{4,6},{6,4},{5,7},{7,5},{8,10},{10,8},{9,1... | collective-permute-start | bytes 196616 | tf_op jit(solution)/shard_map/ppermute | solution.py:18
  704.9 14.8 %collective-permute-start.138 = (bf16[2,128,1024]{2,1,0:T(8,128)(2,1)S(1)}, bf16[2,128,1024]{2,1,0:T(8,128)(2,1)S(1)}, u32[]{:S(2)}, u32[]{:S(2)}) collective-permute-start(bf16[2,128,1024]{2,1,0:T(8,128)(2,1)S(1)} %fusion.113), channel_id=1, source_target_pairs={{0,16},{16,0},{1,17},{17,1},{2,18},{18,2},{3,19},{19,3},{4,20},{20... | collective-permute-start | bytes 1572872 | tf_op jit(solution)/shard_map/ppermute | solution.py:18
  705.7 17.1 %collective-permute-start.140 = (bf16[2,128,1024]{2,1,0:T(8,128)(2,1)S(1)}, bf16[2,128,1024]{2,1,0:T(8,128)(2,1)S(1)}, u32[]{:S(2)}, u32[]{:S(2)}) collective-permute-start(bf16[2,128,1024]{2,1,0:T(8,128)(2,1)S(1)} %fusion.109), channel_id=1, source_target_pairs={{0,8},{8,0},{1,9},{9,1},{2,10},{10,2},{3,11},{11,3},{4,12},{12,4},... | collective-permute-start | bytes 1572872 | tf_op jit(solution)/shard_map/ppermute | solution.py:18
  707.3 26.3 %collective-permute-start.152 = (bf16[2,128,1024]{2,1,0:T(8,128)(2,1)S(1)}, bf16[2,128,1024]{2,1,0:T(8,128)(2,1)S(1)}, u32[]{:S(2)}, u32[]{:S(2)}) collective-permute-start(bf16[2,128,1024]{2,1,0:T(8,128)(2,1)S(1)} %fusion.115), channel_id=1, source_target_pairs={{0,16},{16,0},{1,17},{17,1},{2,18},{18,2},{3,19},{19,3},{4,20},{20... | collective-permute-start | bytes 1572872 | tf_op jit(solution)/shard_map/ppermute | solution.py:18
  709.4 22.4 %collective-permute-start.154 = (bf16[2,128,1024]{2,1,0:T(8,128)(2,1)S(1)}, bf16[2,128,1024]{2,1,0:T(8,128)(2,1)S(1)}, u32[]{:S(2)}, u32[]{:S(2)}) collective-permute-start(bf16[2,128,1024]{2,1,0:T(8,128)(2,1)S(1)} %fusion.111), channel_id=1, source_target_pairs={{0,8},{8,0},{1,9},{9,1},{2,10},{10,2},{3,11},{11,3},{4,12},{12,4},... | collective-permute-start | bytes 1572872 | tf_op jit(solution)/shard_map/ppermute | solution.py:18
  710.4 32.7 %collective-permute-start.97 = (bf16[256,1024]{1,0:T(8,128)(2,1)S(1)}, bf16[256,1024]{1,0:T(8,128)(2,1)S(1)}, u32[]{:S(2)}, u32[]{:S(2)}) collective-permute-start(bf16[256,1024]{1,0:T(8,128)(2,1)S(1)} %fusion.99), channel_id=1, source_target_pairs={{0,1},{1,0},{2,3},{3,2},{4,5},{5,4},{6,7},{7,6},{8,9},{9,8},{10,11... | collective-permute-start | bytes 1572872 | tf_op jit(solution)/shard_map/ppermute | solution.py:18
  720.6 27.0 %collective-permute-start.139 = (bf16[128,1024]{1,0:T(8,128)(2,1)}, bf16[128,1024]{1,0:T(8,128)(2,1)}, u32[]{:S(2)}, u32[]{:S(2)}) collective-permute-start(bf16[128,1024]{1,0:T(8,128)(2,1)} %fusion.149), channel_id=1, source_target_pairs={{0,8},{8,0},{1,9},{9,1},{2,10},{10,2},{3,11},{11,3},{4,12},{12,4},... | collective-permute-start | bytes 786440 | tf_op jit(solution)/shard_map/ppermute | solution.py:18
  734.5 24.3 %collective-permute-start.153 = (bf16[128,1024]{1,0:T(8,128)(2,1)}, bf16[128,1024]{1,0:T(8,128)(2,1)}, u32[]{:S(2)}, u32[]{:S(2)}) collective-permute-start(bf16[128,1024]{1,0:T(8,128)(2,1)} %fusion.153), channel_id=1, source_target_pairs={{0,8},{8,0},{1,9},{9,1},{2,10},{10,2},{3,11},{11,3},{4,12},{12,4},... | collective-permute-start | bytes 786440 | tf_op jit(solution)/shard_map/ppermute | solution.py:18
  737.4 20.0 %collective-permute-start.142 = (bf16[128,1024]{1,0:T(8,128)(2,1)}, bf16[128,1024]{1,0:T(8,128)(2,1)}, u32[]{:S(2)}, u32[]{:S(2)}) collective-permute-start(bf16[128,1024]{1,0:T(8,128)(2,1)} %fusion.131), channel_id=1, source_target_pairs={{0,2},{2,0},{1,3},{3,1},{4,6},{6,4},{5,7},{7,5},{8,10},{10,8},{9,1... | collective-permute-start | bytes 786440 | tf_op jit(solution)/shard_map/ppermute | solution.py:18
  742.5 20.5 %collective-permute-start.156 = (bf16[128,1024]{1,0:T(8,128)(2,1)}, bf16[128,1024]{1,0:T(8,128)(2,1)}, u32[]{:S(2)}, u32[]{:S(2)}) collective-permute-start(bf16[128,1024]{1,0:T(8,128)(2,1)} %fusion.122), channel_id=1, source_target_pairs={{0,2},{2,0},{1,3},{3,1},{4,6},{6,4},{5,7},{7,5},{8,10},{10,8},{9,1... | collective-permute-start | bytes 786440 | tf_op jit(solution)/shard_map/ppermute | solution.py:18
  747.6 22.8 %collective-permute-start.98 = (bf16[256,1024]{1,0:T(8,128)(2,1)}, bf16[256,1024]{1,0:T(8,128)(2,1)}, u32[]{:S(2)}, u32[]{:S(2)}) collective-permute-start(bf16[256,1024]{1,0:T(8,128)(2,1)} %get-tuple-element.66), channel_id=1, source_target_pairs={{0,4},{4,0},{1,5},{5,1},{2,6},{6,2},{3,7},{7,3},{8,12},{12,8},{9,1... | collective-permute-start | bytes 1572872 | tf_op jit(solution)/shard_map/ppermute | solution.py:18
  798.4 26.0 %collective-permute-start.99 = (bf16[256,1024]{1,0:T(8,128)(2,1)S(1)}, bf16[256,1024]{1,0:T(8,128)(2,1)S(1)}, u32[]{:S(2)}, u32[]{:S(2)}) collective-permute-start(bf16[256,1024]{1,0:T(8,128)(2,1)S(1)} %fusion.108), channel_id=1, source_target_pairs={{0,4},{4,0},{1,5},{5,1},{2,6},{6,2},{3,7},{7,3},{8,12},{12,8},{9,1... | collective-permute-start | bytes 1572872 | tf_op jit(solution)/shard_map/ppermute | solution.py:18
  799.0 16.0 %collective-permute-start.112 = (bf16[2,128,768]{2,1,0:T(8,128)(2,1)S(1)}, bf16[2,128,768]{2,1,0:T(8,128)(2,1)S(1)}, u32[]{:S(2)}, u32[]{:S(2)}) collective-permute-start(bf16[2,128,768]{2,1,0:T(8,128)(2,1)S(1)} %copy-done.97), channel_id=1, source_target_pairs={{0,16},{16,0},{1,17},{17,1},{2,18},{18,2},{3,19},{19,3},{4,20},{20... | collective-permute-start | bytes 1179656 | tf_op jit(solution)/shard_map/ppermute | solution.py:18
  799.8 16.8 %collective-permute-start.114 = (bf16[2,128,768]{2,1,0:T(8,128)(2,1)S(1)}, bf16[2,128,768]{2,1,0:T(8,128)(2,1)S(1)}, u32[]{:S(2)}, u32[]{:S(2)}) collective-permute-start(bf16[2,128,768]{2,1,0:T(8,128)(2,1)S(1)} %fusion.135), channel_id=1, source_target_pairs={{0,8},{8,0},{1,9},{9,1},{2,10},{10,2},{3,11},{11,3},{4,12},{12,4},... | collective-permute-start | bytes 1179656 | tf_op jit(solution)/shard_map/ppermute | solution.py:18
  813.0 21.2 %collective-permute-start.128 = (bf16[32,1024]{1,0:T(8,128)(2,1)S(1)}, bf16[32,1024]{1,0:T(8,128)(2,1)S(1)}, u32[]{:S(2)}, u32[]{:S(2)}) collective-permute-start(bf16[32,1024]{1,0:T(8,128)(2,1)S(1)} %fusion.239), channel_id=1, source_target_pairs={{0,8},{8,0},{1,9},{9,1},{2,10},{10,2},{3,11},{11,3},{4,12},{12,4},... | collective-permute-start | bytes 196616 | tf_op jit(solution)/shard_map/ppermute | solution.py:18
  819.6 14.6 %collective-permute-start.131 = (bf16[32,1024]{1,0:T(8,128)(2,1)S(1)}, bf16[32,1024]{1,0:T(8,128)(2,1)S(1)}, u32[]{:S(2)}, u32[]{:S(2)}) collective-permute-start(bf16[32,1024]{1,0:T(8,128)(2,1)S(1)} %fusion.204), channel_id=1, source_target_pairs={{0,2},{2,0},{1,3},{3,1},{4,6},{6,4},{5,7},{7,5},{8,10},{10,8},{9,1... | collective-permute-start | bytes 196616 | tf_op jit(solution)/shard_map/ppermute | solution.py:18
  857.4 24.7 %collective-permute-start.101 = (f32[128,1024]{0,1:T(8,128)S(1)}, f32[128,1024]{0,1:T(8,128)S(1)}, u32[]{:S(2)}, u32[]{:S(2)}) collective-permute-start(f32[128,1024]{0,1:T(8,128)S(1)} %bitcast.1353), channel_id=1, source_target_pairs={{0,0},{2,4},{4,2},{6,6},{1,1},{3,5},{5,3},{7,7},{8,8},{10,12},{12,... | collective-permute-start | bytes 1572872 | tf_op jit(solution)/shard_map/ppermute | solution.py:89
  (278 other events, 3175.7 us)

commit v2 on v1

--- a/solution.py
+++ b/solution.py
@@ -1,6 +1,8 @@
 import jax
 import jax.numpy as jnp
 from jax import lax
+from jax.experimental import pallas as pl
+from jax.experimental.pallas import tpu as pltpu
 from jax.sharding import Mesh, PartitionSpec as P
 
 HEADS = 16
@@ -114,7 +116,7 @@
     return jnp.einsum("td,te->de", left, right, preferred_element_type=F32)
 
 
-def body(
+def wide_body(
     tokens,
     segment_ids,
     group_order,
@@ -383,9 +385,760 @@
     return (final_rows, leave(gx)) + tuple(stacked)
 
 
+def bit(axis, flip):
+    place = lax.axis_index(axis)
+    return 1 - place if flip else place
+
+
+def slot_places():
+    for slot in range(8):
+        yield slot, bit("y", slot & 4), bit("x", slot & 2), bit("zh", slot & 1)
+
+
+def slot_blocks():
+    return [(r, (y * 2 + x) * 2 + zh) for r, y, x, zh in slot_places()]
+
+
+def at(block, size):
+    return pl.ds(pl.multiple_of(block * size, size), size)
+
+
+def run(kernel, outs, *ins, limit=40, flops=0):
+    smem = pl.BlockSpec(memory_space=pltpu.SMEM)
+    vmem = pl.BlockSpec(memory_space=pltpu.VMEM)
+    scratch = getattr(kernel, "scratch", [])
+    moved = sum(v.size * v.dtype.itemsize for v in list(ins) + list(outs))
+    return pl.pallas_call(
+        kernel,
+        out_shape=tuple(outs),
+        in_specs=[smem if v.size == 4 else vmem for v in ins],
+        out_specs=tuple(vmem for _ in outs),
+        scratch_shapes=scratch,
+        compiler_params=pltpu.CompilerParams(vmem_limit_bytes=limit << 20),
+        cost_estimate=pl.CostEstimate(flops=flops, bytes_accessed=moved, transcendentals=0),
+    )(*ins)
+
+
+def shape(*sizes, dtype=BF):
+    return jax.ShapeDtypeStruct(sizes, dtype)
+
+
+def with_scratch(kernel, *scratch):
+    kernel.scratch = list(scratch)
+    return kernel
+
+
+def inner_columns(value):
+    low = lax.broadcasted_iota(jnp.int32, (value.shape[0], 128), 1) < 64
+    parts = []
+    for i in range(0, value.shape[1], 256):
+        a, b = value[:, i : i + 128], value[:, i + 128 : i + 256]
+        parts.append(jnp.where(low, a, pltpu.roll(b, 64, 1)))
+        parts.append(jnp.where(low, pltpu.roll(a, 64, 1), b))
+    return jnp.concatenate(parts, axis=1)
+
+
+def spread(value):
+    n = value.shape[1]
+    if n == 128:
+        return value.astype(F32)
+    hit = lax.broadcasted_iota(jnp.int32, (n, 128), 1) % n == lax.broadcasted_iota(
+        jnp.int32, (n, 128), 0
+    )
+    return dot(value.astype(F32), hit.astype(F32))
+
+
+RANKS = ((0, 0), (1, 0), (0, 1), (1, 1))
+
+
+def qkv_blocks(core, zl):
+    return [
+        (s * 8 + zl * 4 + x * 2 + core, s * 2 + x) for s in range(3) for x in range(2)
+    ]
+
+
+def up_blocks(core, zl):
+    return [
+        (chip * 8 + core * 4 + zh * 2 + zl, chip * 2 + zh)
+        for chip in range(4)
+        for zh in range(2)
+    ]
+
+
+def prepare(g1, b1, bo, g2, b2, bd, qv, up, w_qkv, w_out, w_up, w_down, *outs):
+    first, rest = outs[0:4], outs[4:8]
+    out_a, out_b, down = outs[8:11]
+    rows = [spread(v[...]) for v in (g1, b1, bo, g2, b2, bd, qv, up)]
+    small = jnp.concatenate([v[l : l + 1] for l in range(2) for v in rows], axis=0)
+    for i, (dc, dl) in enumerate(RANKS):
+        core, zl = bit("core", dc), bit("zl", dl)
+        for src, dst in qkv_blocks(core, zl):
+            first[i][0:32, dst * 128 : dst * 128 + 128] = w_qkv[0, :, at(src, 128)]
+            rest[i][:, 1024 + dst * 128 : 1152 + dst * 128] = w_qkv[1, :, at(src, 128)]
+        for src, dst in up_blocks(core, zl):
+            rest[i][:, dst * 128 : dst * 128 + 128] = w_up[0, :, at(src, 128)]
+            rest[i][:, 1792 + dst * 128 : 1920 + dst * 128] = w_up[1, :, at(src, 128)]
+        first[i][32:48, 0:128] = small.astype(BF)
+        first[i][32:48, 128:768] = jnp.zeros((16, 640), BF)
+    low_zl = lax.axis_index("zl") == 0
+    for l in range(2):
+        w = inner_columns(w_out[l].astype(F32)).astype(BF)
+        out_a[l * 32 : l * 32 + 32] = jnp.where(low_zl, w[:, :512], w[:, 512:])
+        out_b[l * 32 : l * 32 + 32] = jnp.where(low_zl, w[:, 512:], w[:, :512])
+        down[l] = inner_columns(w_down[l].astype(F32)).astype(BF)
+
+
+def put_out(piece, layer, out_a, out_b):
+    for ref, flip in ((out_a, 0), (out_b, 1)):
+        zl_from = bit("y", flip)
+        for h in range(2):
+            piece[pl.ds(pl.multiple_of(h * 64 + zl_from * 32, 32), 32), 768:1024] = ref[
+                layer * 32 : layer * 32 + 32, h * 256 : h * 256 + 256
+            ]
+
+
+def pack_first(m0, m1, m2, m3, out_a, out_b, piece):
+    lane = lax.broadcasted_iota(jnp.int32, (16, 128), 1)
+    kind = lax.broadcasted_iota(jnp.int32, (16, 128), 0) % 8
+    one = jnp.zeros((16, 128), F32)
+    two = jnp.zeros((16, 128), F32)
+    for i, m in enumerate((m0, m1, m2, m3)):
+        core, zl = bit("core", RANKS[i][0]), bit("zl", RANKS[i][1])
+        piece[at(core * 2 + zl, 32), 0:768] = m[0:32, :]
+        s = m[32:48, 0:128].astype(F32)
+        mine = (kind < 6) & (lane // 32 == core * 2 + zl)
+        pair = (kind == 6) & (lane // 64 == zl)
+        if i == 0:
+            mine = mine | (kind == 7)
+        one = one + jnp.where(mine | (pair & (core == 0)), s, 0.0)
+        two = two + jnp.where(pair & (core == 1), s, 0.0)
+    put_out(piece, 0, out_a, out_b)
+    piece[128:144, 0:128] = one.astype(BF)
+    piece[128:144, 128:256] = two.astype(BF)
+    piece[128:144, 256:1024] = jnp.zeros((16, 768), BF)
+
+
+def pack_rest(m0, m1, m2, m3, out_a, out_b, down, mlp_0, att_1, mlp_1):
+    for i, m in enumerate((m0, m1, m2, m3)):
+        spot = at(bit("core", RANKS[i][0]) * 2 + bit("zl", RANKS[i][1]), 32)
+        mlp_0[spot, :] = m[:, 0:1024]
+        att_1[spot, 0:768] = m[:, 1024:1792]
+        mlp_1[spot, :] = m[:, 1792:2816]
+    put_out(att_1, 1, out_a, out_b)
+    mlp_0[128:256, :] = down[0]
+    mlp_1[128:256, :] = down[1]
+
+
+def gather_slots(piece):
+    far = swap(piece, "zh")
+    near_x = swap(piece, "x")
+    near_y = swap(piece, "y")
+    far_y = swap(far, "y")
+    far_x = swap(far, "x")
+    near_xy = swap(near_x, "y")
+    far_yx = swap(far_y, "x")
+    return (piece, far, near_x, far_x, near_y, far_y, near_xy, far_yx)
+
+
+def load_rows(pieces, scratch, row, columns):
+    for r, block in slot_blocks():
+        scratch[at(block, 128), :] = pieces[r][row : row + 128, 0:columns]
+
+
+def load_out(pieces, scratch):
+    for r, y, x, zh in slot_places():
+        for h in range(2):
+            scratch[at(x * 2 + zh, 64), at(y * 2 + h, 256)] = pieces[r][
+                h * 64 : h * 64 + 64, 768:1024
+            ]
+
+
+def normal(x):
+    centred = x - jnp.mean(x, axis=-1, keepdims=True)
+    inv = lax.rsqrt(jnp.mean(centred * centred, axis=-1, keepdims=True) + EPSILON)
+    return centred * inv, inv
+
+
+def load_stream(blocks, scratch):
+    for i, (dc, dl) in enumerate(RANKS):
+        spot = at(bit("core", dc) * 2 + bit("zl", dl), 128)
+        scratch[spot, :] = inner_columns(blocks[i][0].astype(F32)).astype(scratch.dtype)
+
+
+def load_cores(mine, other, scratch):
+    scratch[at(bit("core", 0), 256), :] = mine[...]
+    scratch[at(bit("core", 1), 256), :] = other[...]
+
+
+def split_product(left, right, keep, send):
+    mine, other = at(bit("core", 0), 256), at(bit("core", 1), 256)
+    send[...] = right(left[other, :]).astype(BF)
+    keep[...] = right(left[mine, :])
+
+
+def row_positions(order, dim):
+    shape_ = (512, 1) if dim == 0 else (1, 512)
+    row = lax.broadcasted_iota(jnp.int32, shape_, dim)
+    start = jnp.zeros(shape_, jnp.int32)
+    for c in range(4):
+        lead = order[c]
+        start = jnp.where(row // 64 == 2 * c, lead, start)
+        start = jnp.where(row // 64 == 2 * c + 1, 7 - lead, start)
+    return start * 64 + row % 64
+
+
+def masked_distance(seg_a, seg_b, order, dist):
+    same = lax.axis_index("core") == lax.axis_index("zh")
+    seg = jnp.where(same, seg_a[...], seg_b[...])
+    ends = [jnp.sum((seg < d).astype(jnp.int32), axis=1, keepdims=True) for d in (1, 2)]
+
+    def doc(pos):
+        return (pos >= ends[0]).astype(jnp.int32) + (pos >= ends[1]).astype(jnp.int32)
+
+    rows, cols = row_positions(order, 0), row_positions(order, 1)
+    gap = rows - cols
+    fine = (gap >= 0) & (doc(rows) == doc(cols))
+    dist[...] = jnp.where(fine, gap.astype(F32), 1e32)
+
+
+def slope_of(pair, half):
+    core, zl = lax.axis_index("core"), lax.axis_index("zl")
+    value = jnp.float32(0.0)
+    for c in range(2):
+        for z in range(2):
+            head = 8 * z + 4 * pair + 2 * c + half
+            value = jnp.where((core == c) & (zl == z), jnp.float32(2.0 ** (-8.0 * (head + 1) / HEADS)), value)
+    return value
+
+
+def attend(qkv, dist, probs, o):
+    low = lax.broadcasted_iota(jnp.int32, (128, 128), 1) < 64
+    for pair in range(2):
+        k = qkv[:, 256 + pair * 128 : 384 + pair * 128]
+        v = qkv[:, 512 + pair * 128 : 640 + pair * 128]
+
+        def rows(step, carry):
+            spot = at(step, 128)
+            q = qkv[spot, pair * 128 : pair * 128 + 128]
+            d = dist[spot, :]
+            found = []
+            for half in range(2):
+                qh = jnp.where(low == (half == 0), q, jnp.zeros_like(q))
+                s = dot_t(qh, k) * 0.125 - slope_of(pair, half) * d
+                p = jnp.exp(s - jnp.max(s, axis=1, keepdims=True))
+                p = (p / jnp.sum(p, axis=1, keepdims=True)).astype(BF)
+                probs[pair * 2 + half, spot, :] = p
+                found.append(dot(p, v))
+            o[spot, pair * 128 : pair * 128 + 128] = jnp.where(low, *found).astype(BF)
+            return carry
+
+        lax.fori_loop(0, 4, rows, 0)
+
+
+def attention_part(h1, vec, layer, pieces, seg_a, seg_b, order, outs, scratch):
+    qkv, probs, o, keep, send = outs
+    wq, wo, dist = scratch
+    load_rows(pieces, wq, 0, 768)
+    load_out(pieces, wo)
+    masked_distance(seg_a, seg_b, order, dist)
+    qkv[...] = (dot(h1[...], wq[...]) + vec[layer * 8 + 6 : layer * 8 + 7, 0:768]).astype(BF)
+    attend(qkv, dist, probs, o)
+    split_product(o, lambda rows: dot(rows, wo[...]), keep, send)
+
+
+def first_attention(t0, t1, t2, t3, *refs):
+    pieces, (seg_a, seg_b, order), refs = refs[:8], refs[8:11], refs[11:]
+    vec, h1, outs, scratch = refs[0], refs[1], refs[2:7], refs[7:]
+    q_one, q_two, scratch = scratch[0], scratch[1], scratch[2:]
+    for r, block in slot_blocks():
+        vec[:, at(block, 128)] = pieces[r][128:144, 0:128].astype(F32)
+        q_two[:, at(block, 128)] = pieces[r][128:144, 128:256].astype(F32)
+    q_one[...] = vec[...]
+    core, zl = lax.axis_index("core"), lax.axis_index("zl")
+    for l in range(2):
+        row = slice(l * 8 + 6, l * 8 + 7)
+        for base, y in ((0, 0), (512, 1)):
+            block = (y * 2 + zl) * 2 + core
+            vec[row, base : base + 128] = q_one[row, at(block, 128)]
+            vec[row, base + 128 : base + 256] = q_two[row, at(block, 128)]
+        vec[row, 256:512] = jnp.zeros((1, 256), F32)
+    load_stream((t0, t1, t2, t3), h1)
+    for i in range(4):
+        spot = slice(i * 128, i * 128 + 128)
+        z, _ = normal(h1[spot, :].astype(F32))
+        h1[spot, :] = (z * vec[0:1, :] + vec[1:2, :]).astype(BF)
+    attention_part(h1, vec, 0, pieces, seg_a, seg_b, order, outs, scratch)
+
+
+def next_attention(mine, other, *refs):
+    pieces, (vec, seg_a, seg_b, order), refs = refs[:8], refs[8:12], refs[12:]
+    h1, outs, scratch = refs[0], refs[1:6], refs[6:]
+    load_cores(mine, other, h1)
+    attention_part(h1, vec, 1, pieces, seg_a, seg_b, order, outs, scratch)
+
+
+def add_parts(keep, came, out):
+    out[...] = (keep[...] + came[...].astype(F32)).astype(BF)
+
+
+def norm_stage(bias_row, gain_row):
+    def kernel(x, part, came, vec, x_out, h):
+        for i in range(2):
+            spot = slice(i * 128, i * 128 + 128)
+            v = x[spot, :] + part[spot, :].astype(F32) + came[spot, :].astype(F32)
+            v = v + vec[bias_row : bias_row + 1, :]
+            x_out[spot, :] = v
+            z, _ = normal(v)
+            h[spot, :] = (z * vec[gain_row : gain_row + 1] + vec[gain_row + 1 : gain_row + 2]).astype(BF)
+
+    return kernel
+
+
+def first_norm_stage(t0, t2, part, came, vec, x_out, h, x0):
+    x0[at(bit("zl", 0), 128), :] = inner_columns(t0[0].astype(F32))
+    x0[at(bit("zl", 1), 128), :] = inner_columns(t2[0].astype(F32))
+    norm_stage(2, 3)(x0, part, came, vec, x_out, h)
+
+
+def mlp_stage(layer):
+    def kernel(mine, other, *refs):
+        pieces, vec, refs = refs[:8], refs[8], refs[9:]
+        h2, u, a, keep, send, w = refs
+        load_cores(mine, other, h2)
+        load_rows(pieces, w, 0, 1024)
+        for i in range(4):
+            spot = slice(i * 128, i * 128 + 128)
+            z = dot(h2[spot, :], w[...]) + vec[layer * 8 + 7 : layer * 8 + 8, :]
+            u[spot, :] = z
+            a[spot, :] = gelu_tanh(z).astype(BF)
+        load_rows(pieces, w, 128, 1024)
+        split_product(a, lambda rows: dot(rows, w[...]), keep, send)
+
+    return with_scratch(kernel, pltpu.VMEM((1024, 1024), BF))
+
+
+def finish_rows(x, part, came, vec, out):
+    spot = at(bit("zl", 0), 128)
+    v = x[spot, :] + part[spot, :].astype(F32) + came[spot, :].astype(F32) + vec[13:14, :]
+    out[0] = inner_columns(v).astype(BF)
+
+
+def gelu_slope(u):
+    c = 0.7978845608028654
+    t = jnp.tanh(c * (u + 0.044715 * u * u * u))
+    return 0.5 * (1.0 + t) + 0.5 * u * (1.0 - t * t) * (c * (1.0 + 3 * 0.044715 * u * u))
+
+
+def mlp_back_part(gy2, u, pieces, gu, keep, send, w):
+    load_rows(pieces, w, 128, 1024)
+    for i in range(4):
+        spot = slice(i * 128, i * 128 + 128)
+        gu[spot, :] = (dot_t(gy2[spot, :], w[...]) * gelu_slope(u[spot, :])).astype(BF)
+    load_rows(pieces, w, 0, 1024)
+    split_product(gu, lambda rows: dot_t(rows, w[...]), keep, send)
+
+
+def first_mlp_back(c0, c1, c2, c3, u, *refs):
+    pieces, refs = refs[:8], refs[8:]
+    load_stream((c0, c1, c2, c3), refs[0])
+    mlp_back_part(refs[0], u, pieces, *refs[1:])
+
+
+def next_mlp_back(mine, other, u, *refs):
+    pieces, refs = refs[:8], refs[8:]
+    load_cores(mine, other, refs[0])
+    mlp_back_part(refs[0], u, pieces, *refs[1:])
+
+
+def turned_dot(left, right):
+    return lax.dot_general(left, right, (((0,), (0,)), ((), ())), preferred_element_type=F32)
+
+
+def slot_spots(near_send, near_0, near_1, far_send, far_0, far_1):
+    return (
+        near_0, far_0, near_1, far_send.at[0], near_send.at[0], far_1, near_send.at[1], far_send.at[1],
+    )
+
+
+def mlp_grads(h2, a, gy2, gu, *outs):
+    spots = slot_spots(*outs)
+    for r, block in slot_blocks():
+        spots[r][0:128, :] = turned_dot(h2[:, at(block, 128)], gu[...]).astype(BF)
+        spots[r][128:256, :] = turned_dot(a[:, at(block, 128)], gy2[...]).astype(BF)
+
+
+def norm_back(gx, part, came, x, gain, gm, gy, sums):
+    totals = [jnp.zeros((1, x.shape[1]), F32) for _ in range(4)]
+    for i in range(2):
+        spot = slice(i * 128, i * 128 + 128)
+        dh = part[spot, :].astype(F32) + came[spot, :].astype(F32)
+        z, inv = normal(x[spot, :])
+        dz = dh * gain
+        mean_a = jnp.mean(dz, axis=-1, keepdims=True)
+        mean_b = jnp.mean(dz * z, axis=-1, keepdims=True)
+        up = gx[spot, :]
+        g = up + inv * (dz - mean_a - z * mean_b)
+        gm[spot, :] = g
+        rounded = g.astype(BF)
+        gy[spot, :] = rounded
+        new = (dh * z, dh, rounded.astype(F32), up.astype(BF).astype(F32))
+        totals = [t + jnp.sum(v, axis=0, keepdims=True) for t, v in zip(totals, new)]
+    sums[...] = jnp.concatenate(totals + [jnp.zeros((4, x.shape[1]), F32)], axis=0)
+
+
+def norm_back_stage(gain_row):
+    def kernel(gx, part, came, x, vec, gm, gy, sums):
+        norm_back(gx, part, came, x, vec[gain_row : gain_row + 1, :], gm, gy, sums)
+
+    return kernel
+
+
+def first_norm_back(c0, c2, part, came, x, vec, gm, gy, sums, gx):
+    gx[at(bit("zl", 0), 128), :] = inner_columns(c0[0].astype(F32))
+    gx[at(bit("zl", 1), 128), :] = inner_columns(c2[0].astype(F32))
+    norm_back(gx, part, came, x, vec[11:12, :], gm, gy, sums)
+
+
+def last_norm_back(gx, part, came, t0, t2, vec, grad, sums, x, gm, gy):
+    x[at(bit("zl", 0), 128), :] = inner_columns(t0[0].astype(F32))
+    x[at(bit("zl", 1), 128), :] = inner_columns(t2[0].astype(F32))
+    norm_back(gx, part, came, x, vec[0:1, :], gm, gy, sums)
+    grad[0] = inner_columns(gm[at(bit("zl", 0), 128), :]).astype(BF)
+
+
+def attention_back(mine, other, qkv, probs, *refs):
+    pieces, refs = refs[:8], refs[8:]
+    gy1, gqkv, keep, send, wq, wo, go, gk, gv = refs
+    load_cores(mine, other, gy1)
+    load_rows(pieces, wq, 0, 768)
+    load_out(pieces, wo)
+    go[...] = dot_t(gy1[...], wo[...]).astype(BF)
+    low = lax.broadcasted_iota(jnp.int32, (128, 128), 1) < 64
+    low_all = lax.broadcasted_iota(jnp.int32, (512, 128), 1) < 64
+    for pair in range(2):
+        k = qkv[:, 256 + pair * 128 : 384 + pair * 128]
+        v = qkv[:, 512 + pair * 128 : 640 + pair * 128]
+        gk[...] = jnp.zeros_like(gk)
+        gv[...] = jnp.zeros_like(gv)
+
+        def rows(step, carry):
+            spot = at(step, 128)
+            q = qkv[spot, pair * 128 : pair * 128 + 128]
+            g = go[spot, pair * 128 : pair * 128 + 128]
+            gq = []
+            for half in range(2):
+                lanes = low == (half == 0)
+                gh = jnp.where(lanes, g, jnp.zeros_like(g))
+                qh = jnp.where(lanes, q, jnp.zeros_like(q))
+                p = probs[pair * 2 + half, spot, :]
+                pf = p.astype(F32)
+                dp = dot_t(gh, v)
+                ds = (pf * (dp - jnp.sum(dp * pf, axis=1, keepdims=True))).astype(BF)
+                gq.append(dot(ds, k))
+                gk[...] += turned_dot(ds, qh)
+                gv[...] += turned_dot(p, gh)
+            gqkv[spot, pair * 128 : pair * 128 + 128] = (0.125 * jnp.where(low, *gq)).astype(BF)
+            return carry
+
+        lax.fori_loop(0, 4, rows, 0)
+        gqkv[:, 256 + pair * 128 : 384 + pair * 128] = (0.125 * gk[...]).astype(BF)
+        gqkv[:, 512 + pair * 128 : 640 + pair * 128] = gv[...].astype(BF)
+    split_product(gqkv, lambda rows: dot_t(rows, wq[...]), keep, send)
+
+
+def attention_grads(h1, o, gy1, gqkv, *outs):
+    spots, d_out = slot_spots(*outs[:6]), outs[6]
+    d_out[...] = turned_dot(o[...], gy1[...]).astype(BF)
+    for (r, block), (_, y, x, zh) in zip(slot_blocks(), slot_places()):
+        spots[r][0:128, 0:768] = turned_dot(h1[:, at(block, 128)], gqkv[...]).astype(BF)
+        for h in range(2):
+            spots[r][h * 64 : h * 64 + 64, 768:1024] = d_out[at(x * 2 + zh, 64), at(y * 2 + h, 256)]
+
+
+def last_attention_grads(h1, o, gy1, gqkv, g1, e1, e0, gu1, gu0, gq1, *outs):
+    attention_grads(h1, o, gy1, gqkv, *outs[:7])
+    spots, (ups, wide) = slot_spots(*outs[:6]), outs[7:]
+    none = jnp.zeros((2, 1024), F32)
+    parts = [g1[0:2, :], e1[2:3, :], e1[0:2, :], e1[3:4, :], none, none]
+    wide[...] = jnp.concatenate(parts + [e0[2:3, :], e0[0:2, :], e0[3:4, :], none], axis=0)
+    sums = [jnp.sum(v[...].astype(F32), axis=0, keepdims=True) for v in (gu1, gu0)]
+    ups[...] = jnp.concatenate(sums + [jnp.zeros((14, 1024), F32)], axis=0)
+    q = [jnp.sum(v[...].astype(F32), axis=0, keepdims=True) for v in (gq1, gqkv)]
+    q = jnp.concatenate(q + [jnp.zeros((14, 768), F32)], axis=0)
+    core, zl = lax.axis_index("core"), lax.axis_index("zl")
+    for r, block in slot_blocks():
+        rows = slice(128, 144)
+        spots[r][rows, 0:128] = wide[:, at(block, 128)].astype(BF)
+        spots[r][rows, 128:256] = ups[:, at(block, 128)].astype(BF)
+        mine = jnp.where(block == 4 + zl * 2 + core, q[:, 512:768], jnp.zeros((16, 256), F32))
+        mine = jnp.where(block == zl * 2 + core, q[:, 0:256], mine)
+        spots[r][rows, 256:512] = mine.astype(BF)
+        spots[r][rows, 512:1024] = jnp.zeros((16, 512), BF)
+
+
+def scatter_slots(near_send, near_0, near_1, far_send, far_0, far_1):
+    near = swap(near_send, "y")
+    far = swap(far_send, "x")
+    near_2 = swap((near_1.astype(F32) + near[1].astype(F32)).astype(BF), "x")
+    far_2 = swap((far_1.astype(F32) + far[1].astype(F32)).astype(BF), "y")
+    far_all = far_0.astype(F32) + far[0].astype(F32) + far_2.astype(F32)
+    far_3 = swap(far_all.astype(BF), "zh")
+    return near_0, near, near_2, far_3
+
+
+def summed(parts, rows, columns):
+    near_0, near, near_2, far_3 = parts
+    value = near_0[rows, columns].astype(F32) + near[0, rows, columns].astype(F32)
+    return value + near_2[rows, columns].astype(F32) + far_3[rows, columns].astype(F32)
+
+
+def own_out(parts, flip):
+    row = bit("y", flip) * 32
+    halves = []
+    for h in range(2):
+        spot = pl.ds(pl.multiple_of(h * 64 + row, 32), 32)
+        halves.append(summed(parts, spot, slice(768, 1024)))
+    return jnp.concatenate(halves, axis=1)
+
+
+def unpack_rest(*refs):
+    mlp_1, att_1, mlp_0 = refs[0:4], refs[4:8], refs[8:12]
+    mine, sends, a, b, down = refs[12], refs[13:16], refs[16], refs[17], refs[18]
+    for i, (dc, dl) in enumerate(RANKS):
+        rows = at(bit("core", dc) * 2 + bit("zl", dl), 32)
+        to = mine if i == 0 else sends[i - 1]
+        for parts, start, width in ((mlp_0, 0, 1024), (att_1, 1024, 768), (mlp_1, 1792, 1024)):
+            value = summed(parts, rows, slice(0, width))
+            to[:, start : start + width] = value.astype(to.dtype)
+    a[...] = own_out(att_1, 0).astype(BF)
+    b[...] = own_out(att_1, 1).astype(BF)
+    for l, parts in ((0, mlp_0), (1, mlp_1)):
+        down[l] = inner_columns(summed(parts, slice(128, 256), slice(0, 1024)))
+
+
+def unpack_last(near_0, near, near_2, far_3, a1, b1, mine, *refs):
+    parts = (near_0, near, near_2, far_3)
+    sends, (a, b) = refs[0:3], refs[3:5]
+    for i, (dc, dl) in enumerate(RANKS):
+        rows = at(bit("core", dc) * 2 + bit("zl", dl), 32)
+        to = mine if i == 0 else sends[i - 1]
+        to[0:32, :] = summed(parts, rows, slice(0, 768)).astype(to.dtype)
+        to[32:48, :] = summed(parts, slice(128, 144), slice(0, 768)).astype(to.dtype)
+    a[0:32, :] = own_out(parts, 0).astype(BF)
+    b[0:32, :] = own_out(parts, 1).astype(BF)
+    a[32:64, :] = a1[...]
+    b[32:64, :] = b1[...]
+
+
+def finish(rest, r1, r2, r3, last, l1, l2, l3, a, b, total, *outs):
+    g1, b1, w_qkv, qv, w_out, bo, g2, b2, w_up, up, bd = outs
+    for i, (rm, lm) in enumerate(((rest, last), (r1, l1), (r2, l2), (r3, l3))):
+        core, zl = bit("core", RANKS[i][0]), bit("zl", RANKS[i][1])
+        for src, dst in qkv_blocks(core, zl):
+            w_qkv[0, :, at(src, 128)] = lm[0:32, dst * 128 : dst * 128 + 128].astype(F32)
+            w_qkv[1, :, at(src, 128)] = rm[:, 1024 + dst * 128 : 1152 + dst * 128].astype(F32)
+        for src, dst in up_blocks(core, zl):
+            w_up[0, :, at(src, 128)] = rm[:, dst * 128 : dst * 128 + 128].astype(F32)
+            w_up[1, :, at(src, 128)] = rm[:, 1792 + dst * 128 : 1920 + dst * 128].astype(F32)
+    low_zl = lax.axis_index("zl") == 0
+    for l in range(2):
+        va, vb = a[l * 32 : l * 32 + 32].astype(F32), b[l * 32 : l * 32 + 32].astype(F32)
+        w = jnp.concatenate([jnp.where(low_zl, va, vb), jnp.where(low_zl, vb, va)], axis=1)
+        w_out[l] = inner_columns(w)
+    spot = lax.axis_index("core") * 2 + lax.axis_index("zl")
+
+    def chunk(value, size):
+        found = jnp.zeros((value.shape[0], size), F32)
+        for j in range(4):
+            found = jnp.where(spot == j, value[:, j * size : j * size + size], found)
+        return found
+
+    wide = chunk(last[32:48, 0:128] + l1[32:48, 0:128].astype(F32), 32)
+    block = (lax.axis_index("y") * 2 + lax.axis_index("x")) * 2 + lax.axis_index("zh")
+    late = chunk(total[:, at(block, 128)], 32)
+    for row, ref in ((2, bo), (3, g2), (4, b2), (5, bd)):
+        ref[...] = jnp.concatenate([wide[row + 8 : row + 9], wide[row : row + 1]], axis=0)
+    g1[...] = jnp.concatenate([late[0:1], wide[0:1]], axis=0)
+    b1[...] = jnp.concatenate([late[1:2], wide[1:2]], axis=0)
+    up[...] = jnp.concatenate([last[33:34, 128:256], last[32:33, 128:256]], axis=0)
+    both = last[32:48, 256:512]
+    for m in (l1, l2, l3):
+        both = both + m[32:48, 256:512].astype(F32)
+    both = chunk(both, 64)
+    qv[...] = jnp.concatenate([both[1:2], both[0:1]], axis=0)
+
+
+def corner(value):
+    return lax.ppermute(value, ("core", "zh"), [(0, 0), (1, 2), (2, 1), (3, 3)])
+
+
+def to_partners(messages):
+    one, two, three = messages
+    return (
+        swap(one, "core"),
+        swap(two, "zl"),
+        lax.ppermute(three, ("core", "zl"), [(0, 3), (3, 0), (1, 2), (2, 1)]),
+    )
+
+
+def stream_blocks(block):
+    block = corner(block)
+    by_zl = swap(block, "zl")
+    return (block, swap(block, "core"), by_zl, swap(by_zl, "core"))
+
+
+def narrow_body(
+    tokens, segment_ids, group_order, ln1_gain, ln1_bias, qkv_weight, qv_bias, out_weight, out_bias,
+    ln2_gain, ln2_bias, up_weight, up_bias, down_weight, down_bias, cotangent,
+):
+    ready = run(
+        prepare,
+        [shape(48, 768)] * 4 + [shape(32, 2816)] * 4 + [shape(64, 512)] * 2 + [shape(2, 128, 1024)],
+        ln1_gain, ln1_bias, out_bias, ln2_gain, ln2_bias, down_bias, qv_bias, up_bias,
+        qkv_weight, out_weight, up_weight, down_weight,
+    )
+    first = (ready[0],) + to_partners(ready[1:4])
+    out_a = lax.ppermute(ready[8], ("y", "zl"), [(0, 0), (1, 2), (2, 1), (3, 3)])
+    out_b = lax.ppermute(ready[9], ("y", "zl"), [(0, 2), (1, 0), (2, 3), (3, 1)])
+    (att_0,) = run(pack_first, [shape(144, 1024)], *first, out_a, out_b)
+    att_0 = gather_slots(att_0)
+    blocks = stream_blocks(tokens)
+    rest = (ready[4],) + to_partners(ready[5:8])
+    mlp_0, att_1, mlp_1 = run(
+        pack_rest, [shape(256, 1024), shape(128, 1024), shape(256, 1024)],
+        *rest, out_a, out_b, ready[10],
+    )
+    mlp_0, att_1, mlp_1 = gather_slots(mlp_0), gather_slots(att_1), gather_slots(mlp_1)
+    cots = stream_blocks(cotangent)
+    segments = (segment_ids, swap(segment_ids, "core"), group_order)
+
+    def share(keep, send):
+        (part,) = run(add_parts, [shape(256, 1024)], keep, swap(send, "core"))
+        return part, swap(part, "zl")
+
+    def with_other(value):
+        return value, swap(value, "core")
+
+    attention_outs = [
+        shape(512, 1024), shape(512, 768), shape(4, 512, 512), shape(512, 256),
+        shape(256, 1024, dtype=F32), shape(256, 1024),
+    ]
+    weights_scratch = [pltpu.VMEM((1024, 768), BF), pltpu.VMEM((256, 1024), BF)]
+    dist = pltpu.VMEM((512, 512), F32)
+    vec_scratch = [pltpu.VMEM((16, 1024), F32)] * 2
+    rows_out = [shape(256, 1024, dtype=F32), shape(256, 1024)]
+    mlp_outs = [
+        shape(512, 1024), shape(512, 1024, dtype=F32), shape(512, 1024),
+        shape(256, 1024, dtype=F32), shape(256, 1024),
+    ]
+    wide = pltpu.VMEM((1024, 1024), BF)
+
+    vec, h1_0, qkv_0, probs_0, o_0, keep, send = run(
+        with_scratch(first_attention, *vec_scratch, *weights_scratch, dist),
+        [shape(16, 1024, dtype=F32)] + attention_outs, *blocks, *att_0, *segments,
+    )
+    x1_0, h = run(
+        with_scratch(first_norm_stage, pltpu.VMEM((256, 1024), F32)),
+        rows_out, blocks[0], blocks[2], *share(keep, send), vec,
+    )
+    h2_0, u_0, a_0, keep, send = run(mlp_stage(0), mlp_outs, *with_other(h), *mlp_0, vec)
+    x2_0, h = run(norm_stage(5, 8), rows_out, x1_0, *share(keep, send), vec)
+    h1_1, qkv_1, probs_1, o_1, keep, send = run(
+        with_scratch(next_attention, *weights_scratch, dist),
+        attention_outs, *with_other(h), *att_1, vec, *segments,
+    )
+    x1_1, h = run(norm_stage(10, 11), rows_out, x2_0, *share(keep, send), vec)
+    h2_1, u_1, a_1, keep, send = run(mlp_stage(1), mlp_outs, *with_other(h), *mlp_1, vec)
+    (final,) = run(finish_rows, [shape(1, 128, 1024)], x1_1, *share(keep, send), vec)
+    output = corner(final)
+
+    mlp_back_outs = [
+        shape(512, 1024), shape(512, 1024), shape(256, 1024, dtype=F32), shape(256, 1024),
+    ]
+    norm_outs = rows_out + [shape(8, 1024, dtype=F32)]
+    attention_back_outs = [
+        shape(512, 1024), shape(512, 768), shape(256, 1024, dtype=F32), shape(256, 1024),
+    ]
+    attention_back_scratch = weights_scratch + [
+        pltpu.VMEM((512, 256), BF), pltpu.VMEM((512, 128), F32), pltpu.VMEM((512, 128), F32),
+    ]
+
+    def grad_outs(rows):
+        near = [shape(2, rows, 1024), shape(rows, 1024), shape(rows, 1024)]
+        return near + near
+
+    out_scratch = pltpu.VMEM((256, 1024), BF)
+
+    gy2, gu_1, keep, send = run(
+        with_scratch(first_mlp_back, wide), mlp_back_outs, *cots, u_1, *mlp_1
+    )
+    mlp_sums_1 = scatter_slots(*run(mlp_grads, grad_outs(256), h2_1, a_1, gy2, gu_1))
+    gm, gy, e1 = run(
+        with_scratch(first_norm_back, pltpu.VMEM((256, 1024), F32)),
+        norm_outs, cots[0], cots[2], *share(keep, send), x1_1, vec,
+    )
+    gy1, gqkv_1, keep, send = run(
+        with_scratch(attention_back, *attention_back_scratch),
+        attention_back_outs, *with_other(gy), qkv_1, probs_1, *att_1,
+    )
+    att_sums_1 = scatter_slots(
+        *run(with_scratch(attention_grads, out_scratch), grad_outs(128), h1_1, o_1, gy1, gqkv_1)
+    )
+    gx, gy, g1 = run(norm_back_stage(8), norm_outs, gm, *share(keep, send), x2_0, vec)
+    gy2, gu_0, keep, send = run(
+        with_scratch(next_mlp_back, wide), mlp_back_outs, *with_other(gy), u_0, *mlp_0
+    )
+    mlp_sums_0 = scatter_slots(*run(mlp_grads, grad_outs(256), h2_0, a_0, gy2, gu_0))
+    gm, gy, e0 = run(norm_back_stage(3), norm_outs, gx, *share(keep, send), x1_0, vec)
+    gy1, gqkv_0, keep, send = run(
+        with_scratch(attention_back, *attention_back_scratch),
+        attention_back_outs, *with_other(gy), qkv_0, probs_0, *att_0,
+    )
+    att_sums_0 = scatter_slots(
+        *run(
+            with_scratch(
+                last_attention_grads, out_scratch, *vec_scratch
+            ),
+            grad_outs(144), h1_0, o_0, gy1, gqkv_0, g1, e1, e0, gu_1, gu_0, gqkv_1,
+        )
+    )
+    grad, late = run(
+        with_scratch(last_norm_back, *[pltpu.VMEM((256, 1024), F32)] * 2, pltpu.VMEM((256, 1024), BF)),
+        [shape(1, 128, 1024), shape(8, 1024, dtype=F32)],
+        gm, *share(keep, send), blocks[0], blocks[2], vec,
+    )
+    tokens_grad = corner(grad).astype(F32)
+    for axis in ("core", "zh", "x", "y"):
+        late = late + swap(late, axis)
+
+    rest = run(
+        unpack_rest,
+        [shape(32, 2816, dtype=F32)] + [shape(32, 2816)] * 3 + [shape(32, 512)] * 2
+        + [shape(2, 128, 1024, dtype=F32)],
+        *mlp_sums_1, *att_sums_1, *mlp_sums_0,
+    )
+    last = run(
+        unpack_last,
+        [shape(48, 768, dtype=F32)] + [shape(48, 768)] * 3 + [shape(64, 512)] * 2,
+        *att_sums_0, rest[4], rest[5],
+    )
+    back_a = lax.ppermute(last[4], ("y", "zl"), [(0, 0), (1, 2), (2, 1), (3, 3)])
+    back_b = lax.ppermute(last[5], ("y", "zl"), [(0, 1), (1, 3), (2, 0), (3, 2)])
+    sizes = (
+        (2, 32), (2, 32), (2, 32, 3072), (2, 64), (2, 32, 1024), (2, 32), (2, 32), (2, 32),
+        (2, 32, 4096), (2, 128), (2, 32),
+    )
+    g = run(
+        finish, [shape(*s, dtype=F32) for s in sizes],
+        rest[0], *to_partners(rest[1:4]), last[0], *to_partners(last[1:4]), back_a, back_b, late,
+    )
+    return (output, tokens_grad) + tuple(g[:10]) + (rest[6], g[10])
+
+
 def solution(mesh):
     fsdp, ctx = mesh.shape["fsdp"], mesh.shape["ctx"]
     fine = Mesh(mesh.devices.reshape(fsdp // 4, 2, 2, 2, ctx // 2), AXES)
+    body = narrow_body if fine.devices.shape == (2, 2, 2, 2, 2) else wide_body
     stream, place = ("y", "x", "core"), ("zh", "zl")
     rows = P(stream, place, None)
     flat, deep = P(None, AXES), P(None, AXES, None)

time: 896 us -> 488 us (0.54)
  local copies, waits for them, and re-layouts: 227 us -> 30.4 us
  other arithmetic: 119 us -> 9.3 us
  Pallas kernels: 0 us -> 76.6 us
  starting transfers between devices: 170 us -> 107 us
  matrix products: 60.5 us -> 0 us
  waiting for transfers between devices: 302 us -> 257 us
    pallas_call x0 -> x34, Pallas kernels: none -> 76.6 us  [run(): pl.pallas_call(kernel, out_shape=tuple(outs), in_specs=[smem if v.size ==...]
    ppermute x158 -> x89, starting transfers between devices: 163 us -> 97 us  [swap(): return lax.ppermute(value, axis, [(0, 1), (1, 0)])]
    ppermute x158 -> x89, waiting for transfers between devices: 302 us -> 236 us  [swap(): return lax.ppermute(value, axis, [(0, 1), (1, 0)])]
    dot_general x36 -> x0, matrix products: 60.5 us -> none  [the longest x8 15.8 us: dot_t(): lax.dot_general(left, matrix, (((1,), (1,)), ((), ())), preferred_element...]
    unnamed x427 -> x233, local copies, waits for them, and re-layouts: 79.3 us -> 30.4 us
    select_n x59 -> x0, other arithmetic: 43.4 us -> none  [the longest x48 37.7 us: flipped(): return jnp.where(here(axis) == 0, value, jnp.flip(value, dim))]
    another operation x59 -> x0, local copies, waits for them, and re-layouts: 34 us -> none  [the longest x12 13.1 us: gather_shards(): rel = jnp.stack([shard, far, near_x, far_x, near_y, far_y, near_xy, far_yx])]
    another operation x58 -> x0, other arithmetic: 23.9 us -> none  [the longest x45 14.9 us: ordered(): jnp.stack([jnp.where(first, mine, other), jnp.where(first, other, mine)])]
  transfers between devices with their start and end apart: 162 -> 101, of which waited for: 78 -> 45; matrix products, arithmetic and copies ran while one was open for 32% -> 2% of each run, Pallas kernels for 0% -> 12%
where the time goes in v2:
time: 488 us; the launch traced here: 482 us
  waiting for transfers between devices  257 us (53%)
  starting transfers between devices  107 us (22%)
  Pallas kernels  76.6 us (16%)
  local copies, waits for them, and re-layouts  30.4 us (6%)
  other arithmetic  9.3 us (2%)
    ppermute x89, waiting for transfers between devices, swap(): return lax.ppermute(value, axis, [(0, 1), (1, 0)])  236 us
    ppermute x89, starting transfers between devices, swap(): return lax.ppermute(value, axis, [(0, 1), (1, 0)])  97 us
    pallas_call x34, Pallas kernels, run(): pl.pallas_call(kernel, out_shape=tuple(outs), in_specs=[smem if v.size ==...  76.6 us
    unnamed x233, local copies, waits for them, and re-layouts  30.4 us
    ppermute x4, waiting for transfers between devices, to_partners(): lax.ppermute(three, ('core', 'zl'), [(0, 3), (3, 0), (1, 2), (2, 1)])  10.4 us
  transfers between devices with their start and end apart: 101, of which 45 were waited for; matrix products, arithmetic and copies ran while one was open for 2% of the time, Pallas kernels for 12%

profile of v2, /device:TPU:4, one launch (start us, length us, event | category | flops | bytes accessed | tf_op | source)
XLA Modules:
  0.0 482.3 jit_solution(7084000545535222684)
XLA Ops:
  12.2 3.4 collective-permute-start.7
  15.7 4.2 collective-permute-done.7.out_a
  20.8 2.7 collective-permute-start.9
  24.2 1.7 collective-permute-start.20
  29.2 10.3 %collective-permute-done.9.refs_1_ = bf16[144,1024]{1,0:T(8,128)(2,1)S(1)} collective-permute-done((bf16[144,1024]{1,0:T(8,128)(2,1)S(1)}, bf16[144,1024]{1,0:T(8,128)(2,1)S(1)}, u32[]{:S(2)}, u32[]{:S(2)}) %collective-permute-start.9) | collective-permute-done | bytes 294944 | tf_op jit(solution)/shard_map/ppermute | solution.py:20
  43.4 10.4 %collective-permute-done.22.m3 = bf16[32,2816]{1,0:T(8,128)(2,1)S(1)} collective-permute-done((bf16[32,2816]{1,0:T(8,128)(2,1)S(1)}, bf16[32,2816]{1,0:T(8,128)(2,1)S(1)}, u32[]{:S(2)}, u32[]{:S(2)}) %collective-permute-start.22) | collective-permute-done | bytes 180256 | tf_op jit(solution)/shard_map/ppermute | solution.py:980
  58.7 5.0 %collective-permute-done.11.refs_3_ = bf16[144,1024]{1,0:T(8,128)(2,1)S(1)} collective-permute-done((bf16[144,1024]{1,0:T(8,128)(2,1)S(1)}, bf16[144,1024]{1,0:T(8,128)(2,1)S(1)}, u32[]{:S(2)}, u32[]{:S(2)}) %collective-permute-start.11) | collective-permute-done | bytes 294944 | tf_op jit(solution)/shard_map/ppermute | solution.py:20
  64.4 5.1 %collective-permute-done.15.refs_7_ = bf16[144,1024]{1,0:T(8,128)(2,1)S(1)} collective-permute-done((bf16[144,1024]{1,0:T(8,128)(2,1)S(1)}, bf16[144,1024]{1,0:T(8,128)(2,1)S(1)}, u32[]{:S(2)}, u32[]{:S(2)}) %collective-permute-start.15) | collective-permute-done | bytes 294944 | tf_op jit(solution)/shard_map/ppermute | solution.py:20
  69.5 10.7 %shard_map.265 = (f32[16,1024]{1,0:T(8,128)S(1)}, bf16[512,1024]{1,0:T(8,128)(2,1)S(1)}, bf16[512,768]{1,0:T(8,128)(2,1)S(1)}, bf16[4,512,512]{2,1,0:T(8,128)(2,...) custom-call(bf16[1,128,1024]{2,1,0:T(8,128)(2,1)S(1)} %collective-permute-done.t0, ...), custom_call_target="tpu_custom_call" | custom-call | bytes 9244688 | tf_op jit(solution)/shard_map/pallas_call | solution.py:411
  82.0 2.1 collective-permute-done.23.refs_1_
  87.9 7.3 %collective-permute-done.24.refs_2_ = bf16[256,1024]{1,0:T(8,128)(2,1)S(1)} collective-permute-done((bf16[256,1024]{1,0:T(8,128)(2,1)S(1)}, bf16[256,1024]{1,0:T(8,128)(2,1)S(1)}, u32[]{:S(2)}, u32[]{:S(2)}) %collective-permute-start.24) | collective-permute-done | bytes 524320 | tf_op jit(solution)/shard_map/ppermute | solution.py:20
  95.7 3.2 collective-permute-done.27.refs_5_
  101.3 8.8 %collective-permute-done.26.refs_4_ = bf16[256,1024]{1,0:T(8,128)(2,1)S(1)} collective-permute-done((bf16[256,1024]{1,0:T(8,128)(2,1)S(1)}, bf16[256,1024]{1,0:T(8,128)(2,1)S(1)}, u32[]{:S(2)}, u32[]{:S(2)}) %collective-permute-start.26) | collective-permute-done | bytes 524320 | tf_op jit(solution)/shard_map/ppermute | solution.py:20
  110.2 9.7 %collective-permute-done.28.refs_6_ = bf16[256,1024]{1,0:T(8,128)(2,1)S(1)} collective-permute-done((bf16[256,1024]{1,0:T(8,128)(2,1)S(1)}, bf16[256,1024]{1,0:T(8,128)(2,1)S(1)}, u32[]{:S(2)}, u32[]{:S(2)}) %collective-permute-start.28) | collective-permute-done | bytes 524320 | tf_op jit(solution)/shard_map/ppermute | solution.py:20
  119.9 3.1 shard_map.269
  123.1 1.9 collective-permute-done.30.came
  125.2 2.7 collective-permute-start.33
  129.4 13.2 %collective-permute-done.33.refs_1_ = bf16[128,1024]{1,0:T(8,128)(2,1)S(1)} collective-permute-done((bf16[128,1024]{1,0:T(8,128)(2,1)S(1)}, bf16[128,1024]{1,0:T(8,128)(2,1)S(1)}, u32[]{:S(2)}, u32[]{:S(2)}) %collective-permute-start.33) | collective-permute-done | bytes 262176 | tf_op jit(solution)/shard_map/ppermute | solution.py:20
  149.0 2.8 collective-permute-done.37.refs_5_
  153.3 4.1 collective-permute-done.36.refs_4_
  157.4 3.4 collective-permute-start.43
  161.7 9.3 %shard_map.272 = (bf16[512,1024]{1,0:T(8,128)(2,1)S(1)}, bf16[512,768]{1,0:T(8,128)(2,1)S(1)}, bf16[4,512,512]{2,1,0:T(8,128)(2,1)S(1)}, bf16[512,256]{1,0:T(8,1...) custom-call(bf16[256,1024]{1,0:T(8,128)(2,1)S(1)} %get-tuple-element.152.mine, ...), custom_call_target="tpu_custom_call" | custom-call | bytes 8982544 | tf_op jit(solution)/shard_map/pallas_call | solution.py:411
  172.8 8.7 %collective-permute-done.43.refs_1_ = bf16[256,1024]{1,0:T(8,128)(2,1)S(1)} collective-permute-done((bf16[256,1024]{1,0:T(8,128)(2,1)S(1)}, bf16[256,1024]{1,0:T(8,128)(2,1)S(1)}, u32[]{:S(2)}, u32[]{:S(2)}) %collective-permute-start.43) | collective-permute-done | bytes 524320 | tf_op jit(solution)/shard_map/ppermute | solution.py:20
  183.9 2.1 collective-permute-start.54
  188.2 5.8 %collective-permute-done.47.refs_5_ = bf16[256,1024]{1,0:T(8,128)(2,1)S(1)} collective-permute-done((bf16[256,1024]{1,0:T(8,128)(2,1)S(1)}, bf16[256,1024]{1,0:T(8,128)(2,1)S(1)}, u32[]{:S(2)}, u32[]{:S(2)}) %collective-permute-start.47) | collective-permute-done | bytes 524320 | tf_op jit(solution)/shard_map/ppermute | solution.py:20
  195.7 2.8 collective-permute-done.41.came
  201.3 3.1 collective-permute-start.42
  204.4 6.5 %collective-permute-start.55 = (bf16[1,128,1024]{2,1,0:T(8,128)(2,1)S(1)}, bf16[1,128,1024]{2,1,0:T(8,128)(2,1)S(1)}, u32[]{:S(2)}, u32[]{:S(2)}) collective-permute-start(bf16[1,128,1024]{2,1,0:T(8,128)(2,1)S(1)} %collective-permute-done.53.c0), channel_id=1, source_target_pairs={{0,4},{4,0},{1,5},{5,1},{2,6},{6,2},{3,7},{7,3},{8,12},{12,8},{9,1... | collective-permute-start | bytes 786440 | tf_op jit(solution)/shard_map/ppermute | solution.py:20
  211.0 2.1 collective-permute-start.56
  213.1 3.1 shard_map.275
  233.4 5.0 %shard_map.278 = (bf16[512,1024]{1,0:T(8,128)(2,1)S(1)}, bf16[512,1024]{1,0:T(8,128)(2,1)S(1)}, f32[256,1024]{1,0:T(8,128)S(1)}, bf16[256,1024]{1,0:T(8,128)(2,1)S(1)}) custom-call(bf16[1,128,1024]{2,1,0:T(8,128)(2,1)S(1)} %collective-permute-done.53.c0, bf16[1,128,1024]{2,1,0:T(8,128)(2,1)S(1)} %copy-done.91, bf16[1,128,1024]{2,1,0:T(8,128)(2,1)S(1)} %copy-done.71, ...), custom_call_target="tpu_custom_call" | custom-call | bytes 11010048 | tf_op jit(solution)/shard_map/pallas_call | solution.py:411
  238.4 5.7 %collective-permute-start.57 = (bf16[256,1024]{1,0:T(8,128)(2,1)S(1)}, bf16[256,1024]{1,0:T(8,128)(2,1)S(1)}, u32[]{:S(2)}, u32[]{:S(2)}) collective-permute-start(bf16[256,1024]{1,0:T(8,128)(2,1)S(1)} %get-tuple-element.163), channel_id=1, source_target_pairs={{0,4},{4,0},{1,5},{5,1},{2,6},{6,2},{3,7},{7,3},{8,12},{12,8},{9,1... | collective-permute-start | bytes 1572872 | tf_op jit(solution)/shard_map/ppermute | solution.py:20
  245.9 14.2 %collective-permute-done.58.came = bf16[256,1024]{1,0:T(8,128)(2,1)S(1)} collective-permute-done((bf16[256,1024]{1,0:T(8,128)(2,1)S(1)}, bf16[256,1024]{1,0:T(8,128)(2,1)S(1)}, u32[]{:S(2)}, u32[]{:S(2)}) %collective-permute-start.58) | collective-permute-done | bytes 524320 | tf_op jit(solution)/shard_map/ppermute | solution.py:20
  261.4 1.9 collective-permute-done.59.other
  263.4 9.0 %shard_map.281 = (bf16[512,1024]{1,0:T(8,128)(2,1)S(1)}, bf16[512,768]{1,0:T(8,128)(2,1)S(1)}, f32[256,1024]{1,0:T(8,128)S(1)}, bf16[256,1024]{1,0:T(8,128)(2,1)S(1)}) custom-call(bf16[256,1024]{1,0:T(8,128)(2,1)S(1)} %get-tuple-element.165.mine, bf16[256,1024]{1,0:T(8,128)(2,1)S(1)} %collective-permute-done.59.other, bf16[512,768]{1,0:T(8,128)(2,1)S(1)} %copy-done.76, ...), custom_call_target="tpu_custom_call" | custom-call | bytes 9437184 | tf_op jit(solution)/shard_map/pallas_call | solution.py:411
  272.6 1.8 collective-permute-done.60.came
  274.8 13.7 %collective-permute-done.61.came = bf16[256,1024]{1,0:T(8,128)(2,1)S(1)} collective-permute-done((bf16[256,1024]{1,0:T(8,128)(2,1)S(1)}, bf16[256,1024]{1,0:T(8,128)(2,1)S(1)}, u32[]{:S(2)}, u32[]{:S(2)}) %collective-permute-start.61) | collective-permute-done | bytes 524320 | tf_op jit(solution)/shard_map/ppermute | solution.py:20
  291.0 3.2 shard_map.290
  295.7 4.8 shard_map.284
  304.8 15.0 %collective-permute-done.71 = bf16[2,256,1024]{2,1,0:T(8,128)(2,1)} collective-permute-done((bf16[2,256,1024]{2,1,0:T(8,128)(2,1)S(1)}, bf16[2,256,1024]{2,1,0:T(8,128)(2,1)}, u32[]{:S(2)}, u32[]{:S(2)}) %collective-permute-start.71) | collective-permute-done | bytes 1048608 | tf_op jit(solution)/shard_map/ppermute | solution.py:20
  319.8 2.1 fusion.4
  322.2 3.5 shard_map.292
  328.9 2.6 shard_map.291
  331.5 1.8 collective-permute-start.74
  336.2 2.3 collective-permute-done.72
  338.8 2.1 fusion.6
  341.6 8.8 %shard_map.287 = (bf16[512,1024]{1,0:T(8,128)(2,1)S(1)}, bf16[512,768]{1,0:T(8,128)(2,1)S(1)}, f32[256,1024]{1,0:T(8,128)S(1)}, bf16[256,1024]{1,0:T(8,128)(2,1)S(1)}) custom-call(bf16[256,1024]{1,0:T(8,128)(2,1)S(1)} %get-tuple-element.176.mine, bf16[256,1024]{1,0:T(8,128)(2,1)S(1)} %collective-permute-done.65.other, bf16[512,768]{1,0:T(8,128)(2,1)S(1)} %copy-done.74, ...), custom_call_target="tpu_custom_call" | custom-call | bytes 9699328 | tf_op jit(solution)/shard_map/pallas_call | solution.py:411
  350.6 1.8 shard_map.294
  352.4 12.6 %collective-permute-done.76 = bf16[2,128,1024]{2,1,0:T(8,128)(2,1)S(1)} collective-permute-done((bf16[2,128,1024]{2,1,0:T(8,128)(2,1)}, bf16[2,128,1024]{2,1,0:T(8,128)(2,1)S(1)}, u32[]{:S(2)}, u32[]{:S(2)}) %collective-permute-start.76) | collective-permute-done | bytes 524320 | tf_op jit(solution)/shard_map/ppermute | solution.py:20
  366.5 1.8 collective-permute-start.77
  369.6 7.6 %collective-permute-done.77 = bf16[128,1024]{1,0:T(8,128)(2,1)S(1)} collective-permute-done((bf16[128,1024]{1,0:T(8,128)(2,1)S(1)}, bf16[128,1024]{1,0:T(8,128)(2,1)S(1)}, u32[]{:S(2)}, u32[]{:S(2)}) %collective-permute-start.77) | collective-permute-done | bytes 262176 | tf_op jit(solution)/shard_map/ppermute | solution.py:20
  377.8 1.8 collective-permute-start.87
  379.5 7.7 %collective-permute-done.89 = bf16[2,144,1024]{2,1,0:T(8,128)(2,1)S(1)} collective-permute-done((bf16[2,144,1024]{2,1,0:T(8,128)(2,1)S(1)}, bf16[2,144,1024]{2,1,0:T(8,128)(2,1)S(1)}, u32[]{:S(2)}, u32[]{:S(2)}) %collective-permute-start.89) | collective-permute-done | bytes 589856 | tf_op jit(solution)/shard_map/ppermute | solution.py:20
  389.4 13.0 %collective-permute-done.73.refs_3_ = bf16[256,1024]{1,0:T(8,128)(2,1)S(1)} collective-permute-done((bf16[256,1024]{1,0:T(8,128)(2,1)S(1)}, bf16[256,1024]{1,0:T(8,128)(2,1)S(1)}, u32[]{:S(2)}, u32[]{:S(2)}) %collective-permute-start.73) | collective-permute-done | bytes 524320 | tf_op jit(solution)/shard_map/ppermute | solution.py:20
  404.6 11.8 %collective-permute-done.67.came = bf16[256,1024]{1,0:T(8,128)(2,1)S(1)} collective-permute-done((bf16[256,1024]{1,0:T(8,128)(2,1)S(1)}, bf16[256,1024]{1,0:T(8,128)(2,1)S(1)}, u32[]{:S(2)}, u32[]{:S(2)}) %collective-permute-start.67) | collective-permute-done | bytes 524320 | tf_op jit(solution)/shard_map/ppermute | solution.py:20
  420.3 4.0 collective-permute-start.97
  425.6 2.5 collective-permute-start.98
  428.1 21.3 %collective-permute-done.83.refs_11_ = bf16[256,1024]{1,0:T(8,128)(2,1)S(1)} collective-permute-done((bf16[256,1024]{1,0:T(8,128)(2,1)S(1)}, bf16[256,1024]{1,0:T(8,128)(2,1)S(1)}, u32[]{:S(2)}, u32[]{:S(2)}) %collective-permute-start.83) | collective-permute-done | bytes 524320 | tf_op jit(solution)/shard_map/ppermute | solution.py:20
  451.9 10.2 %collective-permute-done.98 = f32[8,1024]{1,0:T(8,128)S(1)} collective-permute-done((f32[8,1024]{1,0:T(8,128)S(1)}, f32[8,1024]{1,0:T(8,128)S(1)}, u32[]{:S(2)}, u32[]{:S(2)}) %collective-permute-start.98) | collective-permute-done | bytes 32800 | tf_op jit(solution)/shard_map/ppermute | solution.py:20
  462.1 1.9 collective-permute-start.99
  464.2 1.9 collective-permute-done.99
  466.1 1.9 collective-permute-start.95
  473.6 5.2 %collective-permute-done.96.b = bf16[64,512]{1,0:T(8,128)(2,1)S(1)} collective-permute-done((bf16[64,512]{1,0:T(8,128)(2,1)S(1)}, bf16[64,512]{1,0:T(8,128)(2,1)S(1)}, u32[]{:S(2)}, u32[]{:S(2)}) %collective-permute-start.96) | collective-permute-done | bytes 65568 | tf_op jit(solution)/shard_map/ppermute | solution.py:1126
  478.8 1.8 shard_map.296
  (422 shorter events, 114.9 us)
Async XLA Ops:
  20.8 18.6 %collective-permute-start.9 = (bf16[144,1024]{1,0:T(8,128)(2,1)S(1)}, bf16[144,1024]{1,0:T(8,128)(2,1)S(1)}, u32[]{:S(2)}, u32[]{:S(2)}) collective-permute-start(bf16[144,1024]{1,0:T(8,128)(2,1)S(1)} %shard_map.264.refs_0_), channel_id=1, source_target_pairs={{0,2},{2,0},{1,3},{3,1},{4,6},{6,4},{5,7},{7,5},{8,10},{10,8},{9,1... | collective-permute-start | bytes 884744 | tf_op jit(solution)/shard_map/ppermute | solution.py:20
  23.5 18.0 %collective-permute-start = (bf16[1,128,1024]{2,1,0:T(8,128)(2,1)S(1)}, bf16[1,128,1024]{2,1,0:T(8,128)(2,1)S(1)}, u32[]{:S(2)}, u32[]{:S(2)}) collective-permute-start(bf16[1,128,1024]{2,1,0:T(8,128)(2,1)S(1)} %copy-done.114), channel_id=1, source_target_pairs={{0,0},{2,4},{4,2},{6,6},{1,1},{3,5},{5,3},{7,7},{8,8},{10,12},{12,... | collective-permute-start | bytes 786440 | tf_op jit(solution)/shard_map/ppermute | solution.py:972
  24.2 15.8 %collective-permute-start.20 = (bf16[32,2816]{1,0:T(8,128)(2,1)S(1)}, bf16[32,2816]{1,0:T(8,128)(2,1)S(1)}, u32[]{:S(2)}, u32[]{:S(2)}) collective-permute-start(bf16[32,2816]{1,0:T(8,128)(2,1)S(1)} %get-tuple-element.144), channel_id=1, source_target_pairs={{0,4},{4,0},{1,5},{5,1},{2,6},{6,2},{3,7},{7,3},{8,12},{12,8},{9,1... | collective-permute-start | bytes 540680 | tf_op jit(solution)/shard_map/ppermute | solution.py:20
  25.9 16.7 %collective-permute-start.21 = (bf16[32,2816]{1,0:T(8,128)(2,1)S(1)}, bf16[32,2816]{1,0:T(8,128)(2,1)S(1)}, u32[]{:S(2)}, u32[]{:S(2)}) collective-permute-start(bf16[32,2816]{1,0:T(8,128)(2,1)S(1)} %get-tuple-element.145), channel_id=1, source_target_pairs={{0,1},{1,0},{2,3},{3,2},{4,5},{5,4},{6,7},{7,6},{8,9},{9,8},{10,11... | collective-permute-start | bytes 540680 | tf_op jit(solution)/shard_map/ppermute | solution.py:20
  27.7 27.7 %collective-permute-start.10 = (bf16[144,1024]{1,0:T(8,128)(2,1)S(1)}, bf16[144,1024]{1,0:T(8,128)(2,1)S(1)}, u32[]{:S(2)}, u32[]{:S(2)}) collective-permute-start(bf16[144,1024]{1,0:T(8,128)(2,1)S(1)} %shard_map.264.refs_0_), channel_id=1, source_target_pairs={{0,8},{8,0},{1,9},{9,1},{2,10},{10,2},{3,11},{11,3},{4,12},{12,4},... | collective-permute-start | bytes 884744 | tf_op jit(solution)/shard_map/ppermute | solution.py:20
  39.5 16.4 %collective-permute-start.13 = (bf16[144,1024]{1,0:T(8,128)(2,1)S(1)}, bf16[144,1024]{1,0:T(8,128)(2,1)S(1)}, u32[]{:S(2)}, u32[]{:S(2)}) collective-permute-start(bf16[144,1024]{1,0:T(8,128)(2,1)S(1)} %collective-permute-done.9.refs_1_), channel_id=1, source_target_pairs={{0,16},{16,0},{1,17},{17,1},{2,18},{18,2},{3,19},{19,3},{4,20},{20... | collective-permute-start | bytes 884744 | tf_op jit(solution)/shard_map/ppermute | solution.py:20
  40.0 16.5 %collective-permute-start.12 = (bf16[144,1024]{1,0:T(8,128)(2,1)S(1)}, bf16[144,1024]{1,0:T(8,128)(2,1)S(1)}, u32[]{:S(2)}, u32[]{:S(2)}) collective-permute-start(bf16[144,1024]{1,0:T(8,128)(2,1)S(1)} %shard_map.264.refs_0_), channel_id=1, source_target_pairs={{0,16},{16,0},{1,17},{17,1},{2,18},{18,2},{3,19},{19,3},{4,20},{20... | collective-permute-start | bytes 884744 | tf_op jit(solution)/shard_map/ppermute | solution.py:20
  41.5 14.9 %collective-permute-start.1 = (bf16[1,128,1024]{2,1,0:T(8,128)(2,1)S(1)}, bf16[1,128,1024]{2,1,0:T(8,128)(2,1)S(1)}, u32[]{:S(2)}, u32[]{:S(2)}) collective-permute-start(bf16[1,128,1024]{2,1,0:T(8,128)(2,1)S(1)} %collective-permute-done.t0), channel_id=1, source_target_pairs={{0,1},{1,0},{2,3},{3,2},{4,5},{5,4},{6,7},{7,6},{8,9},{9,8},{10,11... | collective-permute-start | bytes 786440 | tf_op jit(solution)/shard_map/ppermute | solution.py:20
  55.9 13.7 %collective-permute-start.15 = (bf16[144,1024]{1,0:T(8,128)(2,1)S(1)}, bf16[144,1024]{1,0:T(8,128)(2,1)S(1)}, u32[]{:S(2)}, u32[]{:S(2)}) collective-permute-start(bf16[144,1024]{1,0:T(8,128)(2,1)S(1)} %collective-permute-done.13.refs_5_), channel_id=1, source_target_pairs={{0,8},{8,0},{1,9},{9,1},{2,10},{10,2},{3,11},{11,3},{4,12},{12,4},... | collective-permute-start | bytes 884744 | tf_op jit(solution)/shard_map/ppermute | solution.py:20
  58.0 26.1 %collective-permute-start.23 = (bf16[256,1024]{1,0:T(8,128)(2,1)S(1)}, bf16[256,1024]{1,0:T(8,128)(2,1)S(1)}, u32[]{:S(2)}, u32[]{:S(2)}) collective-permute-start(bf16[256,1024]{1,0:T(8,128)(2,1)S(1)} %get-tuple-element.148.refs_0_), channel_id=1, source_target_pairs={{0,2},{2,0},{1,3},{3,1},{4,6},{6,4},{5,7},{7,5},{8,10},{10,8},{9,1... | collective-permute-start | bytes 1572872 | tf_op jit(solution)/shard_map/ppermute | solution.py:20
  80.4 14.8 %collective-permute-start.24 = (bf16[256,1024]{1,0:T(8,128)(2,1)S(1)}, bf16[256,1024]{1,0:T(8,128)(2,1)S(1)}, u32[]{:S(2)}, u32[]{:S(2)}) collective-permute-start(bf16[256,1024]{1,0:T(8,128)(2,1)S(1)} %get-tuple-element.148.refs_0_), channel_id=1, source_target_pairs={{0,8},{8,0},{1,9},{9,1},{2,10},{10,2},{3,11},{11,3},{4,12},{12,4},... | collective-permute-start | bytes 1572872 | tf_op jit(solution)/shard_map/ppermute | solution.py:20
  84.1 14.9 %collective-permute-start.27 = (bf16[256,1024]{1,0:T(8,128)(2,1)S(1)}, bf16[256,1024]{1,0:T(8,128)(2,1)S(1)}, u32[]{:S(2)}, u32[]{:S(2)}) collective-permute-start(bf16[256,1024]{1,0:T(8,128)(2,1)S(1)} %collective-permute-done.23.refs_1_), channel_id=1, source_target_pairs={{0,16},{16,0},{1,17},{17,1},{2,18},{18,2},{3,19},{19,3},{4,20},{20... | collective-permute-start | bytes 1572872 | tf_op jit(solution)/shard_map/ppermute | solution.py:20
  85.0 15.4 %collective-permute-start.18 = (bf16[256,1024]{1,0:T(8,128)(2,1)S(1)}, bf16[256,1024]{1,0:T(8,128)(2,1)S(1)}, u32[]{:S(2)}, u32[]{:S(2)}) collective-permute-start(bf16[256,1024]{1,0:T(8,128)(2,1)S(1)} %shard_map.266.part), channel_id=1, source_target_pairs={{0,1},{1,0},{2,3},{3,2},{4,5},{5,4},{6,7},{7,6},{8,9},{9,8},{10,11... | collective-permute-start | bytes 1572872 | tf_op jit(solution)/shard_map/ppermute | solution.py:20
  85.1 25.0 %collective-permute-start.26 = (bf16[256,1024]{1,0:T(8,128)(2,1)S(1)}, bf16[256,1024]{1,0:T(8,128)(2,1)S(1)}, u32[]{:S(2)}, u32[]{:S(2)}) collective-permute-start(bf16[256,1024]{1,0:T(8,128)(2,1)S(1)} %get-tuple-element.148.refs_0_), channel_id=1, source_target_pairs={{0,16},{16,0},{1,17},{17,1},{2,18},{18,2},{3,19},{19,3},{4,20},{20... | collective-permute-start | bytes 1572872 | tf_op jit(solution)/shard_map/ppermute | solution.py:20
  86.4 23.7 %collective-permute-start.25 = (bf16[256,1024]{1,0:T(8,128)(2,1)S(1)}, bf16[256,1024]{1,0:T(8,128)(2,1)S(1)}, u32[]{:S(2)}, u32[]{:S(2)}) collective-permute-start(bf16[256,1024]{1,0:T(8,128)(2,1)S(1)} %collective-permute-done.23.refs_1_), channel_id=1, source_target_pairs={{0,8},{8,0},{1,9},{9,1},{2,10},{10,2},{3,11},{11,3},{4,12},{12,4},... | collective-permute-start | bytes 1572872 | tf_op jit(solution)/shard_map/ppermute | solution.py:20
  95.2 24.7 %collective-permute-start.28 = (bf16[256,1024]{1,0:T(8,128)(2,1)S(1)}, bf16[256,1024]{1,0:T(8,128)(2,1)S(1)}, u32[]{:S(2)}, u32[]{:S(2)}) collective-permute-start(bf16[256,1024]{1,0:T(8,128)(2,1)S(1)} %collective-permute-done.24.refs_2_), channel_id=1, source_target_pairs={{0,16},{16,0},{1,17},{17,1},{2,18},{18,2},{3,19},{19,3},{4,20},{20... | collective-permute-start | bytes 1572872 | tf_op jit(solution)/shard_map/ppermute | solution.py:20
  98.9 21.0 %collective-permute-start.29 = (bf16[256,1024]{1,0:T(8,128)(2,1)S(1)}, bf16[256,1024]{1,0:T(8,128)(2,1)S(1)}, u32[]{:S(2)}, u32[]{:S(2)}) collective-permute-start(bf16[256,1024]{1,0:T(8,128)(2,1)S(1)} %collective-permute-done.27.refs_5_), channel_id=1, source_target_pairs={{0,8},{8,0},{1,9},{9,1},{2,10},{10,2},{3,11},{11,3},{4,12},{12,4},... | collective-permute-start | bytes 1572872 | tf_op jit(solution)/shard_map/ppermute | solution.py:20
  101.2 18.7 %collective-permute-start.19 = (bf16[256,1024]{1,0:T(8,128)(2,1)S(1)}, bf16[256,1024]{1,0:T(8,128)(2,1)S(1)}, u32[]{:S(2)}, u32[]{:S(2)}) collective-permute-start(bf16[256,1024]{1,0:T(8,128)(2,1)S(1)} %get-tuple-element.142.mine), channel_id=1, source_target_pairs={{0,4},{4,0},{1,5},{5,1},{2,6},{6,2},{3,7},{7,3},{8,12},{12,8},{9,1... | collective-permute-start | bytes 1572872 | tf_op jit(solution)/shard_map/ppermute | solution.py:20
  125.1 19.6 %collective-permute-start.31 = (bf16[256,1024]{1,0:T(8,128)(2,1)S(1)}, bf16[256,1024]{1,0:T(8,128)(2,1)S(1)}, u32[]{:S(2)}, u32[]{:S(2)}) collective-permute-start(bf16[256,1024]{1,0:T(8,128)(2,1)S(1)} %shard_map.270.part), channel_id=1, source_target_pairs={{0,1},{1,0},{2,3},{3,2},{4,5},{5,4},{6,7},{7,6},{8,9},{9,8},{10,11... | collective-permute-start | bytes 1572872 | tf_op jit(solution)/shard_map/ppermute | solution.py:20
  125.2 17.4 %collective-permute-start.33 = (bf16[128,1024]{1,0:T(8,128)(2,1)S(1)}, bf16[128,1024]{1,0:T(8,128)(2,1)S(1)}, u32[]{:S(2)}, u32[]{:S(2)}) collective-permute-start(bf16[128,1024]{1,0:T(8,128)(2,1)S(1)} %get-tuple-element.153.refs_0_), channel_id=1, source_target_pairs={{0,2},{2,0},{1,3},{3,1},{4,6},{6,4},{5,7},{7,5},{8,10},{10,8},{9,1... | collective-permute-start | bytes 786440 | tf_op jit(solution)/shard_map/ppermute | solution.py:20
  127.9 20.3 %collective-permute-start.34 = (bf16[128,1024]{1,0:T(8,128)(2,1)S(1)}, bf16[128,1024]{1,0:T(8,128)(2,1)S(1)}, u32[]{:S(2)}, u32[]{:S(2)}) collective-permute-start(bf16[128,1024]{1,0:T(8,128)(2,1)S(1)} %get-tuple-element.153.refs_0_), channel_id=1, source_target_pairs={{0,8},{8,0},{1,9},{9,1},{2,10},{10,2},{3,11},{11,3},{4,12},{12,4},... | collective-permute-start | bytes 786440 | tf_op jit(solution)/shard_map/ppermute | solution.py:20
  145.3 16.4 %collective-permute-start.32 = (bf16[256,1024]{1,0:T(8,128)(2,1)S(1)}, bf16[256,1024]{1,0:T(8,128)(2,1)S(1)}, u32[]{:S(2)}, u32[]{:S(2)}) collective-permute-start(bf16[256,1024]{1,0:T(8,128)(2,1)S(1)} %get-tuple-element.152.mine), channel_id=1, source_target_pairs={{0,4},{4,0},{1,5},{5,1},{2,6},{6,2},{3,7},{7,3},{8,12},{12,8},{9,1... | collective-permute-start | bytes 1572872 | tf_op jit(solution)/shard_map/ppermute | solution.py:20
  146.7 14.1 %collective-permute-start.35 = (bf16[128,1024]{1,0:T(8,128)(2,1)S(1)}, bf16[128,1024]{1,0:T(8,128)(2,1)S(1)}, u32[]{:S(2)}, u32[]{:S(2)}) collective-permute-start(bf16[128,1024]{1,0:T(8,128)(2,1)S(1)} %collective-permute-done.33.refs_1_), channel_id=1, source_target_pairs={{0,8},{8,0},{1,9},{9,1},{2,10},{10,2},{3,11},{11,3},{4,12},{12,4},... | collective-permute-start | bytes 786440 | tf_op jit(solution)/shard_map/ppermute | solution.py:20
  148.2 13.4 %collective-permute-start.38 = (bf16[128,1024]{1,0:T(8,128)(2,1)S(1)}, bf16[128,1024]{1,0:T(8,128)(2,1)S(1)}, u32[]{:S(2)}, u32[]{:S(2)}) collective-permute-start(bf16[128,1024]{1,0:T(8,128)(2,1)S(1)} %collective-permute-done.34.refs_2_), channel_id=1, source_target_pairs={{0,16},{16,0},{1,17},{17,1},{2,18},{18,2},{3,19},{19,3},{4,20},{20... | collective-permute-start | bytes 786440 | tf_op jit(solution)/shard_map/ppermute | solution.py:20
  157.4 24.0 %collective-permute-start.43 = (bf16[256,1024]{1,0:T(8,128)(2,1)S(1)}, bf16[256,1024]{1,0:T(8,128)(2,1)S(1)}, u32[]{:S(2)}, u32[]{:S(2)}) collective-permute-start(bf16[256,1024]{1,0:T(8,128)(2,1)S(1)} %get-tuple-element.158.refs_0_), channel_id=1, source_target_pairs={{0,2},{2,0},{1,3},{3,1},{4,6},{6,4},{5,7},{7,5},{8,10},{10,8},{9,1... | collective-permute-start | bytes 1572872 | tf_op jit(solution)/shard_map/ppermute | solution.py:20
  171.2 15.5 %collective-permute-start.44 = (bf16[256,1024]{1,0:T(8,128)(2,1)S(1)}, bf16[256,1024]{1,0:T(8,128)(2,1)S(1)}, u32[]{:S(2)}, u32[]{:S(2)}) collective-permute-start(bf16[256,1024]{1,0:T(8,128)(2,1)S(1)} %get-tuple-element.158.refs_0_), channel_id=1, source_target_pairs={{0,8},{8,0},{1,9},{9,1},{2,10},{10,2},{3,11},{11,3},{4,12},{12,4},... | collective-permute-start | bytes 1572872 | tf_op jit(solution)/shard_map/ppermute | solution.py:20
  181.5 12.5 %collective-permute-start.47 = (bf16[256,1024]{1,0:T(8,128)(2,1)S(1)}, bf16[256,1024]{1,0:T(8,128)(2,1)S(1)}, u32[]{:S(2)}, u32[]{:S(2)}) collective-permute-start(bf16[256,1024]{1,0:T(8,128)(2,1)S(1)} %collective-permute-done.43.refs_1_), channel_id=1, source_target_pairs={{0,16},{16,0},{1,17},{17,1},{2,18},{18,2},{3,19},{19,3},{4,20},{20... | collective-permute-start | bytes 1572872 | tf_op jit(solution)/shard_map/ppermute | solution.py:20
  183.0 15.5 %collective-permute-start.41 = (bf16[256,1024]{1,0:T(8,128)(2,1)S(1)}, bf16[256,1024]{1,0:T(8,128)(2,1)S(1)}, u32[]{:S(2)}, u32[]{:S(2)}) collective-permute-start(bf16[256,1024]{1,0:T(8,128)(2,1)S(1)} %shard_map.273.part), channel_id=1, source_target_pairs={{0,1},{1,0},{2,3},{3,2},{4,5},{5,4},{6,7},{7,6},{8,9},{9,8},{10,11... | collective-permute-start | bytes 1572872 | tf_op jit(solution)/shard_map/ppermute | solution.py:20
  183.9 17.4 %collective-permute-start.54 = (bf16[1,128,1024]{2,1,0:T(8,128)(2,1)S(1)}, bf16[1,128,1024]{2,1,0:T(8,128)(2,1)S(1)}, u32[]{:S(2)}, u32[]{:S(2)}) collective-permute-start(bf16[1,128,1024]{2,1,0:T(8,128)(2,1)S(1)} %collective-permute-done.53.c0), channel_id=1, source_target_pairs={{0,1},{1,0},{2,3},{3,2},{4,5},{5,4},{6,7},{7,6},{8,9},{9,8},{10,11... | collective-permute-start | bytes 786440 | tf_op jit(solution)/shard_map/ppermute | solution.py:20
  186.0 18.5 %collective-permute-start.46 = (bf16[256,1024]{1,0:T(8,128)(2,1)S(1)}, bf16[256,1024]{1,0:T(8,128)(2,1)S(1)}, u32[]{:S(2)}, u32[]{:S(2)}) collective-permute-start(bf16[256,1024]{1,0:T(8,128)(2,1)S(1)} %get-tuple-element.158.refs_0_), channel_id=1, source_target_pairs={{0,16},{16,0},{1,17},{17,1},{2,18},{18,2},{3,19},{19,3},{4,20},{20... | collective-permute-start | bytes 1572872 | tf_op jit(solution)/shard_map/ppermute | solution.py:20
  186.7 24.2 %collective-permute-start.45 = (bf16[256,1024]{1,0:T(8,128)(2,1)S(1)}, bf16[256,1024]{1,0:T(8,128)(2,1)S(1)}, u32[]{:S(2)}, u32[]{:S(2)}) collective-permute-start(bf16[256,1024]{1,0:T(8,128)(2,1)S(1)} %collective-permute-done.43.refs_1_), channel_id=1, source_target_pairs={{0,8},{8,0},{1,9},{9,1},{2,10},{10,2},{3,11},{11,3},{4,12},{12,4},... | collective-permute-start | bytes 1572872 | tf_op jit(solution)/shard_map/ppermute | solution.py:20
  194.0 19.1 %collective-permute-start.48 = (bf16[256,1024]{1,0:T(8,128)(2,1)S(1)}, bf16[256,1024]{1,0:T(8,128)(2,1)S(1)}, u32[]{:S(2)}, u32[]{:S(2)}) collective-permute-start(bf16[256,1024]{1,0:T(8,128)(2,1)S(1)} %collective-permute-done.44.refs_2_), channel_id=1, source_target_pairs={{0,16},{16,0},{1,17},{17,1},{2,18},{18,2},{3,19},{19,3},{4,20},{20... | collective-permute-start | bytes 1572872 | tf_op jit(solution)/shard_map/ppermute | solution.py:20
  198.5 14.6 %collective-permute-start.49 = (bf16[256,1024]{1,0:T(8,128)(2,1)S(1)}, bf16[256,1024]{1,0:T(8,128)(2,1)S(1)}, u32[]{:S(2)}, u32[]{:S(2)}) collective-permute-start(bf16[256,1024]{1,0:T(8,128)(2,1)S(1)} %collective-permute-done.47.refs_5_), channel_id=1, source_target_pairs={{0,8},{8,0},{1,9},{9,1},{2,10},{10,2},{3,11},{11,3},{4,12},{12,4},... | collective-permute-start | bytes 1572872 | tf_op jit(solution)/shard_map/ppermute | solution.py:20
  204.4 16.9 %collective-permute-start.55 = (bf16[1,128,1024]{2,1,0:T(8,128)(2,1)S(1)}, bf16[1,128,1024]{2,1,0:T(8,128)(2,1)S(1)}, u32[]{:S(2)}, u32[]{:S(2)}) collective-permute-start(bf16[1,128,1024]{2,1,0:T(8,128)(2,1)S(1)} %collective-permute-done.53.c0), channel_id=1, source_target_pairs={{0,4},{4,0},{1,5},{5,1},{2,6},{6,2},{3,7},{7,3},{8,12},{12,8},{9,1... | collective-permute-start | bytes 786440 | tf_op jit(solution)/shard_map/ppermute | solution.py:20
  245.8 14.3 %collective-permute-start.58 = (bf16[256,1024]{1,0:T(8,128)(2,1)S(1)}, bf16[256,1024]{1,0:T(8,128)(2,1)S(1)}, u32[]{:S(2)}, u32[]{:S(2)}) collective-permute-start(bf16[256,1024]{1,0:T(8,128)(2,1)S(1)} %shard_map.279.part), channel_id=1, source_target_pairs={{0,1},{1,0},{2,3},{3,2},{4,5},{5,4},{6,7},{7,6},{8,9},{9,8},{10,11... | collective-permute-start | bytes 1572872 | tf_op jit(solution)/shard_map/ppermute | solution.py:20
  274.5 14.0 %collective-permute-start.61 = (bf16[256,1024]{1,0:T(8,128)(2,1)S(1)}, bf16[256,1024]{1,0:T(8,128)(2,1)S(1)}, u32[]{:S(2)}, u32[]{:S(2)}) collective-permute-start(bf16[256,1024]{1,0:T(8,128)(2,1)S(1)} %shard_map.282.part), channel_id=1, source_target_pairs={{0,1},{1,0},{2,3},{3,2},{4,5},{5,4},{6,7},{7,6},{8,9},{9,8},{10,11... | collective-permute-start | bytes 1572872 | tf_op jit(solution)/shard_map/ppermute | solution.py:20
  294.2 25.6 %collective-permute-start.71 = (bf16[2,256,1024]{2,1,0:T(8,128)(2,1)S(1)}, bf16[2,256,1024]{2,1,0:T(8,128)(2,1)}, u32[]{:S(2)}, u32[]{:S(2)}) collective-permute-start(bf16[2,256,1024]{2,1,0:T(8,128)(2,1)S(1)} %get-tuple-element.190), channel_id=1, source_target_pairs={{0,8},{8,0},{1,9},{9,1},{2,10},{10,2},{3,11},{11,3},{4,12},{12,4},... | collective-permute-start | bytes 3145736 | tf_op jit(solution)/shard_map/ppermute | solution.py:20
  301.1 33.9 %collective-permute-start.69 = (bf16[2,256,1024]{2,1,0:T(8,128)(2,1)}, bf16[2,256,1024]{2,1,0:T(8,128)(2,1)S(1)}, u32[]{:S(2)}, u32[]{:S(2)}) collective-permute-start(bf16[2,256,1024]{2,1,0:T(8,128)(2,1)} %get-tuple-element.187), channel_id=1, source_target_pairs={{0,16},{16,0},{1,17},{17,1},{2,18},{18,2},{3,19},{19,3},{4,20},{20... | collective-permute-start | bytes 3145736 | tf_op jit(solution)/shard_map/ppermute | solution.py:20
  302.6 29.0 %collective-permute-start.64 = (bf16[256,1024]{1,0:T(8,128)(2,1)S(1)}, bf16[256,1024]{1,0:T(8,128)(2,1)S(1)}, u32[]{:S(2)}, u32[]{:S(2)}) collective-permute-start(bf16[256,1024]{1,0:T(8,128)(2,1)S(1)} %shard_map.285.part), channel_id=1, source_target_pairs={{0,1},{1,0},{2,3},{3,2},{4,5},{5,4},{6,7},{7,6},{8,9},{9,8},{10,11... | collective-permute-start | bytes 1572872 | tf_op jit(solution)/shard_map/ppermute | solution.py:20
  303.3 31.1 %collective-permute-start.51 = (bf16[256,1024]{1,0:T(8,128)(2,1)S(1)}, bf16[256,1024]{1,0:T(8,128)(2,1)S(1)}, u32[]{:S(2)}, u32[]{:S(2)}) collective-permute-start(bf16[256,1024]{1,0:T(8,128)(2,1)S(1)} %shard_map.276.part), channel_id=1, source_target_pairs={{0,1},{1,0},{2,3},{3,2},{4,5},{5,4},{6,7},{7,6},{8,9},{9,8},{10,11... | collective-permute-start | bytes 1572872 | tf_op jit(solution)/shard_map/ppermute | solution.py:20
  321.9 16.6 %collective-permute-start.72 = (bf16[256,1024]{1,0:T(8,128)(2,1)}, bf16[256,1024]{1,0:T(8,128)(2,1)S(1)}, u32[]{:S(2)}, u32[]{:S(2)}) collective-permute-start(bf16[256,1024]{1,0:T(8,128)(2,1)} %fusion.4), channel_id=1, source_target_pairs={{0,16},{16,0},{1,17},{17,1},{2,18},{18,2},{3,19},{19,3},{4,20},{20... | collective-permute-start | bytes 1572872 | tf_op jit(solution)/shard_map/ppermute | solution.py:20
  327.4 39.1 %collective-permute-start.81 = (bf16[2,256,1024]{2,1,0:T(8,128)(2,1)}, bf16[2,256,1024]{2,1,0:T(8,128)(2,1)}, u32[]{:S(2)}, u32[]{:S(2)}) collective-permute-start(bf16[2,256,1024]{2,1,0:T(8,128)(2,1)} %get-tuple-element.210), channel_id=1, source_target_pairs={{0,8},{8,0},{1,9},{9,1},{2,10},{10,2},{3,11},{11,3},{4,12},{12,4},... | collective-permute-start | bytes 3145736 | tf_op jit(solution)/shard_map/ppermute | solution.py:20
  331.5 18.9 %collective-permute-start.74 = (bf16[2,128,1024]{2,1,0:T(8,128)(2,1)S(1)}, bf16[2,128,1024]{2,1,0:T(8,128)(2,1)S(1)}, u32[]{:S(2)}, u32[]{:S(2)}) collective-permute-start(bf16[2,128,1024]{2,1,0:T(8,128)(2,1)S(1)} %get-tuple-element.197), channel_id=1, source_target_pairs={{0,16},{16,0},{1,17},{17,1},{2,18},{18,2},{3,19},{19,3},{4,20},{20... | collective-permute-start | bytes 1572872 | tf_op jit(solution)/shard_map/ppermute | solution.py:20
  334.4 30.6 %collective-permute-start.76 = (bf16[2,128,1024]{2,1,0:T(8,128)(2,1)}, bf16[2,128,1024]{2,1,0:T(8,128)(2,1)S(1)}, u32[]{:S(2)}, u32[]{:S(2)}) collective-permute-start(bf16[2,128,1024]{2,1,0:T(8,128)(2,1)} %get-tuple-element.200), channel_id=1, source_target_pairs={{0,8},{8,0},{1,9},{9,1},{2,10},{10,2},{3,11},{11,3},{4,12},{12,4},... | collective-permute-start | bytes 1572872 | tf_op jit(solution)/shard_map/ppermute | solution.py:20
  338.5 39.3 %collective-permute-start.79 = (bf16[2,256,1024]{2,1,0:T(8,128)(2,1)S(1)}, bf16[2,256,1024]{2,1,0:T(8,128)(2,1)S(1)}, u32[]{:S(2)}, u32[]{:S(2)}) collective-permute-start(bf16[2,256,1024]{2,1,0:T(8,128)(2,1)S(1)} %copy-done.110), channel_id=1, source_target_pairs={{0,16},{16,0},{1,17},{17,1},{2,18},{18,2},{3,19},{19,3},{4,20},{20... | collective-permute-start | bytes 3145736 | tf_op jit(solution)/shard_map/ppermute | solution.py:20
  340.9 46.9 %collective-permute-start.70 = (bf16[256,1024]{1,0:T(8,128)(2,1)}, bf16[256,1024]{1,0:T(8,128)(2,1)S(1)}, u32[]{:S(2)}, u32[]{:S(2)}) collective-permute-start(bf16[256,1024]{1,0:T(8,128)(2,1)} %fusion.7), channel_id=1, source_target_pairs={{0,8},{8,0},{1,9},{9,1},{2,10},{10,2},{3,11},{11,3},{4,12},{12,4},... | collective-permute-start | bytes 1572872 | tf_op jit(solution)/shard_map/ppermute | solution.py:20
  350.4 26.7 %collective-permute-start.66 = (bf16[256,1024]{1,0:T(8,128)(2,1)S(1)}, bf16[256,1024]{1,0:T(8,128)(2,1)S(1)}, u32[]{:S(2)}, u32[]{:S(2)}) collective-permute-start(bf16[256,1024]{1,0:T(8,128)(2,1)S(1)} %get-tuple-element.180), channel_id=1, source_target_pairs={{0,4},{4,0},{1,5},{5,1},{2,6},{6,2},{3,7},{7,3},{8,12},{12,8},{9,1... | collective-permute-start | bytes 1572872 | tf_op jit(solution)/shard_map/ppermute | solution.py:20
  365.0 22.3 %collective-permute-start.89 = (bf16[2,144,1024]{2,1,0:T(8,128)(2,1)S(1)}, bf16[2,144,1024]{2,1,0:T(8,128)(2,1)S(1)}, u32[]{:S(2)}, u32[]{:S(2)}) collective-permute-start(bf16[2,144,1024]{2,1,0:T(8,128)(2,1)S(1)} %get-tuple-element.227), channel_id=1, source_target_pairs={{0,8},{8,0},{1,9},{9,1},{2,10},{10,2},{3,11},{11,3},{4,12},{12,4},... | collective-permute-start | bytes 1769480 | tf_op jit(solution)/shard_map/ppermute | solution.py:20
  377.1 25.2 %collective-permute-start.73 = (bf16[256,1024]{1,0:T(8,128)(2,1)S(1)}, bf16[256,1024]{1,0:T(8,128)(2,1)S(1)}, u32[]{:S(2)}, u32[]{:S(2)}) collective-permute-start(bf16[256,1024]{1,0:T(8,128)(2,1)S(1)} %copy-done.113), channel_id=1, source_target_pairs={{0,2},{2,0},{1,3},{3,1},{4,6},{6,4},{5,7},{7,5},{8,10},{10,8},{9,1... | collective-permute-start | bytes 1572872 | tf_op jit(solution)/shard_map/ppermute | solution.py:20
  377.1 25.2 %collective-permute-start.82 = (bf16[256,1024]{1,0:T(8,128)(2,1)S(1)}, bf16[256,1024]{1,0:T(8,128)(2,1)S(1)}, u32[]{:S(2)}, u32[]{:S(2)}) collective-permute-start(bf16[256,1024]{1,0:T(8,128)(2,1)S(1)} %fusion), channel_id=1, source_target_pairs={{0,16},{16,0},{1,17},{17,1},{2,18},{18,2},{3,19},{19,3},{4,20},{20... | collective-permute-start | bytes 1572872 | tf_op jit(solution)/shard_map/ppermute | solution.py:20
  377.8 26.2 %collective-permute-start.87 = (bf16[2,144,1024]{2,1,0:T(8,128)(2,1)S(1)}, bf16[2,144,1024]{2,1,0:T(8,128)(2,1)S(1)}, u32[]{:S(2)}, u32[]{:S(2)}) collective-permute-start(bf16[2,144,1024]{2,1,0:T(8,128)(2,1)S(1)} %get-tuple-element.224), channel_id=1, source_target_pairs={{0,16},{16,0},{1,17},{17,1},{2,18},{18,2},{3,19},{19,3},{4,20},{20... | collective-permute-start | bytes 1769480 | tf_op jit(solution)/shard_map/ppermute | solution.py:20
  387.2 29.1 %collective-permute-start.67 = (bf16[256,1024]{1,0:T(8,128)(2,1)S(1)}, bf16[256,1024]{1,0:T(8,128)(2,1)S(1)}, u32[]{:S(2)}, u32[]{:S(2)}) collective-permute-start(bf16[256,1024]{1,0:T(8,128)(2,1)S(1)} %shard_map.288.part), channel_id=1, source_target_pairs={{0,1},{1,0},{2,3},{3,2},{4,5},{5,4},{6,7},{7,6},{8,9},{9,8},{10,11... | collective-permute-start | bytes 1572872 | tf_op jit(solution)/shard_map/ppermute | solution.py:20
  387.8 30.1 %collective-permute-start.75 = (bf16[128,1024]{1,0:T(8,128)(2,1)S(1)}, bf16[128,1024]{1,0:T(8,128)(2,1)S(1)}, u32[]{:S(2)}, u32[]{:S(2)}) collective-permute-start(bf16[128,1024]{1,0:T(8,128)(2,1)S(1)} %fusion.15), channel_id=1, source_target_pairs={{0,8},{8,0},{1,9},{9,1},{2,10},{10,2},{3,11},{11,3},{4,12},{12,4},... | collective-permute-start | bytes 786440 | tf_op jit(solution)/shard_map/ppermute | solution.py:20
  402.3 16.4 %collective-permute-start.78 = (bf16[128,1024]{1,0:T(8,128)(2,1)S(1)}, bf16[128,1024]{1,0:T(8,128)(2,1)S(1)}, u32[]{:S(2)}, u32[]{:S(2)}) collective-permute-start(bf16[128,1024]{1,0:T(8,128)(2,1)S(1)} %fusion.14), channel_id=1, source_target_pairs={{0,2},{2,0},{1,3},{3,1},{4,6},{6,4},{5,7},{7,5},{8,10},{10,8},{9,1... | collective-permute-start | bytes 786440 | tf_op jit(solution)/shard_map/ppermute | solution.py:20
  402.3 17.9 %collective-permute-start.90 = (bf16[144,1024]{1,0:T(8,128)(2,1)S(1)}, bf16[144,1024]{1,0:T(8,128)(2,1)S(1)}, u32[]{:S(2)}, u32[]{:S(2)}) collective-permute-start(bf16[144,1024]{1,0:T(8,128)(2,1)S(1)} %fusion.8), channel_id=1, source_target_pairs={{0,16},{16,0},{1,17},{17,1},{2,18},{18,2},{3,19},{19,3},{4,20},{20... | collective-permute-start | bytes 884744 | tf_op jit(solution)/shard_map/ppermute | solution.py:20
  404.0 21.7 %collective-permute-start.80 = (bf16[256,1024]{1,0:T(8,128)(2,1)S(1)}, bf16[256,1024]{1,0:T(8,128)(2,1)S(1)}, u32[]{:S(2)}, u32[]{:S(2)}) collective-permute-start(bf16[256,1024]{1,0:T(8,128)(2,1)S(1)} %fusion.3), channel_id=1, source_target_pairs={{0,8},{8,0},{1,9},{9,1},{2,10},{10,2},{3,11},{11,3},{4,12},{12,4},... | collective-permute-start | bytes 1572872 | tf_op jit(solution)/shard_map/ppermute | solution.py:20
  416.3 33.1 %collective-permute-start.83 = (bf16[256,1024]{1,0:T(8,128)(2,1)S(1)}, bf16[256,1024]{1,0:T(8,128)(2,1)S(1)}, u32[]{:S(2)}, u32[]{:S(2)}) collective-permute-start(bf16[256,1024]{1,0:T(8,128)(2,1)S(1)} %fusion.2), channel_id=1, source_target_pairs={{0,2},{2,0},{1,3},{3,1},{4,6},{6,4},{5,7},{7,5},{8,10},{10,8},{9,1... | collective-permute-start | bytes 1572872 | tf_op jit(solution)/shard_map/ppermute | solution.py:20
  417.9 33.2 %collective-permute-start.52 = (bf16[1,128,1024]{2,1,0:T(8,128)(2,1)S(1)}, bf16[1,128,1024]{2,1,0:T(8,128)(2,1)S(1)}, u32[]{:S(2)}, u32[]{:S(2)}) collective-permute-start(bf16[1,128,1024]{2,1,0:T(8,128)(2,1)S(1)} %shard_map.277), channel_id=1, source_target_pairs={{0,0},{2,4},{4,2},{6,6},{1,1},{3,5},{5,3},{7,7},{8,8},{10,12},{12,... | collective-permute-start | bytes 786440 | tf_op jit(solution)/shard_map/ppermute | solution.py:972
  418.8 33.0 %collective-permute-start.88 = (bf16[144,1024]{1,0:T(8,128)(2,1)S(1)}, bf16[144,1024]{1,0:T(8,128)(2,1)S(1)}, u32[]{:S(2)}, u32[]{:S(2)}) collective-permute-start(bf16[144,1024]{1,0:T(8,128)(2,1)S(1)} %fusion.11), channel_id=1, source_target_pairs={{0,8},{8,0},{1,9},{9,1},{2,10},{10,2},{3,11},{11,3},{4,12},{12,4},... | collective-permute-start | bytes 884744 | tf_op jit(solution)/shard_map/ppermute | solution.py:20
  425.1 37.0 %collective-permute-start.91 = (bf16[144,1024]{1,0:T(8,128)(2,1)S(1)}, bf16[144,1024]{1,0:T(8,128)(2,1)S(1)}, u32[]{:S(2)}, u32[]{:S(2)}) collective-permute-start(bf16[144,1024]{1,0:T(8,128)(2,1)S(1)} %fusion.10), channel_id=1, source_target_pairs={{0,2},{2,0},{1,3},{3,1},{4,6},{6,4},{5,7},{7,5},{8,10},{10,8},{9,1... | collective-permute-start | bytes 884744 | tf_op jit(solution)/shard_map/ppermute | solution.py:20
  425.6 36.4 %collective-permute-start.98 = (f32[8,1024]{1,0:T(8,128)S(1)}, f32[8,1024]{1,0:T(8,128)S(1)}, u32[]{:S(2)}, u32[]{:S(2)}) collective-permute-start(f32[8,1024]{1,0:T(8,128)S(1)} %add.76), channel_id=1, source_target_pairs={{0,2},{2,0},{1,3},{3,1},{4,6},{6,4},{5,7},{7,5},{8,10},{10,8},{9,1... | collective-permute-start | bytes 98312 | tf_op jit(solution)/shard_map/ppermute | solution.py:20
  451.1 16.9 %collective-permute-start.84 = (bf16[32,2816]{1,0:T(8,128)(2,1)S(1)}, bf16[32,2816]{1,0:T(8,128)(2,1)S(1)}, u32[]{:S(2)}, u32[]{:S(2)}) collective-permute-start(bf16[32,2816]{1,0:T(8,128)(2,1)S(1)} %get-tuple-element.213), channel_id=1, source_target_pairs={{0,4},{4,0},{1,5},{5,1},{2,6},{6,2},{3,7},{7,3},{8,12},{12,8},{9,1... | collective-permute-start | bytes 540680 | tf_op jit(solution)/shard_map/ppermute | solution.py:20
  451.1 29.5 %collective-permute-start.68 = (bf16[1,128,1024]{2,1,0:T(8,128)(2,1)S(1)}, bf16[1,128,1024]{2,1,0:T(8,128)(2,1)S(1)}, u32[]{:S(2)}, u32[]{:S(2)}) collective-permute-start(bf16[1,128,1024]{2,1,0:T(8,128)(2,1)S(1)} %get-tuple-element.181), channel_id=1, source_target_pairs={{0,0},{2,4},{4,2},{6,6},{1,1},{3,5},{5,3},{7,7},{8,8},{10,12},{12,... | collective-permute-start | bytes 786440 | tf_op jit(solution)/shard_map/ppermute | solution.py:972
  451.8 17.2 %collective-permute-start.85 = (bf16[32,2816]{1,0:T(8,128)(2,1)S(1)}, bf16[32,2816]{1,0:T(8,128)(2,1)S(1)}, u32[]{:S(2)}, u32[]{:S(2)}) collective-permute-start(bf16[32,2816]{1,0:T(8,128)(2,1)S(1)} %get-tuple-element.214), channel_id=1, source_target_pairs={{0,1},{1,0},{2,3},{3,2},{4,5},{5,4},{6,7},{7,6},{8,9},{9,8},{10,11... | collective-permute-start | bytes 540680 | tf_op jit(solution)/shard_map/ppermute | solution.py:20
  (153 other events, 1685.7 us)

commit v3 on v2

--- a/solution.py
+++ b/solution.py
@@ -395,6 +395,119 @@
         yield slot, bit("y", slot & 4), bit("x", slot & 2), bit("zh", slot & 1)
 
 
+class View:
+    def __init__(self, ref, row):
+        self.ref, self.row = ref, row
+
+    def _spot(self, spot):
+        rows, columns = spot if isinstance(spot, tuple) else (spot, slice(None))
+        if isinstance(rows, slice):
+            return slice(rows.start + self.row, rows.stop + self.row), columns
+        return pl.ds(rows.start + self.row, rows.size), columns
+
+    def __getitem__(self, spot):
+        return self.ref[self._spot(spot)]
+
+    def __setitem__(self, spot, value):
+        self.ref[self._spot(spot)] = value
+
+
+class Rows:
+    def __init__(self, refs):
+        self.refs, self.size = refs, refs[0].shape[0]
+
+    def _span(self, spot):
+        rows = spot[0] if isinstance(spot, tuple) else spot
+        if rows is Ellipsis:
+            return 0, len(self.refs)
+        return rows.start // self.size, rows.stop // self.size
+
+    def __getitem__(self, spot):
+        first, last = self._span(spot)
+        return jnp.concatenate([r[...] for r in self.refs[first:last]], axis=0)
+
+    def __setitem__(self, spot, value):
+        first, last = self._span(spot)
+        for i in range(first, last):
+            self.refs[i][...] = value[(i - first) * self.size : (i - first + 1) * self.size]
+
+    def block(self, which):
+        low, high = self[slice(0, 128), :], self[slice(128, 256), :]
+        return jnp.where(which == 0, low, high)
+
+
+class Joined:
+    def __init__(self, low, high, cut):
+        self.low, self.high, self.cut = low, high, cut
+
+    def __getitem__(self, spot):
+        rows, columns = spot
+        parts = []
+        if rows.start < self.cut:
+            parts.append(self.low[rows.start : min(rows.stop, self.cut), columns])
+        if rows.stop > self.cut:
+            parts.append(self.high[max(rows.start, self.cut) - self.cut : rows.stop - self.cut, columns])
+        return parts[0] if len(parts) == 1 else jnp.concatenate(parts, axis=0)
+
+
+def eight_slots(own, far, near_x, near_y, by_x, by_y, both, rows):
+    cut = 128 if rows == 256 else 64
+    across = Joined(View(by_y, rows), View(by_x, rows), cut)
+    return own, far, near_x, by_x, near_y, by_y, across, both
+
+
+def att_0_slots(refs):
+    return eight_slots(*refs, 144)
+
+
+def mlp_0_slots(refs):
+    own, far_up, far_down, *refs = refs
+    return eight_slots(own, Joined(far_up, far_down, 128), *refs, 256)
+
+
+def att_1_slots(refs):
+    own, far, by_x_1, by_y_1, by_x, by_y, both = refs
+    return eight_slots(own, View(far, 0), View(by_x_1, 256), View(by_y_1, 256), by_x, by_y, both, 128)
+
+
+def mlp_1_slots(refs):
+    own, own_down, far, far_down, by_x_1, by_y_1, by_x, by_y, both = refs
+    own, far = Joined(View(own, 128), own_down, 128), Joined(View(far, 128), far_down, 128)
+    return eight_slots(own, far, View(by_x_1, 192), View(by_y_1, 192), by_x, by_y, both, 256)
+
+
+def second_message(far, near_x, near_y, to_x, to_y, rows):
+    cut = 128 if rows == 256 else 64
+    to_x[0:rows, :] = far[0:rows, :]
+    to_y[0:rows, :] = far[0:rows, :]
+    to_y[rows : rows + cut, :] = near_x[0:cut, :]
+    to_x[rows : 2 * rows - cut, :] = near_y[cut:rows, :]
+
+
+def att_0_message(far, near_x, near_y, to_x, to_y):
+    second_message(far, near_x, near_y, to_x, to_y, 144)
+
+
+def mlp_0_message(far_up, far_down, near_x, near_y, to_x, to_y, to_both):
+    far = Joined(far_up, far_down, 128)
+    to_both[...] = far[0:256, :]
+    second_message(far, near_x, near_y, to_x, to_y, 256)
+
+
+def att_1_message(far, near_x, near_y, own, own_down, to_x, to_y, to_both):
+    to_both[...] = far[0:128, :]
+    second_message(far, View(near_x, 256), View(near_y, 256), to_x, to_y, 128)
+    for to in (to_x, to_y):
+        to[192:320, :] = own[128:256, :]
+        to[320:448, :] = own_down[...]
+
+
+def mlp_1_message(far, far_down, near_x, near_y, to_x, to_y, to_both):
+    far = Joined(View(far, 128), far_down, 128)
+    to_both[...] = far[0:256, :]
+    second_message(far, View(near_x, 192), View(near_y, 192), to_x, to_y, 256)
+
+
 def slot_blocks():
     return [(r, (y * 2 + x) * 2 + zh) for r, y, x, zh in slot_places()]
 
@@ -403,20 +516,43 @@
     return pl.ds(pl.multiple_of(block * size, size), size)
 
 
-def run(kernel, outs, *ins, limit=40, flops=0):
+def run(kernel, outs, *ins, after=(), us=1.0, anywhere=False, limit=16):
     smem = pl.BlockSpec(memory_space=pltpu.SMEM)
     vmem = pl.BlockSpec(memory_space=pltpu.VMEM)
-    scratch = getattr(kernel, "scratch", [])
-    moved = sum(v.size * v.dtype.itemsize for v in list(ins) + list(outs))
+    free = pl.BlockSpec(memory_space=pl.ANY)
+    skip = len(after)
+
+    def body(*refs):
+        kernel(*refs[skip:])
+
     return pl.pallas_call(
-        kernel,
+        body,
         out_shape=tuple(outs),
-        in_specs=[smem if v.size == 4 else vmem for v in ins],
+        in_specs=[free] * skip
+        + [smem if v.size == 4 else free if anywhere else vmem for v in ins],
         out_specs=tuple(vmem for _ in outs),
-        scratch_shapes=scratch,
+        scratch_shapes=getattr(kernel, "scratch", []),
         compiler_params=pltpu.CompilerParams(vmem_limit_bytes=limit << 20),
-        cost_estimate=pl.CostEstimate(flops=flops, bytes_accessed=moved, transcendentals=0),
-    )(*ins)
+        cost_estimate=pl.CostEstimate(flops=int(us * 1e7), bytes_accessed=0, transcendentals=0),
+    )(*after, *ins)
+
+
+def gate(after, *values):
+    skip = len(after)
+
+    def body(*refs):
+        refs[-1][...] = jnp.zeros_like(refs[-1])
+
+    free = pl.BlockSpec(memory_space=pl.ANY)
+    return pl.pallas_call(
+        body,
+        out_shape=tuple(shape(*v.shape, dtype=v.dtype) for v in values) + (shape(8, 128, dtype=F32),),
+        in_specs=[free] * (skip + len(values)),
+        out_specs=tuple(free for _ in values) + (pl.BlockSpec(memory_space=pltpu.VMEM),),
+        input_output_aliases={skip + i: i for i in range(len(values))},
+        compiler_params=pltpu.CompilerParams(vmem_limit_bytes=16 << 20),
+        cost_estimate=pl.CostEstimate(flops=10**4, bytes_accessed=0, transcendentals=0),
+    )(*after, *values)
 
 
 def shape(*sizes, dtype=BF):
@@ -465,19 +601,24 @@
     ]
 
 
-def prepare(g1, b1, bo, g2, b2, bd, qv, up, w_qkv, w_out, w_up, w_down, *outs):
-    first, rest = outs[0:4], outs[4:8]
-    out_a, out_b, down = outs[8:11]
-    rows = [spread(v[...]) for v in (g1, b1, bo, g2, b2, bd, qv, up)]
+def fetch(sources, held, sems):
+    copies = [pltpu.make_async_copy(*pair, sems.at[i]) for i, pair in enumerate(zip(sources, held))]
+    for copy in copies:
+        copy.start()
+    for copy in copies:
+        copy.wait()
+
+
+def prepare_first(*refs):
+    sources, refs = refs[:11], refs[11:]
+    first, (out_a, out_b, down), (held, sems) = refs[0:4], refs[4:7], (refs[7:18], refs[18])
+    fetch(sources[:9] + (sources[9].at[0], sources[10].at[0]), held, sems)
+    rows = [spread(v[...]) for v in held[:8]]
+    w_out, w_qkv, w_down = held[8:]
     small = jnp.concatenate([v[l : l + 1] for l in range(2) for v in rows], axis=0)
     for i, (dc, dl) in enumerate(RANKS):
-        core, zl = bit("core", dc), bit("zl", dl)
-        for src, dst in qkv_blocks(core, zl):
-            first[i][0:32, dst * 128 : dst * 128 + 128] = w_qkv[0, :, at(src, 128)]
-            rest[i][:, 1024 + dst * 128 : 1152 + dst * 128] = w_qkv[1, :, at(src, 128)]
-        for src, dst in up_blocks(core, zl):
-            rest[i][:, dst * 128 : dst * 128 + 128] = w_up[0, :, at(src, 128)]
-            rest[i][:, 1792 + dst * 128 : 1920 + dst * 128] = w_up[1, :, at(src, 128)]
+        for src, dst in qkv_blocks(bit("core", dc), bit("zl", dl)):
+            first[i][0:32, dst * 128 : dst * 128 + 128] = w_qkv[:, at(src, 128)]
         first[i][32:48, 0:128] = small.astype(BF)
         first[i][32:48, 128:768] = jnp.zeros((16, 640), BF)
     low_zl = lax.axis_index("zl") == 0
@@ -485,7 +626,23 @@
         w = inner_columns(w_out[l].astype(F32)).astype(BF)
         out_a[l * 32 : l * 32 + 32] = jnp.where(low_zl, w[:, :512], w[:, 512:])
         out_b[l * 32 : l * 32 + 32] = jnp.where(low_zl, w[:, 512:], w[:, :512])
-        down[l] = inner_columns(w_down[l].astype(F32)).astype(BF)
+    down[...] = inner_columns(w_down[...].astype(F32)).astype(BF)
+
+
+def prepare_rest(*refs):
+    sources, refs = refs[:4], refs[4:]
+    rest, (down, cot), (held, sems) = refs[0:4], refs[4:6], (refs[6:10], refs[10])
+    fetch((sources[0].at[1], sources[1], sources[2].at[1], sources[3].at[0]), held, sems)
+    w_qkv, w_up, w_down, cot_in = held
+    for i, (dc, dl) in enumerate(RANKS):
+        core, zl = bit("core", dc), bit("zl", dl)
+        for src, dst in qkv_blocks(core, zl):
+            rest[i][:, 1024 + dst * 128 : 1152 + dst * 128] = w_qkv[:, at(src, 128)]
+        for src, dst in up_blocks(core, zl):
+            rest[i][:, dst * 128 : dst * 128 + 128] = w_up[0, :, at(src, 128)]
+            rest[i][:, 1792 + dst * 128 : 1920 + dst * 128] = w_up[1, :, at(src, 128)]
+    down[...] = inner_columns(w_down[...].astype(F32)).astype(BF)
+    cot[...] = inner_columns(cot_in[...].astype(F32)).astype(BF)
 
 
 def put_out(piece, layer, out_a, out_b):
@@ -518,26 +675,25 @@
     piece[128:144, 256:1024] = jnp.zeros((16, 768), BF)
 
 
-def pack_rest(m0, m1, m2, m3, out_a, out_b, down, mlp_0, att_1, mlp_1):
+def pack_rest(m0, m1, m2, m3, out_a, out_b, down_0, mlp_0, up_0, deep, pair):
     for i, m in enumerate((m0, m1, m2, m3)):
         spot = at(bit("core", RANKS[i][0]) * 2 + bit("zl", RANKS[i][1]), 32)
-        mlp_0[spot, :] = m[:, 0:1024]
-        att_1[spot, 0:768] = m[:, 1024:1792]
-        mlp_1[spot, :] = m[:, 1792:2816]
-    put_out(att_1, 1, out_a, out_b)
-    mlp_0[128:256, :] = down[0]
-    mlp_1[128:256, :] = down[1]
-
-
-def gather_slots(piece):
-    far = swap(piece, "zh")
-    near_x = swap(piece, "x")
-    near_y = swap(piece, "y")
-    far_y = swap(far, "y")
-    far_x = swap(far, "x")
-    near_xy = swap(near_x, "y")
-    far_yx = swap(far_y, "x")
-    return (piece, far, near_x, far_x, near_y, far_y, near_xy, far_yx)
+        up_0[spot, :] = m[:, 0:1024]
+        deep[spot, 0:768] = m[:, 1024:1792]
+        deep[at(4 + bit("core", RANKS[i][0]) * 2 + bit("zl", RANKS[i][1]), 32), :] = m[:, 1792:2816]
+    put_out(deep, 1, out_a, out_b)
+    mlp_0[0:128, :] = up_0[...]
+    mlp_0[128:256, :] = down_0[...]
+    pair[0:256, :] = mlp_0[...]
+    pair[256:384, :] = deep[0:128, :]
+
+
+def both_ways(value):
+    return lax.ppermute(value, ("y", "x"), [(0, 3), (3, 0), (1, 2), (2, 1)])
+
+
+def first_hops(piece):
+    return swap(piece, "zh"), swap(piece, "x"), swap(piece, "y")
 
 
 def load_rows(pieces, scratch, row, columns):
@@ -565,14 +721,19 @@
         scratch[spot, :] = inner_columns(blocks[i][0].astype(F32)).astype(scratch.dtype)
 
 
+def load_blocks(blocks, scratch):
+    for i, (dc, dl) in enumerate(RANKS):
+        scratch[at(bit("core", dc) * 2 + bit("zl", dl), 128), :] = blocks[i][...]
+
+
 def load_cores(mine, other, scratch):
-    scratch[at(bit("core", 0), 256), :] = mine[...]
-    scratch[at(bit("core", 1), 256), :] = other[...]
+    scratch[at(bit("core", 0), 256), :] = Rows(mine)[...]
+    scratch[at(bit("core", 1), 256), :] = Rows(other)[...]
 
 
 def split_product(left, right, keep, send):
     mine, other = at(bit("core", 0), 256), at(bit("core", 1), 256)
-    send[...] = right(left[other, :]).astype(BF)
+    Rows(send)[...] = right(left[other, :]).astype(BF)
     keep[...] = right(left[mine, :])
 
 
@@ -636,7 +797,7 @@
 
 
 def attention_part(h1, vec, layer, pieces, seg_a, seg_b, order, outs, scratch):
-    qkv, probs, o, keep, send = outs
+    qkv, probs, o, keep, *send = outs
     wq, wo, dist = scratch
     load_rows(pieces, wq, 0, 768)
     load_out(pieces, wo)
@@ -647,8 +808,8 @@
 
 
 def first_attention(t0, t1, t2, t3, *refs):
-    pieces, (seg_a, seg_b, order), refs = refs[:8], refs[8:11], refs[11:]
-    vec, h1, outs, scratch = refs[0], refs[1], refs[2:7], refs[7:]
+    pieces, (seg_a, seg_b, order), refs = att_0_slots(refs[:7]), refs[7:10], refs[10:]
+    vec, h1, outs, scratch = refs[0], refs[1], refs[2:10], refs[10:]
     q_one, q_two, scratch = scratch[0], scratch[1], scratch[2:]
     for r, block in slot_blocks():
         vec[:, at(block, 128)] = pieces[r][128:144, 0:128].astype(F32)
@@ -670,19 +831,22 @@
     attention_part(h1, vec, 0, pieces, seg_a, seg_b, order, outs, scratch)
 
 
-def next_attention(mine, other, *refs):
-    pieces, (vec, seg_a, seg_b, order), refs = refs[:8], refs[8:12], refs[12:]
-    h1, outs, scratch = refs[0], refs[1:6], refs[6:]
+def next_attention(*refs):
+    mine, other, refs = refs[:4], refs[4:8], refs[8:]
+    pieces, (vec, seg_a, seg_b, order), refs = att_1_slots(refs[:7]), refs[7:11], refs[11:]
+    h1, outs, scratch = refs[0], refs[1:9], refs[9:]
     load_cores(mine, other, h1)
     attention_part(h1, vec, 1, pieces, seg_a, seg_b, order, outs, scratch)
 
 
-def add_parts(keep, came, out):
+def add_parts(keep, *refs):
+    came, out = Rows(refs[:4]), refs[4]
     out[...] = (keep[...] + came[...].astype(F32)).astype(BF)
 
 
 def norm_stage(bias_row, gain_row):
-    def kernel(x, part, came, vec, x_out, h):
+    def kernel(x, part, came, vec, x_out, *h):
+        h = Rows(h)
         for i in range(2):
             spot = slice(i * 128, i * 128 + 128)
             v = x[spot, :] + part[spot, :].astype(F32) + came[spot, :].astype(F32)
@@ -694,16 +858,23 @@
     return kernel
 
 
-def first_norm_stage(t0, t2, part, came, vec, x_out, h, x0):
+def first_norm_stage(t0, t2, part, came, vec, *refs):
+    x_out, h, x0 = refs[0], refs[1:5], refs[5]
     x0[at(bit("zl", 0), 128), :] = inner_columns(t0[0].astype(F32))
     x0[at(bit("zl", 1), 128), :] = inner_columns(t2[0].astype(F32))
-    norm_stage(2, 3)(x0, part, came, vec, x_out, h)
+    norm_stage(2, 3)(x0, part, came, vec, x_out, *h)
+
+
+def mlp_weights(refs, layer):
+    count = 9 if layer else 8
+    return (mlp_1_slots if layer else mlp_0_slots)(refs[:count]), refs[count:]
 
 
 def mlp_stage(layer):
-    def kernel(mine, other, *refs):
-        pieces, vec, refs = refs[:8], refs[8], refs[9:]
-        h2, u, a, keep, send, w = refs
+    def kernel(*refs):
+        mine, other, refs = refs[:4], refs[4:8], refs[8:]
+        pieces, refs = mlp_weights(refs, layer)
+        vec, h2, u, a, keep, *send, w = refs
         load_cores(mine, other, h2)
         load_rows(pieces, w, 0, 1024)
         for i in range(4):
@@ -718,9 +889,15 @@
 
 
 def finish_rows(x, part, came, vec, out):
-    spot = at(bit("zl", 0), 128)
-    v = x[spot, :] + part[spot, :].astype(F32) + came[spot, :].astype(F32) + vec[13:14, :]
+    v = x[at(bit("zl", 0), 128), :] + part[...].astype(F32) + came[...].astype(F32) + vec[13:14, :]
     out[0] = inner_columns(v).astype(BF)
+
+
+def add_split(keep, *refs):
+    came, mine, other = Rows(refs[:4]), refs[4], refs[5]
+    for to, flip in ((mine, 0), (other, 1)):
+        which = bit("zl", flip)
+        to[...] = (keep[at(which, 128), :] + came.block(which).astype(F32)).astype(BF)
 
 
 def gelu_slope(u):
@@ -729,47 +906,54 @@
     return 0.5 * (1.0 + t) + 0.5 * u * (1.0 - t * t) * (c * (1.0 + 3 * 0.044715 * u * u))
 
 
-def mlp_back_part(gy2, u, pieces, gu, keep, send, w):
-    load_rows(pieces, w, 128, 1024)
-    for i in range(4):
-        spot = slice(i * 128, i * 128 + 128)
-        gu[spot, :] = (dot_t(gy2[spot, :], w[...]) * gelu_slope(u[spot, :])).astype(BF)
-    load_rows(pieces, w, 0, 1024)
-    split_product(gu, lambda rows: dot_t(rows, w[...]), keep, send)
-
-
-def first_mlp_back(c0, c1, c2, c3, u, *refs):
-    pieces, refs = refs[:8], refs[8:]
-    load_stream((c0, c1, c2, c3), refs[0])
-    mlp_back_part(refs[0], u, pieces, *refs[1:])
-
-
-def next_mlp_back(mine, other, u, *refs):
-    pieces, refs = refs[:8], refs[8:]
-    load_cores(mine, other, refs[0])
-    mlp_back_part(refs[0], u, pieces, *refs[1:])
+def mlp_back(layer):
+    def kernel(*refs):
+        if layer == 1:
+            blocks, u, refs = refs[:4], refs[4], refs[5:]
+        else:
+            blocks, u, refs = refs[:8], refs[8], refs[9:]
+        pieces, (gy2, gu, keep, *send, w) = mlp_weights(refs, layer)
+        load_blocks(blocks, gy2) if layer == 1 else load_cores(blocks[:4], blocks[4:], gy2)
+        load_rows(pieces, w, 128, 1024)
+        for i in range(4):
+            spot = slice(i * 128, i * 128 + 128)
+            gu[spot, :] = (dot_t(gy2[spot, :], w[...]) * gelu_slope(u[spot, :])).astype(BF)
+        load_rows(pieces, w, 0, 1024)
+        split_product(gu, lambda rows: dot_t(rows, w[...]), keep, send)
+
+    return with_scratch(kernel, pltpu.VMEM((1024, 1024), BF))
 
 
 def turned_dot(left, right):
     return lax.dot_general(left, right, (((0,), (0,)), ((), ())), preferred_element_type=F32)
 
 
-def slot_spots(near_send, near_0, near_1, far_send, far_0, far_1):
+def slot_spots(rows, to_y, to_x, near_0, near_1, far_0, far_1):
     return (
-        near_0, far_0, near_1, far_send.at[0], near_send.at[0], far_1, near_send.at[1], far_send.at[1],
+        near_0, far_0, near_1, View(to_x, 0), View(to_y, 0), far_1, View(to_y, rows), View(to_x, rows),
     )
 
 
 def mlp_grads(h2, a, gy2, gu, *outs):
-    spots = slot_spots(*outs)
+    spots = slot_spots(256, *outs)
     for r, block in slot_blocks():
         spots[r][0:128, :] = turned_dot(h2[:, at(block, 128)], gu[...]).astype(BF)
         spots[r][128:256, :] = turned_dot(a[:, at(block, 128)], gy2[...]).astype(BF)
 
 
+def second_sums(rows, near_1, near, far_1, far, to_x, to_y):
+    to_x[0:rows, :] = (near_1[...].astype(F32) + near[0:rows, :].astype(F32)).astype(BF)
+    to_y[0:rows, :] = (far_1[...].astype(F32) + far[0:rows, :].astype(F32)).astype(BF)
+
+
+def third_sum(rows, far_0, far, far_2, out):
+    total = far_0[...].astype(F32) + far[0:rows, :].astype(F32) + far_2[0:rows, :].astype(F32)
+    out[...] = total.astype(BF)
+
+
 def norm_back(gx, part, came, x, gain, gm, gy, sums):
     totals = [jnp.zeros((1, x.shape[1]), F32) for _ in range(4)]
-    for i in range(2):
+    for i in range(part.shape[0] // 128):
         spot = slice(i * 128, i * 128 + 128)
         dh = part[spot, :].astype(F32) + came[spot, :].astype(F32)
         z, inv = normal(x[spot, :])
@@ -787,28 +971,37 @@
 
 
 def norm_back_stage(gain_row):
-    def kernel(gx, part, came, x, vec, gm, gy, sums):
-        norm_back(gx, part, came, x, vec[gain_row : gain_row + 1, :], gm, gy, sums)
+    def kernel(gx, part, came, x, vec, gm, *refs):
+        norm_back(gx, part, came, x, vec[gain_row : gain_row + 1, :], gm, Rows(refs[:4]), refs[4])
 
     return kernel
 
 
-def first_norm_back(c0, c2, part, came, x, vec, gm, gy, sums, gx):
-    gx[at(bit("zl", 0), 128), :] = inner_columns(c0[0].astype(F32))
-    gx[at(bit("zl", 1), 128), :] = inner_columns(c2[0].astype(F32))
+def first_norm_back(c0, c2, part, came, x, vec, gm, *refs):
+    gy, sums, gx = Rows(refs[:4]), refs[4], refs[5]
+    gx[at(bit("zl", 0), 128), :] = c0[...].astype(F32)
+    gx[at(bit("zl", 1), 128), :] = c2[...].astype(F32)
     norm_back(gx, part, came, x, vec[11:12, :], gm, gy, sums)
 
 
-def last_norm_back(gx, part, came, t0, t2, vec, grad, sums, x, gm, gy):
-    x[at(bit("zl", 0), 128), :] = inner_columns(t0[0].astype(F32))
-    x[at(bit("zl", 1), 128), :] = inner_columns(t2[0].astype(F32))
-    norm_back(gx, part, came, x, vec[0:1, :], gm, gy, sums)
-    grad[0] = inner_columns(gm[at(bit("zl", 0), 128), :]).astype(BF)
-
-
-def attention_back(mine, other, qkv, probs, *refs):
-    pieces, refs = refs[:8], refs[8:]
-    gy1, gqkv, keep, send, wq, wo, go, gk, gv = refs
+def last_norm_back(gx, part, came, t0, vec, grad, up, x, gm, gy, sums):
+    x[...] = inner_columns(t0[0].astype(F32))
+    up[...] = gx[at(bit("zl", 0), 128), :]
+    norm_back(up, part, came, x, vec[0:1, :], gm, gy, sums)
+    grad[0] = inner_columns(gm[...]).astype(BF)
+
+
+def attention_back(layer):
+    def kernel(*refs):
+        mine, other, (qkv, probs), refs = refs[:4], refs[4:8], refs[8:10], refs[10:]
+        pieces = (att_1_slots if layer else att_0_slots)(refs[:7])
+        attention_back_part(mine, other, qkv, probs, pieces, *refs[7:])
+
+    return kernel
+
+
+def attention_back_part(mine, other, qkv, probs, pieces, *refs):
+    gy1, gqkv, keep, *send, wq, wo, go, gk, gv = refs
     load_cores(mine, other, gy1)
     load_rows(pieces, wq, 0, 768)
     load_out(pieces, wo)
@@ -846,20 +1039,69 @@
     split_product(gqkv, lambda rows: dot_t(rows, wq[...]), keep, send)
 
 
-def attention_grads(h1, o, gy1, gqkv, *outs):
-    spots, d_out = slot_spots(*outs[:6]), outs[6]
+def attention_grads(rows, h1, o, gy1, gqkv, outs, d_out):
+    spots = slot_spots(rows, *outs)
     d_out[...] = turned_dot(o[...], gy1[...]).astype(BF)
     for (r, block), (_, y, x, zh) in zip(slot_blocks(), slot_places()):
         spots[r][0:128, 0:768] = turned_dot(h1[:, at(block, 128)], gqkv[...]).astype(BF)
         for h in range(2):
             spots[r][h * 64 : h * 64 + 64, 768:1024] = d_out[at(x * 2 + zh, 64), at(y * 2 + h, 256)]
-
-
-def last_attention_grads(h1, o, gy1, gqkv, g1, e1, e0, gu1, gu0, gq1, *outs):
-    attention_grads(h1, o, gy1, gqkv, *outs[:7])
-    spots, (ups, wide) = slot_spots(*outs[:6]), outs[7:]
+    return spots
+
+
+def window_1(h2, a, gy2, gu, *outs):
+    mlp_grads(h2, a, gy2, gu, *outs)
+
+
+def window_2(h1, o, gy1, gqkv, near_1, y_1, far_1, x_1, to_y, to_x, *rest):
+    attention_grads(128, h1, o, gy1, gqkv, (to_y, to_x) + rest[:4], rest[4])
+    second_sums(256, near_1, View(y_1, 256), far_1, View(x_1, 256), View(to_x, 256), View(to_y, 256))
+
+
+def window_3(h2, a, gy2, gu, near_1, y_2, far_1, x_2, far_0, x_1, to_y, to_x, *rest):
+    mlp_grads(h2, a, gy2, gu, to_y, to_x, *rest[:4])
+    second_sums(128, near_1, View(y_2, 128), far_1, View(x_2, 128), View(to_x, 512), View(to_y, 512))
+    third_sum(256, far_0, x_1, View(y_2, 256), rest[4])
+
+
+def window_4(near_1, y_3, far_1, x_3, far_0, x_2, to_x, to_y, to_zh):
+    second_sums(256, near_1, View(y_3, 256), far_1, View(x_3, 256), to_x, to_y)
+    third_sum(128, far_0, x_2, View(y_3, 512), to_zh)
+
+
+def window_5(*refs):
+    grads, (to_y, to_x), rest = refs[:19], refs[19:21], refs[21:]
+    last_attention_grads(*grads, (to_y, to_x) + rest[:4], *rest[4:])
+
+
+def second_only(near_1, y, far_1, x, to_x, to_y):
+    second_sums(144, near_1, View(y, 144), far_1, View(x, 144), to_x, to_y)
+
+
+def third_only(far_0, x, y, to_zh):
+    third_sum(256, far_0, x, y, to_zh)
+
+
+def window_6(far_0, x_4, y_5, to_zh):
+    third_sum(144, far_0, x_4, y_5, to_zh)
+
+
+def last_attention_grads(
+    h1, o, gy1, gqkv, g1, e1, e0, gu1, gu0, gq1, keep, s0, s1, s2, s3, t0, t1, t2, t3, outs, d_out, ups, wide
+):
+    spots = attention_grads(144, h1, o, gy1, gqkv, outs, d_out)
+    send = Rows((s0, s1, s2, s3))
     none = jnp.zeros((2, 1024), F32)
-    parts = [g1[0:2, :], e1[2:3, :], e1[0:2, :], e1[3:4, :], none, none]
+    gain = jnp.zeros((1, 1024), F32)
+    shift = jnp.zeros((1, 1024), F32)
+    for i, block in enumerate((t0, t1, t2, t3)):
+        dc, dl = RANKS[i]
+        z, _ = normal(inner_columns(block[0].astype(F32)))
+        which = bit("zl", dl)
+        dh = send.block(which).astype(F32) if dc else keep[at(which, 128), :]
+        gain = gain + jnp.sum(dh * z, axis=0, keepdims=True)
+        shift = shift + jnp.sum(dh, axis=0, keepdims=True)
+    parts = [g1[0:2, :], e1[2:3, :], e1[0:2, :], e1[3:4, :], none, gain, shift]
     wide[...] = jnp.concatenate(parts + [e0[2:3, :], e0[0:2, :], e0[3:4, :], none], axis=0)
     sums = [jnp.sum(v[...].astype(F32), axis=0, keepdims=True) for v in (gu1, gu0)]
     ups[...] = jnp.concatenate(sums + [jnp.zeros((14, 1024), F32)], axis=0)
@@ -876,20 +1118,11 @@
         spots[r][rows, 512:1024] = jnp.zeros((16, 512), BF)
 
 
-def scatter_slots(near_send, near_0, near_1, far_send, far_0, far_1):
-    near = swap(near_send, "y")
-    far = swap(far_send, "x")
-    near_2 = swap((near_1.astype(F32) + near[1].astype(F32)).astype(BF), "x")
-    far_2 = swap((far_1.astype(F32) + far[1].astype(F32)).astype(BF), "y")
-    far_all = far_0.astype(F32) + far[0].astype(F32) + far_2.astype(F32)
-    far_3 = swap(far_all.astype(BF), "zh")
-    return near_0, near, near_2, far_3
-
-
 def summed(parts, rows, columns):
-    near_0, near, near_2, far_3 = parts
-    value = near_0[rows, columns].astype(F32) + near[0, rows, columns].astype(F32)
-    return value + near_2[rows, columns].astype(F32) + far_3[rows, columns].astype(F32)
+    value = parts[0][rows, columns].astype(F32)
+    for part in parts[1:]:
+        value = value + part[rows, columns].astype(F32)
+    return value
 
 
 def own_out(parts, flip):
@@ -901,45 +1134,52 @@
     return jnp.concatenate(halves, axis=1)
 
 
-def unpack_rest(*refs):
-    mlp_1, att_1, mlp_0 = refs[0:4], refs[4:8], refs[8:12]
-    mine, sends, a, b, down = refs[12], refs[13:16], refs[16], refs[17], refs[18]
-    for i, (dc, dl) in enumerate(RANKS):
-        rows = at(bit("core", dc) * 2 + bit("zl", dl), 32)
+def rank_rows(i):
+    return at(bit("core", RANKS[i][0]) * 2 + bit("zl", RANKS[i][1]), 32)
+
+
+def unpack_first(y_1, y_2, x_2, x_3, m_near, m_far, a_near, a_far, mine, *refs):
+    mlp = (m_near, y_1, View(x_2, 256), m_far)
+    att = (a_near, y_2, View(x_3, 512), a_far)
+    sends, a, b, down = refs[0:3], refs[3], refs[4], refs[5]
+    for i in range(4):
         to = mine if i == 0 else sends[i - 1]
-        for parts, start, width in ((mlp_0, 0, 1024), (att_1, 1024, 768), (mlp_1, 1792, 1024)):
-            value = summed(parts, rows, slice(0, width))
+        for parts, start, width in ((att, 0, 768), (mlp, 768, 1024)):
+            value = summed(parts, rank_rows(i), slice(0, width))
             to[:, start : start + width] = value.astype(to.dtype)
-    a[...] = own_out(att_1, 0).astype(BF)
-    b[...] = own_out(att_1, 1).astype(BF)
-    for l, parts in ((0, mlp_0), (1, mlp_1)):
-        down[l] = inner_columns(summed(parts, slice(128, 256), slice(0, 1024)))
-
-
-def unpack_last(near_0, near, near_2, far_3, a1, b1, mine, *refs):
-    parts = (near_0, near, near_2, far_3)
-    sends, (a, b) = refs[0:3], refs[3:5]
-    for i, (dc, dl) in enumerate(RANKS):
-        rows = at(bit("core", dc) * 2 + bit("zl", dl), 32)
+    a[...] = own_out(att, 0).astype(BF)
+    b[...] = own_out(att, 1).astype(BF)
+    down[...] = inner_columns(summed(mlp, slice(128, 256), slice(0, 1024)))
+
+
+def unpack_last(y_3, y_5, x_4, x_6, m_near, m_far, a_near, a_far, a1, b1, down_1, mine, *refs):
+    mlp = (m_near, y_3, x_4, m_far)
+    att = (a_near, y_5, x_6, a_far)
+    sends, (a, b), down = refs[0:3], refs[3:5], refs[5]
+    for i in range(4):
         to = mine if i == 0 else sends[i - 1]
-        to[0:32, :] = summed(parts, rows, slice(0, 768)).astype(to.dtype)
-        to[32:48, :] = summed(parts, slice(128, 144), slice(0, 768)).astype(to.dtype)
-    a[0:32, :] = own_out(parts, 0).astype(BF)
-    b[0:32, :] = own_out(parts, 1).astype(BF)
+        to[0:32, 0:768] = summed(att, rank_rows(i), slice(0, 768)).astype(to.dtype)
+        to[0:32, 768:1792] = summed(mlp, rank_rows(i), slice(0, 1024)).astype(to.dtype)
+        to[32:48, 0:768] = summed(att, slice(128, 144), slice(0, 768)).astype(to.dtype)
+        to[32:48, 768:1792] = jnp.zeros((16, 1024), to.dtype)
+    a[0:32, :] = own_out(att, 0).astype(BF)
+    b[0:32, :] = own_out(att, 1).astype(BF)
     a[32:64, :] = a1[...]
     b[32:64, :] = b1[...]
-
-
-def finish(rest, r1, r2, r3, last, l1, l2, l3, a, b, total, *outs):
+    down[0] = inner_columns(summed(mlp, slice(128, 256), slice(0, 1024)))
+    down[1] = down_1[...]
+
+
+def finish(rest, r1, r2, r3, last, l1, l2, l3, a, b, *outs):
     g1, b1, w_qkv, qv, w_out, bo, g2, b2, w_up, up, bd = outs
     for i, (rm, lm) in enumerate(((rest, last), (r1, l1), (r2, l2), (r3, l3))):
         core, zl = bit("core", RANKS[i][0]), bit("zl", RANKS[i][1])
         for src, dst in qkv_blocks(core, zl):
             w_qkv[0, :, at(src, 128)] = lm[0:32, dst * 128 : dst * 128 + 128].astype(F32)
-            w_qkv[1, :, at(src, 128)] = rm[:, 1024 + dst * 128 : 1152 + dst * 128].astype(F32)
+            w_qkv[1, :, at(src, 128)] = rm[:, dst * 128 : dst * 128 + 128].astype(F32)
         for src, dst in up_blocks(core, zl):
-            w_up[0, :, at(src, 128)] = rm[:, dst * 128 : dst * 128 + 128].astype(F32)
-            w_up[1, :, at(src, 128)] = rm[:, 1792 + dst * 128 : 1920 + dst * 128].astype(F32)
+            w_up[0, :, at(src, 128)] = lm[0:32, 768 + dst * 128 : 896 + dst * 128].astype(F32)
+            w_up[1, :, at(src, 128)] = rm[:, 768 + dst * 128 : 896 + dst * 128].astype(F32)
     low_zl = lax.axis_index("zl") == 0
     for l in range(2):
         va, vb = a[l * 32 : l * 32 + 32].astype(F32), b[l * 32 : l * 32 + 32].astype(F32)
@@ -953,13 +1193,14 @@
             found = jnp.where(spot == j, value[:, j * size : j * size + size], found)
         return found
 
-    wide = chunk(last[32:48, 0:128] + l1[32:48, 0:128].astype(F32), 32)
-    block = (lax.axis_index("y") * 2 + lax.axis_index("x")) * 2 + lax.axis_index("zh")
-    late = chunk(total[:, at(block, 128)], 32)
+    mine, by_core = last[32:48, 0:128], l1[32:48, 0:128].astype(F32)
+    wide = chunk(mine + by_core, 32)
+    late = l2[32:48, 0:128].astype(F32) + l3[32:48, 0:128].astype(F32)
+    late = chunk(mine + by_core + late, 32)
     for row, ref in ((2, bo), (3, g2), (4, b2), (5, bd)):
         ref[...] = jnp.concatenate([wide[row + 8 : row + 9], wide[row : row + 1]], axis=0)
-    g1[...] = jnp.concatenate([late[0:1], wide[0:1]], axis=0)
-    b1[...] = jnp.concatenate([late[1:2], wide[1:2]], axis=0)
+    g1[...] = jnp.concatenate([late[8:9], wide[0:1]], axis=0)
+    b1[...] = jnp.concatenate([late[9:10], wide[1:2]], axis=0)
     up[...] = jnp.concatenate([last[33:34, 128:256], last[32:33, 128:256]], axis=0)
     both = last[32:48, 256:512]
     for m in (l1, l2, l3):
@@ -981,146 +1222,219 @@
     )
 
 
-def stream_blocks(block):
-    block = corner(block)
-    by_zl = swap(block, "zl")
-    return (block, swap(block, "core"), by_zl, swap(by_zl, "core"))
-
-
 def narrow_body(
     tokens, segment_ids, group_order, ln1_gain, ln1_bias, qkv_weight, qv_bias, out_weight, out_bias,
     ln2_gain, ln2_bias, up_weight, up_bias, down_weight, down_bias, cotangent,
 ):
+    small = (ln1_gain, ln1_bias, out_bias, ln2_gain, ln2_bias, down_bias, qv_bias, up_bias)
+
+    def held(*values):
+        return [pltpu.VMEM(v, BF) for v in values] + [pltpu.SemaphoreType.DMA((len(values),))]
+
+    row, rowf = shape(256, 1024), shape(256, 1024, dtype=F32)
+    quarters = [shape(64, 1024)] * 4
+
     ready = run(
-        prepare,
-        [shape(48, 768)] * 4 + [shape(32, 2816)] * 4 + [shape(64, 512)] * 2 + [shape(2, 128, 1024)],
-        ln1_gain, ln1_bias, out_bias, ln2_gain, ln2_bias, down_bias, qv_bias, up_bias,
-        qkv_weight, out_weight, up_weight, down_weight,
-    )
+        with_scratch(
+            prepare_first, *held(*[v.shape for v in small], (2, 32, 1024), (32, 3072), (128, 1024))
+        ),
+        [shape(48, 768)] * 4 + [shape(64, 512)] * 2 + [shape(128, 1024)],
+        *small, out_weight, qkv_weight, down_weight, anywhere=True, limit=60, us=3,
+    )
+    out_b = lax.ppermute(ready[5], ("y", "zl"), [(0, 2), (1, 0), (2, 3), (3, 1)])
+    out_a = lax.ppermute(ready[4], ("y", "zl"), [(0, 0), (1, 2), (2, 1), (3, 3)])
     first = (ready[0],) + to_partners(ready[1:4])
-    out_a = lax.ppermute(ready[8], ("y", "zl"), [(0, 0), (1, 2), (2, 1), (3, 3)])
-    out_b = lax.ppermute(ready[9], ("y", "zl"), [(0, 2), (1, 0), (2, 3), (3, 1)])
     (att_0,) = run(pack_first, [shape(144, 1024)], *first, out_a, out_b)
-    att_0 = gather_slots(att_0)
-    blocks = stream_blocks(tokens)
-    rest = (ready[4],) + to_partners(ready[5:8])
-    mlp_0, att_1, mlp_1 = run(
-        pack_rest, [shape(256, 1024), shape(128, 1024), shape(256, 1024)],
-        *rest, out_a, out_b, ready[10],
-    )
-    mlp_0, att_1, mlp_1 = gather_slots(mlp_0), gather_slots(att_1), gather_slots(mlp_1)
-    cots = stream_blocks(cotangent)
+    far, near_x, near_y = first_hops(att_0)
+    block = corner(tokens)
+    rest = run(
+        with_scratch(
+            prepare_rest, *held((32, 3072), (2, 32, 4096), (128, 1024), (128, 1024))
+        ),
+        [shape(32, 2816)] * 4 + [shape(128, 1024)] * 2,
+        qkv_weight, up_weight, down_weight, cotangent, after=(ready[0],), anywhere=True, us=2,
+    )
+    cot = rest[5]
+    mlp_0, up_0, deep, pair = run(
+        pack_rest, [row, shape(128, 1024), row, shape(384, 1024)],
+        rest[0], *to_partners(gate((att_0,), *rest[1:4])[:3]), out_a, out_b, ready[6],
+    )
+    down_1 = rest[4]
+    def second_hops(kernel, rows_x, rows_y, *ins, after=(), rows=0):
+        outs = [shape(n, 1024) for n in (rows_x, rows_y, rows) if n]
+        to = run(kernel, outs, *ins, after=after)
+        return swap(to[0], "x"), swap(to[1], "y"), both_ways(to[2] if rows else ins[0]), to[0]
+
+    by_x, by_y, both, sent = second_hops(
+        att_0_message, 224, 208, far, near_x, near_y, after=(pair,)
+    )
+    att_0 = (att_0, far, near_x, near_y, by_x, by_y, both)
+    up_0, down_0, _ = gate((sent,), up_0, ready[6])
+    far_up, far_down = swap(up_0, "zh"), swap(down_0, "zh")
+    pair, deep, token = gate((by_x, by_y, both, far_up), pair, deep)
+    pair_x, pair_y = swap(pair, "x"), swap(pair, "y")
+    by_zl = swap(block, "zl")
+    blocks = (block, swap(block, "core"), by_zl, swap(by_zl, "core"))
     segments = (segment_ids, swap(segment_ids, "core"), group_order)
 
-    def share(keep, send):
-        (part,) = run(add_parts, [shape(256, 1024)], keep, swap(send, "core"))
+    def cores(values):
+        return [swap(v, "core") for v in values]
+
+    def summed_core(keep, *send):
+        (part,) = run(add_parts, [row], keep, *cores(send))
         return part, swap(part, "zl")
 
-    def with_other(value):
-        return value, swap(value, "core")
+    def split_core(keep, *send, after=()):
+        part, other = run(add_split, [shape(128, 1024)] * 2, keep, *cores(send), after=after)
+        return part, swap(other, "zl")
+
+    def with_other(values):
+        return (*values, *cores(values))
 
     attention_outs = [
-        shape(512, 1024), shape(512, 768), shape(4, 512, 512), shape(512, 256),
-        shape(256, 1024, dtype=F32), shape(256, 1024),
+        shape(512, 1024), shape(512, 768), shape(4, 512, 512), shape(512, 256), rowf, *quarters,
     ]
     weights_scratch = [pltpu.VMEM((1024, 768), BF), pltpu.VMEM((256, 1024), BF)]
     dist = pltpu.VMEM((512, 512), F32)
     vec_scratch = [pltpu.VMEM((16, 1024), F32)] * 2
-    rows_out = [shape(256, 1024, dtype=F32), shape(256, 1024)]
-    mlp_outs = [
-        shape(512, 1024), shape(512, 1024, dtype=F32), shape(512, 1024),
-        shape(256, 1024, dtype=F32), shape(256, 1024),
-    ]
-    wide = pltpu.VMEM((1024, 1024), BF)
-
-    vec, h1_0, qkv_0, probs_0, o_0, keep, send = run(
+    mlp_outs = [shape(512, 1024), shape(512, 1024, dtype=F32), shape(512, 1024), rowf, *quarters]
+
+    vec, h1_0, qkv_0, probs_0, o_0, keep, *send = run(
         with_scratch(first_attention, *vec_scratch, *weights_scratch, dist),
-        [shape(16, 1024, dtype=F32)] + attention_outs, *blocks, *att_0, *segments,
-    )
-    x1_0, h = run(
+        [shape(16, 1024, dtype=F32)] + attention_outs, *blocks, *att_0, *segments, after=(token,), us=10,
+    )
+    far_down, pair_x, pair_y, deep, down_1, *send, _ = gate(
+        (keep,), far_down, pair_x, pair_y, deep, down_1, *send
+    )
+    deep_far = swap(deep, "zh")
+    part, came = summed_core(keep, *send)
+    by_x, by_y, both, token = second_hops(
+        mlp_0_message, 384, 384, far_up, far_down, pair_x, pair_y, after=(part,), rows=256
+    )
+    mlp_0 = (mlp_0, far_up, far_down, pair_x, pair_y, by_x, by_y, both)
+    x1_0, *h = run(
         with_scratch(first_norm_stage, pltpu.VMEM((256, 1024), F32)),
-        rows_out, blocks[0], blocks[2], *share(keep, send), vec,
-    )
-    h2_0, u_0, a_0, keep, send = run(mlp_stage(0), mlp_outs, *with_other(h), *mlp_0, vec)
-    x2_0, h = run(norm_stage(5, 8), rows_out, x1_0, *share(keep, send), vec)
-    h1_1, qkv_1, probs_1, o_1, keep, send = run(
+        [rowf, *quarters], blocks[0], blocks[2], part, came, vec, after=(token,), us=1.5,
+    )
+    h2_0, u_0, a_0, keep, *send = run(
+        mlp_stage(0), mlp_outs, *with_other(h), *mlp_0, vec, after=(deep_far,), us=4
+    )
+    down_1_far = swap(down_1, "zh")
+    one_x, one_y, both, token = second_hops(
+        att_1_message, 448, 448, deep_far, pair_x, pair_y, deep, down_1, after=(keep,), rows=128
+    )
+    att_1 = (deep, deep_far, pair_x, pair_y, one_x, one_y, both)
+    part, came = summed_core(keep, *send)
+    x2_0, *h = run(norm_stage(5, 8), [rowf, *quarters], x1_0, part, came, vec, after=(token, down_1_far), us=1)
+    by_x, by_y, both, token = second_hops(
+        mlp_1_message, 384, 384, deep_far, down_1_far, one_x, one_y, rows=256
+    )
+    h1_1, qkv_1, probs_1, o_1, keep, *send = run(
         with_scratch(next_attention, *weights_scratch, dist),
-        attention_outs, *with_other(h), *att_1, vec, *segments,
-    )
-    x1_1, h = run(norm_stage(10, 11), rows_out, x2_0, *share(keep, send), vec)
-    h2_1, u_1, a_1, keep, send = run(mlp_stage(1), mlp_outs, *with_other(h), *mlp_1, vec)
-    (final,) = run(finish_rows, [shape(1, 128, 1024)], x1_1, *share(keep, send), vec)
-    output = corner(final)
-
-    mlp_back_outs = [
-        shape(512, 1024), shape(512, 1024), shape(256, 1024, dtype=F32), shape(256, 1024),
-    ]
-    norm_outs = rows_out + [shape(8, 1024, dtype=F32)]
-    attention_back_outs = [
-        shape(512, 1024), shape(512, 768), shape(256, 1024, dtype=F32), shape(256, 1024),
-    ]
+        attention_outs, *with_other(h), *att_1, vec, *segments, after=(token,), us=9,
+    )
+    mlp_1 = (deep, down_1, deep_far, down_1_far, one_x, one_y, by_x, by_y, both)
+    cot, _ = gate((keep,), cot)
+    cot = corner(cot)
+    part, came = summed_core(keep, *send)
+    x1_1, *h = run(norm_stage(10, 11), [rowf, *quarters], x2_0, part, came, vec, after=(token,), us=1)
+    by_zl = swap(cot, "zl")
+    cots = (cot, swap(cot, "core"), by_zl, swap(by_zl, "core"))
+    h2_1, u_1, a_1, keep, *send = run(mlp_stage(1), mlp_outs, *with_other(h), *mlp_1, vec, us=4)
+
+    mlp_back_outs = [shape(512, 1024), shape(512, 1024), rowf, *quarters]
+    norm_outs = [rowf, *quarters, shape(8, 1024, dtype=F32)]
+    attention_back_outs = [shape(512, 1024), shape(512, 768), rowf, *quarters]
     attention_back_scratch = weights_scratch + [
         pltpu.VMEM((512, 256), BF), pltpu.VMEM((512, 128), F32), pltpu.VMEM((512, 128), F32),
     ]
 
-    def grad_outs(rows):
-        near = [shape(2, rows, 1024), shape(rows, 1024), shape(rows, 1024)]
-        return near + near
+    def grad_outs(sent, rows):
+        return [shape(sent, 1024)] * 2 + [shape(rows, 1024)] * 4
 
     out_scratch = pltpu.VMEM((256, 1024), BF)
 
-    gy2, gu_1, keep, send = run(
-        with_scratch(first_mlp_back, wide), mlp_back_outs, *cots, u_1, *mlp_1
-    )
-    mlp_sums_1 = scatter_slots(*run(mlp_grads, grad_outs(256), h2_1, a_1, gy2, gu_1))
-    gm, gy, e1 = run(
+    keep_last, send_last = keep, send
+    gy2, gu_1, keep, *send = run(mlp_back(1), mlp_back_outs, *cots, u_1, *mlp_1, us=6)
+    part, came = summed_core(keep, *send)
+    to_y, to_x, m1_near_0, m1_near_1, m1_far_0, m1_far_1 = run(
+        window_1, grad_outs(512, 256), h2_1, a_1, gy2, gu_1, after=(part,), us=4
+    )
+    y_1, x_1 = swap(to_y, "y"), swap(to_x, "x")
+    gm, *gy, e1 = run(
         with_scratch(first_norm_back, pltpu.VMEM((256, 1024), F32)),
-        norm_outs, cots[0], cots[2], *share(keep, send), x1_1, vec,
-    )
-    gy1, gqkv_1, keep, send = run(
-        with_scratch(attention_back, *attention_back_scratch),
-        attention_back_outs, *with_other(gy), qkv_1, probs_1, *att_1,
-    )
-    att_sums_1 = scatter_slots(
-        *run(with_scratch(attention_grads, out_scratch), grad_outs(128), h1_1, o_1, gy1, gqkv_1)
-    )
-    gx, gy, g1 = run(norm_back_stage(8), norm_outs, gm, *share(keep, send), x2_0, vec)
-    gy2, gu_0, keep, send = run(
-        with_scratch(next_mlp_back, wide), mlp_back_outs, *with_other(gy), u_0, *mlp_0
-    )
-    mlp_sums_0 = scatter_slots(*run(mlp_grads, grad_outs(256), h2_0, a_0, gy2, gu_0))
-    gm, gy, e0 = run(norm_back_stage(3), norm_outs, gx, *share(keep, send), x1_0, vec)
-    gy1, gqkv_0, keep, send = run(
-        with_scratch(attention_back, *attention_back_scratch),
-        attention_back_outs, *with_other(gy), qkv_0, probs_0, *att_0,
-    )
-    att_sums_0 = scatter_slots(
-        *run(
-            with_scratch(
-                last_attention_grads, out_scratch, *vec_scratch
-            ),
-            grad_outs(144), h1_0, o_0, gy1, gqkv_0, g1, e1, e0, gu_1, gu_0, gqkv_1,
-        )
-    )
-    grad, late = run(
-        with_scratch(last_norm_back, *[pltpu.VMEM((256, 1024), F32)] * 2, pltpu.VMEM((256, 1024), BF)),
-        [shape(1, 128, 1024), shape(8, 1024, dtype=F32)],
-        gm, *share(keep, send), blocks[0], blocks[2], vec,
+        norm_outs, cots[0], cots[2], part, came, x1_1, vec, after=(m1_far_1,), us=1.5,
+    )
+    gy1, gqkv_1, keep, *send = run(
+        with_scratch(attention_back(1), *attention_back_scratch),
+        attention_back_outs, *with_other(gy), qkv_1, probs_1, *att_1, us=9,
+    )
+    part, came = summed_core(keep, *send)
+    to_y, to_x, a1_near_0, a1_near_1, a1_far_0, a1_far_1 = run(
+        with_scratch(window_2, out_scratch), grad_outs(512, 128), h1_1, o_1, gy1, gqkv_1,
+        m1_near_1, y_1, m1_far_1, x_1, after=(part,), us=3,
+    )
+    y_2, x_2 = swap(to_y, "y"), swap(to_x, "x")
+    part_last, came_last = split_core(keep_last, *send_last)
+    (final,) = run(finish_rows, [shape(1, 128, 1024)], x1_1, part_last, came_last, vec)
+    output = corner(final)
+    gx, *gy, g1 = run(
+        norm_back_stage(8), norm_outs, gm, part, came, x2_0, vec, after=(a1_far_1,), us=1.5
+    )
+    gy2, gu_0, keep, *send = run(
+        mlp_back(0), mlp_back_outs, *with_other(gy), u_0, *mlp_0, us=6
+    )
+    part, came = summed_core(keep, *send)
+    to_y, to_x, m0_near_0, m0_near_1, m0_far_0, m0_far_1, to_zh = run(
+        window_3, grad_outs(640, 256) + [row], h2_0, a_0, gy2, gu_0,
+        a1_near_1, y_2, a1_far_1, x_2, m1_far_0, x_1, after=(part,), us=4,
+    )
+    y_3, x_3, m1_far_3 = swap(to_y, "y"), swap(to_x, "x"), swap(to_zh, "zh")
+    gm, *gy, e0 = run(
+        norm_back_stage(3), norm_outs, gx, part, came, x1_0, vec, after=(m0_far_1,), us=1.5
+    )
+    gy1, gqkv_0, keep, *send = run(
+        with_scratch(attention_back(0), *attention_back_scratch),
+        attention_back_outs, *with_other(gy), qkv_0, probs_0, *att_0, us=9,
+    )
+    part, came = split_core(keep, *send, after=(m1_far_3, output))
+    to_x, to_y, to_zh = run(
+        window_4, [row, row, shape(128, 1024)], m0_near_1, y_3, m0_far_1, x_3, a1_far_0, x_2, after=(part,)
+    )
+    x_4, y_4, a1_far_3 = swap(to_x, "x"), swap(to_y, "y"), swap(to_zh, "zh")
+    to_y, to_x, a0_near_0, a0_near_1, a0_far_0, a0_far_1 = run(
+        with_scratch(window_5, out_scratch, *vec_scratch), grad_outs(288, 144),
+        h1_0, o_0, gy1, gqkv_0, g1, e1, e0, gu_1, gu_0, gqkv_1, keep, *send, *blocks,
+        after=(part, to_zh), us=3,
+    )
+    y_5, x_5 = swap(to_y, "y"), swap(to_x, "x")
+    (grad,) = run(
+        with_scratch(
+            last_norm_back, *[pltpu.VMEM((128, 1024), F32)] * 3, pltpu.VMEM((128, 1024), BF),
+            pltpu.VMEM((8, 1024), F32),
+        ),
+        [shape(1, 128, 1024)], gm, part, came, blocks[0], vec, after=(a0_far_1,), us=1.5,
     )
     tokens_grad = corner(grad).astype(F32)
-    for axis in ("core", "zh", "x", "y"):
-        late = late + swap(late, axis)
-
+    (to_zh,) = run(third_only, [row], m0_far_0, x_3, y_4, after=(grad, a1_far_3))
+    m0_far_3 = swap(to_zh, "zh")
+    to_x, to_y = run(second_only, [shape(144, 1024)] * 2, a0_near_1, y_5, a0_far_1, x_5, after=(to_zh,))
+    x_6, y_6 = swap(to_x, "x"), swap(to_y, "y")
     rest = run(
-        unpack_rest,
-        [shape(32, 2816, dtype=F32)] + [shape(32, 2816)] * 3 + [shape(32, 512)] * 2
-        + [shape(2, 128, 1024, dtype=F32)],
-        *mlp_sums_1, *att_sums_1, *mlp_sums_0,
-    )
+        unpack_first,
+        [shape(32, 1792, dtype=F32)] + [shape(32, 1792)] * 3 + [shape(32, 512)] * 2
+        + [shape(128, 1024, dtype=F32)],
+        y_1, y_2, x_2, x_3, m1_near_0, m1_far_3, a1_near_0, a1_far_3, us=2,
+    )
+    rest_came = to_partners(rest[1:4])
+    (to_zh,) = run(window_6, [shape(144, 1024)], a0_far_0, x_5, y_6)
+    a0_far_3 = swap(to_zh, "zh")
     last = run(
         unpack_last,
-        [shape(48, 768, dtype=F32)] + [shape(48, 768)] * 3 + [shape(64, 512)] * 2,
-        *att_sums_0, rest[4], rest[5],
+        [shape(48, 1792, dtype=F32)] + [shape(48, 1792)] * 3 + [shape(64, 512)] * 2
+        + [shape(2, 128, 1024, dtype=F32)],
+        y_3, y_5, x_4, x_6, m0_near_0, m0_far_3, a0_near_0, a0_far_3, rest[4], rest[5], rest[6],
+        after=rest_came,
     )
     back_a = lax.ppermute(last[4], ("y", "zl"), [(0, 0), (1, 2), (2, 1), (3, 3)])
     back_b = lax.ppermute(last[5], ("y", "zl"), [(0, 1), (1, 3), (2, 0), (3, 2)])
@@ -1130,9 +1444,9 @@
     )
     g = run(
         finish, [shape(*s, dtype=F32) for s in sizes],
-        rest[0], *to_partners(rest[1:4]), last[0], *to_partners(last[1:4]), back_a, back_b, late,
-    )
-    return (output, tokens_grad) + tuple(g[:10]) + (rest[6], g[10])
+        rest[0], *rest_came, last[0], *to_partners(last[1:4]), back_a, back_b, us=2,
+    )
+    return (output, tokens_grad) + tuple(g[:10]) + (last[6], g[10])
 
 
 def solution(mesh):

time: 488 us -> 414 us (0.85)
  waiting for transfers between devices: 257 us -> 225 us
  local copies, waits for them, and re-layouts: 30.4 us -> 5.63 us
  starting transfers between devices: 107 us -> 95.3 us
  other arithmetic: 9.3 us -> 0.84 us
    ppermute x89 -> x112, waiting for transfers between devices: 236 us -> 193 us  [swap(): return lax.ppermute(value, axis, [(0, 1), (1, 0)])]
    unnamed x233 -> x19, local copies, waits for them, and re-layouts: 30.4 us -> 5.63 us
    ppermute x89 -> x112, starting transfers between devices: 97 us -> 76.8 us  [swap(): return lax.ppermute(value, axis, [(0, 1), (1, 0)])]
    ppermute x2 -> x6, waiting for transfers between devices: 5.04 us -> 17.3 us  [the longest x4 17.3 us: both_ways(): return lax.ppermute(value, ('y', 'x'), [(0, 3), (3, 0), (1, 2), (2, 1)])]
    convert_element_type x12 -> x0, other arithmetic: 8.44 us -> none  [the longest x4 3.68 us: scatter_slots(): far_3 = swap(far_all.astype(BF), 'zh')]
    ppermute x2 -> x6, starting transfers between devices: 3.47 us -> 10.9 us  [the longest x4 7.4 us: both_ways(): return lax.ppermute(value, ('y', 'x'), [(0, 3), (3, 0), (1, 2), (2, 1)])]
    ppermute x1, waiting for transfers between devices: 0.37 us -> 7.55 us  [narrow_body(): lax.ppermute(last[4], ('y', 'zl'), [(0, 0), (1, 2), (2, 1), (3, 3)])]
    ppermute x1, waiting for transfers between devices: 5.16 us -> 0.01 us  [narrow_body(): lax.ppermute(last[5], ('y', 'zl'), [(0, 1), (1, 3), (2, 0), (3, 2)])]
  transfers between devices with their start and end apart: 101 -> 128, of which waited for: 45 -> 65; matrix products, arithmetic and copies ran while one was open for 2% -> 0% of each run, Pallas kernels for 12% -> 13%
where the time goes in v3:
time: 414 us; the launch traced here: 409 us
  waiting for transfers between devices  225 us (54%)
  starting transfers between devices  95.3 us (23%)
  Pallas kernels  81.1 us (20%)
  local copies, waits for them, and re-layouts  5.63 us (1%)
    ppermute x112, waiting for transfers between devices, swap(): return lax.ppermute(value, axis, [(0, 1), (1, 0)])  193 us
    pallas_call x43, Pallas kernels, run(): pl.pallas_call(body, out_shape=tuple(outs), in_specs=[free] * skip + [sme...  78.7 us
    ppermute x112, starting transfers between devices, swap(): return lax.ppermute(value, axis, [(0, 1), (1, 0)])  76.8 us
    ppermute x4, waiting for transfers between devices, both_ways(): return lax.ppermute(value, ('y', 'x'), [(0, 3), (3, 0), (1, 2), (2, 1)])  17.3 us
  transfers between devices with their start and end apart: 128, of which 65 were waited for; matrix products, arithmetic and copies ran while one was open for 0% of the time, Pallas kernels for 13%

profile of v3, /device:TPU:4, one launch (start us, length us, event | category | flops | bytes accessed | tf_op | source)
XLA Modules:
  0.0 409.1 jit_solution(5026271089827116395)
XLA Ops:
  0.6 2.3 shard_map.263
  3.1 1.6 collective-permute-start.1
  4.9 3.4 collective-permute-start.3
  14.8 1.9 collective-permute-start.10
  16.7 1.5 collective-permute-start.9
  18.2 2.6 collective-permute-start.8
  21.8 12.7 %collective-permute-done.6.refs_2_ = bf16[32,2816]{1,0:T(8,128)(2,1)S(1)} collective-permute-done((bf16[32,2816]{1,0:T(8,128)(2,1)S(1)}, bf16[32,2816]{1,0:T(8,128)(2,1)S(1)}, u32[]{:S(2)}, u32[]{:S(2)}) %collective-permute-start.6) | collective-permute-done | bytes 180256 | tf_op jit(solution)/shard_map/ppermute | solution.py:20
  36.6 3.0 collective-permute-start.13
  40.8 17.1 %collective-permute-done.14.refs_3_.refs_1_.refs_10_ = bf16[128,1024]{1,0:T(8,128)(2,1)S(1)} collective-permute-done((bf16[128,1024]{1,0:T(8,128)(2,1)S(1)}, bf16[128,1024]{1,0:T(8,128)(2,1)S(1)}, u32[]{:S(2)}, u32[]{:S(2)}) %collective-permute-start.14) | collective-permute-done | bytes 262176 | tf_op jit(solution)/shard_map/ppermute | solution.py:20
  58.8 1.7 collective-permute-start.16
  60.5 6.8 %collective-permute-done.17.refs_3_.refs_2_.refs_19_ = bf16[1,128,1024]{2,1,0:T(8,128)(2,1)S(1)} collective-permute-done((bf16[1,128,1024]{2,1,0:T(8,128)(2,1)S(1)}, bf16[1,128,1024]{2,1,0:T(8,128)(2,1)S(1)}, u32[]{:S(2)}, u32[]{:S(2)}) %collective-permute-start.17) | collective-permute-done | bytes 262176 | tf_op jit(solution)/shard_map/ppermute | solution.py:20
  69.3 10.4 %shard_map.271 = (f32[16,1024]{1,0:T(8,128)S(1)}, bf16[512,1024]{1,0:T(8,128)(2,1)S(1)}, bf16[512,768]{1,0:T(8,128)(2,1)S(1)}, bf16[4,512,512]{2,1,0:T(8,128)(2,...) custom-call(f32[8,128]{1,0:T(8,128)S(1)} %get-tuple-element.235.refs, ...), custom_call_target="tpu_custom_call" | custom-call | flops 100000000 | tf_op jit(solution)/shard_map/pallas_call | solution.py:528
  79.7 4.1 collective-permute-done.20.refs_1_
  89.8 1.5 collective-permute-start.36
  91.4 17.1 %collective-permute-done.29.refs_4_ = bf16[256,1024]{1,0:T(8,128)(2,1)S(1)} collective-permute-done((bf16[256,1024]{1,0:T(8,128)(2,1)S(1)}, bf16[256,1024]{1,0:T(8,128)(2,1)S(1)}, u32[]{:S(2)}, u32[]{:S(2)}) %collective-permute-start.29) | collective-permute-done | bytes 524320 | tf_op jit(solution)/shard_map/ppermute | solution.py:20
  109.4 5.3 %collective-permute-done.23.refs_0_.refs_1_.refs_10_.refs_7_.refs_11_ = bf16[256,1024]{1,0:T(8,128)(2,1)S(1)} collective-permute-done((bf16[256,1024]{1,0:T(8,128)(2,1)S(1)}, bf16[256,1024]{1,0:T(8,128)(2,1)S(1)}, u32[]{:S(2)}, u32[]{:S(2)}) %collective-permute-start.23) | collective-permute-done | bytes 524320 | tf_op jit(solution)/shard_map/ppermute | solution.py:20
  114.7 4.4 %collective-permute-done.36.refs_16_ = bf16[256,1024]{1,0:T(8,128)(2,1)S(1)} collective-permute-done((bf16[256,1024]{1,0:T(8,128)(2,1)S(1)}, bf16[256,1024]{1,0:T(8,128)(2,1)S(1)}, u32[]{:S(2)}, u32[]{:S(2)}) %collective-permute-start.36) | collective-permute-done | bytes 524320 | tf_op jit(solution)/shard_map/ppermute | solution.py:692
  120.6 3.2 shard_map.276
  128.8 1.8 collective-permute-start.43
  130.6 1.5 collective-permute-start.48
  132.1 15.7 %collective-permute-done.24.refs_1_.refs_11_.refs_8_ = bf16[128,1024]{1,0:T(8,128)(2,1)S(1)} collective-permute-done((bf16[128,1024]{1,0:T(8,128)(2,1)S(1)}, bf16[128,1024]{1,0:T(8,128)(2,1)S(1)}, u32[]{:S(2)}, u32[]{:S(2)}) %collective-permute-start.24) | collective-permute-done | bytes 262176 | tf_op jit(solution)/shard_map/ppermute | solution.py:20
  150.2 3.2 collective-permute-done.48.refs_15_.refs_16_
  153.4 9.4 %shard_map.281 = (bf16[512,1024]{1,0:T(8,128)(2,1)S(1)}, bf16[512,768]{1,0:T(8,128)(2,1)S(1)}, bf16[4,512,512]{2,1,0:T(8,128)(2,1)S(1)}, bf16[512,256]{1,0:T(8,1...) custom-call(bf16[384,1024]{1,0:T(8,128)(2,1)S(1)} %get-tuple-element, ...), custom_call_target="tpu_custom_call" | custom-call | flops 90000000 | tf_op jit(solution)/shard_map/pallas_call | solution.py:528
  166.0 1.8 collective-permute-start.53
  167.8 1.4 collective-permute-start.60
  171.3 11.0 %collective-permute-done.53.refs_3_ = bf16[256,1024]{1,0:T(8,128)(2,1)S(1)} collective-permute-done((bf16[256,1024]{1,0:T(8,128)(2,1)S(1)}, bf16[256,1024]{1,0:T(8,128)(2,1)S(1)}, u32[]{:S(2)}, u32[]{:S(2)}) %collective-permute-start.53) | collective-permute-done | bytes 524320 | tf_op jit(solution)/shard_map/ppermute | solution.py:20
  182.8 3.2 collective-permute-start.54
  186.0 9.8 %collective-permute-done.60.refs_16_.refs_13_ = bf16[256,1024]{1,0:T(8,128)(2,1)S(1)} collective-permute-done((bf16[256,1024]{1,0:T(8,128)(2,1)S(1)}, bf16[256,1024]{1,0:T(8,128)(2,1)S(1)}, u32[]{:S(2)}, u32[]{:S(2)}) %collective-permute-start.60) | collective-permute-done | bytes 524320 | tf_op jit(solution)/shard_map/ppermute | solution.py:692
  198.3 3.1 shard_map.284
  201.5 4.8 %shard_map.288 = (bf16[512,1024]{1,0:T(8,128)(2,1)S(1)}, bf16[512,1024]{1,0:T(8,128)(2,1)S(1)}, f32[256,1024]{1,0:T(8,128)S(1)}, bf16[64,1024]{1,0:T(8,128)(2,1)...) custom-call(bf16[128,1024]{1,0:T(8,128)(2,1)S(1)} %collective-permute-done.67.refs_0_, ...), custom_call_target="tpu_custom_call" | custom-call | flops 60000000 | tf_op jit(solution)/shard_map/pallas_call | solution.py:528
  208.5 1.8 collective-permute-start.75
  210.3 2.5 shard_map.290
  215.0 7.7 %collective-permute-done.75.refs_4_ = bf16[256,1024]{1,0:T(8,128)(2,1)S(1)} collective-permute-done((bf16[256,1024]{1,0:T(8,128)(2,1)S(1)}, bf16[256,1024]{1,0:T(8,128)(2,1)S(1)}, u32[]{:S(2)}, u32[]{:S(2)}) %collective-permute-start.75) | collective-permute-done | bytes 524320 | tf_op jit(solution)/shard_map/ppermute | solution.py:20
  226.7 8.8 %shard_map.292 = (bf16[512,1024]{1,0:T(8,128)(2,1)S(1)}, bf16[512,768]{1,0:T(8,128)(2,1)S(1)}, f32[256,1024]{1,0:T(8,128)S(1)}, bf16[64,1024]{1,0:T(8,128)(2,1)S...) custom-call(bf16[64,1024]{1,0:T(8,128)(2,1)S(1)} %get-tuple-element.310.refs_0_, ...), custom_call_target="tpu_custom_call" | custom-call | flops 90000000 | tf_op jit(solution)/shard_map/pallas_call | solution.py:528
  238.4 1.8 collective-permute-start.86
  240.2 1.9 shard_map.294
  242.1 1.4 collective-permute-start.95
  244.3 8.1 %collective-permute-done.86.refs_3_ = bf16[256,1024]{1,0:T(8,128)(2,1)S(1)} collective-permute-done((bf16[256,1024]{1,0:T(8,128)(2,1)S(1)}, bf16[256,1024]{1,0:T(8,128)(2,1)S(1)}, u32[]{:S(2)}, u32[]{:S(2)}) %collective-permute-start.86) | collective-permute-done | bytes 524320 | tf_op jit(solution)/shard_map/ppermute | solution.py:20
  256.3 4.8 %shard_map.296 = (bf16[512,1024]{1,0:T(8,128)(2,1)S(1)}, bf16[512,1024]{1,0:T(8,128)(2,1)S(1)}, f32[256,1024]{1,0:T(8,128)S(1)}, bf16[64,1024]{1,0:T(8,128)(2,1)...) custom-call(bf16[64,1024]{1,0:T(8,128)(2,1)S(1)} %get-tuple-element.330.refs_0_, ...), custom_call_target="tpu_custom_call" | custom-call | flops 60000000 | tf_op jit(solution)/shard_map/pallas_call | solution.py:528
  263.9 3.1 collective-permute-done.95.refs_6_.refs_1_
  268.1 3.0 shard_map.298
  271.9 1.5 collective-permute-start.108
  277.0 1.8 collective-permute-start.65
  278.8 9.4 %collective-permute-done.98.refs_3_ = bf16[256,1024]{1,0:T(8,128)(2,1)S(1)} collective-permute-done((bf16[256,1024]{1,0:T(8,128)(2,1)S(1)}, bf16[256,1024]{1,0:T(8,128)(2,1)S(1)}, u32[]{:S(2)}, u32[]{:S(2)}) %collective-permute-start.98) | collective-permute-done | bytes 524320 | tf_op jit(solution)/shard_map/ppermute | solution.py:20
  291.9 4.3 %collective-permute-start.97 = (bf16[256,1024]{1,0:T(8,128)(2,1)S(1)}, bf16[256,1024]{1,0:T(8,128)(2,1)S(1)}, u32[]{:S(2)}, u32[]{:S(2)}) collective-permute-start(bf16[256,1024]{1,0:T(8,128)(2,1)S(1)} %get-tuple-element.348), channel_id=1, source_target_pairs={{0,2},{2,0},{1,3},{3,1},{4,6},{6,4},{5,7},{7,5},{8,10},{10,8},{9,1... | collective-permute-start | bytes 1572872 | tf_op jit(solution)/shard_map/ppermute | solution.py:20
  297.5 8.8 %shard_map.300 = (bf16[512,1024]{1,0:T(8,128)(2,1)S(1)}, bf16[512,768]{1,0:T(8,128)(2,1)S(1)}, f32[256,1024]{1,0:T(8,128)S(1)}, bf16[64,1024]{1,0:T(8,128)(2,1)S...) custom-call(bf16[64,1024]{1,0:T(8,128)(2,1)S(1)} %get-tuple-element.351.refs_0_, ...), custom_call_target="tpu_custom_call" | custom-call | flops 90000000 | tf_op jit(solution)/shard_map/pallas_call | solution.py:528
  306.6 10.2 %collective-permute-start.104 = (bf16[64,1024]{1,0:T(8,128)(2,1)S(1)}, bf16[64,1024]{1,0:T(8,128)(2,1)S(1)}, u32[]{:S(2)}, u32[]{:S(2)}) collective-permute-start(bf16[64,1024]{1,0:T(8,128)(2,1)S(1)} %get-tuple-element.359.refs_14_), channel_id=1, source_target_pairs={{0,4},{4,0},{1,5},{5,1},{2,6},{6,2},{3,7},{7,3},{8,12},{12,8},{9,1... | collective-permute-start | bytes 393224 | tf_op jit(solution)/shard_map/ppermute | solution.py:20
  319.1 6.1 %collective-permute-done.97.refs_0_.refs_5_ = bf16[256,1024]{1,0:T(8,128)(2,1)S(1)} collective-permute-done((bf16[256,1024]{1,0:T(8,128)(2,1)S(1)}, bf16[256,1024]{1,0:T(8,128)(2,1)S(1)}, u32[]{:S(2)}, u32[]{:S(2)}) %collective-permute-start.97) | collective-permute-done | bytes 524320 | tf_op jit(solution)/shard_map/ppermute | solution.py:20
  325.8 2.8 shard_map.303
  331.2 9.3 %collective-permute-done.109.refs_3_ = bf16[128,1024]{1,0:T(8,128)(2,1)S(1)} collective-permute-done((bf16[128,1024]{1,0:T(8,128)(2,1)S(1)}, bf16[128,1024]{1,0:T(8,128)(2,1)S(1)}, u32[]{:S(2)}, u32[]{:S(2)}) %collective-permute-start.109) | collective-permute-done | bytes 262176 | tf_op jit(solution)/shard_map/ppermute | solution.py:20
  341.2 2.2 collective-permute-done.111.refs_7_.refs_1_
  343.4 9.5 %collective-permute-done.117.refs_4_ = bf16[256,1024]{1,0:T(8,128)(2,1)S(1)} collective-permute-done((bf16[256,1024]{1,0:T(8,128)(2,1)S(1)}, bf16[256,1024]{1,0:T(8,128)(2,1)S(1)}, u32[]{:S(2)}, u32[]{:S(2)}) %collective-permute-start.117) | collective-permute-done | bytes 524320 | tf_op jit(solution)/shard_map/ppermute | solution.py:20
  355.8 1.7 collective-permute-start.113
  357.5 2.6 collective-permute-done.121.refs_2_
  360.8 6.9 %collective-permute-done.113.refs_1_.refs_2_ = bf16[32,1792]{1,0:T(8,128)(2,1)S(1)} collective-permute-done((bf16[32,1792]{1,0:T(8,128)(2,1)S(1)}, bf16[32,1792]{1,0:T(8,128)(2,1)S(1)}, u32[]{:S(2)}, u32[]{:S(2)}) %collective-permute-start.113) | collective-permute-done | bytes 114720 | tf_op jit(solution)/shard_map/ppermute | solution.py:20
  367.7 5.7 %collective-permute-done.114.refs_2_.refs_3_ = bf16[32,1792]{1,0:T(8,128)(2,1)S(1)} collective-permute-done((bf16[32,1792]{1,0:T(8,128)(2,1)S(1)}, bf16[32,1792]{1,0:T(8,128)(2,1)S(1)}, u32[]{:S(2)}, u32[]{:S(2)}) %collective-permute-start.114) | collective-permute-done | bytes 114720 | tf_op jit(solution)/shard_map/ppermute | solution.py:1221
  374.1 11.8 %collective-permute-done.120.refs_8_ = bf16[256,1024]{1,0:T(8,128)(2,1)S(1)} collective-permute-done((bf16[256,1024]{1,0:T(8,128)(2,1)S(1)}, bf16[256,1024]{1,0:T(8,128)(2,1)S(1)}, u32[]{:S(2)}, u32[]{:S(2)}) %collective-permute-start.120) | collective-permute-done | bytes 524320 | tf_op jit(solution)/shard_map/ppermute | solution.py:20
  385.9 3.2 collective-permute-done.122.refs_10_
  389.0 1.4 shard_map.309
  390.5 2.7 collective-permute-start.123
  393.1 1.4 collective-permute-start.124
  394.6 3.3 collective-permute-start.126
  398.8 7.5 %collective-permute-done.126.refs_8_ = bf16[64,512]{1,0:T(8,128)(2,1)S(1)} collective-permute-done((bf16[64,512]{1,0:T(8,128)(2,1)S(1)}, bf16[64,512]{1,0:T(8,128)(2,1)S(1)}, u32[]{:S(2)}, u32[]{:S(2)}) %collective-permute-start.126) | collective-permute-done | bytes 65568 | tf_op jit(solution)/shard_map/ppermute | solution.py:1439
  406.4 1.7 shard_map.310
  (260 shorter events, 79.4 us)
Async XLA Ops:
  3.0 11.0 %collective-permute-start = (bf16[48,768]{1,0:T(8,128)(2,1)}, bf16[48,768]{1,0:T(8,128)(2,1)S(1)}, u32[]{:S(2)}, u32[]{:S(2)}) collective-permute-start(bf16[48,768]{1,0:T(8,128)(2,1)} %get-tuple-element.217), channel_id=1, source_target_pairs={{0,4},{4,0},{1,5},{5,1},{2,6},{6,2},{3,7},{7,3},{8,12},{12,8},{9,1... | collective-permute-start | bytes 221192 | tf_op jit(solution)/shard_map/ppermute | solution.py:20
  3.1 11.0 %collective-permute-start.1 = (bf16[48,768]{1,0:T(8,128)(2,1)}, bf16[48,768]{1,0:T(8,128)(2,1)S(1)}, u32[]{:S(2)}, u32[]{:S(2)}) collective-permute-start(bf16[48,768]{1,0:T(8,128)(2,1)} %get-tuple-element.218), channel_id=1, source_target_pairs={{0,1},{1,0},{2,3},{3,2},{4,5},{5,4},{6,7},{7,6},{8,9},{9,8},{10,11... | collective-permute-start | bytes 221192 | tf_op jit(solution)/shard_map/ppermute | solution.py:20
  4.7 9.3 %collective-permute-start.2 = (bf16[48,768]{1,0:T(8,128)(2,1)}, bf16[48,768]{1,0:T(8,128)(2,1)S(1)}, u32[]{:S(2)}, u32[]{:S(2)}) collective-permute-start(bf16[48,768]{1,0:T(8,128)(2,1)} %get-tuple-element.219), channel_id=1, source_target_pairs={{0,5},{5,0},{1,4},{4,1},{2,7},{7,2},{3,6},{6,3},{8,13},{13,8},{9,1... | collective-permute-start | bytes 221192 | tf_op jit(solution)/shard_map/ppermute | solution.py:1221
  4.9 9.1 %collective-permute-start.3 = (bf16[64,512]{1,0:T(8,128)(2,1)}, bf16[64,512]{1,0:T(8,128)(2,1)S(1)}, u32[]{:S(2)}, u32[]{:S(2)}) collective-permute-start(bf16[64,512]{1,0:T(8,128)(2,1)} %get-tuple-element.220), channel_id=1, source_target_pairs={{0,0},{1,16},{16,1},{17,17},{2,2},{3,18},{18,3},{19,19},{4,4},{5,2... | collective-permute-start | bytes 196616 | tf_op jit(solution)/shard_map/ppermute | solution.py:1245
  14.8 21.0 %collective-permute-start.10 = (bf16[144,1024]{1,0:T(8,128)(2,1)S(1)}, bf16[144,1024]{1,0:T(8,128)(2,1)S(1)}, u32[]{:S(2)}, u32[]{:S(2)}) collective-permute-start(bf16[144,1024]{1,0:T(8,128)(2,1)S(1)} %shard_map.265.refs_0_.refs_5_.refs_10_), channel_id=1, source_target_pairs={{0,16},{16,0},{1,17},{17,1},{2,18},{18,2},{3,19},{19,3},{4,20},{20... | collective-permute-start | bytes 884744 | tf_op jit(solution)/shard_map/ppermute | solution.py:20
  16.7 19.1 %collective-permute-start.9 = (bf16[144,1024]{1,0:T(8,128)(2,1)S(1)}, bf16[144,1024]{1,0:T(8,128)(2,1)S(1)}, u32[]{:S(2)}, u32[]{:S(2)}) collective-permute-start(bf16[144,1024]{1,0:T(8,128)(2,1)S(1)} %shard_map.265.refs_0_.refs_5_.refs_10_), channel_id=1, source_target_pairs={{0,8},{8,0},{1,9},{9,1},{2,10},{10,2},{3,11},{11,3},{4,12},{12,4},... | collective-permute-start | bytes 884744 | tf_op jit(solution)/shard_map/ppermute | solution.py:20
  18.2 17.6 %collective-permute-start.8 = (bf16[144,1024]{1,0:T(8,128)(2,1)S(1)}, bf16[144,1024]{1,0:T(8,128)(2,1)S(1)}, u32[]{:S(2)}, u32[]{:S(2)}) collective-permute-start(bf16[144,1024]{1,0:T(8,128)(2,1)S(1)} %shard_map.265.refs_0_.refs_5_.refs_10_), channel_id=1, source_target_pairs={{0,2},{2,0},{1,3},{3,1},{4,6},{6,4},{5,7},{7,5},{8,10},{10,8},{9,1... | collective-permute-start | bytes 884744 | tf_op jit(solution)/shard_map/ppermute | solution.py:20
  20.8 13.7 %collective-permute-start.6 = (bf16[32,2816]{1,0:T(8,128)(2,1)S(1)}, bf16[32,2816]{1,0:T(8,128)(2,1)S(1)}, u32[]{:S(2)}, u32[]{:S(2)}) collective-permute-start(bf16[32,2816]{1,0:T(8,128)(2,1)S(1)} %get-tuple-element.226), channel_id=1, source_target_pairs={{0,1},{1,0},{2,3},{3,2},{4,5},{5,4},{6,7},{7,6},{8,9},{9,8},{10,11... | collective-permute-start | bytes 540680 | tf_op jit(solution)/shard_map/ppermute | solution.py:20
  20.8 14.8 %collective-permute-start.7 = (bf16[32,2816]{1,0:T(8,128)(2,1)S(1)}, bf16[32,2816]{1,0:T(8,128)(2,1)S(1)}, u32[]{:S(2)}, u32[]{:S(2)}) collective-permute-start(bf16[32,2816]{1,0:T(8,128)(2,1)S(1)} %get-tuple-element.227), channel_id=1, source_target_pairs={{0,5},{5,0},{1,4},{4,1},{2,7},{7,2},{3,6},{6,3},{8,13},{13,8},{9,1... | collective-permute-start | bytes 540680 | tf_op jit(solution)/shard_map/ppermute | solution.py:1221
  36.0 21.9 %collective-permute-start.11 = (bf16[224,1024]{1,0:T(8,128)(2,1)S(1)}, bf16[224,1024]{1,0:T(8,128)(2,1)S(1)}, u32[]{:S(2)}, u32[]{:S(2)}) collective-permute-start(bf16[224,1024]{1,0:T(8,128)(2,1)S(1)} %get-tuple-element.230.refs_0_), channel_id=1, source_target_pairs={{0,8},{8,0},{1,9},{9,1},{2,10},{10,2},{3,11},{11,3},{4,12},{12,4},... | collective-permute-start | bytes 1376264 | tf_op jit(solution)/shard_map/ppermute | solution.py:20
  36.6 21.3 %collective-permute-start.12 = (bf16[208,1024]{1,0:T(8,128)(2,1)S(1)}, bf16[208,1024]{1,0:T(8,128)(2,1)S(1)}, u32[]{:S(2)}, u32[]{:S(2)}) collective-permute-start(bf16[208,1024]{1,0:T(8,128)(2,1)S(1)} %get-tuple-element.231), channel_id=1, source_target_pairs={{0,16},{16,0},{1,17},{17,1},{2,18},{18,2},{3,19},{19,3},{4,20},{20... | collective-permute-start | bytes 1277960 | tf_op jit(solution)/shard_map/ppermute | solution.py:20
  36.6 21.3 %collective-permute-start.13 = (bf16[144,1024]{1,0:T(8,128)(2,1)S(1)}, bf16[144,1024]{1,0:T(8,128)(2,1)S(1)}, u32[]{:S(2)}, u32[]{:S(2)}) collective-permute-start(bf16[144,1024]{1,0:T(8,128)(2,1)S(1)} %collective-permute-done.8.refs_1_.refs_6_.refs_11_), channel_id=1, source_target_pairs={{0,24},{24,0},{8,16},{16,8},{1,25},{25,1},{9,17},{17,9},{2,26},{26... | collective-permute-start | bytes 884744 | tf_op jit(solution)/shard_map/ppermute | solution.py:692
  40.1 17.7 %collective-permute-start.14 = (bf16[128,1024]{1,0:T(8,128)(2,1)S(1)}, bf16[128,1024]{1,0:T(8,128)(2,1)S(1)}, u32[]{:S(2)}, u32[]{:S(2)}) collective-permute-start(bf16[128,1024]{1,0:T(8,128)(2,1)S(1)} %get-tuple-element.233), channel_id=1, source_target_pairs={{0,2},{2,0},{1,3},{3,1},{4,6},{6,4},{5,7},{7,5},{8,10},{10,8},{9,1... | collective-permute-start | bytes 786440 | tf_op jit(solution)/shard_map/ppermute | solution.py:20
  40.1 18.7 %collective-permute-start.15 = (bf16[1,128,1024]{2,1,0:T(8,128)(2,1)S(1)}, bf16[1,128,1024]{2,1,0:T(8,128)(2,1)S(1)}, u32[]{:S(2)}, u32[]{:S(2)}) collective-permute-start(bf16[1,128,1024]{2,1,0:T(8,128)(2,1)S(1)} %copy-done.8), channel_id=1, source_target_pairs={{0,0},{2,4},{4,2},{6,6},{1,1},{3,5},{5,3},{7,7},{8,8},{10,12},{12,... | collective-permute-start | bytes 786440 | tf_op jit(solution)/shard_map/ppermute | solution.py:1213
  57.9 25.9 %collective-permute-start.22 = (bf16[384,1024]{1,0:T(8,128)(2,1)S(1)}, bf16[384,1024]{1,0:T(8,128)(2,1)S(1)}, u32[]{:S(2)}, u32[]{:S(2)}) collective-permute-start(bf16[384,1024]{1,0:T(8,128)(2,1)S(1)} %get-tuple-element.238), channel_id=1, source_target_pairs={{0,16},{16,0},{1,17},{17,1},{2,18},{18,2},{3,19},{19,3},{4,20},{20... | collective-permute-start | bytes 2359304 | tf_op jit(solution)/shard_map/ppermute | solution.py:20
  58.2 25.6 %collective-permute-start.21 = (bf16[384,1024]{1,0:T(8,128)(2,1)S(1)}, bf16[384,1024]{1,0:T(8,128)(2,1)S(1)}, u32[]{:S(2)}, u32[]{:S(2)}) collective-permute-start(bf16[384,1024]{1,0:T(8,128)(2,1)S(1)} %get-tuple-element.238), channel_id=1, source_target_pairs={{0,8},{8,0},{1,9},{9,1},{2,10},{10,2},{3,11},{11,3},{4,12},{12,4},... | collective-permute-start | bytes 2359304 | tf_op jit(solution)/shard_map/ppermute | solution.py:20
  58.8 10.5 %collective-permute-start.16 = (bf16[1,128,1024]{2,1,0:T(8,128)(2,1)S(1)}, bf16[1,128,1024]{2,1,0:T(8,128)(2,1)S(1)}, u32[]{:S(2)}, u32[]{:S(2)}) collective-permute-start(bf16[1,128,1024]{2,1,0:T(8,128)(2,1)S(1)} %collective-permute-done.15.refs_1_.refs_17_.refs_4_), channel_id=1, source_target_pairs={{0,4},{4,0},{1,5},{5,1},{2,6},{6,2},{3,7},{7,3},{8,12},{12,8},{9,1... | collective-permute-start | bytes 786440 | tf_op jit(solution)/shard_map/ppermute | solution.py:20
  69.2 14.5 %collective-permute-start.20 = (bf16[128,1024]{1,0:T(8,128)(2,1)S(1)}, bf16[128,1024]{1,0:T(8,128)(2,1)S(1)}, u32[]{:S(2)}, u32[]{:S(2)}) collective-permute-start(bf16[128,1024]{1,0:T(8,128)(2,1)S(1)} %get-tuple-element.237), channel_id=1, source_target_pairs={{0,2},{2,0},{1,3},{3,1},{4,6},{6,4},{5,7},{7,5},{8,10},{10,8},{9,1... | collective-permute-start | bytes 786440 | tf_op jit(solution)/shard_map/ppermute | solution.py:20
  86.6 21.9 %collective-permute-start.29 = (bf16[256,1024]{1,0:T(8,128)(2,1)S(1)}, bf16[256,1024]{1,0:T(8,128)(2,1)S(1)}, u32[]{:S(2)}, u32[]{:S(2)}) collective-permute-start(bf16[256,1024]{1,0:T(8,128)(2,1)S(1)} %shard_map.273.refs_0_.refs_3_), channel_id=1, source_target_pairs={{0,1},{1,0},{2,3},{3,2},{4,5},{5,4},{6,7},{7,6},{8,9},{9,8},{10,11... | collective-permute-start | bytes 1572872 | tf_op jit(solution)/shard_map/ppermute | solution.py:20
  86.8 33.8 %collective-permute-start.35 = (bf16[384,1024]{1,0:T(8,128)(2,1)S(1)}, bf16[384,1024]{1,0:T(8,128)(2,1)S(1)}, u32[]{:S(2)}, u32[]{:S(2)}) collective-permute-start(bf16[384,1024]{1,0:T(8,128)(2,1)S(1)} %get-tuple-element.261), channel_id=1, source_target_pairs={{0,16},{16,0},{1,17},{17,1},{2,18},{18,2},{3,19},{19,3},{4,20},{20... | collective-permute-start | bytes 2359304 | tf_op jit(solution)/shard_map/ppermute | solution.py:20
  88.1 32.4 %collective-permute-start.34 = (bf16[384,1024]{1,0:T(8,128)(2,1)S(1)}, bf16[384,1024]{1,0:T(8,128)(2,1)S(1)}, u32[]{:S(2)}, u32[]{:S(2)}) collective-permute-start(bf16[384,1024]{1,0:T(8,128)(2,1)S(1)} %get-tuple-element.254.refs_0_), channel_id=1, source_target_pairs={{0,8},{8,0},{1,9},{9,1},{2,10},{10,2},{3,11},{11,3},{4,12},{12,4},... | collective-permute-start | bytes 2359304 | tf_op jit(solution)/shard_map/ppermute | solution.py:20
  88.9 25.8 %collective-permute-start.23 = (bf16[256,1024]{1,0:T(8,128)(2,1)S(1)}, bf16[256,1024]{1,0:T(8,128)(2,1)S(1)}, u32[]{:S(2)}, u32[]{:S(2)}) collective-permute-start(bf16[256,1024]{1,0:T(8,128)(2,1)S(1)} %get-tuple-element.245.refs_4_.refs_9_.refs_8_.refs_5_.refs_10_), channel_id=1, source_target_pairs={{0,2},{2,0},{1,3},{3,1},{4,6},{6,4},{5,7},{7,5},{8,10},{10,8},{9,1... | collective-permute-start | bytes 1572872 | tf_op jit(solution)/shard_map/ppermute | solution.py:20
  89.8 29.2 %collective-permute-start.36 = (bf16[256,1024]{1,0:T(8,128)(2,1)S(1)}, bf16[256,1024]{1,0:T(8,128)(2,1)S(1)}, u32[]{:S(2)}, u32[]{:S(2)}) collective-permute-start(bf16[256,1024]{1,0:T(8,128)(2,1)S(1)} %get-tuple-element.262), channel_id=1, source_target_pairs={{0,24},{24,0},{8,16},{16,8},{1,25},{25,1},{9,17},{17,9},{2,26},{26... | collective-permute-start | bytes 1572872 | tf_op jit(solution)/shard_map/ppermute | solution.py:692
  109.3 9.8 %collective-permute-start.30 = (bf16[64,1024]{1,0:T(8,128)(2,1)S(1)}, bf16[64,1024]{1,0:T(8,128)(2,1)S(1)}, u32[]{:S(2)}, u32[]{:S(2)}) collective-permute-start(bf16[64,1024]{1,0:T(8,128)(2,1)S(1)} %get-tuple-element.256.refs_1_), channel_id=1, source_target_pairs={{0,4},{4,0},{1,5},{5,1},{2,6},{6,2},{3,7},{7,3},{8,12},{12,8},{9,1... | collective-permute-start | bytes 393224 | tf_op jit(solution)/shard_map/ppermute | solution.py:20
  123.9 25.6 %collective-permute-start.38 = (bf16[448,1024]{1,0:T(8,128)(2,1)S(1)}, bf16[448,1024]{1,0:T(8,128)(2,1)S(1)}, u32[]{:S(2)}, u32[]{:S(2)}) collective-permute-start(bf16[448,1024]{1,0:T(8,128)(2,1)S(1)} %get-tuple-element.265), channel_id=1, source_target_pairs={{0,16},{16,0},{1,17},{17,1},{2,18},{18,2},{3,19},{19,3},{4,20},{20... | collective-permute-start | bytes 2752520 | tf_op jit(solution)/shard_map/ppermute | solution.py:20
  125.3 24.4 %collective-permute-start.37 = (bf16[448,1024]{1,0:T(8,128)(2,1)S(1)}, bf16[448,1024]{1,0:T(8,128)(2,1)S(1)}, u32[]{:S(2)}, u32[]{:S(2)}) collective-permute-start(bf16[448,1024]{1,0:T(8,128)(2,1)S(1)} %get-tuple-element.264.refs_0_), channel_id=1, source_target_pairs={{0,8},{8,0},{1,9},{9,1},{2,10},{10,2},{3,11},{11,3},{4,12},{12,4},... | collective-permute-start | bytes 2752520 | tf_op jit(solution)/shard_map/ppermute | solution.py:20
  128.8 19.7 %collective-permute-start.43 = (bf16[256,1024]{1,0:T(8,128)(2,1)S(1)}, bf16[256,1024]{1,0:T(8,128)(2,1)S(1)}, u32[]{:S(2)}, u32[]{:S(2)}) collective-permute-start(bf16[256,1024]{1,0:T(8,128)(2,1)S(1)} %shard_map.279.refs_3_), channel_id=1, source_target_pairs={{0,1},{1,0},{2,3},{3,2},{4,5},{5,4},{6,7},{7,6},{8,9},{9,8},{10,11... | collective-permute-start | bytes 1572872 | tf_op jit(solution)/shard_map/ppermute | solution.py:20
  130.6 17.1 %collective-permute-start.24 = (bf16[128,1024]{1,0:T(8,128)(2,1)S(1)}, bf16[128,1024]{1,0:T(8,128)(2,1)S(1)}, u32[]{:S(2)}, u32[]{:S(2)}) collective-permute-start(bf16[128,1024]{1,0:T(8,128)(2,1)S(1)} %get-tuple-element.246.refs_5_.refs_9_.refs_6_), channel_id=1, source_target_pairs={{0,2},{2,0},{1,3},{3,1},{4,6},{6,4},{5,7},{7,5},{8,10},{10,8},{9,1... | collective-permute-start | bytes 786440 | tf_op jit(solution)/shard_map/ppermute | solution.py:20
  130.6 22.8 %collective-permute-start.48 = (bf16[128,1024]{1,0:T(8,128)(2,1)S(1)}, bf16[128,1024]{1,0:T(8,128)(2,1)S(1)}, u32[]{:S(2)}, u32[]{:S(2)}) collective-permute-start(bf16[128,1024]{1,0:T(8,128)(2,1)S(1)} %get-tuple-element.277), channel_id=1, source_target_pairs={{0,24},{24,0},{8,16},{16,8},{1,25},{25,1},{9,17},{17,9},{2,26},{26... | collective-permute-start | bytes 786440 | tf_op jit(solution)/shard_map/ppermute | solution.py:692
  163.9 32.5 %collective-permute-start.59 = (bf16[384,1024]{1,0:T(8,128)(2,1)S(1)}, bf16[384,1024]{1,0:T(8,128)(2,1)S(1)}, u32[]{:S(2)}, u32[]{:S(2)}) collective-permute-start(bf16[384,1024]{1,0:T(8,128)(2,1)S(1)} %get-tuple-element.288), channel_id=1, source_target_pairs={{0,16},{16,0},{1,17},{17,1},{2,18},{18,2},{3,19},{19,3},{4,20},{20... | collective-permute-start | bytes 2359304 | tf_op jit(solution)/shard_map/ppermute | solution.py:20
  165.2 31.2 %collective-permute-start.58 = (bf16[384,1024]{1,0:T(8,128)(2,1)S(1)}, bf16[384,1024]{1,0:T(8,128)(2,1)S(1)}, u32[]{:S(2)}, u32[]{:S(2)}) collective-permute-start(bf16[384,1024]{1,0:T(8,128)(2,1)S(1)} %get-tuple-element.266.refs_0_), channel_id=1, source_target_pairs={{0,8},{8,0},{1,9},{9,1},{2,10},{10,2},{3,11},{11,3},{4,12},{12,4},... | collective-permute-start | bytes 2359304 | tf_op jit(solution)/shard_map/ppermute | solution.py:20
  166.0 16.3 %collective-permute-start.53 = (bf16[256,1024]{1,0:T(8,128)(2,1)S(1)}, bf16[256,1024]{1,0:T(8,128)(2,1)S(1)}, u32[]{:S(2)}, u32[]{:S(2)}) collective-permute-start(bf16[256,1024]{1,0:T(8,128)(2,1)S(1)} %shard_map.282.refs_2_), channel_id=1, source_target_pairs={{0,1},{1,0},{2,3},{3,2},{4,5},{5,4},{6,7},{7,6},{8,9},{9,8},{10,11... | collective-permute-start | bytes 1572872 | tf_op jit(solution)/shard_map/ppermute | solution.py:20
  167.8 28.0 %collective-permute-start.60 = (bf16[256,1024]{1,0:T(8,128)(2,1)S(1)}, bf16[256,1024]{1,0:T(8,128)(2,1)S(1)}, u32[]{:S(2)}, u32[]{:S(2)}) collective-permute-start(bf16[256,1024]{1,0:T(8,128)(2,1)S(1)} %get-tuple-element.289), channel_id=1, source_target_pairs={{0,24},{24,0},{8,16},{16,8},{1,25},{25,1},{9,17},{17,9},{2,26},{26... | collective-permute-start | bytes 1572872 | tf_op jit(solution)/shard_map/ppermute | solution.py:692
  170.9 24.9 %collective-permute-start.69 = (bf16[128,1024]{1,0:T(8,128)(2,1)S(1)}, bf16[128,1024]{1,0:T(8,128)(2,1)S(1)}, u32[]{:S(2)}, u32[]{:S(2)}) collective-permute-start(bf16[128,1024]{1,0:T(8,128)(2,1)S(1)} %collective-permute-done.67.refs_0_.refs_1_), channel_id=1, source_target_pairs={{0,1},{1,0},{2,3},{3,2},{4,5},{5,4},{6,7},{7,6},{8,9},{9,8},{10,11... | collective-permute-start | bytes 786440 | tf_op jit(solution)/shard_map/ppermute | solution.py:20
  182.8 14.0 %collective-permute-start.54 = (bf16[64,1024]{1,0:T(8,128)(2,1)S(1)}, bf16[64,1024]{1,0:T(8,128)(2,1)S(1)}, u32[]{:S(2)}, u32[]{:S(2)}) collective-permute-start(bf16[64,1024]{1,0:T(8,128)(2,1)S(1)} %get-tuple-element.284.refs_0_), channel_id=1, source_target_pairs={{0,4},{4,0},{1,5},{5,1},{2,6},{6,2},{3,7},{7,3},{8,12},{12,8},{9,1... | collective-permute-start | bytes 393224 | tf_op jit(solution)/shard_map/ppermute | solution.py:20
  208.5 14.2 %collective-permute-start.75 = (bf16[256,1024]{1,0:T(8,128)(2,1)S(1)}, bf16[256,1024]{1,0:T(8,128)(2,1)S(1)}, u32[]{:S(2)}, u32[]{:S(2)}) collective-permute-start(bf16[256,1024]{1,0:T(8,128)(2,1)S(1)} %shard_map.289.refs_0_.refs_3_), channel_id=1, source_target_pairs={{0,1},{1,0},{2,3},{3,2},{4,5},{5,4},{6,7},{7,6},{8,9},{9,8},{10,11... | collective-permute-start | bytes 1572872 | tf_op jit(solution)/shard_map/ppermute | solution.py:20
  212.8 27.4 %collective-permute-start.84 = (bf16[512,1024]{1,0:T(8,128)(2,1)S(1)}, bf16[512,1024]{1,0:T(8,128)(2,1)S(1)}, u32[]{:S(2)}, u32[]{:S(2)}) collective-permute-start(bf16[512,1024]{1,0:T(8,128)(2,1)S(1)} %get-tuple-element.326), channel_id=1, source_target_pairs={{0,16},{16,0},{1,17},{17,1},{2,18},{18,2},{3,19},{19,3},{4,20},{20... | collective-permute-start | bytes 3145736 | tf_op jit(solution)/shard_map/ppermute | solution.py:20
  214.2 26.0 %collective-permute-start.85 = (bf16[512,1024]{1,0:T(8,128)(2,1)S(1)}, bf16[512,1024]{1,0:T(8,128)(2,1)S(1)}, u32[]{:S(2)}, u32[]{:S(2)}) collective-permute-start(bf16[512,1024]{1,0:T(8,128)(2,1)S(1)} %get-tuple-element.327), channel_id=1, source_target_pairs={{0,8},{8,0},{1,9},{9,1},{2,10},{10,2},{3,11},{11,3},{4,12},{12,4},... | collective-permute-start | bytes 3145736 | tf_op jit(solution)/shard_map/ppermute | solution.py:20
  238.4 14.1 %collective-permute-start.86 = (bf16[256,1024]{1,0:T(8,128)(2,1)S(1)}, bf16[256,1024]{1,0:T(8,128)(2,1)S(1)}, u32[]{:S(2)}, u32[]{:S(2)}) collective-permute-start(bf16[256,1024]{1,0:T(8,128)(2,1)S(1)} %shard_map.293.refs_0_.refs_2_), channel_id=1, source_target_pairs={{0,1},{1,0},{2,3},{3,2},{4,5},{5,4},{6,7},{7,6},{8,9},{9,8},{10,11... | collective-permute-start | bytes 1572872 | tf_op jit(solution)/shard_map/ppermute | solution.py:20
  242.1 25.0 %collective-permute-start.95 = (bf16[512,1024]{1,0:T(8,128)(2,1)S(1)}, bf16[512,1024]{1,0:T(8,128)(2,1)S(1)}, u32[]{:S(2)}, u32[]{:S(2)}) collective-permute-start(bf16[512,1024]{1,0:T(8,128)(2,1)S(1)} %get-tuple-element.345), channel_id=1, source_target_pairs={{0,16},{16,0},{1,17},{17,1},{2,18},{18,2},{3,19},{19,3},{4,20},{20... | collective-permute-start | bytes 3145736 | tf_op jit(solution)/shard_map/ppermute | solution.py:20
  243.5 24.7 %collective-permute-start.96 = (bf16[512,1024]{1,0:T(8,128)(2,1)S(1)}, bf16[512,1024]{1,0:T(8,128)(2,1)S(1)}, u32[]{:S(2)}, u32[]{:S(2)}) collective-permute-start(bf16[512,1024]{1,0:T(8,128)(2,1)S(1)} %get-tuple-element.346), channel_id=1, source_target_pairs={{0,8},{8,0},{1,9},{9,1},{2,10},{10,2},{3,11},{11,3},{4,12},{12,4},... | collective-permute-start | bytes 3145736 | tf_op jit(solution)/shard_map/ppermute | solution.py:20
  271.1 54.3 %collective-permute-start.107 = (bf16[640,1024]{1,0:T(8,128)(2,1)S(1)}, bf16[640,1024]{1,0:T(8,128)(2,1)S(1)}, u32[]{:S(2)}, u32[]{:S(2)}) collective-permute-start(bf16[640,1024]{1,0:T(8,128)(2,1)S(1)} %get-tuple-element.364), channel_id=1, source_target_pairs={{0,16},{16,0},{1,17},{17,1},{2,18},{18,2},{3,19},{19,3},{4,20},{20... | collective-permute-start | bytes 3932168 | tf_op jit(solution)/shard_map/ppermute | solution.py:20
  271.9 53.6 %collective-permute-start.108 = (bf16[640,1024]{1,0:T(8,128)(2,1)S(1)}, bf16[640,1024]{1,0:T(8,128)(2,1)S(1)}, u32[]{:S(2)}, u32[]{:S(2)}) collective-permute-start(bf16[640,1024]{1,0:T(8,128)(2,1)S(1)} %get-tuple-element.365), channel_id=1, source_target_pairs={{0,8},{8,0},{1,9},{9,1},{2,10},{10,2},{3,11},{11,3},{4,12},{12,4},... | collective-permute-start | bytes 3932168 | tf_op jit(solution)/shard_map/ppermute | solution.py:20
  273.4 14.8 %collective-permute-start.98 = (bf16[256,1024]{1,0:T(8,128)(2,1)S(1)}, bf16[256,1024]{1,0:T(8,128)(2,1)S(1)}, u32[]{:S(2)}, u32[]{:S(2)}) collective-permute-start(bf16[256,1024]{1,0:T(8,128)(2,1)S(1)} %shard_map.297.refs_0_.refs_2_), channel_id=1, source_target_pairs={{0,1},{1,0},{2,3},{3,2},{4,5},{5,4},{6,7},{7,6},{8,9},{9,8},{10,11... | collective-permute-start | bytes 1572872 | tf_op jit(solution)/shard_map/ppermute | solution.py:20
  277.0 14.0 %collective-permute-start.65 = (bf16[128,1024]{1,0:T(8,128)(2,1)S(1)}, bf16[128,1024]{1,0:T(8,128)(2,1)S(1)}, u32[]{:S(2)}, u32[]{:S(2)}) collective-permute-start(bf16[128,1024]{1,0:T(8,128)(2,1)S(1)} %get-tuple-element.296), channel_id=1, source_target_pairs={{0,1},{1,0},{2,3},{3,2},{4,5},{5,4},{6,7},{7,6},{8,9},{9,8},{10,11... | collective-permute-start | bytes 786440 | tf_op jit(solution)/shard_map/ppermute | solution.py:20
  291.2 15.5 %collective-permute-start.66 = (bf16[1,128,1024]{2,1,0:T(8,128)(2,1)S(1)}, bf16[1,128,1024]{2,1,0:T(8,128)(2,1)S(1)}, u32[]{:S(2)}, u32[]{:S(2)}) collective-permute-start(bf16[1,128,1024]{2,1,0:T(8,128)(2,1)S(1)} %shard_map.286), channel_id=1, source_target_pairs={{0,0},{2,4},{4,2},{6,6},{1,1},{3,5},{5,3},{7,7},{8,8},{10,12},{12,... | collective-permute-start | bytes 786440 | tf_op jit(solution)/shard_map/ppermute | solution.py:1213
  291.9 33.4 %collective-permute-start.97 = (bf16[256,1024]{1,0:T(8,128)(2,1)S(1)}, bf16[256,1024]{1,0:T(8,128)(2,1)S(1)}, u32[]{:S(2)}, u32[]{:S(2)}) collective-permute-start(bf16[256,1024]{1,0:T(8,128)(2,1)S(1)} %get-tuple-element.348), channel_id=1, source_target_pairs={{0,2},{2,0},{1,3},{3,1},{4,6},{6,4},{5,7},{7,5},{8,10},{10,8},{9,1... | collective-permute-start | bytes 1572872 | tf_op jit(solution)/shard_map/ppermute | solution.py:20
  306.4 10.4 %collective-permute-start.103 = (bf16[64,1024]{1,0:T(8,128)(2,1)S(1)}, bf16[64,1024]{1,0:T(8,128)(2,1)S(1)}, u32[]{:S(2)}, u32[]{:S(2)}) collective-permute-start(bf16[64,1024]{1,0:T(8,128)(2,1)S(1)} %get-tuple-element.358.refs_13_), channel_id=1, source_target_pairs={{0,4},{4,0},{1,5},{5,1},{2,6},{6,2},{3,7},{7,3},{8,12},{12,8},{9,1... | collective-permute-start | bytes 393224 | tf_op jit(solution)/shard_map/ppermute | solution.py:20
  306.6 11.2 %collective-permute-start.104 = (bf16[64,1024]{1,0:T(8,128)(2,1)S(1)}, bf16[64,1024]{1,0:T(8,128)(2,1)S(1)}, u32[]{:S(2)}, u32[]{:S(2)}) collective-permute-start(bf16[64,1024]{1,0:T(8,128)(2,1)S(1)} %get-tuple-element.359.refs_14_), channel_id=1, source_target_pairs={{0,4},{4,0},{1,5},{5,1},{2,6},{6,2},{3,7},{7,3},{8,12},{12,8},{9,1... | collective-permute-start | bytes 393224 | tf_op jit(solution)/shard_map/ppermute | solution.py:20
  328.6 24.6 %collective-permute-start.115 = (bf16[288,1024]{1,0:T(8,128)(2,1)S(1)}, bf16[288,1024]{1,0:T(8,128)(2,1)S(1)}, u32[]{:S(2)}, u32[]{:S(2)}) collective-permute-start(bf16[288,1024]{1,0:T(8,128)(2,1)S(1)} %get-tuple-element.384), channel_id=1, source_target_pairs={{0,16},{16,0},{1,17},{17,1},{2,18},{18,2},{3,19},{19,3},{4,20},{20... | collective-permute-start | bytes 1769480 | tf_op jit(solution)/shard_map/ppermute | solution.py:20
  329.3 23.9 %collective-permute-start.118 = (bf16[288,1024]{1,0:T(8,128)(2,1)S(1)}, bf16[288,1024]{1,0:T(8,128)(2,1)S(1)}, u32[]{:S(2)}, u32[]{:S(2)}) collective-permute-start(bf16[288,1024]{1,0:T(8,128)(2,1)S(1)} %get-tuple-element.389), channel_id=1, source_target_pairs={{0,8},{8,0},{1,9},{9,1},{2,10},{10,2},{3,11},{11,3},{4,12},{12,4},... | collective-permute-start | bytes 1769480 | tf_op jit(solution)/shard_map/ppermute | solution.py:20
  330.5 22.4 %collective-permute-start.117 = (bf16[256,1024]{1,0:T(8,128)(2,1)S(1)}, bf16[256,1024]{1,0:T(8,128)(2,1)S(1)}, u32[]{:S(2)}, u32[]{:S(2)}) collective-permute-start(bf16[256,1024]{1,0:T(8,128)(2,1)S(1)} %get-tuple-element.387), channel_id=1, source_target_pairs={{0,16},{16,0},{1,17},{17,1},{2,18},{18,2},{3,19},{19,3},{4,20},{20... | collective-permute-start | bytes 1572872 | tf_op jit(solution)/shard_map/ppermute | solution.py:20
  331.2 9.3 %collective-permute-start.109 = (bf16[128,1024]{1,0:T(8,128)(2,1)S(1)}, bf16[128,1024]{1,0:T(8,128)(2,1)S(1)}, u32[]{:S(2)}, u32[]{:S(2)}) collective-permute-start(bf16[128,1024]{1,0:T(8,128)(2,1)S(1)} %get-tuple-element.377), channel_id=1, source_target_pairs={{0,1},{1,0},{2,3},{3,2},{4,5},{5,4},{6,7},{7,6},{8,9},{9,8},{10,11... | collective-permute-start | bytes 786440 | tf_op jit(solution)/shard_map/ppermute | solution.py:20
  331.2 12.2 %collective-permute-start.111 = (bf16[128,1024]{1,0:T(8,128)(2,1)S(1)}, bf16[128,1024]{1,0:T(8,128)(2,1)S(1)}, u32[]{:S(2)}, u32[]{:S(2)}) collective-permute-start(bf16[128,1024]{1,0:T(8,128)(2,1)S(1)} %get-tuple-element.367.refs_1_), channel_id=1, source_target_pairs={{0,2},{2,0},{1,3},{3,1},{4,6},{6,4},{5,7},{7,5},{8,10},{10,8},{9,1... | collective-permute-start | bytes 786440 | tf_op jit(solution)/shard_map/ppermute | solution.py:20
  354.0 20.0 %collective-permute-start.116 = (bf16[256,1024]{1,0:T(8,128)(2,1)S(1)}, bf16[256,1024]{1,0:T(8,128)(2,1)S(1)}, u32[]{:S(2)}, u32[]{:S(2)}) collective-permute-start(bf16[256,1024]{1,0:T(8,128)(2,1)S(1)} %get-tuple-element.385), channel_id=1, source_target_pairs={{0,8},{8,0},{1,9},{9,1},{2,10},{10,2},{3,11},{11,3},{4,12},{12,4},... | collective-permute-start | bytes 1572872 | tf_op jit(solution)/shard_map/ppermute | solution.py:20
  355.2 30.6 %collective-permute-start.120 = (bf16[256,1024]{1,0:T(8,128)(2,1)S(1)}, bf16[256,1024]{1,0:T(8,128)(2,1)S(1)}, u32[]{:S(2)}, u32[]{:S(2)}) collective-permute-start(bf16[256,1024]{1,0:T(8,128)(2,1)S(1)} %shard_map.306.refs_0_), channel_id=1, source_target_pairs={{0,2},{2,0},{1,3},{3,1},{4,6},{6,4},{5,7},{7,5},{8,10},{10,8},{9,1... | collective-permute-start | bytes 1572872 | tf_op jit(solution)/shard_map/ppermute | solution.py:20
  355.8 11.9 %collective-permute-start.113 = (bf16[32,1792]{1,0:T(8,128)(2,1)S(1)}, bf16[32,1792]{1,0:T(8,128)(2,1)S(1)}, u32[]{:S(2)}, u32[]{:S(2)}) collective-permute-start(bf16[32,1792]{1,0:T(8,128)(2,1)S(1)} %get-tuple-element.382), channel_id=1, source_target_pairs={{0,1},{1,0},{2,3},{3,2},{4,5},{5,4},{6,7},{7,6},{8,9},{9,8},{10,11... | collective-permute-start | bytes 344072 | tf_op jit(solution)/shard_map/ppermute | solution.py:20
  360.1 14.0 %collective-permute-start.119 = (bf16[144,1024]{1,0:T(8,128)(2,1)S(1)}, bf16[144,1024]{1,0:T(8,128)(2,1)S(1)}, u32[]{:S(2)}, u32[]{:S(2)}) collective-permute-start(bf16[144,1024]{1,0:T(8,128)(2,1)S(1)} %get-tuple-element.390), channel_id=1, source_target_pairs={{0,8},{8,0},{1,9},{9,1},{2,10},{10,2},{3,11},{11,3},{4,12},{12,4},... | collective-permute-start | bytes 884744 | tf_op jit(solution)/shard_map/ppermute | solution.py:20
  360.8 28.3 %collective-permute-start.122 = (bf16[144,1024]{1,0:T(8,128)(2,1)S(1)}, bf16[144,1024]{1,0:T(8,128)(2,1)S(1)}, u32[]{:S(2)}, u32[]{:S(2)}) collective-permute-start(bf16[144,1024]{1,0:T(8,128)(2,1)S(1)} %shard_map.308), channel_id=1, source_target_pairs={{0,2},{2,0},{1,3},{3,1},{4,6},{6,4},{5,7},{7,5},{8,10},{10,8},{9,1... | collective-permute-start | bytes 884744 | tf_op jit(solution)/shard_map/ppermute | solution.py:20
  373.4 24.5 %collective-permute-start.110 = (bf16[1,128,1024]{2,1,0:T(8,128)(2,1)S(1)}, bf16[1,128,1024]{2,1,0:T(8,128)(2,1)S(1)}, u32[]{:S(2)}, u32[]{:S(2)}) collective-permute-start(bf16[1,128,1024]{2,1,0:T(8,128)(2,1)S(1)} %shard_map.304.refs_0_), channel_id=1, source_target_pairs={{0,0},{2,4},{4,2},{6,6},{1,1},{3,5},{5,3},{7,7},{8,8},{10,12},{12,... | collective-permute-start | bytes 786440 | tf_op jit(solution)/shard_map/ppermute | solution.py:1213
  390.5 15.9 %collective-permute-start.123 = (bf16[48,1792]{1,0:T(8,128)(2,1)S(1)}, bf16[48,1792]{1,0:T(8,128)(2,1)S(1)}, u32[]{:S(2)}, u32[]{:S(2)}) collective-permute-start(bf16[48,1792]{1,0:T(8,128)(2,1)S(1)} %get-tuple-element.399), channel_id=1, source_target_pairs={{0,4},{4,0},{1,5},{5,1},{2,6},{6,2},{3,7},{7,3},{8,12},{12,8},{9,1... | collective-permute-start | bytes 516104 | tf_op jit(solution)/shard_map/ppermute | solution.py:20
  393.1 13.2 %collective-permute-start.124 = (bf16[48,1792]{1,0:T(8,128)(2,1)S(1)}, bf16[48,1792]{1,0:T(8,128)(2,1)S(1)}, u32[]{:S(2)}, u32[]{:S(2)}) collective-permute-start(bf16[48,1792]{1,0:T(8,128)(2,1)S(1)} %get-tuple-element.400), channel_id=1, source_target_pairs={{0,1},{1,0},{2,3},{3,2},{4,5},{5,4},{6,7},{7,6},{8,9},{9,8},{10,11... | collective-permute-start | bytes 516104 | tf_op jit(solution)/shard_map/ppermute | solution.py:20
  394.6 11.8 %collective-permute-start.125 = (bf16[48,1792]{1,0:T(8,128)(2,1)S(1)}, bf16[48,1792]{1,0:T(8,128)(2,1)S(1)}, u32[]{:S(2)}, u32[]{:S(2)}) collective-permute-start(bf16[48,1792]{1,0:T(8,128)(2,1)S(1)} %get-tuple-element.401), channel_id=1, source_target_pairs={{0,5},{5,0},{1,4},{4,1},{2,7},{7,2},{3,6},{6,3},{8,13},{13,8},{9,1... | collective-permute-start | bytes 516104 | tf_op jit(solution)/shard_map/ppermute | solution.py:1221
  394.6 11.8 %collective-permute-start.126 = (bf16[64,512]{1,0:T(8,128)(2,1)S(1)}, bf16[64,512]{1,0:T(8,128)(2,1)S(1)}, u32[]{:S(2)}, u32[]{:S(2)}) collective-permute-start(bf16[64,512]{1,0:T(8,128)(2,1)S(1)} %get-tuple-element.402), channel_id=1, source_target_pairs={{0,0},{1,16},{16,1},{17,17},{2,2},{3,18},{18,3},{19,19},{4,4},{5,2... | collective-permute-start | bytes 196616 | tf_op jit(solution)/shard_map/ppermute | solution.py:1439
  (73 other events, 277.7 us)

commit v4 on v3

--- a/solution.py
+++ b/solution.py
@@ -471,9 +471,10 @@
 
 
 def mlp_1_slots(refs):
-    own, own_down, far, far_down, by_x_1, by_y_1, by_x, by_y, both = refs
+    own, own_down, far, far_down, by_x_1, by_y_1, by_x, by_y, across_x, across_y, both = refs
     own, far = Joined(View(own, 128), own_down, 128), Joined(View(far, 128), far_down, 128)
-    return eight_slots(own, far, View(by_x_1, 192), View(by_y_1, 192), by_x, by_y, both, 256)
+    across = Joined(across_y, across_x, 128)
+    return own, far, View(by_x_1, 192), by_x, View(by_y_1, 192), by_y, across, both
 
 
 def second_message(far, near_x, near_y, to_x, to_y, rows):
@@ -502,10 +503,10 @@
         to[320:448, :] = own_down[...]
 
 
-def mlp_1_message(far, far_down, near_x, near_y, to_x, to_y, to_both):
-    far = Joined(View(far, 128), far_down, 128)
-    to_both[...] = far[0:256, :]
-    second_message(far, View(near_x, 192), View(near_y, 192), to_x, to_y, 256)
+def mlp_1_message(far, far_down, near_x, near_y, to_all, to_x, to_y):
+    to_all[...] = Joined(View(far, 128), far_down, 128)[0:256, :]
+    to_y[...] = near_x[192:320, :]
+    to_x[...] = near_y[320:448, :]
 
 
 def slot_blocks():
@@ -866,7 +867,7 @@
 
 
 def mlp_weights(refs, layer):
-    count = 9 if layer else 8
+    count = 11 if layer else 8
     return (mlp_1_slots if layer else mlp_0_slots)(refs[:count]), refs[count:]
 
 
@@ -1266,22 +1267,22 @@
         return swap(to[0], "x"), swap(to[1], "y"), both_ways(to[2] if rows else ins[0]), to[0]
 
     by_x, by_y, both, sent = second_hops(
-        att_0_message, 224, 208, far, near_x, near_y, after=(pair,)
+        att_0_message, 224, 208, far, near_x, near_y, after=(pair, block)
     )
     att_0 = (att_0, far, near_x, near_y, by_x, by_y, both)
     up_0, down_0, _ = gate((sent,), up_0, ready[6])
     far_up, far_down = swap(up_0, "zh"), swap(down_0, "zh")
-    pair, deep, token = gate((by_x, by_y, both, far_up), pair, deep)
+    by_zl = swap(block, "zl")
+    pair, deep, token = gate((by_x, by_y, both, far_up, by_zl), pair, deep)
     pair_x, pair_y = swap(pair, "x"), swap(pair, "y")
-    by_zl = swap(block, "zl")
     blocks = (block, swap(block, "core"), by_zl, swap(by_zl, "core"))
     segments = (segment_ids, swap(segment_ids, "core"), group_order)
 
     def cores(values):
         return [swap(v, "core") for v in values]
 
-    def summed_core(keep, *send):
-        (part,) = run(add_parts, [row], keep, *cores(send))
+    def summed_core(keep, *send, after=()):
+        (part,) = run(add_parts, [row], keep, *cores(send), after=after)
         return part, swap(part, "zl")
 
     def split_core(keep, *send, after=()):
@@ -1326,14 +1327,20 @@
     att_1 = (deep, deep_far, pair_x, pair_y, one_x, one_y, both)
     part, came = summed_core(keep, *send)
     x2_0, *h = run(norm_stage(5, 8), [rowf, *quarters], x1_0, part, came, vec, after=(token, down_1_far), us=1)
-    by_x, by_y, both, token = second_hops(
-        mlp_1_message, 384, 384, deep_far, down_1_far, one_x, one_y, rows=256
-    )
+    to_all, to_x, to_y = run(
+        mlp_1_message, [row, shape(128, 1024), shape(128, 1024)], deep_far, down_1_far, one_x, one_y,
+        after=(both,),
+    )
+    by_x, by_y = swap(to_all, "x"), swap(to_all, "y")
     h1_1, qkv_1, probs_1, o_1, keep, *send = run(
         with_scratch(next_attention, *weights_scratch, dist),
-        attention_outs, *with_other(h), *att_1, vec, *segments, after=(token,), us=9,
-    )
-    mlp_1 = (deep, down_1, deep_far, down_1_far, one_x, one_y, by_x, by_y, both)
+        attention_outs, *with_other(h), *att_1, vec, *segments, after=(to_all,), us=9,
+    )
+    by_x, by_y, to_x, to_y, *send, _ = gate((keep,), by_x, by_y, to_x, to_y, *send)
+    mlp_1 = (
+        deep, down_1, deep_far, down_1_far, one_x, one_y, by_x, by_y,
+        swap(to_x, "x"), swap(to_y, "y"), both_ways(to_all),
+    )
     cot, _ = gate((keep,), cot)
     cot = corner(cot)
     part, came = summed_core(keep, *send)
@@ -1355,8 +1362,9 @@
     out_scratch = pltpu.VMEM((256, 1024), BF)
 
     keep_last, send_last = keep, send
-    gy2, gu_1, keep, *send = run(mlp_back(1), mlp_back_outs, *cots, u_1, *mlp_1, us=6)
-    part, came = summed_core(keep, *send)
+    part_last, came_last = split_core(keep_last, *send_last)
+    gy2, gu_1, keep, *send = run(mlp_back(1), mlp_back_outs, *cots, u_1, *mlp_1, after=(part_last,), us=6)
+    part, came = summed_core(keep, *send, after=(came_last,))
     to_y, to_x, m1_near_0, m1_near_1, m1_far_0, m1_far_1 = run(
         window_1, grad_outs(512, 256), h2_1, a_1, gy2, gu_1, after=(part,), us=4
     )
@@ -1370,14 +1378,13 @@
         attention_back_outs, *with_other(gy), qkv_1, probs_1, *att_1, us=9,
     )
     part, came = summed_core(keep, *send)
+    (final,) = run(finish_rows, [shape(1, 128, 1024)], x1_1, part_last, came_last, vec)
+    output = corner(final)
     to_y, to_x, a1_near_0, a1_near_1, a1_far_0, a1_far_1 = run(
         with_scratch(window_2, out_scratch), grad_outs(512, 128), h1_1, o_1, gy1, gqkv_1,
-        m1_near_1, y_1, m1_far_1, x_1, after=(part,), us=3,
+        m1_near_1, y_1, m1_far_1, x_1, after=(part, output), us=3,
     )
     y_2, x_2 = swap(to_y, "y"), swap(to_x, "x")
-    part_last, came_last = split_core(keep_last, *send_last)
-    (final,) = run(finish_rows, [shape(1, 128, 1024)], x1_1, part_last, came_last, vec)
-    output = corner(final)
     gx, *gy, g1 = run(
         norm_back_stage(8), norm_outs, gm, part, came, x2_0, vec, after=(a1_far_1,), us=1.5
     )
@@ -1397,28 +1404,28 @@
         with_scratch(attention_back(0), *attention_back_scratch),
         attention_back_outs, *with_other(gy), qkv_0, probs_0, *att_0, us=9,
     )
-    part, came = split_core(keep, *send, after=(m1_far_3, output))
     to_x, to_y, to_zh = run(
-        window_4, [row, row, shape(128, 1024)], m0_near_1, y_3, m0_far_1, x_3, a1_far_0, x_2, after=(part,)
+        window_4, [row, row, shape(128, 1024)], m0_near_1, y_3, m0_far_1, x_3, a1_far_0, x_2, after=(keep,)
     )
     x_4, y_4, a1_far_3 = swap(to_x, "x"), swap(to_y, "y"), swap(to_zh, "zh")
+    part, came = split_core(keep, *send, after=(to_zh, m1_far_3))
     to_y, to_x, a0_near_0, a0_near_1, a0_far_0, a0_far_1 = run(
         with_scratch(window_5, out_scratch, *vec_scratch), grad_outs(288, 144),
         h1_0, o_0, gy1, gqkv_0, g1, e1, e0, gu_1, gu_0, gqkv_1, keep, *send, *blocks,
-        after=(part, to_zh), us=3,
+        after=(part, x_4, y_4), us=3,
     )
     y_5, x_5 = swap(to_y, "y"), swap(to_x, "x")
+    (to_zh,) = run(third_only, [row], m0_far_0, x_3, y_4, after=(a0_far_1,))
+    m0_far_3 = swap(to_zh, "zh")
     (grad,) = run(
         with_scratch(
             last_norm_back, *[pltpu.VMEM((128, 1024), F32)] * 3, pltpu.VMEM((128, 1024), BF),
             pltpu.VMEM((8, 1024), F32),
         ),
-        [shape(1, 128, 1024)], gm, part, came, blocks[0], vec, after=(a0_far_1,), us=1.5,
+        [shape(1, 128, 1024)], gm, part, came, blocks[0], vec, after=(to_zh,), us=1.5,
     )
     tokens_grad = corner(grad).astype(F32)
-    (to_zh,) = run(third_only, [row], m0_far_0, x_3, y_4, after=(grad, a1_far_3))
-    m0_far_3 = swap(to_zh, "zh")
-    to_x, to_y = run(second_only, [shape(144, 1024)] * 2, a0_near_1, y_5, a0_far_1, x_5, after=(to_zh,))
+    to_x, to_y = run(second_only, [shape(144, 1024)] * 2, a0_near_1, y_5, a0_far_1, x_5, after=(grad,))
     x_6, y_6 = swap(to_x, "x"), swap(to_y, "y")
     rest = run(
         unpack_first,
@@ -1427,7 +1434,7 @@
         y_1, y_2, x_2, x_3, m1_near_0, m1_far_3, a1_near_0, a1_far_3, us=2,
     )
     rest_came = to_partners(rest[1:4])
-    (to_zh,) = run(window_6, [shape(144, 1024)], a0_far_0, x_5, y_6)
+    (to_zh,) = run(window_6, [shape(144, 1024)], a0_far_0, x_5, y_6, after=rest_came)
     a0_far_3 = swap(to_zh, "zh")
     last = run(
         unpack_last,

time: 414 us -> 394 us (0.952)
  waiting for transfers between devices: 225 us -> 205 us
    ppermute x112 -> x114, waiting for transfers between devices: 193 us -> 179 us  [swap(): return lax.ppermute(value, axis, [(0, 1), (1, 0)])]
    ppermute x4, waiting for transfers between devices: 17.3 us -> 10.4 us  [both_ways(): return lax.ppermute(value, ('y', 'x'), [(0, 3), (3, 0), (1, 2), (2, 1)])]
    ppermute x112 -> x114, starting transfers between devices: 76.8 us -> 78.1 us  [swap(): return lax.ppermute(value, axis, [(0, 1), (1, 0)])]
  transfers between devices with their start and end apart: 128 -> 130, of which waited for: 65 -> 77; matrix products, arithmetic and copies ran while one was open for 0% -> 0% of each run, Pallas kernels for 13% -> 17%
where the time goes in v4:
time: 394 us; the launch traced here: 389 us
  waiting for transfers between devices  205 us (52%)
  starting transfers between devices  95.3 us (24%)
  Pallas kernels  81.2 us (21%)
  local copies, waits for them, and re-layouts  5.63 us (1%)
    ppermute x114, waiting for transfers between devices, swap(): return lax.ppermute(value, axis, [(0, 1), (1, 0)])  179 us
    pallas_call x43, Pallas kernels, run(): pl.pallas_call(body, out_shape=tuple(outs), in_specs=[free] * skip + [sme...  78.3 us
    ppermute x114, starting transfers between devices, swap(): return lax.ppermute(value, axis, [(0, 1), (1, 0)])  78.1 us
    ppermute x4, waiting for transfers between devices, both_ways(): return lax.ppermute(value, ('y', 'x'), [(0, 3), (3, 0), (1, 2), (2, 1)])  10.4 us
    ppermute x4, waiting for transfers between devices, to_partners(): lax.ppermute(three, ('core', 'zl'), [(0, 3), (3, 0), (1, 2), (2, 1)])  8.5 us
  transfers between devices with their start and end apart: 130, of which 77 were waited for; matrix products, arithmetic and copies ran while one was open for 0% of the time, Pallas kernels for 17%

profile of v4, /device:TPU:4, one launch (start us, length us, event | category | flops | bytes accessed | tf_op | source)
XLA Modules:
  0.0 389.4 jit_solution(14120564943926329372)
XLA Ops:
  0.7 2.4 shard_map.263
  3.1 1.6 collective-permute-start.1
  5.0 3.4 collective-permute-start.3
  14.8 1.9 collective-permute-start.6
  16.8 1.5 collective-permute-start.10
  18.3 2.6 collective-permute-start.9
  21.6 2.4 collective-permute-done.6.refs_2_
  24.9 7.3 %collective-permute-done.7.refs_3_ = bf16[32,2816]{1,0:T(8,128)(2,1)S(1)} collective-permute-done((bf16[32,2816]{1,0:T(8,128)(2,1)S(1)}, bf16[32,2816]{1,0:T(8,128)(2,1)S(1)}, u32[]{:S(2)}, u32[]{:S(2)}) %collective-permute-start.7) | collective-permute-done | bytes 180256 | tf_op jit(solution)/shard_map/ppermute | solution.py:1222
  32.4 4.8 %collective-permute-done.9.refs_2_.refs_6_.refs_11_ = bf16[144,1024]{1,0:T(8,128)(2,1)S(1)} collective-permute-done((bf16[144,1024]{1,0:T(8,128)(2,1)S(1)}, bf16[144,1024]{1,0:T(8,128)(2,1)S(1)}, u32[]{:S(2)}, u32[]{:S(2)}) %collective-permute-start.9) | collective-permute-done | bytes 294944 | tf_op jit(solution)/shard_map/ppermute | solution.py:20
  37.9 1.7 collective-permute-start.13
  42.4 6.0 %collective-permute-start.15 = (bf16[128,1024]{1,0:T(8,128)(2,1)S(1)}, bf16[128,1024]{1,0:T(8,128)(2,1)S(1)}, u32[]{:S(2)}, u32[]{:S(2)}) collective-permute-start(bf16[128,1024]{1,0:T(8,128)(2,1)S(1)} %get-tuple-element.241), channel_id=1, source_target_pairs={{0,2},{2,0},{1,3},{3,1},{4,6},{6,4},{5,7},{7,5},{8,10},{10,8},{9,1... | collective-permute-start | bytes 786440 | tf_op jit(solution)/shard_map/ppermute | solution.py:20
  48.4 1.9 collective-permute-done.16.refs_4_.refs_3_.refs_2_.refs_20_
  50.4 8.4 %collective-permute-done.15.refs_3_.refs_1_.refs_10_ = bf16[128,1024]{1,0:T(8,128)(2,1)S(1)} collective-permute-done((bf16[128,1024]{1,0:T(8,128)(2,1)S(1)}, bf16[128,1024]{1,0:T(8,128)(2,1)S(1)}, u32[]{:S(2)}, u32[]{:S(2)}) %collective-permute-start.15) | collective-permute-done | bytes 262176 | tf_op jit(solution)/shard_map/ppermute | solution.py:20
  60.8 1.4 collective-permute-done.19.refs_13_.refs_18_
  62.3 10.4 %shard_map.271 = (f32[16,1024]{1,0:T(8,128)S(1)}, bf16[512,1024]{1,0:T(8,128)(2,1)S(1)}, bf16[512,768]{1,0:T(8,128)(2,1)S(1)}, bf16[4,512,512]{2,1,0:T(8,128)(2,...) custom-call(f32[8,128]{1,0:T(8,128)S(1)} %get-tuple-element.243.refs, ...), custom_call_target="tpu_custom_call" | custom-call | flops 100000000 | tf_op jit(solution)/shard_map/pallas_call | solution.py:529
  72.7 3.7 collective-permute-done.20.refs_1_
  76.4 1.5 collective-permute-done.22.refs_3_
  81.5 1.4 collective-permute-start.34
  85.4 17.6 %collective-permute-done.28.refs_4_ = bf16[256,1024]{1,0:T(8,128)(2,1)S(1)} collective-permute-done((bf16[256,1024]{1,0:T(8,128)(2,1)S(1)}, bf16[256,1024]{1,0:T(8,128)(2,1)S(1)}, u32[]{:S(2)}, u32[]{:S(2)}) %collective-permute-start.28) | collective-permute-done | bytes 524320 | tf_op jit(solution)/shard_map/ppermute | solution.py:20
  103.8 5.2 %collective-permute-done.23.refs_0_.refs_1_.refs_10_.refs_8_.refs_11_ = bf16[256,1024]{1,0:T(8,128)(2,1)S(1)} collective-permute-done((bf16[256,1024]{1,0:T(8,128)(2,1)S(1)}, bf16[256,1024]{1,0:T(8,128)(2,1)S(1)}, u32[]{:S(2)}, u32[]{:S(2)}) %collective-permute-start.23) | collective-permute-done | bytes 524320 | tf_op jit(solution)/shard_map/ppermute | solution.py:20
  109.0 4.5 %collective-permute-done.35.refs_16_ = bf16[256,1024]{1,0:T(8,128)(2,1)S(1)} collective-permute-done((bf16[256,1024]{1,0:T(8,128)(2,1)S(1)}, bf16[256,1024]{1,0:T(8,128)(2,1)S(1)}, u32[]{:S(2)}, u32[]{:S(2)}) %collective-permute-start.35) | collective-permute-done | bytes 524320 | tf_op jit(solution)/shard_map/ppermute | solution.py:693
  115.1 3.1 shard_map.276
  123.1 1.7 collective-permute-start.41
  124.8 1.5 collective-permute-start.42
  126.3 15.6 %collective-permute-done.36.refs_1_.refs_2_.refs_11_.refs_9_ = bf16[128,1024]{1,0:T(8,128)(2,1)S(1)} collective-permute-done((bf16[128,1024]{1,0:T(8,128)(2,1)S(1)}, bf16[128,1024]{1,0:T(8,128)(2,1)S(1)}, u32[]{:S(2)}, u32[]{:S(2)}) %collective-permute-start.36) | collective-permute-done | bytes 262176 | tf_op jit(solution)/shard_map/ppermute | solution.py:20
  141.9 5.8 %collective-permute-done.42.refs_0_.refs_15_.refs_16_ = bf16[128,1024]{1,0:T(8,128)(2,1)S(1)} collective-permute-done((bf16[128,1024]{1,0:T(8,128)(2,1)S(1)}, bf16[128,1024]{1,0:T(8,128)(2,1)S(1)}, u32[]{:S(2)}, u32[]{:S(2)}) %collective-permute-start.42) | collective-permute-done | bytes 262176 | tf_op jit(solution)/shard_map/ppermute | solution.py:693
  147.8 1.4 collective-permute-start.50
  153.0 9.3 %shard_map.281 = (bf16[512,1024]{1,0:T(8,128)(2,1)S(1)}, bf16[512,768]{1,0:T(8,128)(2,1)S(1)}, bf16[4,512,512]{2,1,0:T(8,128)(2,1)S(1)}, bf16[512,256]{1,0:T(8,1...) custom-call(bf16[256,1024]{1,0:T(8,128)(2,1)S(1)} %get-tuple-element, ...), custom_call_target="tpu_custom_call" | custom-call | flops 90000000 | tf_op jit(solution)/shard_map/pallas_call | solution.py:529
  165.1 1.7 collective-permute-start.55
  169.8 1.5 collective-permute-start.60
  172.4 9.7 %collective-permute-done.55.refs_3_ = bf16[256,1024]{1,0:T(8,128)(2,1)S(1)} collective-permute-done((bf16[256,1024]{1,0:T(8,128)(2,1)S(1)}, bf16[256,1024]{1,0:T(8,128)(2,1)S(1)}, u32[]{:S(2)}, u32[]{:S(2)}) %collective-permute-start.55) | collective-permute-done | bytes 524320 | tf_op jit(solution)/shard_map/ppermute | solution.py:20
  182.6 3.4 collective-permute-start.56
  188.6 3.1 shard_map.285
  195.4 4.8 %shard_map.289 = (bf16[512,1024]{1,0:T(8,128)(2,1)S(1)}, bf16[512,1024]{1,0:T(8,128)(2,1)S(1)}, f32[256,1024]{1,0:T(8,128)S(1)}, bf16[64,1024]{1,0:T(8,128)(2,1)...) custom-call(bf16[128,1024]{1,0:T(8,128)(2,1)S(1)} %get-tuple-element.311.refs_1_.refs, ...), custom_call_target="tpu_custom_call" | custom-call | flops 60000000 | tf_op jit(solution)/shard_map/pallas_call | solution.py:529
  204.0 2.5 shard_map.291
  208.7 8.0 %collective-permute-done.77.refs_4_ = bf16[256,1024]{1,0:T(8,128)(2,1)S(1)} collective-permute-done((bf16[256,1024]{1,0:T(8,128)(2,1)S(1)}, bf16[256,1024]{1,0:T(8,128)(2,1)S(1)}, u32[]{:S(2)}, u32[]{:S(2)}) %collective-permute-start.77) | collective-permute-done | bytes 524320 | tf_op jit(solution)/shard_map/ppermute | solution.py:20
  220.8 8.8 %shard_map.293 = (bf16[512,1024]{1,0:T(8,128)(2,1)S(1)}, bf16[512,768]{1,0:T(8,128)(2,1)S(1)}, f32[256,1024]{1,0:T(8,128)S(1)}, bf16[64,1024]{1,0:T(8,128)(2,1)S...) custom-call(bf16[64,1024]{1,0:T(8,128)(2,1)S(1)} %get-tuple-element.326.refs_0_, ...), custom_call_target="tpu_custom_call" | custom-call | flops 90000000 | tf_op jit(solution)/shard_map/pallas_call | solution.py:529
  231.0 3.7 collective-permute-start.84
  236.9 1.9 shard_map.295
  240.7 11.4 %collective-permute-done.88.refs_3_ = bf16[256,1024]{1,0:T(8,128)(2,1)S(1)} collective-permute-done((bf16[256,1024]{1,0:T(8,128)(2,1)S(1)}, bf16[256,1024]{1,0:T(8,128)(2,1)S(1)}, u32[]{:S(2)}, u32[]{:S(2)}) %collective-permute-start.88) | collective-permute-done | bytes 524320 | tf_op jit(solution)/shard_map/ppermute | solution.py:20
  255.9 4.8 %shard_map.297 = (bf16[512,1024]{1,0:T(8,128)(2,1)S(1)}, bf16[512,1024]{1,0:T(8,128)(2,1)S(1)}, f32[256,1024]{1,0:T(8,128)S(1)}, bf16[64,1024]{1,0:T(8,128)(2,1)...) custom-call(bf16[64,1024]{1,0:T(8,128)(2,1)S(1)} %get-tuple-element.346.refs_0_, ...), custom_call_target="tpu_custom_call" | custom-call | flops 60000000 | tf_op jit(solution)/shard_map/pallas_call | solution.py:529
  263.6 3.0 shard_map.299
  266.6 1.5 collective-permute-start.104
  268.5 2.4 collective-permute-start.99
  270.9 12.1 %collective-permute-done.99.refs_3_ = bf16[256,1024]{1,0:T(8,128)(2,1)S(1)} collective-permute-done((bf16[256,1024]{1,0:T(8,128)(2,1)S(1)}, bf16[256,1024]{1,0:T(8,128)(2,1)S(1)}, u32[]{:S(2)}, u32[]{:S(2)}) %collective-permute-start.99) | collective-permute-done | bytes 524320 | tf_op jit(solution)/shard_map/ppermute | solution.py:20
  287.5 8.8 %shard_map.301 = (bf16[512,1024]{1,0:T(8,128)(2,1)S(1)}, bf16[512,768]{1,0:T(8,128)(2,1)S(1)}, f32[256,1024]{1,0:T(8,128)S(1)}, bf16[64,1024]{1,0:T(8,128)(2,1)S...) custom-call(bf16[64,1024]{1,0:T(8,128)(2,1)S(1)} %get-tuple-element.366.refs_0_, ...), custom_call_target="tpu_custom_call" | custom-call | flops 90000000 | tf_op jit(solution)/shard_map/pallas_call | solution.py:529
  297.0 2.5 collective-permute-done.105.refs_4_.refs_2_.refs_3_
  300.0 2.3 collective-permute-start.112
  305.2 7.5 %collective-permute-done.106.refs_1_.refs_5_ = bf16[256,1024]{1,0:T(8,128)(2,1)S(1)} collective-permute-done((bf16[256,1024]{1,0:T(8,128)(2,1)S(1)}, bf16[256,1024]{1,0:T(8,128)(2,1)S(1)}, u32[]{:S(2)}, u32[]{:S(2)}) %collective-permute-start.106) | collective-permute-done | bytes 524320 | tf_op jit(solution)/shard_map/ppermute | solution.py:20
  314.3 2.7 shard_map.304
  317.0 1.8 collective-permute-start.119
  319.2 2.1 collective-permute-start.113
  321.4 6.7 %collective-permute-done.113.refs_3_ = bf16[128,1024]{1,0:T(8,128)(2,1)S(1)} collective-permute-done((bf16[128,1024]{1,0:T(8,128)(2,1)S(1)}, bf16[128,1024]{1,0:T(8,128)(2,1)S(1)}, u32[]{:S(2)}, u32[]{:S(2)}) %collective-permute-start.113) | collective-permute-done | bytes 262176 | tf_op jit(solution)/shard_map/ppermute | solution.py:20
  328.7 3.0 collective-permute-done.119.refs_2_.refs_4_
  335.0 1.7 collective-permute-start.117
  337.7 9.3 %collective-permute-done.117.refs_1_.refs_2_ = bf16[32,1792]{1,0:T(8,128)(2,1)S(1)} collective-permute-done((bf16[32,1792]{1,0:T(8,128)(2,1)S(1)}, bf16[32,1792]{1,0:T(8,128)(2,1)S(1)}, u32[]{:S(2)}, u32[]{:S(2)}) %collective-permute-start.117) | collective-permute-done | bytes 114720 | tf_op jit(solution)/shard_map/ppermute | solution.py:20
  348.4 4.3 %collective-permute-start.124 = (bf16[144,1024]{1,0:T(8,128)(2,1)S(1)}, bf16[144,1024]{1,0:T(8,128)(2,1)S(1)}, u32[]{:S(2)}, u32[]{:S(2)}) collective-permute-start(bf16[144,1024]{1,0:T(8,128)(2,1)S(1)} %shard_map.309), channel_id=1, source_target_pairs={{0,2},{2,0},{1,3},{3,1},{4,6},{6,4},{5,7},{7,5},{8,10},{10,8},{9,1... | collective-permute-start | bytes 884744 | tf_op jit(solution)/shard_map/ppermute | solution.py:20
  353.3 15.4 %collective-permute-done.122.refs_8_ = bf16[256,1024]{1,0:T(8,128)(2,1)S(1)} collective-permute-done((bf16[256,1024]{1,0:T(8,128)(2,1)S(1)}, bf16[256,1024]{1,0:T(8,128)(2,1)S(1)}, u32[]{:S(2)}, u32[]{:S(2)}) %collective-permute-start.122) | collective-permute-done | bytes 524320 | tf_op jit(solution)/shard_map/ppermute | solution.py:20
  368.7 4.4 %collective-permute-done.124.refs_10_ = bf16[144,1024]{1,0:T(8,128)(2,1)S(1)} collective-permute-done((bf16[144,1024]{1,0:T(8,128)(2,1)S(1)}, bf16[144,1024]{1,0:T(8,128)(2,1)S(1)}, u32[]{:S(2)}, u32[]{:S(2)}) %collective-permute-start.124) | collective-permute-done | bytes 294944 | tf_op jit(solution)/shard_map/ppermute | solution.py:20
  373.1 1.4 shard_map.310
  374.6 1.9 collective-permute-start.127
  376.4 2.5 collective-permute-start.128
  379.9 6.9 %collective-permute-done.128.refs_8_ = bf16[64,512]{1,0:T(8,128)(2,1)S(1)} collective-permute-done((bf16[64,512]{1,0:T(8,128)(2,1)S(1)}, bf16[64,512]{1,0:T(8,128)(2,1)S(1)}, u32[]{:S(2)}, u32[]{:S(2)}) %collective-permute-start.128) | collective-permute-done | bytes 65568 | tf_op jit(solution)/shard_map/ppermute | solution.py:1446
  386.8 1.7 shard_map.311
  (265 shorter events, 87.1 us)
Async XLA Ops:
  3.0 11.0 %collective-permute-start = (bf16[48,768]{1,0:T(8,128)(2,1)}, bf16[48,768]{1,0:T(8,128)(2,1)S(1)}, u32[]{:S(2)}, u32[]{:S(2)}) collective-permute-start(bf16[48,768]{1,0:T(8,128)(2,1)} %get-tuple-element.225), channel_id=1, source_target_pairs={{0,4},{4,0},{1,5},{5,1},{2,6},{6,2},{3,7},{7,3},{8,12},{12,8},{9,1... | collective-permute-start | bytes 221192 | tf_op jit(solution)/shard_map/ppermute | solution.py:20
  3.1 11.0 %collective-permute-start.1 = (bf16[48,768]{1,0:T(8,128)(2,1)}, bf16[48,768]{1,0:T(8,128)(2,1)S(1)}, u32[]{:S(2)}, u32[]{:S(2)}) collective-permute-start(bf16[48,768]{1,0:T(8,128)(2,1)} %get-tuple-element.226), channel_id=1, source_target_pairs={{0,1},{1,0},{2,3},{3,2},{4,5},{5,4},{6,7},{7,6},{8,9},{9,8},{10,11... | collective-permute-start | bytes 221192 | tf_op jit(solution)/shard_map/ppermute | solution.py:20
  4.8 9.3 %collective-permute-start.2 = (bf16[48,768]{1,0:T(8,128)(2,1)}, bf16[48,768]{1,0:T(8,128)(2,1)S(1)}, u32[]{:S(2)}, u32[]{:S(2)}) collective-permute-start(bf16[48,768]{1,0:T(8,128)(2,1)} %get-tuple-element.227), channel_id=1, source_target_pairs={{0,5},{5,0},{1,4},{4,1},{2,7},{7,2},{3,6},{6,3},{8,13},{13,8},{9,1... | collective-permute-start | bytes 221192 | tf_op jit(solution)/shard_map/ppermute | solution.py:1222
  5.0 9.1 %collective-permute-start.3 = (bf16[64,512]{1,0:T(8,128)(2,1)}, bf16[64,512]{1,0:T(8,128)(2,1)S(1)}, u32[]{:S(2)}, u32[]{:S(2)}) collective-permute-start(bf16[64,512]{1,0:T(8,128)(2,1)} %get-tuple-element.228), channel_id=1, source_target_pairs={{0,0},{1,16},{16,1},{17,17},{2,2},{3,18},{18,3},{19,19},{4,4},{5,2... | collective-permute-start | bytes 196616 | tf_op jit(solution)/shard_map/ppermute | solution.py:1246
  14.8 9.2 %collective-permute-start.6 = (bf16[32,2816]{1,0:T(8,128)(2,1)S(1)}, bf16[32,2816]{1,0:T(8,128)(2,1)S(1)}, u32[]{:S(2)}, u32[]{:S(2)}) collective-permute-start(bf16[32,2816]{1,0:T(8,128)(2,1)S(1)} %get-tuple-element.234), channel_id=1, source_target_pairs={{0,1},{1,0},{2,3},{3,2},{4,5},{5,4},{6,7},{7,6},{8,9},{9,8},{10,11... | collective-permute-start | bytes 540680 | tf_op jit(solution)/shard_map/ppermute | solution.py:20
  16.7 15.6 %collective-permute-start.11 = (bf16[144,1024]{1,0:T(8,128)(2,1)S(1)}, bf16[144,1024]{1,0:T(8,128)(2,1)S(1)}, u32[]{:S(2)}, u32[]{:S(2)}) collective-permute-start(bf16[144,1024]{1,0:T(8,128)(2,1)S(1)} %shard_map.265.refs_0_.refs_5_.refs_10_), channel_id=1, source_target_pairs={{0,16},{16,0},{1,17},{17,1},{2,18},{18,2},{3,19},{19,3},{4,20},{20... | collective-permute-start | bytes 884744 | tf_op jit(solution)/shard_map/ppermute | solution.py:20
  16.8 15.6 %collective-permute-start.10 = (bf16[144,1024]{1,0:T(8,128)(2,1)S(1)}, bf16[144,1024]{1,0:T(8,128)(2,1)S(1)}, u32[]{:S(2)}, u32[]{:S(2)}) collective-permute-start(bf16[144,1024]{1,0:T(8,128)(2,1)S(1)} %shard_map.265.refs_0_.refs_5_.refs_10_), channel_id=1, source_target_pairs={{0,8},{8,0},{1,9},{9,1},{2,10},{10,2},{3,11},{11,3},{4,12},{12,4},... | collective-permute-start | bytes 884744 | tf_op jit(solution)/shard_map/ppermute | solution.py:20
  18.3 18.9 %collective-permute-start.9 = (bf16[144,1024]{1,0:T(8,128)(2,1)S(1)}, bf16[144,1024]{1,0:T(8,128)(2,1)S(1)}, u32[]{:S(2)}, u32[]{:S(2)}) collective-permute-start(bf16[144,1024]{1,0:T(8,128)(2,1)S(1)} %shard_map.265.refs_0_.refs_5_.refs_10_), channel_id=1, source_target_pairs={{0,2},{2,0},{1,3},{3,1},{4,6},{6,4},{5,7},{7,5},{8,10},{10,8},{9,1... | collective-permute-start | bytes 884744 | tf_op jit(solution)/shard_map/ppermute | solution.py:20
  20.9 11.5 %collective-permute-start.8 = (bf16[1,128,1024]{2,1,0:T(8,128)(2,1)S(1)}, bf16[1,128,1024]{2,1,0:T(8,128)(2,1)S(1)}, u32[]{:S(2)}, u32[]{:S(2)}) collective-permute-start(bf16[1,128,1024]{2,1,0:T(8,128)(2,1)S(1)} %copy-done.8), channel_id=1, source_target_pairs={{0,0},{2,4},{4,2},{6,6},{1,1},{3,5},{5,3},{7,7},{8,8},{10,12},{12,... | collective-permute-start | bytes 786440 | tf_op jit(solution)/shard_map/ppermute | solution.py:1214
  24.0 8.2 %collective-permute-start.7 = (bf16[32,2816]{1,0:T(8,128)(2,1)S(1)}, bf16[32,2816]{1,0:T(8,128)(2,1)S(1)}, u32[]{:S(2)}, u32[]{:S(2)}) collective-permute-start(bf16[32,2816]{1,0:T(8,128)(2,1)S(1)} %get-tuple-element.235), channel_id=1, source_target_pairs={{0,5},{5,0},{1,4},{4,1},{2,7},{7,2},{3,6},{6,3},{8,13},{13,8},{9,1... | collective-permute-start | bytes 540680 | tf_op jit(solution)/shard_map/ppermute | solution.py:1222
  37.3 21.5 %collective-permute-start.12 = (bf16[224,1024]{1,0:T(8,128)(2,1)S(1)}, bf16[224,1024]{1,0:T(8,128)(2,1)S(1)}, u32[]{:S(2)}, u32[]{:S(2)}) collective-permute-start(bf16[224,1024]{1,0:T(8,128)(2,1)S(1)} %get-tuple-element.238.refs_0_), channel_id=1, source_target_pairs={{0,8},{8,0},{1,9},{9,1},{2,10},{10,2},{3,11},{11,3},{4,12},{12,4},... | collective-permute-start | bytes 1376264 | tf_op jit(solution)/shard_map/ppermute | solution.py:20
  37.9 20.9 %collective-permute-start.13 = (bf16[208,1024]{1,0:T(8,128)(2,1)S(1)}, bf16[208,1024]{1,0:T(8,128)(2,1)S(1)}, u32[]{:S(2)}, u32[]{:S(2)}) collective-permute-start(bf16[208,1024]{1,0:T(8,128)(2,1)S(1)} %get-tuple-element.239), channel_id=1, source_target_pairs={{0,16},{16,0},{1,17},{17,1},{2,18},{18,2},{3,19},{19,3},{4,20},{20... | collective-permute-start | bytes 1277960 | tf_op jit(solution)/shard_map/ppermute | solution.py:20
  39.6 19.2 %collective-permute-start.14 = (bf16[144,1024]{1,0:T(8,128)(2,1)S(1)}, bf16[144,1024]{1,0:T(8,128)(2,1)S(1)}, u32[]{:S(2)}, u32[]{:S(2)}) collective-permute-start(bf16[144,1024]{1,0:T(8,128)(2,1)S(1)} %collective-permute-done.9.refs_2_.refs_6_.refs_11_), channel_id=1, source_target_pairs={{0,24},{24,0},{8,16},{16,8},{1,25},{25,1},{9,17},{17,9},{2,26},{26... | collective-permute-start | bytes 884744 | tf_op jit(solution)/shard_map/ppermute | solution.py:693
  40.8 9.5 %collective-permute-start.16 = (bf16[1,128,1024]{2,1,0:T(8,128)(2,1)S(1)}, bf16[1,128,1024]{2,1,0:T(8,128)(2,1)S(1)}, u32[]{:S(2)}, u32[]{:S(2)}) collective-permute-start(bf16[1,128,1024]{2,1,0:T(8,128)(2,1)S(1)} %collective-permute-done.8.refs_1_.refs_18_.refs_4_), channel_id=1, source_target_pairs={{0,1},{1,0},{2,3},{3,2},{4,5},{5,4},{6,7},{7,6},{8,9},{9,8},{10,11... | collective-permute-start | bytes 786440 | tf_op jit(solution)/shard_map/ppermute | solution.py:20
  42.4 16.4 %collective-permute-start.15 = (bf16[128,1024]{1,0:T(8,128)(2,1)S(1)}, bf16[128,1024]{1,0:T(8,128)(2,1)S(1)}, u32[]{:S(2)}, u32[]{:S(2)}) collective-permute-start(bf16[128,1024]{1,0:T(8,128)(2,1)S(1)} %get-tuple-element.241), channel_id=1, source_target_pairs={{0,2},{2,0},{1,3},{3,1},{4,6},{6,4},{5,7},{7,5},{8,10},{10,8},{9,1... | collective-permute-start | bytes 786440 | tf_op jit(solution)/shard_map/ppermute | solution.py:20
  58.8 19.0 %collective-permute-start.22 = (bf16[384,1024]{1,0:T(8,128)(2,1)S(1)}, bf16[384,1024]{1,0:T(8,128)(2,1)S(1)}, u32[]{:S(2)}, u32[]{:S(2)}) collective-permute-start(bf16[384,1024]{1,0:T(8,128)(2,1)S(1)} %get-tuple-element.246), channel_id=1, source_target_pairs={{0,16},{16,0},{1,17},{17,1},{2,18},{18,2},{3,19},{19,3},{4,20},{20... | collective-permute-start | bytes 2359304 | tf_op jit(solution)/shard_map/ppermute | solution.py:20
  59.8 18.1 %collective-permute-start.21 = (bf16[384,1024]{1,0:T(8,128)(2,1)S(1)}, bf16[384,1024]{1,0:T(8,128)(2,1)S(1)}, u32[]{:S(2)}, u32[]{:S(2)}) collective-permute-start(bf16[384,1024]{1,0:T(8,128)(2,1)S(1)} %get-tuple-element.246), channel_id=1, source_target_pairs={{0,8},{8,0},{1,9},{9,1},{2,10},{10,2},{3,11},{11,3},{4,12},{12,4},... | collective-permute-start | bytes 2359304 | tf_op jit(solution)/shard_map/ppermute | solution.py:20
  62.2 14.1 %collective-permute-start.20 = (bf16[128,1024]{1,0:T(8,128)(2,1)S(1)}, bf16[128,1024]{1,0:T(8,128)(2,1)S(1)}, u32[]{:S(2)}, u32[]{:S(2)}) collective-permute-start(bf16[128,1024]{1,0:T(8,128)(2,1)S(1)} %get-tuple-element.245), channel_id=1, source_target_pairs={{0,2},{2,0},{1,3},{3,1},{4,6},{6,4},{5,7},{7,5},{8,10},{10,8},{9,1... | collective-permute-start | bytes 786440 | tf_op jit(solution)/shard_map/ppermute | solution.py:20
  80.7 22.3 %collective-permute-start.28 = (bf16[256,1024]{1,0:T(8,128)(2,1)S(1)}, bf16[256,1024]{1,0:T(8,128)(2,1)S(1)}, u32[]{:S(2)}, u32[]{:S(2)}) collective-permute-start(bf16[256,1024]{1,0:T(8,128)(2,1)S(1)} %shard_map.273.refs_0_.refs_3_), channel_id=1, source_target_pairs={{0,1},{1,0},{2,3},{3,2},{4,5},{5,4},{6,7},{7,6},{8,9},{9,8},{10,11... | collective-permute-start | bytes 1572872 | tf_op jit(solution)/shard_map/ppermute | solution.py:20
  81.5 33.5 %collective-permute-start.34 = (bf16[384,1024]{1,0:T(8,128)(2,1)S(1)}, bf16[384,1024]{1,0:T(8,128)(2,1)S(1)}, u32[]{:S(2)}, u32[]{:S(2)}) collective-permute-start(bf16[384,1024]{1,0:T(8,128)(2,1)S(1)} %get-tuple-element.268), channel_id=1, source_target_pairs={{0,16},{16,0},{1,17},{17,1},{2,18},{18,2},{3,19},{19,3},{4,20},{20... | collective-permute-start | bytes 2359304 | tf_op jit(solution)/shard_map/ppermute | solution.py:20
  82.9 32.1 %collective-permute-start.33 = (bf16[384,1024]{1,0:T(8,128)(2,1)S(1)}, bf16[384,1024]{1,0:T(8,128)(2,1)S(1)}, u32[]{:S(2)}, u32[]{:S(2)}) collective-permute-start(bf16[384,1024]{1,0:T(8,128)(2,1)S(1)} %get-tuple-element.261.refs_0_), channel_id=1, source_target_pairs={{0,8},{8,0},{1,9},{9,1},{2,10},{10,2},{3,11},{11,3},{4,12},{12,4},... | collective-permute-start | bytes 2359304 | tf_op jit(solution)/shard_map/ppermute | solution.py:20
  83.5 25.5 %collective-permute-start.23 = (bf16[256,1024]{1,0:T(8,128)(2,1)S(1)}, bf16[256,1024]{1,0:T(8,128)(2,1)S(1)}, u32[]{:S(2)}, u32[]{:S(2)}) collective-permute-start(bf16[256,1024]{1,0:T(8,128)(2,1)S(1)} %get-tuple-element.253.refs_4_.refs_9_.refs_8_.refs_6_.refs_10_), channel_id=1, source_target_pairs={{0,2},{2,0},{1,3},{3,1},{4,6},{6,4},{5,7},{7,5},{8,10},{10,8},{9,1... | collective-permute-start | bytes 1572872 | tf_op jit(solution)/shard_map/ppermute | solution.py:20
  84.5 29.0 %collective-permute-start.35 = (bf16[256,1024]{1,0:T(8,128)(2,1)S(1)}, bf16[256,1024]{1,0:T(8,128)(2,1)S(1)}, u32[]{:S(2)}, u32[]{:S(2)}) collective-permute-start(bf16[256,1024]{1,0:T(8,128)(2,1)S(1)} %get-tuple-element.269), channel_id=1, source_target_pairs={{0,24},{24,0},{8,16},{16,8},{1,25},{25,1},{9,17},{17,9},{2,26},{26... | collective-permute-start | bytes 1572872 | tf_op jit(solution)/shard_map/ppermute | solution.py:693
  103.8 9.8 %collective-permute-start.29 = (bf16[64,1024]{1,0:T(8,128)(2,1)S(1)}, bf16[64,1024]{1,0:T(8,128)(2,1)S(1)}, u32[]{:S(2)}, u32[]{:S(2)}) collective-permute-start(bf16[64,1024]{1,0:T(8,128)(2,1)S(1)} %get-tuple-element.263.refs_1_), channel_id=1, source_target_pairs={{0,4},{4,0},{1,5},{5,1},{2,6},{6,2},{3,7},{7,3},{8,12},{12,8},{9,1... | collective-permute-start | bytes 393224 | tf_op jit(solution)/shard_map/ppermute | solution.py:20
  118.3 29.4 %collective-permute-start.44 = (bf16[448,1024]{1,0:T(8,128)(2,1)S(1)}, bf16[448,1024]{1,0:T(8,128)(2,1)S(1)}, u32[]{:S(2)}, u32[]{:S(2)}) collective-permute-start(bf16[448,1024]{1,0:T(8,128)(2,1)S(1)} %get-tuple-element.280), channel_id=1, source_target_pairs={{0,16},{16,0},{1,17},{17,1},{2,18},{18,2},{3,19},{19,3},{4,20},{20... | collective-permute-start | bytes 2752520 | tf_op jit(solution)/shard_map/ppermute | solution.py:20
  119.7 28.1 %collective-permute-start.43 = (bf16[448,1024]{1,0:T(8,128)(2,1)S(1)}, bf16[448,1024]{1,0:T(8,128)(2,1)S(1)}, u32[]{:S(2)}, u32[]{:S(2)}) collective-permute-start(bf16[448,1024]{1,0:T(8,128)(2,1)S(1)} %get-tuple-element.272.refs_0_), channel_id=1, source_target_pairs={{0,8},{8,0},{1,9},{9,1},{2,10},{10,2},{3,11},{11,3},{4,12},{12,4},... | collective-permute-start | bytes 2752520 | tf_op jit(solution)/shard_map/ppermute | solution.py:20
  123.1 26.7 %collective-permute-start.41 = (bf16[256,1024]{1,0:T(8,128)(2,1)S(1)}, bf16[256,1024]{1,0:T(8,128)(2,1)S(1)}, u32[]{:S(2)}, u32[]{:S(2)}) collective-permute-start(bf16[256,1024]{1,0:T(8,128)(2,1)S(1)} %shard_map.278.refs_3_), channel_id=1, source_target_pairs={{0,1},{1,0},{2,3},{3,2},{4,5},{5,4},{6,7},{7,6},{8,9},{9,8},{10,11... | collective-permute-start | bytes 1572872 | tf_op jit(solution)/shard_map/ppermute | solution.py:20
  124.8 17.1 %collective-permute-start.36 = (bf16[128,1024]{1,0:T(8,128)(2,1)S(1)}, bf16[128,1024]{1,0:T(8,128)(2,1)S(1)}, u32[]{:S(2)}, u32[]{:S(2)}) collective-permute-start(bf16[128,1024]{1,0:T(8,128)(2,1)S(1)} %get-tuple-element.271.refs_5_.refs_9_.refs_7_), channel_id=1, source_target_pairs={{0,2},{2,0},{1,3},{3,1},{4,6},{6,4},{5,7},{7,5},{8,10},{10,8},{9,1... | collective-permute-start | bytes 786440 | tf_op jit(solution)/shard_map/ppermute | solution.py:20
  124.8 23.0 %collective-permute-start.42 = (bf16[128,1024]{1,0:T(8,128)(2,1)S(1)}, bf16[128,1024]{1,0:T(8,128)(2,1)S(1)}, u32[]{:S(2)}, u32[]{:S(2)}) collective-permute-start(bf16[128,1024]{1,0:T(8,128)(2,1)S(1)} %get-tuple-element.279), channel_id=1, source_target_pairs={{0,24},{24,0},{8,16},{16,8},{1,25},{25,1},{9,17},{17,9},{2,26},{26... | collective-permute-start | bytes 786440 | tf_op jit(solution)/shard_map/ppermute | solution.py:693
  147.8 14.5 %collective-permute-start.50 = (bf16[256,1024]{1,0:T(8,128)(2,1)S(1)}, bf16[256,1024]{1,0:T(8,128)(2,1)S(1)}, u32[]{:S(2)}, u32[]{:S(2)}) collective-permute-start(bf16[256,1024]{1,0:T(8,128)(2,1)S(1)} %get-tuple-element.281.refs_0_), channel_id=1, source_target_pairs={{0,16},{16,0},{1,17},{17,1},{2,18},{18,2},{3,19},{19,3},{4,20},{20... | collective-permute-start | bytes 1572872 | tf_op jit(solution)/shard_map/ppermute | solution.py:20
  149.2 13.2 %collective-permute-start.49 = (bf16[256,1024]{1,0:T(8,128)(2,1)S(1)}, bf16[256,1024]{1,0:T(8,128)(2,1)S(1)}, u32[]{:S(2)}, u32[]{:S(2)}) collective-permute-start(bf16[256,1024]{1,0:T(8,128)(2,1)S(1)} %get-tuple-element.281.refs_0_), channel_id=1, source_target_pairs={{0,8},{8,0},{1,9},{9,1},{2,10},{10,2},{3,11},{11,3},{4,12},{12,4},... | collective-permute-start | bytes 1572872 | tf_op jit(solution)/shard_map/ppermute | solution.py:20
  165.1 17.0 %collective-permute-start.55 = (bf16[256,1024]{1,0:T(8,128)(2,1)S(1)}, bf16[256,1024]{1,0:T(8,128)(2,1)S(1)}, u32[]{:S(2)}, u32[]{:S(2)}) collective-permute-start(bf16[256,1024]{1,0:T(8,128)(2,1)S(1)} %shard_map.283.refs_2_), channel_id=1, source_target_pairs={{0,1},{1,0},{2,3},{3,2},{4,5},{5,4},{6,7},{7,6},{8,9},{9,8},{10,11... | collective-permute-start | bytes 1572872 | tf_op jit(solution)/shard_map/ppermute | solution.py:20
  166.8 19.2 %collective-permute-start.62 = (bf16[256,1024]{1,0:T(8,128)(2,1)S(1)}, bf16[256,1024]{1,0:T(8,128)(2,1)S(1)}, u32[]{:S(2)}, u32[]{:S(2)}) collective-permute-start(bf16[256,1024]{1,0:T(8,128)(2,1)S(1)} %get-tuple-element.281.refs_0_), channel_id=1, source_target_pairs={{0,24},{24,0},{8,16},{16,8},{1,25},{25,1},{9,17},{17,9},{2,26},{26... | collective-permute-start | bytes 1572872 | tf_op jit(solution)/shard_map/ppermute | solution.py:693
  169.8 17.3 %collective-permute-start.60 = (bf16[128,1024]{1,0:T(8,128)(2,1)S(1)}, bf16[128,1024]{1,0:T(8,128)(2,1)S(1)}, u32[]{:S(2)}, u32[]{:S(2)}) collective-permute-start(bf16[128,1024]{1,0:T(8,128)(2,1)S(1)} %get-tuple-element.304), channel_id=1, source_target_pairs={{0,8},{8,0},{1,9},{9,1},{2,10},{10,2},{3,11},{11,3},{4,12},{12,4},... | collective-permute-start | bytes 786440 | tf_op jit(solution)/shard_map/ppermute | solution.py:20
  171.3 15.9 %collective-permute-start.61 = (bf16[128,1024]{1,0:T(8,128)(2,1)S(1)}, bf16[128,1024]{1,0:T(8,128)(2,1)S(1)}, u32[]{:S(2)}, u32[]{:S(2)}) collective-permute-start(bf16[128,1024]{1,0:T(8,128)(2,1)S(1)} %get-tuple-element.305), channel_id=1, source_target_pairs={{0,16},{16,0},{1,17},{17,1},{2,18},{18,2},{3,19},{19,3},{4,20},{20... | collective-permute-start | bytes 786440 | tf_op jit(solution)/shard_map/ppermute | solution.py:20
  172.1 20.2 %collective-permute-start.71 = (bf16[128,1024]{1,0:T(8,128)(2,1)S(1)}, bf16[128,1024]{1,0:T(8,128)(2,1)S(1)}, u32[]{:S(2)}, u32[]{:S(2)}) collective-permute-start(bf16[128,1024]{1,0:T(8,128)(2,1)S(1)} %collective-permute-done.69.refs_1_), channel_id=1, source_target_pairs={{0,1},{1,0},{2,3},{3,2},{4,5},{5,4},{6,7},{7,6},{8,9},{9,8},{10,11... | collective-permute-start | bytes 786440 | tf_op jit(solution)/shard_map/ppermute | solution.py:20
  194.7 8.5 %collective-permute-start.67 = (bf16[128,1024]{1,0:T(8,128)(2,1)S(1)}, bf16[128,1024]{1,0:T(8,128)(2,1)S(1)}, u32[]{:S(2)}, u32[]{:S(2)}) collective-permute-start(bf16[128,1024]{1,0:T(8,128)(2,1)S(1)} %get-tuple-element.312), channel_id=1, source_target_pairs={{0,1},{1,0},{2,3},{3,2},{4,5},{5,4},{6,7},{7,6},{8,9},{9,8},{10,11... | collective-permute-start | bytes 786440 | tf_op jit(solution)/shard_map/ppermute | solution.py:20
  203.3 13.3 %collective-permute-start.77 = (bf16[256,1024]{1,0:T(8,128)(2,1)S(1)}, bf16[256,1024]{1,0:T(8,128)(2,1)S(1)}, u32[]{:S(2)}, u32[]{:S(2)}) collective-permute-start(bf16[256,1024]{1,0:T(8,128)(2,1)S(1)} %shard_map.290.refs_0_.refs_3_), channel_id=1, source_target_pairs={{0,1},{1,0},{2,3},{3,2},{4,5},{5,4},{6,7},{7,6},{8,9},{9,8},{10,11... | collective-permute-start | bytes 1572872 | tf_op jit(solution)/shard_map/ppermute | solution.py:20
  206.5 30.3 %collective-permute-start.86 = (bf16[512,1024]{1,0:T(8,128)(2,1)S(1)}, bf16[512,1024]{1,0:T(8,128)(2,1)S(1)}, u32[]{:S(2)}, u32[]{:S(2)}) collective-permute-start(bf16[512,1024]{1,0:T(8,128)(2,1)S(1)} %get-tuple-element.342), channel_id=1, source_target_pairs={{0,16},{16,0},{1,17},{17,1},{2,18},{18,2},{3,19},{19,3},{4,20},{20... | collective-permute-start | bytes 3145736 | tf_op jit(solution)/shard_map/ppermute | solution.py:20
  207.7 29.2 %collective-permute-start.87 = (bf16[512,1024]{1,0:T(8,128)(2,1)S(1)}, bf16[512,1024]{1,0:T(8,128)(2,1)S(1)}, u32[]{:S(2)}, u32[]{:S(2)}) collective-permute-start(bf16[512,1024]{1,0:T(8,128)(2,1)S(1)} %get-tuple-element.343), channel_id=1, source_target_pairs={{0,8},{8,0},{1,9},{9,1},{2,10},{10,2},{3,11},{11,3},{4,12},{12,4},... | collective-permute-start | bytes 3145736 | tf_op jit(solution)/shard_map/ppermute | solution.py:20
  236.2 15.9 %collective-permute-start.88 = (bf16[256,1024]{1,0:T(8,128)(2,1)S(1)}, bf16[256,1024]{1,0:T(8,128)(2,1)S(1)}, u32[]{:S(2)}, u32[]{:S(2)}) collective-permute-start(bf16[256,1024]{1,0:T(8,128)(2,1)S(1)} %shard_map.294.refs_0_.refs_2_), channel_id=1, source_target_pairs={{0,1},{1,0},{2,3},{3,2},{4,5},{5,4},{6,7},{7,6},{8,9},{9,8},{10,11... | collective-permute-start | bytes 1572872 | tf_op jit(solution)/shard_map/ppermute | solution.py:20
  238.7 24.9 %collective-permute-start.97 = (bf16[512,1024]{1,0:T(8,128)(2,1)S(1)}, bf16[512,1024]{1,0:T(8,128)(2,1)S(1)}, u32[]{:S(2)}, u32[]{:S(2)}) collective-permute-start(bf16[512,1024]{1,0:T(8,128)(2,1)S(1)} %get-tuple-element.361), channel_id=1, source_target_pairs={{0,16},{16,0},{1,17},{17,1},{2,18},{18,2},{3,19},{19,3},{4,20},{20... | collective-permute-start | bytes 3145736 | tf_op jit(solution)/shard_map/ppermute | solution.py:20
  240.1 23.5 %collective-permute-start.98 = (bf16[512,1024]{1,0:T(8,128)(2,1)S(1)}, bf16[512,1024]{1,0:T(8,128)(2,1)S(1)}, u32[]{:S(2)}, u32[]{:S(2)}) collective-permute-start(bf16[512,1024]{1,0:T(8,128)(2,1)S(1)} %get-tuple-element.362), channel_id=1, source_target_pairs={{0,8},{8,0},{1,9},{9,1},{2,10},{10,2},{3,11},{11,3},{4,12},{12,4},... | collective-permute-start | bytes 3145736 | tf_op jit(solution)/shard_map/ppermute | solution.py:20
  266.6 30.3 %collective-permute-start.104 = (bf16[640,1024]{1,0:T(8,128)(2,1)S(1)}, bf16[640,1024]{1,0:T(8,128)(2,1)S(1)}, u32[]{:S(2)}, u32[]{:S(2)}) collective-permute-start(bf16[640,1024]{1,0:T(8,128)(2,1)S(1)} %get-tuple-element.374), channel_id=1, source_target_pairs={{0,16},{16,0},{1,17},{17,1},{2,18},{18,2},{3,19},{19,3},{4,20},{20... | collective-permute-start | bytes 3932168 | tf_op jit(solution)/shard_map/ppermute | solution.py:20
  268.1 31.3 %collective-permute-start.105 = (bf16[640,1024]{1,0:T(8,128)(2,1)S(1)}, bf16[640,1024]{1,0:T(8,128)(2,1)S(1)}, u32[]{:S(2)}, u32[]{:S(2)}) collective-permute-start(bf16[640,1024]{1,0:T(8,128)(2,1)S(1)} %get-tuple-element.375), channel_id=1, source_target_pairs={{0,8},{8,0},{1,9},{9,1},{2,10},{10,2},{3,11},{11,3},{4,12},{12,4},... | collective-permute-start | bytes 3932168 | tf_op jit(solution)/shard_map/ppermute | solution.py:20
  268.5 14.5 %collective-permute-start.99 = (bf16[256,1024]{1,0:T(8,128)(2,1)S(1)}, bf16[256,1024]{1,0:T(8,128)(2,1)S(1)}, u32[]{:S(2)}, u32[]{:S(2)}) collective-permute-start(bf16[256,1024]{1,0:T(8,128)(2,1)S(1)} %shard_map.298.refs_0_.refs_2_), channel_id=1, source_target_pairs={{0,1},{1,0},{2,3},{3,2},{4,5},{5,4},{6,7},{7,6},{8,9},{9,8},{10,11... | collective-permute-start | bytes 1572872 | tf_op jit(solution)/shard_map/ppermute | solution.py:20
  286.5 26.1 %collective-permute-start.106 = (bf16[256,1024]{1,0:T(8,128)(2,1)S(1)}, bf16[256,1024]{1,0:T(8,128)(2,1)S(1)}, u32[]{:S(2)}, u32[]{:S(2)}) collective-permute-start(bf16[256,1024]{1,0:T(8,128)(2,1)S(1)} %get-tuple-element.378), channel_id=1, source_target_pairs={{0,2},{2,0},{1,3},{3,1},{4,6},{6,4},{5,7},{7,5},{8,10},{10,8},{9,1... | collective-permute-start | bytes 1572872 | tf_op jit(solution)/shard_map/ppermute | solution.py:20
  299.7 14.3 %collective-permute-start.111 = (bf16[256,1024]{1,0:T(8,128)(2,1)S(1)}, bf16[256,1024]{1,0:T(8,128)(2,1)S(1)}, u32[]{:S(2)}, u32[]{:S(2)}) collective-permute-start(bf16[256,1024]{1,0:T(8,128)(2,1)S(1)} %get-tuple-element.384), channel_id=1, source_target_pairs={{0,8},{8,0},{1,9},{9,1},{2,10},{10,2},{3,11},{11,3},{4,12},{12,4},... | collective-permute-start | bytes 1572872 | tf_op jit(solution)/shard_map/ppermute | solution.py:20
  300.0 14.2 %collective-permute-start.112 = (bf16[256,1024]{1,0:T(8,128)(2,1)S(1)}, bf16[256,1024]{1,0:T(8,128)(2,1)S(1)}, u32[]{:S(2)}, u32[]{:S(2)}) collective-permute-start(bf16[256,1024]{1,0:T(8,128)(2,1)S(1)} %get-tuple-element.385), channel_id=1, source_target_pairs={{0,16},{16,0},{1,17},{17,1},{2,18},{18,2},{3,19},{19,3},{4,20},{20... | collective-permute-start | bytes 1572872 | tf_op jit(solution)/shard_map/ppermute | solution.py:20
  317.0 14.8 %collective-permute-start.119 = (bf16[288,1024]{1,0:T(8,128)(2,1)S(1)}, bf16[288,1024]{1,0:T(8,128)(2,1)S(1)}, u32[]{:S(2)}, u32[]{:S(2)}) collective-permute-start(bf16[288,1024]{1,0:T(8,128)(2,1)S(1)} %get-tuple-element.403), channel_id=1, source_target_pairs={{0,16},{16,0},{1,17},{17,1},{2,18},{18,2},{3,19},{19,3},{4,20},{20... | collective-permute-start | bytes 1769480 | tf_op jit(solution)/shard_map/ppermute | solution.py:20
  318.8 14.0 %collective-permute-start.120 = (bf16[288,1024]{1,0:T(8,128)(2,1)S(1)}, bf16[288,1024]{1,0:T(8,128)(2,1)S(1)}, u32[]{:S(2)}, u32[]{:S(2)}) collective-permute-start(bf16[288,1024]{1,0:T(8,128)(2,1)S(1)} %get-tuple-element.405), channel_id=1, source_target_pairs={{0,8},{8,0},{1,9},{9,1},{2,10},{10,2},{3,11},{11,3},{4,12},{12,4},... | collective-permute-start | bytes 1769480 | tf_op jit(solution)/shard_map/ppermute | solution.py:20
  319.2 9.0 %collective-permute-start.113 = (bf16[128,1024]{1,0:T(8,128)(2,1)S(1)}, bf16[128,1024]{1,0:T(8,128)(2,1)S(1)}, u32[]{:S(2)}, u32[]{:S(2)}) collective-permute-start(bf16[128,1024]{1,0:T(8,128)(2,1)S(1)} %get-tuple-element.396), channel_id=1, source_target_pairs={{0,1},{1,0},{2,3},{3,2},{4,5},{5,4},{6,7},{7,6},{8,9},{9,8},{10,11... | collective-permute-start | bytes 786440 | tf_op jit(solution)/shard_map/ppermute | solution.py:20
  321.2 13.2 %collective-permute-start.115 = (bf16[128,1024]{1,0:T(8,128)(2,1)S(1)}, bf16[128,1024]{1,0:T(8,128)(2,1)S(1)}, u32[]{:S(2)}, u32[]{:S(2)}) collective-permute-start(bf16[128,1024]{1,0:T(8,128)(2,1)S(1)} %get-tuple-element.377.refs_0_), channel_id=1, source_target_pairs={{0,2},{2,0},{1,3},{3,1},{4,6},{6,4},{5,7},{7,5},{8,10},{10,8},{9,1... | collective-permute-start | bytes 786440 | tf_op jit(solution)/shard_map/ppermute | solution.py:20
  332.9 15.4 %collective-permute-start.123 = (bf16[144,1024]{1,0:T(8,128)(2,1)S(1)}, bf16[144,1024]{1,0:T(8,128)(2,1)S(1)}, u32[]{:S(2)}, u32[]{:S(2)}) collective-permute-start(bf16[144,1024]{1,0:T(8,128)(2,1)S(1)} %get-tuple-element.410), channel_id=1, source_target_pairs={{0,16},{16,0},{1,17},{17,1},{2,18},{18,2},{3,19},{19,3},{4,20},{20... | collective-permute-start | bytes 884744 | tf_op jit(solution)/shard_map/ppermute | solution.py:20
  333.7 35.0 %collective-permute-start.122 = (bf16[256,1024]{1,0:T(8,128)(2,1)S(1)}, bf16[256,1024]{1,0:T(8,128)(2,1)S(1)}, u32[]{:S(2)}, u32[]{:S(2)}) collective-permute-start(bf16[256,1024]{1,0:T(8,128)(2,1)S(1)} %shard_map.305.refs_0_), channel_id=1, source_target_pairs={{0,2},{2,0},{1,3},{3,1},{4,6},{6,4},{5,7},{7,5},{8,10},{10,8},{9,1... | collective-permute-start | bytes 1572872 | tf_op jit(solution)/shard_map/ppermute | solution.py:20
  335.0 12.1 %collective-permute-start.117 = (bf16[32,1792]{1,0:T(8,128)(2,1)S(1)}, bf16[32,1792]{1,0:T(8,128)(2,1)S(1)}, u32[]{:S(2)}, u32[]{:S(2)}) collective-permute-start(bf16[32,1792]{1,0:T(8,128)(2,1)S(1)} %get-tuple-element.401), channel_id=1, source_target_pairs={{0,1},{1,0},{2,3},{3,2},{4,5},{5,4},{6,7},{7,6},{8,9},{9,8},{10,11... | collective-permute-start | bytes 344072 | tf_op jit(solution)/shard_map/ppermute | solution.py:20
  336.7 11.6 %collective-permute-start.118 = (bf16[32,1792]{1,0:T(8,128)(2,1)S(1)}, bf16[32,1792]{1,0:T(8,128)(2,1)S(1)}, u32[]{:S(2)}, u32[]{:S(2)}) collective-permute-start(bf16[32,1792]{1,0:T(8,128)(2,1)S(1)} %get-tuple-element.402), channel_id=1, source_target_pairs={{0,5},{5,0},{1,4},{4,1},{2,7},{7,2},{3,6},{6,3},{8,13},{13,8},{9,1... | collective-permute-start | bytes 344072 | tf_op jit(solution)/shard_map/ppermute | solution.py:1222
  336.8 31.9 %collective-permute-start.121 = (bf16[144,1024]{1,0:T(8,128)(2,1)S(1)}, bf16[144,1024]{1,0:T(8,128)(2,1)S(1)}, u32[]{:S(2)}, u32[]{:S(2)}) collective-permute-start(bf16[144,1024]{1,0:T(8,128)(2,1)S(1)} %get-tuple-element.406), channel_id=1, source_target_pairs={{0,8},{8,0},{1,9},{9,1},{2,10},{10,2},{3,11},{11,3},{4,12},{12,4},... | collective-permute-start | bytes 884744 | tf_op jit(solution)/shard_map/ppermute | solution.py:20
  348.4 24.7 %collective-permute-start.124 = (bf16[144,1024]{1,0:T(8,128)(2,1)S(1)}, bf16[144,1024]{1,0:T(8,128)(2,1)S(1)}, u32[]{:S(2)}, u32[]{:S(2)}) collective-permute-start(bf16[144,1024]{1,0:T(8,128)(2,1)S(1)} %shard_map.309), channel_id=1, source_target_pairs={{0,2},{2,0},{1,3},{3,1},{4,6},{6,4},{5,7},{7,5},{8,10},{10,8},{9,1... | collective-permute-start | bytes 884744 | tf_op jit(solution)/shard_map/ppermute | solution.py:20
  352.7 26.3 %collective-permute-start.114 = (bf16[1,128,1024]{2,1,0:T(8,128)(2,1)S(1)}, bf16[1,128,1024]{2,1,0:T(8,128)(2,1)S(1)}, u32[]{:S(2)}, u32[]{:S(2)}) collective-permute-start(bf16[1,128,1024]{2,1,0:T(8,128)(2,1)S(1)} %shard_map.306.refs_0_), channel_id=1, source_target_pairs={{0,0},{2,4},{4,2},{6,6},{1,1},{3,5},{5,3},{7,7},{8,8},{10,12},{12,... | collective-permute-start | bytes 786440 | tf_op jit(solution)/shard_map/ppermute | solution.py:1214
  374.6 12.2 %collective-permute-start.125 = (bf16[48,1792]{1,0:T(8,128)(2,1)S(1)}, bf16[48,1792]{1,0:T(8,128)(2,1)S(1)}, u32[]{:S(2)}, u32[]{:S(2)}) collective-permute-start(bf16[48,1792]{1,0:T(8,128)(2,1)S(1)} %get-tuple-element.415), channel_id=1, source_target_pairs={{0,4},{4,0},{1,5},{5,1},{2,6},{6,2},{3,7},{7,3},{8,12},{12,8},{9,1... | collective-permute-start | bytes 516104 | tf_op jit(solution)/shard_map/ppermute | solution.py:20
  374.6 12.2 %collective-permute-start.126 = (bf16[48,1792]{1,0:T(8,128)(2,1)S(1)}, bf16[48,1792]{1,0:T(8,128)(2,1)S(1)}, u32[]{:S(2)}, u32[]{:S(2)}) collective-permute-start(bf16[48,1792]{1,0:T(8,128)(2,1)S(1)} %get-tuple-element.416), channel_id=1, source_target_pairs={{0,1},{1,0},{2,3},{3,2},{4,5},{5,4},{6,7},{7,6},{8,9},{9,8},{10,11... | collective-permute-start | bytes 516104 | tf_op jit(solution)/shard_map/ppermute | solution.py:20
  374.6 12.2 %collective-permute-start.127 = (bf16[48,1792]{1,0:T(8,128)(2,1)S(1)}, bf16[48,1792]{1,0:T(8,128)(2,1)S(1)}, u32[]{:S(2)}, u32[]{:S(2)}) collective-permute-start(bf16[48,1792]{1,0:T(8,128)(2,1)S(1)} %get-tuple-element.417), channel_id=1, source_target_pairs={{0,5},{5,0},{1,4},{4,1},{2,7},{7,2},{3,6},{6,3},{8,13},{13,8},{9,1... | collective-permute-start | bytes 516104 | tf_op jit(solution)/shard_map/ppermute | solution.py:1222
  376.4 10.3 %collective-permute-start.128 = (bf16[64,512]{1,0:T(8,128)(2,1)S(1)}, bf16[64,512]{1,0:T(8,128)(2,1)S(1)}, u32[]{:S(2)}, u32[]{:S(2)}) collective-permute-start(bf16[64,512]{1,0:T(8,128)(2,1)S(1)} %get-tuple-element.418), channel_id=1, source_target_pairs={{0,0},{1,16},{16,1},{17,17},{2,2},{3,18},{18,3},{19,19},{4,4},{5,2... | collective-permute-start | bytes 196616 | tf_op jit(solution)/shard_map/ppermute | solution.py:1446
  (75 other events, 227.8 us)

commit v5 on v4

--- a/solution.py
+++ b/solution.py
@@ -774,27 +774,25 @@
 
 
 def attend(qkv, dist, probs, o):
-    low = lax.broadcasted_iota(jnp.int32, (128, 128), 1) < 64
-    for pair in range(2):
-        k = qkv[:, 256 + pair * 128 : 384 + pair * 128]
-        v = qkv[:, 512 + pair * 128 : 640 + pair * 128]
-
-        def rows(step, carry):
-            spot = at(step, 128)
-            q = qkv[spot, pair * 128 : pair * 128 + 128]
-            d = dist[spot, :]
-            found = []
-            for half in range(2):
-                qh = jnp.where(low == (half == 0), q, jnp.zeros_like(q))
-                s = dot_t(qh, k) * 0.125 - slope_of(pair, half) * d
-                p = jnp.exp(s - jnp.max(s, axis=1, keepdims=True))
-                p = (p / jnp.sum(p, axis=1, keepdims=True)).astype(BF)
-                probs[pair * 2 + half, spot, :] = p
-                found.append(dot(p, v))
-            o[spot, pair * 128 : pair * 128 + 128] = jnp.where(low, *found).astype(BF)
-            return carry
-
-        lax.fori_loop(0, 4, rows, 0)
+    low = lax.broadcasted_iota(jnp.int32, (512, 128), 1) < 64
+
+    def heads(pair, carry):
+        q = qkv[:, at(pair, 128)]
+        k = qkv[:, at(2 + pair, 128)]
+        v = qkv[:, at(4 + pair, 128)]
+        found = []
+        for half in range(2):
+            qh = jnp.where(low == (half == 0), q, jnp.zeros_like(q))
+            slope = jnp.where(pair == 0, slope_of(0, half), slope_of(1, half))
+            s = dot_t(qh, k) * 0.125 - slope * dist[...]
+            p = jnp.exp(s - jnp.max(s, axis=1, keepdims=True))
+            p = (p / jnp.sum(p, axis=1, keepdims=True)).astype(BF)
+            probs[pair * 2 + half] = p
+            found.append(dot(p, v))
+        o[:, at(pair, 128)] = jnp.where(low, *found).astype(BF)
+        return carry
+
+    lax.fori_loop(0, 2, heads, 0)
 
 
 def attention_part(h1, vec, layer, pieces, seg_a, seg_b, order, outs, scratch):
@@ -810,7 +808,7 @@
 
 def first_attention(t0, t1, t2, t3, *refs):
     pieces, (seg_a, seg_b, order), refs = att_0_slots(refs[:7]), refs[7:10], refs[10:]
-    vec, h1, outs, scratch = refs[0], refs[1], refs[2:10], refs[10:]
+    vec, h1, outs, scratch = refs[0], refs[1], refs[2:8], refs[8:]
     q_one, q_two, scratch = scratch[0], scratch[1], scratch[2:]
     for r, block in slot_blocks():
         vec[:, at(block, 128)] = pieces[r][128:144, 0:128].astype(F32)
@@ -833,15 +831,15 @@
 
 
 def next_attention(*refs):
-    mine, other, refs = refs[:4], refs[4:8], refs[8:]
+    mine, other, refs = refs[:2], refs[2:4], refs[4:]
     pieces, (vec, seg_a, seg_b, order), refs = att_1_slots(refs[:7]), refs[7:11], refs[11:]
-    h1, outs, scratch = refs[0], refs[1:9], refs[9:]
+    h1, outs, scratch = refs[0], refs[1:7], refs[7:]
     load_cores(mine, other, h1)
     attention_part(h1, vec, 1, pieces, seg_a, seg_b, order, outs, scratch)
 
 
 def add_parts(keep, *refs):
-    came, out = Rows(refs[:4]), refs[4]
+    came, out = Rows(refs[:2]), refs[2]
     out[...] = (keep[...] + came[...].astype(F32)).astype(BF)
 
 
@@ -860,7 +858,7 @@
 
 
 def first_norm_stage(t0, t2, part, came, vec, *refs):
-    x_out, h, x0 = refs[0], refs[1:5], refs[5]
+    x_out, h, x0 = refs[0], refs[1:3], refs[3]
     x0[at(bit("zl", 0), 128), :] = inner_columns(t0[0].astype(F32))
     x0[at(bit("zl", 1), 128), :] = inner_columns(t2[0].astype(F32))
     norm_stage(2, 3)(x0, part, came, vec, x_out, *h)
@@ -873,7 +871,7 @@
 
 def mlp_stage(layer):
     def kernel(*refs):
-        mine, other, refs = refs[:4], refs[4:8], refs[8:]
+        mine, other, refs = refs[:2], refs[2:4], refs[4:]
         pieces, refs = mlp_weights(refs, layer)
         vec, h2, u, a, keep, *send, w = refs
         load_cores(mine, other, h2)
@@ -895,7 +893,7 @@
 
 
 def add_split(keep, *refs):
-    came, mine, other = Rows(refs[:4]), refs[4], refs[5]
+    came, mine, other = Rows(refs[:2]), refs[2], refs[3]
     for to, flip in ((mine, 0), (other, 1)):
         which = bit("zl", flip)
         to[...] = (keep[at(which, 128), :] + came.block(which).astype(F32)).astype(BF)
@@ -912,9 +910,9 @@
         if layer == 1:
             blocks, u, refs = refs[:4], refs[4], refs[5:]
         else:
-            blocks, u, refs = refs[:8], refs[8], refs[9:]
+            blocks, u, refs = refs[:4], refs[4], refs[5:]
         pieces, (gy2, gu, keep, *send, w) = mlp_weights(refs, layer)
-        load_blocks(blocks, gy2) if layer == 1 else load_cores(blocks[:4], blocks[4:], gy2)
+        load_blocks(blocks, gy2) if layer == 1 else load_cores(blocks[:2], blocks[2:], gy2)
         load_rows(pieces, w, 128, 1024)
         for i in range(4):
             spot = slice(i * 128, i * 128 + 128)
@@ -973,13 +971,13 @@
 
 def norm_back_stage(gain_row):
     def kernel(gx, part, came, x, vec, gm, *refs):
-        norm_back(gx, part, came, x, vec[gain_row : gain_row + 1, :], gm, Rows(refs[:4]), refs[4])
+        norm_back(gx, part, came, x, vec[gain_row : gain_row + 1, :], gm, Rows(refs[:2]), refs[2])
 
     return kernel
 
 
 def first_norm_back(c0, c2, part, came, x, vec, gm, *refs):
-    gy, sums, gx = Rows(refs[:4]), refs[4], refs[5]
+    gy, sums, gx = Rows(refs[:2]), refs[2], refs[3]
     gx[at(bit("zl", 0), 128), :] = c0[...].astype(F32)
     gx[at(bit("zl", 1), 128), :] = c2[...].astype(F32)
     norm_back(gx, part, came, x, vec[11:12, :], gm, gy, sums)
@@ -994,7 +992,7 @@
 
 def attention_back(layer):
     def kernel(*refs):
-        mine, other, (qkv, probs), refs = refs[:4], refs[4:8], refs[8:10], refs[10:]
+        mine, other, (qkv, probs), refs = refs[:2], refs[2:4], refs[4:6], refs[6:]
         pieces = (att_1_slots if layer else att_0_slots)(refs[:7])
         attention_back_part(mine, other, qkv, probs, pieces, *refs[7:])
 
@@ -1007,36 +1005,28 @@
     load_rows(pieces, wq, 0, 768)
     load_out(pieces, wo)
     go[...] = dot_t(gy1[...], wo[...]).astype(BF)
-    low = lax.broadcasted_iota(jnp.int32, (128, 128), 1) < 64
-    low_all = lax.broadcasted_iota(jnp.int32, (512, 128), 1) < 64
-    for pair in range(2):
-        k = qkv[:, 256 + pair * 128 : 384 + pair * 128]
-        v = qkv[:, 512 + pair * 128 : 640 + pair * 128]
-        gk[...] = jnp.zeros_like(gk)
-        gv[...] = jnp.zeros_like(gv)
-
-        def rows(step, carry):
-            spot = at(step, 128)
-            q = qkv[spot, pair * 128 : pair * 128 + 128]
-            g = go[spot, pair * 128 : pair * 128 + 128]
-            gq = []
-            for half in range(2):
-                lanes = low == (half == 0)
-                gh = jnp.where(lanes, g, jnp.zeros_like(g))
-                qh = jnp.where(lanes, q, jnp.zeros_like(q))
-                p = probs[pair * 2 + half, spot, :]
-                pf = p.astype(F32)
-                dp = dot_t(gh, v)
-                ds = (pf * (dp - jnp.sum(dp * pf, axis=1, keepdims=True))).astype(BF)
-                gq.append(dot(ds, k))
-                gk[...] += turned_dot(ds, qh)
-                gv[...] += turned_dot(p, gh)
-            gqkv[spot, pair * 128 : pair * 128 + 128] = (0.125 * jnp.where(low, *gq)).astype(BF)
-            return carry
-
-        lax.fori_loop(0, 4, rows, 0)
-        gqkv[:, 256 + pair * 128 : 384 + pair * 128] = (0.125 * gk[...]).astype(BF)
-        gqkv[:, 512 + pair * 128 : 640 + pair * 128] = gv[...].astype(BF)
+    low = lax.broadcasted_iota(jnp.int32, (512, 128), 1) < 64
+
+    def heads(pair, carry):
+        q = qkv[:, at(pair, 128)]
+        k = qkv[:, at(2 + pair, 128)]
+        v = qkv[:, at(4 + pair, 128)]
+        g = go[:, at(pair, 128)]
+        found = []
+        for half in range(2):
+            lanes = low == (half == 0)
+            gh = jnp.where(lanes, g, jnp.zeros_like(g))
+            p = probs[pair * 2 + half]
+            pf = p.astype(F32)
+            dp = dot_t(gh, v)
+            ds = (pf * (dp - jnp.sum(dp * pf, axis=1, keepdims=True))).astype(BF)
+            found.append((dot(ds, k), turned_dot(ds, q), turned_dot(p, g)))
+        for part, scale in ((0, 0.125), (1, 0.125), (2, 1.0)):
+            value = scale * jnp.where(low, found[0][part], found[1][part])
+            gqkv[:, at(part * 2 + pair, 128)] = value.astype(BF)
+        return carry
+
+    lax.fori_loop(0, 2, heads, 0)
     split_product(gqkv, lambda rows: dot_t(rows, wq[...]), keep, send)
 
 
@@ -1071,7 +1061,7 @@
 
 
 def window_5(*refs):
-    grads, (to_y, to_x), rest = refs[:19], refs[19:21], refs[21:]
+    grads, (to_y, to_x), rest = refs[:17], refs[17:19], refs[19:]
     last_attention_grads(*grads, (to_y, to_x) + rest[:4], *rest[4:])
 
 
@@ -1088,10 +1078,10 @@
 
 
 def last_attention_grads(
-    h1, o, gy1, gqkv, g1, e1, e0, gu1, gu0, gq1, keep, s0, s1, s2, s3, t0, t1, t2, t3, outs, d_out, ups, wide
+    h1, o, gy1, gqkv, g1, e1, e0, gu1, gu0, gq1, keep, s0, s1, t0, t1, t2, t3, outs, d_out, ups, wide
 ):
     spots = attention_grads(144, h1, o, gy1, gqkv, outs, d_out)
-    send = Rows((s0, s1, s2, s3))
+    send = Rows((s0, s1))
     none = jnp.zeros((2, 1024), F32)
     gain = jnp.zeros((1, 1024), F32)
     shift = jnp.zeros((1, 1024), F32)
@@ -1233,7 +1223,7 @@
         return [pltpu.VMEM(v, BF) for v in values] + [pltpu.SemaphoreType.DMA((len(values),))]
 
     row, rowf = shape(256, 1024), shape(256, 1024, dtype=F32)
-    quarters = [shape(64, 1024)] * 4
+    halves = [shape(128, 1024)] * 2
 
     ready = run(
         with_scratch(
@@ -1293,12 +1283,12 @@
         return (*values, *cores(values))
 
     attention_outs = [
-        shape(512, 1024), shape(512, 768), shape(4, 512, 512), shape(512, 256), rowf, *quarters,
+        shape(512, 1024), shape(512, 768), shape(4, 512, 512), shape(512, 256), rowf, *halves,
     ]
     weights_scratch = [pltpu.VMEM((1024, 768), BF), pltpu.VMEM((256, 1024), BF)]
     dist = pltpu.VMEM((512, 512), F32)
     vec_scratch = [pltpu.VMEM((16, 1024), F32)] * 2
-    mlp_outs = [shape(512, 1024), shape(512, 1024, dtype=F32), shape(512, 1024), rowf, *quarters]
+    mlp_outs = [shape(512, 1024), shape(512, 1024, dtype=F32), shape(512, 1024), rowf, *halves]
 
     vec, h1_0, qkv_0, probs_0, o_0, keep, *send = run(
         with_scratch(first_attention, *vec_scratch, *weights_scratch, dist),
@@ -1315,7 +1305,7 @@
     mlp_0 = (mlp_0, far_up, far_down, pair_x, pair_y, by_x, by_y, both)
     x1_0, *h = run(
         with_scratch(first_norm_stage, pltpu.VMEM((256, 1024), F32)),
-        [rowf, *quarters], blocks[0], blocks[2], part, came, vec, after=(token,), us=1.5,
+        [rowf, *halves], blocks[0], blocks[2], part, came, vec, after=(token,), us=1.5,
     )
     h2_0, u_0, a_0, keep, *send = run(
         mlp_stage(0), mlp_outs, *with_other(h), *mlp_0, vec, after=(deep_far,), us=4
@@ -1326,7 +1316,7 @@
     )
     att_1 = (deep, deep_far, pair_x, pair_y, one_x, one_y, both)
     part, came = summed_core(keep, *send)
-    x2_0, *h = run(norm_stage(5, 8), [rowf, *quarters], x1_0, part, came, vec, after=(token, down_1_far), us=1)
+    x2_0, *h = run(norm_stage(5, 8), [rowf, *halves], x1_0, part, came, vec, after=(token, down_1_far), us=1)
     to_all, to_x, to_y = run(
         mlp_1_message, [row, shape(128, 1024), shape(128, 1024)], deep_far, down_1_far, one_x, one_y,
         after=(both,),
@@ -1344,14 +1334,14 @@
     cot, _ = gate((keep,), cot)
     cot = corner(cot)
     part, came = summed_core(keep, *send)
-    x1_1, *h = run(norm_stage(10, 11), [rowf, *quarters], x2_0, part, came, vec, after=(token,), us=1)
+    x1_1, *h = run(norm_stage(10, 11), [rowf, *halves], x2_0, part, came, vec, after=(token,), us=1)
     by_zl = swap(cot, "zl")
     cots = (cot, swap(cot, "core"), by_zl, swap(by_zl, "core"))
     h2_1, u_1, a_1, keep, *send = run(mlp_stage(1), mlp_outs, *with_other(h), *mlp_1, vec, us=4)
 
-    mlp_back_outs = [shape(512, 1024), shape(512, 1024), rowf, *quarters]
-    norm_outs = [rowf, *quarters, shape(8, 1024, dtype=F32)]
-    attention_back_outs = [shape(512, 1024), shape(512, 768), rowf, *quarters]
+    mlp_back_outs = [shape(512, 1024), shape(512, 1024), rowf, *halves]
+    norm_outs = [rowf, *halves, shape(8, 1024, dtype=F32)]
+    attention_back_outs = [shape(512, 1024), shape(512, 768), rowf, *halves]
     attention_back_scratch = weights_scratch + [
         pltpu.VMEM((512, 256), BF), pltpu.VMEM((512, 128), F32), pltpu.VMEM((512, 128), F32),
     ]
@@ -1364,7 +1354,8 @@
     keep_last, send_last = keep, send
     part_last, came_last = split_core(keep_last, *send_last)
     gy2, gu_1, keep, *send = run(mlp_back(1), mlp_back_outs, *cots, u_1, *mlp_1, after=(part_last,), us=6)
-    part, came = summed_core(keep, *send, after=(came_last,))
+    came_last, *send, _ = gate((keep,), came_last, *send)
+    part, came = summed_core(keep, *send)
     to_y, to_x, m1_near_0, m1_near_1, m1_far_0, m1_far_1 = run(
         window_1, grad_outs(512, 256), h2_1, a_1, gy2, gu_1, after=(part,), us=4
     )

time: 394 us -> 380 us (0.964)
  Pallas kernels: 81.2 us -> 66.2 us
    pallas_call x43, Pallas kernels: 78.3 us -> 62.6 us  [run(): pl.pallas_call(body, out_shape=tuple(outs), in_specs=[free] * skip + [sme...]
    ppermute x114 -> x86, starting transfers between devices: 78.1 us -> 76.3 us  [swap(): return lax.ppermute(value, axis, [(0, 1), (1, 0)])]
    ppermute x114 -> x86, waiting for transfers between devices: 179 us -> 181 us  [swap(): return lax.ppermute(value, axis, [(0, 1), (1, 0)])]
  transfers between devices with their start and end apart: 130 -> 102, of which waited for: 77 -> 62; matrix products, arithmetic and copies ran while one was open for 0% -> 0% of each run, Pallas kernels for 17% -> 13%
where the time goes in v5:
time: 380 us; the launch traced here: 375 us
  waiting for transfers between devices  207 us (54%)
  starting transfers between devices  94.2 us (25%)
  Pallas kernels  66.2 us (17%)
  local copies, waits for them, and re-layouts  5.63 us (1%)
    ppermute x86, waiting for transfers between devices, swap(): return lax.ppermute(value, axis, [(0, 1), (1, 0)])  181 us
    ppermute x86, starting transfers between devices, swap(): return lax.ppermute(value, axis, [(0, 1), (1, 0)])  76.3 us
    pallas_call x43, Pallas kernels, run(): pl.pallas_call(body, out_shape=tuple(outs), in_specs=[free] * skip + [sme...  62.6 us
    ppermute x4, waiting for transfers between devices, both_ways(): return lax.ppermute(value, ('y', 'x'), [(0, 3), (3, 0), (1, 2), (2, 1)])  10.8 us
    ppermute x4, waiting for transfers between devices, to_partners(): lax.ppermute(three, ('core', 'zl'), [(0, 3), (3, 0), (1, 2), (2, 1)])  8.51 us
  transfers between devices with their start and end apart: 102, of which 62 were waited for; matrix products, arithmetic and copies ran while one was open for 0% of the time, Pallas kernels for 13%

profile of v5, /device:TPU:4, one launch (start us, length us, event | category | flops | bytes accessed | tf_op | source)
XLA Modules:
  0.0 375.3 jit_solution(242006354296992597)
XLA Ops:
  0.7 2.4 shard_map.263
  3.1 1.6 collective-permute-start.1
  5.0 3.4 collective-permute-start.3
  14.8 1.9 collective-permute-start.6
  16.8 1.5 collective-permute-start.10
  18.3 2.6 collective-permute-start.9
  21.6 2.4 collective-permute-done.6.refs_2_
  24.9 7.3 %collective-permute-done.7.refs_3_ = bf16[32,2816]{1,0:T(8,128)(2,1)S(1)} collective-permute-done((bf16[32,2816]{1,0:T(8,128)(2,1)S(1)}, bf16[32,2816]{1,0:T(8,128)(2,1)S(1)}, u32[]{:S(2)}, u32[]{:S(2)}) %collective-permute-start.7) | collective-permute-done | bytes 180256 | tf_op jit(solution)/shard_map/ppermute | solution.py:1212
  32.4 4.8 %collective-permute-done.9.refs_2_.refs_6_.refs_7_ = bf16[144,1024]{1,0:T(8,128)(2,1)S(1)} collective-permute-done((bf16[144,1024]{1,0:T(8,128)(2,1)S(1)}, bf16[144,1024]{1,0:T(8,128)(2,1)S(1)}, u32[]{:S(2)}, u32[]{:S(2)}) %collective-permute-start.9) | collective-permute-done | bytes 294944 | tf_op jit(solution)/shard_map/ppermute | solution.py:20
  37.9 1.7 collective-permute-start.13
  42.4 6.0 %collective-permute-start.15 = (bf16[128,1024]{1,0:T(8,128)(2,1)S(1)}, bf16[128,1024]{1,0:T(8,128)(2,1)S(1)}, u32[]{:S(2)}, u32[]{:S(2)}) collective-permute-start(bf16[128,1024]{1,0:T(8,128)(2,1)S(1)} %get-tuple-element.212), channel_id=1, source_target_pairs={{0,2},{2,0},{1,3},{3,1},{4,6},{6,4},{5,7},{7,5},{8,10},{10,8},{9,1... | collective-permute-start | bytes 786440 | tf_op jit(solution)/shard_map/ppermute | solution.py:20
  48.4 1.9 collective-permute-done.16.refs_4_.refs_3_.refs_2_.refs_18_
  50.4 8.4 %collective-permute-done.15.refs_3_.refs_1_.refs_6_ = bf16[128,1024]{1,0:T(8,128)(2,1)S(1)} collective-permute-done((bf16[128,1024]{1,0:T(8,128)(2,1)S(1)}, bf16[128,1024]{1,0:T(8,128)(2,1)S(1)}, u32[]{:S(2)}, u32[]{:S(2)}) %collective-permute-start.15) | collective-permute-done | bytes 262176 | tf_op jit(solution)/shard_map/ppermute | solution.py:20
  62.3 6.3 %shard_map.271 = (f32[16,1024]{1,0:T(8,128)S(1)}, bf16[512,1024]{1,0:T(8,128)(2,1)S(1)}, bf16[512,768]{1,0:T(8,128)(2,1)S(1)}, bf16[4,512,512]{2,1,0:T(8,128)(2,...) custom-call(f32[8,128]{1,0:T(8,128)S(1)} %get-tuple-element.214.refs, ...), custom_call_target="tpu_custom_call" | custom-call | flops 100000000 | tf_op jit(solution)/shard_map/pallas_call | solution.py:529
  68.6 7.8 %collective-permute-done.20.refs_1_ = bf16[128,1024]{1,0:T(8,128)(2,1)S(1)} collective-permute-done((bf16[128,1024]{1,0:T(8,128)(2,1)S(1)}, bf16[128,1024]{1,0:T(8,128)(2,1)S(1)}, u32[]{:S(2)}, u32[]{:S(2)}) %collective-permute-start.20) | collective-permute-done | bytes 262176 | tf_op jit(solution)/shard_map/ppermute | solution.py:20
  76.4 1.5 collective-permute-done.22.refs_3_
  85.2 18.9 %collective-permute-done.26.refs_4_ = bf16[256,1024]{1,0:T(8,128)(2,1)S(1)} collective-permute-done((bf16[256,1024]{1,0:T(8,128)(2,1)S(1)}, bf16[256,1024]{1,0:T(8,128)(2,1)S(1)}, u32[]{:S(2)}, u32[]{:S(2)}) %collective-permute-start.26) | collective-permute-done | bytes 524320 | tf_op jit(solution)/shard_map/ppermute | solution.py:20
  105.1 2.1 collective-permute-done.23.refs_0_.refs_1_.refs_6_.refs_8_.refs_7_
  107.1 6.1 %collective-permute-done.31.refs_12_ = bf16[256,1024]{1,0:T(8,128)(2,1)S(1)} collective-permute-done((bf16[256,1024]{1,0:T(8,128)(2,1)S(1)}, bf16[256,1024]{1,0:T(8,128)(2,1)S(1)}, u32[]{:S(2)}, u32[]{:S(2)}) %collective-permute-start.31) | collective-permute-done | bytes 524320 | tf_op jit(solution)/shard_map/ppermute | solution.py:693
  113.2 3.1 shard_map.276
  122.2 2.6 collective-permute-start.32
  126.1 13.2 %collective-permute-done.32.refs_1_.refs_2_.refs_7_.refs_9_ = bf16[128,1024]{1,0:T(8,128)(2,1)S(1)} collective-permute-done((bf16[128,1024]{1,0:T(8,128)(2,1)S(1)}, bf16[128,1024]{1,0:T(8,128)(2,1)S(1)}, u32[]{:S(2)}, u32[]{:S(2)}) %collective-permute-start.32) | collective-permute-done | bytes 262176 | tf_op jit(solution)/shard_map/ppermute | solution.py:20
  139.3 4.7 %collective-permute-done.36.refs_0_.refs_11_.refs_12_ = bf16[128,1024]{1,0:T(8,128)(2,1)S(1)} collective-permute-done((bf16[128,1024]{1,0:T(8,128)(2,1)S(1)}, bf16[128,1024]{1,0:T(8,128)(2,1)S(1)}, u32[]{:S(2)}, u32[]{:S(2)}) %collective-permute-start.36) | collective-permute-done | bytes 262176 | tf_op jit(solution)/shard_map/ppermute | solution.py:693
  144.1 1.6 collective-permute-start.42
  149.2 5.2 %shard_map.281 = (bf16[512,1024]{1,0:T(8,128)(2,1)S(1)}, bf16[512,768]{1,0:T(8,128)(2,1)S(1)}, bf16[4,512,512]{2,1,0:T(8,128)(2,1)S(1)}, bf16[512,256]{1,0:T(8,1...) custom-call(bf16[256,1024]{1,0:T(8,128)(2,1)S(1)} %get-tuple-element.244.refs_0_, ...), custom_call_target="tpu_custom_call" | custom-call | flops 90000000 | tf_op jit(solution)/shard_map/pallas_call | solution.py:529
  159.1 2.0 collective-permute-start.45
  164.7 1.7 collective-permute-start.49
  166.3 9.8 %collective-permute-done.45.refs_3_ = bf16[256,1024]{1,0:T(8,128)(2,1)S(1)} collective-permute-done((bf16[256,1024]{1,0:T(8,128)(2,1)S(1)}, bf16[256,1024]{1,0:T(8,128)(2,1)S(1)}, u32[]{:S(2)}, u32[]{:S(2)}) %collective-permute-start.45) | collective-permute-done | bytes 524320 | tf_op jit(solution)/shard_map/ppermute | solution.py:20
  177.9 2.4 collective-permute-done.48.refs_12_.refs_14_
  181.2 3.1 shard_map.285
  187.0 4.8 %shard_map.288 = (bf16[512,1024]{1,0:T(8,128)(2,1)S(1)}, bf16[512,1024]{1,0:T(8,128)(2,1)S(1)}, f32[256,1024]{1,0:T(8,128)S(1)}, bf16[128,1024]{1,0:T(8,128)(2,1)S(1)}, bf16[128,1024]{1,0:T(8,128)(2,1)S(1)}) custom-call(bf16[128,1024]{1,0:T(8,128)(2,1)S(1)} %get-tuple-element.264.refs_0_.refs_1_, bf16[128,1024]{1,0:T(8,128)(2,1)S(1)} %collective-permute-done.53.refs_1_, ...), custom_call_target="tpu_custom_call" | custom-call | flops 60000000 | tf_op jit(solution)/shard_map/pallas_call | solution.py:529
  191.8 3.0 collective-permute-done.57.refs_1_
  197.9 2.5 shard_map.292
  202.3 9.2 %collective-permute-done.61.refs_4_ = bf16[256,1024]{1,0:T(8,128)(2,1)S(1)} collective-permute-done((bf16[256,1024]{1,0:T(8,128)(2,1)S(1)}, bf16[256,1024]{1,0:T(8,128)(2,1)S(1)}, u32[]{:S(2)}, u32[]{:S(2)}) %collective-permute-start.61) | collective-permute-done | bytes 524320 | tf_op jit(solution)/shard_map/ppermute | solution.py:20
  214.8 5.3 %shard_map.294 = (bf16[512,1024]{1,0:T(8,128)(2,1)S(1)}, bf16[512,768]{1,0:T(8,128)(2,1)S(1)}, f32[256,1024]{1,0:T(8,128)S(1)}, bf16[128,1024]{1,0:T(8,128)(2,1)S(1)}, bf16[128,1024]{1,0:T(8,128)(2,1)S(1)}) custom-call(bf16[128,1024]{1,0:T(8,128)(2,1)S(1)} %get-tuple-element.280.refs_0_, bf16[128,1024]{1,0:T(8,128)(2,1)S(1)} %get-tuple-element.281.refs_1_, ...), custom_call_target="tpu_custom_call" | custom-call | flops 90000000 | tf_op jit(solution)/shard_map/pallas_call | solution.py:529
  222.7 2.7 collective-permute-done.66.refs_7_.refs_0_
  225.8 1.9 shard_map.296
  229.6 8.8 %collective-permute-done.68.refs_3_ = bf16[256,1024]{1,0:T(8,128)(2,1)S(1)} collective-permute-done((bf16[256,1024]{1,0:T(8,128)(2,1)S(1)}, bf16[256,1024]{1,0:T(8,128)(2,1)S(1)}, u32[]{:S(2)}, u32[]{:S(2)}) %collective-permute-start.68) | collective-permute-done | bytes 524320 | tf_op jit(solution)/shard_map/ppermute | solution.py:20
  239.5 1.7 collective-permute-start.69
  242.7 4.8 %shard_map.298 = (bf16[512,1024]{1,0:T(8,128)(2,1)S(1)}, bf16[512,1024]{1,0:T(8,128)(2,1)S(1)}, f32[256,1024]{1,0:T(8,128)S(1)}, bf16[128,1024]{1,0:T(8,128)(2,1)S(1)}, bf16[128,1024]{1,0:T(8,128)(2,1)S(1)}) custom-call(bf16[128,1024]{1,0:T(8,128)(2,1)S(1)} %get-tuple-element.296.refs_0_, bf16[128,1024]{1,0:T(8,128)(2,1)S(1)} %get-tuple-element.297.refs_1_, ...), custom_call_target="tpu_custom_call" | custom-call | flops 60000000 | tf_op jit(solution)/shard_map/pallas_call | solution.py:529
  250.3 3.0 shard_map.300
  253.4 1.7 collective-permute-start.79
  255.1 3.0 collective-permute-start.75
  258.0 10.4 %collective-permute-done.75.refs_3_ = bf16[256,1024]{1,0:T(8,128)(2,1)S(1)} collective-permute-done((bf16[256,1024]{1,0:T(8,128)(2,1)S(1)}, bf16[256,1024]{1,0:T(8,128)(2,1)S(1)}, u32[]{:S(2)}, u32[]{:S(2)}) %collective-permute-start.75) | collective-permute-done | bytes 524320 | tf_op jit(solution)/shard_map/ppermute | solution.py:20
  269.6 2.5 collective-permute-start.76
  273.6 5.3 %shard_map.302 = (bf16[512,1024]{1,0:T(8,128)(2,1)S(1)}, bf16[512,768]{1,0:T(8,128)(2,1)S(1)}, f32[256,1024]{1,0:T(8,128)S(1)}, bf16[128,1024]{1,0:T(8,128)(2,1)S(1)}, bf16[128,1024]{1,0:T(8,128)(2,1)S(1)}) custom-call(bf16[128,1024]{1,0:T(8,128)(2,1)S(1)} %get-tuple-element.312.refs_0_, bf16[128,1024]{1,0:T(8,128)(2,1)S(1)} %get-tuple-element.313.refs_1_, ...), custom_call_target="tpu_custom_call" | custom-call | flops 90000000 | tf_op jit(solution)/shard_map/pallas_call | solution.py:529
  279.0 2.3 collective-permute-done.78.refs_2_.refs_3_
  281.6 2.0 collective-permute-start.83
  284.0 3.3 collective-permute-start.81
  287.3 11.4 %collective-permute-done.80.refs_1_.refs_5_ = bf16[256,1024]{1,0:T(8,128)(2,1)S(1)} collective-permute-done((bf16[256,1024]{1,0:T(8,128)(2,1)S(1)}, bf16[256,1024]{1,0:T(8,128)(2,1)S(1)}, u32[]{:S(2)}, u32[]{:S(2)}) %collective-permute-start.80) | collective-permute-done | bytes 524320 | tf_op jit(solution)/shard_map/ppermute | solution.py:20
  298.9 2.6 shard_map.305
  301.9 2.0 collective-permute-start.92
  304.0 2.9 collective-permute-start.85
  307.1 7.5 %collective-permute-done.85.refs_3_ = bf16[128,1024]{1,0:T(8,128)(2,1)S(1)} collective-permute-done((bf16[128,1024]{1,0:T(8,128)(2,1)S(1)}, bf16[128,1024]{1,0:T(8,128)(2,1)S(1)}, u32[]{:S(2)}, u32[]{:S(2)}) %collective-permute-start.85) | collective-permute-done | bytes 262176 | tf_op jit(solution)/shard_map/ppermute | solution.py:20
  317.0 1.5 collective-permute-start.95
  318.5 3.5 collective-permute-done.87.refs_7_
  324.6 8.8 %collective-permute-done.89.refs_1_.refs_2_ = bf16[32,1792]{1,0:T(8,128)(2,1)S(1)} collective-permute-done((bf16[32,1792]{1,0:T(8,128)(2,1)S(1)}, bf16[32,1792]{1,0:T(8,128)(2,1)S(1)}, u32[]{:S(2)}, u32[]{:S(2)}) %collective-permute-start.89) | collective-permute-done | bytes 114720 | tf_op jit(solution)/shard_map/ppermute | solution.py:20
  334.7 5.8 %collective-permute-start.96 = (bf16[144,1024]{1,0:T(8,128)(2,1)S(1)}, bf16[144,1024]{1,0:T(8,128)(2,1)S(1)}, u32[]{:S(2)}, u32[]{:S(2)}) collective-permute-start(bf16[144,1024]{1,0:T(8,128)(2,1)S(1)} %shard_map.310), channel_id=1, source_target_pairs={{0,2},{2,0},{1,3},{3,1},{4,6},{6,4},{5,7},{7,5},{8,10},{10,8},{9,1... | collective-permute-start | bytes 884744 | tf_op jit(solution)/shard_map/ppermute | solution.py:20
  341.2 13.4 %collective-permute-done.94.refs_8_ = bf16[256,1024]{1,0:T(8,128)(2,1)S(1)} collective-permute-done((bf16[256,1024]{1,0:T(8,128)(2,1)S(1)}, bf16[256,1024]{1,0:T(8,128)(2,1)S(1)}, u32[]{:S(2)}, u32[]{:S(2)}) %collective-permute-start.94) | collective-permute-done | bytes 524320 | tf_op jit(solution)/shard_map/ppermute | solution.py:20
  354.6 4.7 %collective-permute-done.96.refs_10_ = bf16[144,1024]{1,0:T(8,128)(2,1)S(1)} collective-permute-done((bf16[144,1024]{1,0:T(8,128)(2,1)S(1)}, bf16[144,1024]{1,0:T(8,128)(2,1)S(1)}, u32[]{:S(2)}, u32[]{:S(2)}) %collective-permute-start.96) | collective-permute-done | bytes 294944 | tf_op jit(solution)/shard_map/ppermute | solution.py:20
  360.7 1.9 collective-permute-start.99
  362.6 2.1 collective-permute-start.100
  365.6 6.9 %collective-permute-done.100.refs_8_ = bf16[64,512]{1,0:T(8,128)(2,1)S(1)} collective-permute-done((bf16[64,512]{1,0:T(8,128)(2,1)S(1)}, bf16[64,512]{1,0:T(8,128)(2,1)S(1)}, u32[]{:S(2)}, u32[]{:S(2)}) %collective-permute-start.100) | collective-permute-done | bytes 65568 | tf_op jit(solution)/shard_map/ppermute | solution.py:1437
  372.6 1.7 shard_map.312
  (210 shorter events, 80.9 us)
Async XLA Ops:
  3.0 11.0 %collective-permute-start = (bf16[48,768]{1,0:T(8,128)(2,1)}, bf16[48,768]{1,0:T(8,128)(2,1)S(1)}, u32[]{:S(2)}, u32[]{:S(2)}) collective-permute-start(bf16[48,768]{1,0:T(8,128)(2,1)} %get-tuple-element.196), channel_id=1, source_target_pairs={{0,4},{4,0},{1,5},{5,1},{2,6},{6,2},{3,7},{7,3},{8,12},{12,8},{9,1... | collective-permute-start | bytes 221192 | tf_op jit(solution)/shard_map/ppermute | solution.py:20
  3.1 11.0 %collective-permute-start.1 = (bf16[48,768]{1,0:T(8,128)(2,1)}, bf16[48,768]{1,0:T(8,128)(2,1)S(1)}, u32[]{:S(2)}, u32[]{:S(2)}) collective-permute-start(bf16[48,768]{1,0:T(8,128)(2,1)} %get-tuple-element.197), channel_id=1, source_target_pairs={{0,1},{1,0},{2,3},{3,2},{4,5},{5,4},{6,7},{7,6},{8,9},{9,8},{10,11... | collective-permute-start | bytes 221192 | tf_op jit(solution)/shard_map/ppermute | solution.py:20
  4.8 9.3 %collective-permute-start.2 = (bf16[48,768]{1,0:T(8,128)(2,1)}, bf16[48,768]{1,0:T(8,128)(2,1)S(1)}, u32[]{:S(2)}, u32[]{:S(2)}) collective-permute-start(bf16[48,768]{1,0:T(8,128)(2,1)} %get-tuple-element.198), channel_id=1, source_target_pairs={{0,5},{5,0},{1,4},{4,1},{2,7},{7,2},{3,6},{6,3},{8,13},{13,8},{9,1... | collective-permute-start | bytes 221192 | tf_op jit(solution)/shard_map/ppermute | solution.py:1212
  5.0 9.1 %collective-permute-start.3 = (bf16[64,512]{1,0:T(8,128)(2,1)}, bf16[64,512]{1,0:T(8,128)(2,1)S(1)}, u32[]{:S(2)}, u32[]{:S(2)}) collective-permute-start(bf16[64,512]{1,0:T(8,128)(2,1)} %get-tuple-element.199), channel_id=1, source_target_pairs={{0,0},{1,16},{16,1},{17,17},{2,2},{3,18},{18,3},{19,19},{4,4},{5,2... | collective-permute-start | bytes 196616 | tf_op jit(solution)/shard_map/ppermute | solution.py:1236
  14.8 9.2 %collective-permute-start.6 = (bf16[32,2816]{1,0:T(8,128)(2,1)S(1)}, bf16[32,2816]{1,0:T(8,128)(2,1)S(1)}, u32[]{:S(2)}, u32[]{:S(2)}) collective-permute-start(bf16[32,2816]{1,0:T(8,128)(2,1)S(1)} %get-tuple-element.205), channel_id=1, source_target_pairs={{0,1},{1,0},{2,3},{3,2},{4,5},{5,4},{6,7},{7,6},{8,9},{9,8},{10,11... | collective-permute-start | bytes 540680 | tf_op jit(solution)/shard_map/ppermute | solution.py:20
  16.7 15.6 %collective-permute-start.11 = (bf16[144,1024]{1,0:T(8,128)(2,1)S(1)}, bf16[144,1024]{1,0:T(8,128)(2,1)S(1)}, u32[]{:S(2)}, u32[]{:S(2)}) collective-permute-start(bf16[144,1024]{1,0:T(8,128)(2,1)S(1)} %shard_map.265.refs_0_.refs_5_.refs_6_), channel_id=1, source_target_pairs={{0,16},{16,0},{1,17},{17,1},{2,18},{18,2},{3,19},{19,3},{4,20},{20... | collective-permute-start | bytes 884744 | tf_op jit(solution)/shard_map/ppermute | solution.py:20
  16.8 15.6 %collective-permute-start.10 = (bf16[144,1024]{1,0:T(8,128)(2,1)S(1)}, bf16[144,1024]{1,0:T(8,128)(2,1)S(1)}, u32[]{:S(2)}, u32[]{:S(2)}) collective-permute-start(bf16[144,1024]{1,0:T(8,128)(2,1)S(1)} %shard_map.265.refs_0_.refs_5_.refs_6_), channel_id=1, source_target_pairs={{0,8},{8,0},{1,9},{9,1},{2,10},{10,2},{3,11},{11,3},{4,12},{12,4},... | collective-permute-start | bytes 884744 | tf_op jit(solution)/shard_map/ppermute | solution.py:20
  18.3 18.9 %collective-permute-start.9 = (bf16[144,1024]{1,0:T(8,128)(2,1)S(1)}, bf16[144,1024]{1,0:T(8,128)(2,1)S(1)}, u32[]{:S(2)}, u32[]{:S(2)}) collective-permute-start(bf16[144,1024]{1,0:T(8,128)(2,1)S(1)} %shard_map.265.refs_0_.refs_5_.refs_6_), channel_id=1, source_target_pairs={{0,2},{2,0},{1,3},{3,1},{4,6},{6,4},{5,7},{7,5},{8,10},{10,8},{9,1... | collective-permute-start | bytes 884744 | tf_op jit(solution)/shard_map/ppermute | solution.py:20
  20.9 11.5 %collective-permute-start.8 = (bf16[1,128,1024]{2,1,0:T(8,128)(2,1)S(1)}, bf16[1,128,1024]{2,1,0:T(8,128)(2,1)S(1)}, u32[]{:S(2)}, u32[]{:S(2)}) collective-permute-start(bf16[1,128,1024]{2,1,0:T(8,128)(2,1)S(1)} %copy-done.8), channel_id=1, source_target_pairs={{0,0},{2,4},{4,2},{6,6},{1,1},{3,5},{5,3},{7,7},{8,8},{10,12},{12,... | collective-permute-start | bytes 786440 | tf_op jit(solution)/shard_map/ppermute | solution.py:1204
  37.3 21.5 %collective-permute-start.12 = (bf16[224,1024]{1,0:T(8,128)(2,1)S(1)}, bf16[224,1024]{1,0:T(8,128)(2,1)S(1)}, u32[]{:S(2)}, u32[]{:S(2)}) collective-permute-start(bf16[224,1024]{1,0:T(8,128)(2,1)S(1)} %get-tuple-element.209.refs_0_), channel_id=1, source_target_pairs={{0,8},{8,0},{1,9},{9,1},{2,10},{10,2},{3,11},{11,3},{4,12},{12,4},... | collective-permute-start | bytes 1376264 | tf_op jit(solution)/shard_map/ppermute | solution.py:20
  37.9 20.9 %collective-permute-start.13 = (bf16[208,1024]{1,0:T(8,128)(2,1)S(1)}, bf16[208,1024]{1,0:T(8,128)(2,1)S(1)}, u32[]{:S(2)}, u32[]{:S(2)}) collective-permute-start(bf16[208,1024]{1,0:T(8,128)(2,1)S(1)} %get-tuple-element.210), channel_id=1, source_target_pairs={{0,16},{16,0},{1,17},{17,1},{2,18},{18,2},{3,19},{19,3},{4,20},{20... | collective-permute-start | bytes 1277960 | tf_op jit(solution)/shard_map/ppermute | solution.py:20
  39.6 19.2 %collective-permute-start.14 = (bf16[144,1024]{1,0:T(8,128)(2,1)S(1)}, bf16[144,1024]{1,0:T(8,128)(2,1)S(1)}, u32[]{:S(2)}, u32[]{:S(2)}) collective-permute-start(bf16[144,1024]{1,0:T(8,128)(2,1)S(1)} %collective-permute-done.9.refs_2_.refs_6_.refs_7_), channel_id=1, source_target_pairs={{0,24},{24,0},{8,16},{16,8},{1,25},{25,1},{9,17},{17,9},{2,26},{26... | collective-permute-start | bytes 884744 | tf_op jit(solution)/shard_map/ppermute | solution.py:693
  40.8 9.5 %collective-permute-start.16 = (bf16[1,128,1024]{2,1,0:T(8,128)(2,1)S(1)}, bf16[1,128,1024]{2,1,0:T(8,128)(2,1)S(1)}, u32[]{:S(2)}, u32[]{:S(2)}) collective-permute-start(bf16[1,128,1024]{2,1,0:T(8,128)(2,1)S(1)} %collective-permute-done.8.refs_1_.refs_16_.refs_4_), channel_id=1, source_target_pairs={{0,1},{1,0},{2,3},{3,2},{4,5},{5,4},{6,7},{7,6},{8,9},{9,8},{10,11... | collective-permute-start | bytes 786440 | tf_op jit(solution)/shard_map/ppermute | solution.py:20
  42.4 16.4 %collective-permute-start.15 = (bf16[128,1024]{1,0:T(8,128)(2,1)S(1)}, bf16[128,1024]{1,0:T(8,128)(2,1)S(1)}, u32[]{:S(2)}, u32[]{:S(2)}) collective-permute-start(bf16[128,1024]{1,0:T(8,128)(2,1)S(1)} %get-tuple-element.212), channel_id=1, source_target_pairs={{0,2},{2,0},{1,3},{3,1},{4,6},{6,4},{5,7},{7,5},{8,10},{10,8},{9,1... | collective-permute-start | bytes 786440 | tf_op jit(solution)/shard_map/ppermute | solution.py:20
  58.8 19.0 %collective-permute-start.22 = (bf16[384,1024]{1,0:T(8,128)(2,1)S(1)}, bf16[384,1024]{1,0:T(8,128)(2,1)S(1)}, u32[]{:S(2)}, u32[]{:S(2)}) collective-permute-start(bf16[384,1024]{1,0:T(8,128)(2,1)S(1)} %get-tuple-element.217), channel_id=1, source_target_pairs={{0,16},{16,0},{1,17},{17,1},{2,18},{18,2},{3,19},{19,3},{4,20},{20... | collective-permute-start | bytes 2359304 | tf_op jit(solution)/shard_map/ppermute | solution.py:20
  59.8 18.1 %collective-permute-start.21 = (bf16[384,1024]{1,0:T(8,128)(2,1)S(1)}, bf16[384,1024]{1,0:T(8,128)(2,1)S(1)}, u32[]{:S(2)}, u32[]{:S(2)}) collective-permute-start(bf16[384,1024]{1,0:T(8,128)(2,1)S(1)} %get-tuple-element.217), channel_id=1, source_target_pairs={{0,8},{8,0},{1,9},{9,1},{2,10},{10,2},{3,11},{11,3},{4,12},{12,4},... | collective-permute-start | bytes 2359304 | tf_op jit(solution)/shard_map/ppermute | solution.py:20
  62.2 14.1 %collective-permute-start.20 = (bf16[128,1024]{1,0:T(8,128)(2,1)S(1)}, bf16[128,1024]{1,0:T(8,128)(2,1)S(1)}, u32[]{:S(2)}, u32[]{:S(2)}) collective-permute-start(bf16[128,1024]{1,0:T(8,128)(2,1)S(1)} %get-tuple-element.216), channel_id=1, source_target_pairs={{0,2},{2,0},{1,3},{3,1},{4,6},{6,4},{5,7},{7,5},{8,10},{10,8},{9,1... | collective-permute-start | bytes 786440 | tf_op jit(solution)/shard_map/ppermute | solution.py:20
  80.5 23.7 %collective-permute-start.26 = (bf16[256,1024]{1,0:T(8,128)(2,1)S(1)}, bf16[256,1024]{1,0:T(8,128)(2,1)S(1)}, u32[]{:S(2)}, u32[]{:S(2)}) collective-permute-start(bf16[256,1024]{1,0:T(8,128)(2,1)S(1)} %shard_map.273.refs_0_.refs_3_), channel_id=1, source_target_pairs={{0,1},{1,0},{2,3},{3,2},{4,5},{5,4},{6,7},{7,6},{8,9},{9,8},{10,11... | collective-permute-start | bytes 1572872 | tf_op jit(solution)/shard_map/ppermute | solution.py:20
  81.3 25.9 %collective-permute-start.23 = (bf16[256,1024]{1,0:T(8,128)(2,1)S(1)}, bf16[256,1024]{1,0:T(8,128)(2,1)S(1)}, u32[]{:S(2)}, u32[]{:S(2)}) collective-permute-start(bf16[256,1024]{1,0:T(8,128)(2,1)S(1)} %get-tuple-element.222.refs_4_.refs_5_.refs_6_), channel_id=1, source_target_pairs={{0,2},{2,0},{1,3},{3,1},{4,6},{6,4},{5,7},{7,5},{8,10},{10,8},{9,1... | collective-permute-start | bytes 1572872 | tf_op jit(solution)/shard_map/ppermute | solution.py:20
  81.7 31.5 %collective-permute-start.30 = (bf16[384,1024]{1,0:T(8,128)(2,1)S(1)}, bf16[384,1024]{1,0:T(8,128)(2,1)S(1)}, u32[]{:S(2)}, u32[]{:S(2)}) collective-permute-start(bf16[384,1024]{1,0:T(8,128)(2,1)S(1)} %get-tuple-element.233), channel_id=1, source_target_pairs={{0,16},{16,0},{1,17},{17,1},{2,18},{18,2},{3,19},{19,3},{4,20},{20... | collective-permute-start | bytes 2359304 | tf_op jit(solution)/shard_map/ppermute | solution.py:20
  83.0 30.2 %collective-permute-start.29 = (bf16[384,1024]{1,0:T(8,128)(2,1)S(1)}, bf16[384,1024]{1,0:T(8,128)(2,1)S(1)}, u32[]{:S(2)}, u32[]{:S(2)}) collective-permute-start(bf16[384,1024]{1,0:T(8,128)(2,1)S(1)} %get-tuple-element.228.refs_0_), channel_id=1, source_target_pairs={{0,8},{8,0},{1,9},{9,1},{2,10},{10,2},{3,11},{11,3},{4,12},{12,4},... | collective-permute-start | bytes 2359304 | tf_op jit(solution)/shard_map/ppermute | solution.py:20
  84.4 28.8 %collective-permute-start.31 = (bf16[256,1024]{1,0:T(8,128)(2,1)S(1)}, bf16[256,1024]{1,0:T(8,128)(2,1)S(1)}, u32[]{:S(2)}, u32[]{:S(2)}) collective-permute-start(bf16[256,1024]{1,0:T(8,128)(2,1)S(1)} %get-tuple-element.234), channel_id=1, source_target_pairs={{0,24},{24,0},{8,16},{16,8},{1,25},{25,1},{9,17},{17,9},{2,26},{26... | collective-permute-start | bytes 1572872 | tf_op jit(solution)/shard_map/ppermute | solution.py:693
  116.5 27.5 %collective-permute-start.38 = (bf16[448,1024]{1,0:T(8,128)(2,1)S(1)}, bf16[448,1024]{1,0:T(8,128)(2,1)S(1)}, u32[]{:S(2)}, u32[]{:S(2)}) collective-permute-start(bf16[448,1024]{1,0:T(8,128)(2,1)S(1)} %get-tuple-element.243), channel_id=1, source_target_pairs={{0,16},{16,0},{1,17},{17,1},{2,18},{18,2},{3,19},{19,3},{4,20},{20... | collective-permute-start | bytes 2752520 | tf_op jit(solution)/shard_map/ppermute | solution.py:20
  117.9 26.1 %collective-permute-start.37 = (bf16[448,1024]{1,0:T(8,128)(2,1)S(1)}, bf16[448,1024]{1,0:T(8,128)(2,1)S(1)}, u32[]{:S(2)}, u32[]{:S(2)}) collective-permute-start(bf16[448,1024]{1,0:T(8,128)(2,1)S(1)} %get-tuple-element.237.refs_0_), channel_id=1, source_target_pairs={{0,8},{8,0},{1,9},{9,1},{2,10},{10,2},{3,11},{11,3},{4,12},{12,4},... | collective-permute-start | bytes 2752520 | tf_op jit(solution)/shard_map/ppermute | solution.py:20
  121.1 25.6 %collective-permute-start.35 = (bf16[256,1024]{1,0:T(8,128)(2,1)S(1)}, bf16[256,1024]{1,0:T(8,128)(2,1)S(1)}, u32[]{:S(2)}, u32[]{:S(2)}) collective-permute-start(bf16[256,1024]{1,0:T(8,128)(2,1)S(1)} %shard_map.278.refs_3_), channel_id=1, source_target_pairs={{0,1},{1,0},{2,3},{3,2},{4,5},{5,4},{6,7},{7,6},{8,9},{9,8},{10,11... | collective-permute-start | bytes 1572872 | tf_op jit(solution)/shard_map/ppermute | solution.py:20
  122.2 17.1 %collective-permute-start.32 = (bf16[128,1024]{1,0:T(8,128)(2,1)S(1)}, bf16[128,1024]{1,0:T(8,128)(2,1)S(1)}, u32[]{:S(2)}, u32[]{:S(2)}) collective-permute-start(bf16[128,1024]{1,0:T(8,128)(2,1)S(1)} %get-tuple-element.236.refs_5_.refs_7_), channel_id=1, source_target_pairs={{0,2},{2,0},{1,3},{3,1},{4,6},{6,4},{5,7},{7,5},{8,10},{10,8},{9,1... | collective-permute-start | bytes 786440 | tf_op jit(solution)/shard_map/ppermute | solution.py:20
  124.8 19.2 %collective-permute-start.36 = (bf16[128,1024]{1,0:T(8,128)(2,1)S(1)}, bf16[128,1024]{1,0:T(8,128)(2,1)S(1)}, u32[]{:S(2)}, u32[]{:S(2)}) collective-permute-start(bf16[128,1024]{1,0:T(8,128)(2,1)S(1)} %get-tuple-element.242), channel_id=1, source_target_pairs={{0,24},{24,0},{8,16},{16,8},{1,25},{25,1},{9,17},{17,9},{2,26},{26... | collective-permute-start | bytes 786440 | tf_op jit(solution)/shard_map/ppermute | solution.py:693
  144.1 11.1 %collective-permute-start.42 = (bf16[256,1024]{1,0:T(8,128)(2,1)S(1)}, bf16[256,1024]{1,0:T(8,128)(2,1)S(1)}, u32[]{:S(2)}, u32[]{:S(2)}) collective-permute-start(bf16[256,1024]{1,0:T(8,128)(2,1)S(1)} %get-tuple-element.244.refs_0_), channel_id=1, source_target_pairs={{0,16},{16,0},{1,17},{17,1},{2,18},{18,2},{3,19},{19,3},{4,20},{20... | collective-permute-start | bytes 1572872 | tf_op jit(solution)/shard_map/ppermute | solution.py:20
  145.6 10.9 %collective-permute-start.41 = (bf16[256,1024]{1,0:T(8,128)(2,1)S(1)}, bf16[256,1024]{1,0:T(8,128)(2,1)S(1)}, u32[]{:S(2)}, u32[]{:S(2)}) collective-permute-start(bf16[256,1024]{1,0:T(8,128)(2,1)S(1)} %get-tuple-element.244.refs_0_), channel_id=1, source_target_pairs={{0,8},{8,0},{1,9},{9,1},{2,10},{10,2},{3,11},{11,3},{4,12},{12,4},... | collective-permute-start | bytes 1572872 | tf_op jit(solution)/shard_map/ppermute | solution.py:20
  159.1 17.0 %collective-permute-start.45 = (bf16[256,1024]{1,0:T(8,128)(2,1)S(1)}, bf16[256,1024]{1,0:T(8,128)(2,1)S(1)}, u32[]{:S(2)}, u32[]{:S(2)}) collective-permute-start(bf16[256,1024]{1,0:T(8,128)(2,1)S(1)} %shard_map.283.refs_2_), channel_id=1, source_target_pairs={{0,1},{1,0},{2,3},{3,2},{4,5},{5,4},{6,7},{7,6},{8,9},{9,8},{10,11... | collective-permute-start | bytes 1572872 | tf_op jit(solution)/shard_map/ppermute | solution.py:20
  161.1 16.1 %collective-permute-start.50 = (bf16[256,1024]{1,0:T(8,128)(2,1)S(1)}, bf16[256,1024]{1,0:T(8,128)(2,1)S(1)}, u32[]{:S(2)}, u32[]{:S(2)}) collective-permute-start(bf16[256,1024]{1,0:T(8,128)(2,1)S(1)} %get-tuple-element.244.refs_0_), channel_id=1, source_target_pairs={{0,24},{24,0},{8,16},{16,8},{1,25},{25,1},{9,17},{17,9},{2,26},{26... | collective-permute-start | bytes 1572872 | tf_op jit(solution)/shard_map/ppermute | solution.py:693
  163.0 13.8 %collective-permute-start.53 = (bf16[128,1024]{1,0:T(8,128)(2,1)S(1)}, bf16[128,1024]{1,0:T(8,128)(2,1)S(1)}, u32[]{:S(2)}, u32[]{:S(2)}) collective-permute-start(bf16[128,1024]{1,0:T(8,128)(2,1)S(1)} %get-tuple-element.266), channel_id=1, source_target_pairs={{0,0},{2,4},{4,2},{6,6},{1,1},{3,5},{5,3},{7,7},{8,8},{10,12},{12,... | collective-permute-start | bytes 786440 | tf_op jit(solution)/shard_map/ppermute | solution.py:1204
  164.0 16.2 %collective-permute-start.48 = (bf16[128,1024]{1,0:T(8,128)(2,1)S(1)}, bf16[128,1024]{1,0:T(8,128)(2,1)S(1)}, u32[]{:S(2)}, u32[]{:S(2)}) collective-permute-start(bf16[128,1024]{1,0:T(8,128)(2,1)S(1)} %get-tuple-element.259), channel_id=1, source_target_pairs={{0,8},{8,0},{1,9},{9,1},{2,10},{10,2},{3,11},{11,3},{4,12},{12,4},... | collective-permute-start | bytes 786440 | tf_op jit(solution)/shard_map/ppermute | solution.py:20
  164.7 16.5 %collective-permute-start.49 = (bf16[128,1024]{1,0:T(8,128)(2,1)S(1)}, bf16[128,1024]{1,0:T(8,128)(2,1)S(1)}, u32[]{:S(2)}, u32[]{:S(2)}) collective-permute-start(bf16[128,1024]{1,0:T(8,128)(2,1)S(1)} %get-tuple-element.260), channel_id=1, source_target_pairs={{0,16},{16,0},{1,17},{17,1},{2,18},{18,2},{3,19},{19,3},{4,20},{20... | collective-permute-start | bytes 786440 | tf_op jit(solution)/shard_map/ppermute | solution.py:20
  186.4 8.5 %collective-permute-start.57 = (bf16[128,1024]{1,0:T(8,128)(2,1)S(1)}, bf16[128,1024]{1,0:T(8,128)(2,1)S(1)}, u32[]{:S(2)}, u32[]{:S(2)}) collective-permute-start(bf16[128,1024]{1,0:T(8,128)(2,1)S(1)} %get-tuple-element.269), channel_id=1, source_target_pairs={{0,1},{1,0},{2,3},{3,2},{4,5},{5,4},{6,7},{7,6},{8,9},{9,8},{10,11... | collective-permute-start | bytes 786440 | tf_op jit(solution)/shard_map/ppermute | solution.py:20
  197.5 14.0 %collective-permute-start.61 = (bf16[256,1024]{1,0:T(8,128)(2,1)S(1)}, bf16[256,1024]{1,0:T(8,128)(2,1)S(1)}, u32[]{:S(2)}, u32[]{:S(2)}) collective-permute-start(bf16[256,1024]{1,0:T(8,128)(2,1)S(1)} %shard_map.291.refs_0_.refs_3_), channel_id=1, source_target_pairs={{0,1},{1,0},{2,3},{3,2},{4,5},{5,4},{6,7},{7,6},{8,9},{9,8},{10,11... | collective-permute-start | bytes 1572872 | tf_op jit(solution)/shard_map/ppermute | solution.py:20
  200.4 25.0 %collective-permute-start.66 = (bf16[512,1024]{1,0:T(8,128)(2,1)S(1)}, bf16[512,1024]{1,0:T(8,128)(2,1)S(1)}, u32[]{:S(2)}, u32[]{:S(2)}) collective-permute-start(bf16[512,1024]{1,0:T(8,128)(2,1)S(1)} %get-tuple-element.292), channel_id=1, source_target_pairs={{0,16},{16,0},{1,17},{17,1},{2,18},{18,2},{3,19},{19,3},{4,20},{20... | collective-permute-start | bytes 3145736 | tf_op jit(solution)/shard_map/ppermute | solution.py:20
  201.1 24.6 %collective-permute-start.67 = (bf16[512,1024]{1,0:T(8,128)(2,1)S(1)}, bf16[512,1024]{1,0:T(8,128)(2,1)S(1)}, u32[]{:S(2)}, u32[]{:S(2)}) collective-permute-start(bf16[512,1024]{1,0:T(8,128)(2,1)S(1)} %get-tuple-element.293), channel_id=1, source_target_pairs={{0,8},{8,0},{1,9},{9,1},{2,10},{10,2},{3,11},{11,3},{4,12},{12,4},... | collective-permute-start | bytes 3145736 | tf_op jit(solution)/shard_map/ppermute | solution.py:20
  222.2 16.2 %collective-permute-start.68 = (bf16[256,1024]{1,0:T(8,128)(2,1)S(1)}, bf16[256,1024]{1,0:T(8,128)(2,1)S(1)}, u32[]{:S(2)}, u32[]{:S(2)}) collective-permute-start(bf16[256,1024]{1,0:T(8,128)(2,1)S(1)} %shard_map.295.refs_0_.refs_2_), channel_id=1, source_target_pairs={{0,1},{1,0},{2,3},{3,2},{4,5},{5,4},{6,7},{7,6},{8,9},{9,8},{10,11... | collective-permute-start | bytes 1572872 | tf_op jit(solution)/shard_map/ppermute | solution.py:20
  227.6 21.9 %collective-permute-start.73 = (bf16[512,1024]{1,0:T(8,128)(2,1)S(1)}, bf16[512,1024]{1,0:T(8,128)(2,1)S(1)}, u32[]{:S(2)}, u32[]{:S(2)}) collective-permute-start(bf16[512,1024]{1,0:T(8,128)(2,1)S(1)} %get-tuple-element.307), channel_id=1, source_target_pairs={{0,16},{16,0},{1,17},{17,1},{2,18},{18,2},{3,19},{19,3},{4,20},{20... | collective-permute-start | bytes 3145736 | tf_op jit(solution)/shard_map/ppermute | solution.py:20
  229.1 21.2 %collective-permute-start.74 = (bf16[512,1024]{1,0:T(8,128)(2,1)S(1)}, bf16[512,1024]{1,0:T(8,128)(2,1)S(1)}, u32[]{:S(2)}, u32[]{:S(2)}) collective-permute-start(bf16[512,1024]{1,0:T(8,128)(2,1)S(1)} %get-tuple-element.308), channel_id=1, source_target_pairs={{0,8},{8,0},{1,9},{9,1},{2,10},{10,2},{3,11},{11,3},{4,12},{12,4},... | collective-permute-start | bytes 3145736 | tf_op jit(solution)/shard_map/ppermute | solution.py:20
  253.3 28.0 %collective-permute-start.78 = (bf16[640,1024]{1,0:T(8,128)(2,1)S(1)}, bf16[640,1024]{1,0:T(8,128)(2,1)S(1)}, u32[]{:S(2)}, u32[]{:S(2)}) collective-permute-start(bf16[640,1024]{1,0:T(8,128)(2,1)S(1)} %get-tuple-element.318), channel_id=1, source_target_pairs={{0,16},{16,0},{1,17},{17,1},{2,18},{18,2},{3,19},{19,3},{4,20},{20... | collective-permute-start | bytes 3932168 | tf_op jit(solution)/shard_map/ppermute | solution.py:20
  253.4 27.9 %collective-permute-start.79 = (bf16[640,1024]{1,0:T(8,128)(2,1)S(1)}, bf16[640,1024]{1,0:T(8,128)(2,1)S(1)}, u32[]{:S(2)}, u32[]{:S(2)}) collective-permute-start(bf16[640,1024]{1,0:T(8,128)(2,1)S(1)} %get-tuple-element.319), channel_id=1, source_target_pairs={{0,8},{8,0},{1,9},{9,1},{2,10},{10,2},{3,11},{11,3},{4,12},{12,4},... | collective-permute-start | bytes 3932168 | tf_op jit(solution)/shard_map/ppermute | solution.py:20
  255.1 13.4 %collective-permute-start.75 = (bf16[256,1024]{1,0:T(8,128)(2,1)S(1)}, bf16[256,1024]{1,0:T(8,128)(2,1)S(1)}, u32[]{:S(2)}, u32[]{:S(2)}) collective-permute-start(bf16[256,1024]{1,0:T(8,128)(2,1)S(1)} %shard_map.299.refs_0_.refs_2_), channel_id=1, source_target_pairs={{0,1},{1,0},{2,3},{3,2},{4,5},{5,4},{6,7},{7,6},{8,9},{9,8},{10,11... | collective-permute-start | bytes 1572872 | tf_op jit(solution)/shard_map/ppermute | solution.py:20
  272.2 26.6 %collective-permute-start.80 = (bf16[256,1024]{1,0:T(8,128)(2,1)S(1)}, bf16[256,1024]{1,0:T(8,128)(2,1)S(1)}, u32[]{:S(2)}, u32[]{:S(2)}) collective-permute-start(bf16[256,1024]{1,0:T(8,128)(2,1)S(1)} %get-tuple-element.322), channel_id=1, source_target_pairs={{0,2},{2,0},{1,3},{3,1},{4,6},{6,4},{5,7},{7,5},{8,10},{10,8},{9,1... | collective-permute-start | bytes 1572872 | tf_op jit(solution)/shard_map/ppermute | solution.py:20
  281.6 17.3 %collective-permute-start.83 = (bf16[256,1024]{1,0:T(8,128)(2,1)S(1)}, bf16[256,1024]{1,0:T(8,128)(2,1)S(1)}, u32[]{:S(2)}, u32[]{:S(2)}) collective-permute-start(bf16[256,1024]{1,0:T(8,128)(2,1)S(1)} %get-tuple-element.326), channel_id=1, source_target_pairs={{0,8},{8,0},{1,9},{9,1},{2,10},{10,2},{3,11},{11,3},{4,12},{12,4},... | collective-permute-start | bytes 1572872 | tf_op jit(solution)/shard_map/ppermute | solution.py:20
  283.6 15.3 %collective-permute-start.84 = (bf16[256,1024]{1,0:T(8,128)(2,1)S(1)}, bf16[256,1024]{1,0:T(8,128)(2,1)S(1)}, u32[]{:S(2)}, u32[]{:S(2)}) collective-permute-start(bf16[256,1024]{1,0:T(8,128)(2,1)S(1)} %get-tuple-element.327), channel_id=1, source_target_pairs={{0,16},{16,0},{1,17},{17,1},{2,18},{18,2},{3,19},{19,3},{4,20},{20... | collective-permute-start | bytes 1572872 | tf_op jit(solution)/shard_map/ppermute | solution.py:20
  284.0 14.7 %collective-permute-start.81 = (bf16[128,1024]{1,0:T(8,128)(2,1)S(1)}, bf16[128,1024]{1,0:T(8,128)(2,1)S(1)}, u32[]{:S(2)}, u32[]{:S(2)}) collective-permute-start(bf16[128,1024]{1,0:T(8,128)(2,1)S(1)} %get-tuple-element.323.refs_14_), channel_id=1, source_target_pairs={{0,4},{4,0},{1,5},{5,1},{2,6},{6,2},{3,7},{7,3},{8,12},{12,8},{9,1... | collective-permute-start | bytes 786440 | tf_op jit(solution)/shard_map/ppermute | solution.py:20
  287.3 11.4 %collective-permute-start.82 = (bf16[128,1024]{1,0:T(8,128)(2,1)S(1)}, bf16[128,1024]{1,0:T(8,128)(2,1)S(1)}, u32[]{:S(2)}, u32[]{:S(2)}) collective-permute-start(bf16[128,1024]{1,0:T(8,128)(2,1)S(1)} %get-tuple-element.324.refs_15_), channel_id=1, source_target_pairs={{0,4},{4,0},{1,5},{5,1},{2,6},{6,2},{3,7},{7,3},{8,12},{12,8},{9,1... | collective-permute-start | bytes 786440 | tf_op jit(solution)/shard_map/ppermute | solution.py:20
  301.5 15.0 %collective-permute-start.91 = (bf16[288,1024]{1,0:T(8,128)(2,1)S(1)}, bf16[288,1024]{1,0:T(8,128)(2,1)S(1)}, u32[]{:S(2)}, u32[]{:S(2)}) collective-permute-start(bf16[288,1024]{1,0:T(8,128)(2,1)S(1)} %get-tuple-element.345), channel_id=1, source_target_pairs={{0,16},{16,0},{1,17},{17,1},{2,18},{18,2},{3,19},{19,3},{4,20},{20... | collective-permute-start | bytes 1769480 | tf_op jit(solution)/shard_map/ppermute | solution.py:20
  301.9 14.9 %collective-permute-start.92 = (bf16[288,1024]{1,0:T(8,128)(2,1)S(1)}, bf16[288,1024]{1,0:T(8,128)(2,1)S(1)}, u32[]{:S(2)}, u32[]{:S(2)}) collective-permute-start(bf16[288,1024]{1,0:T(8,128)(2,1)S(1)} %get-tuple-element.347), channel_id=1, source_target_pairs={{0,8},{8,0},{1,9},{9,1},{2,10},{10,2},{3,11},{11,3},{4,12},{12,4},... | collective-permute-start | bytes 1769480 | tf_op jit(solution)/shard_map/ppermute | solution.py:20
  304.0 10.6 %collective-permute-start.85 = (bf16[128,1024]{1,0:T(8,128)(2,1)S(1)}, bf16[128,1024]{1,0:T(8,128)(2,1)S(1)}, u32[]{:S(2)}, u32[]{:S(2)}) collective-permute-start(bf16[128,1024]{1,0:T(8,128)(2,1)S(1)} %get-tuple-element.338), channel_id=1, source_target_pairs={{0,1},{1,0},{2,3},{3,2},{4,5},{5,4},{6,7},{7,6},{8,9},{9,8},{10,11... | collective-permute-start | bytes 786440 | tf_op jit(solution)/shard_map/ppermute | solution.py:20
  306.9 15.1 %collective-permute-start.87 = (bf16[128,1024]{1,0:T(8,128)(2,1)S(1)}, bf16[128,1024]{1,0:T(8,128)(2,1)S(1)}, u32[]{:S(2)}, u32[]{:S(2)}) collective-permute-start(bf16[128,1024]{1,0:T(8,128)(2,1)S(1)} %get-tuple-element.321.refs_0_), channel_id=1, source_target_pairs={{0,2},{2,0},{1,3},{3,1},{4,6},{6,4},{5,7},{7,5},{8,10},{10,8},{9,1... | collective-permute-start | bytes 786440 | tf_op jit(solution)/shard_map/ppermute | solution.py:20
  317.0 17.6 %collective-permute-start.95 = (bf16[144,1024]{1,0:T(8,128)(2,1)S(1)}, bf16[144,1024]{1,0:T(8,128)(2,1)S(1)}, u32[]{:S(2)}, u32[]{:S(2)}) collective-permute-start(bf16[144,1024]{1,0:T(8,128)(2,1)S(1)} %get-tuple-element.352), channel_id=1, source_target_pairs={{0,16},{16,0},{1,17},{17,1},{2,18},{18,2},{3,19},{19,3},{4,20},{20... | collective-permute-start | bytes 884744 | tf_op jit(solution)/shard_map/ppermute | solution.py:20
  318.5 36.1 %collective-permute-start.94 = (bf16[256,1024]{1,0:T(8,128)(2,1)S(1)}, bf16[256,1024]{1,0:T(8,128)(2,1)S(1)}, u32[]{:S(2)}, u32[]{:S(2)}) collective-permute-start(bf16[256,1024]{1,0:T(8,128)(2,1)S(1)} %shard_map.306.refs_0_), channel_id=1, source_target_pairs={{0,2},{2,0},{1,3},{3,1},{4,6},{6,4},{5,7},{7,5},{8,10},{10,8},{9,1... | collective-permute-start | bytes 1572872 | tf_op jit(solution)/shard_map/ppermute | solution.py:20
  322.5 10.9 %collective-permute-start.89 = (bf16[32,1792]{1,0:T(8,128)(2,1)S(1)}, bf16[32,1792]{1,0:T(8,128)(2,1)S(1)}, u32[]{:S(2)}, u32[]{:S(2)}) collective-permute-start(bf16[32,1792]{1,0:T(8,128)(2,1)S(1)} %get-tuple-element.343), channel_id=1, source_target_pairs={{0,1},{1,0},{2,3},{3,2},{4,5},{5,4},{6,7},{7,6},{8,9},{9,8},{10,11... | collective-permute-start | bytes 344072 | tf_op jit(solution)/shard_map/ppermute | solution.py:20
  322.9 11.6 %collective-permute-start.90 = (bf16[32,1792]{1,0:T(8,128)(2,1)S(1)}, bf16[32,1792]{1,0:T(8,128)(2,1)S(1)}, u32[]{:S(2)}, u32[]{:S(2)}) collective-permute-start(bf16[32,1792]{1,0:T(8,128)(2,1)S(1)} %get-tuple-element.344), channel_id=1, source_target_pairs={{0,5},{5,0},{1,4},{4,1},{2,7},{7,2},{3,6},{6,3},{8,13},{13,8},{9,1... | collective-permute-start | bytes 344072 | tf_op jit(solution)/shard_map/ppermute | solution.py:1212
  324.3 30.2 %collective-permute-start.93 = (bf16[144,1024]{1,0:T(8,128)(2,1)S(1)}, bf16[144,1024]{1,0:T(8,128)(2,1)S(1)}, u32[]{:S(2)}, u32[]{:S(2)}) collective-permute-start(bf16[144,1024]{1,0:T(8,128)(2,1)S(1)} %get-tuple-element.348), channel_id=1, source_target_pairs={{0,8},{8,0},{1,9},{9,1},{2,10},{10,2},{3,11},{11,3},{4,12},{12,4},... | collective-permute-start | bytes 884744 | tf_op jit(solution)/shard_map/ppermute | solution.py:20
  334.7 24.6 %collective-permute-start.96 = (bf16[144,1024]{1,0:T(8,128)(2,1)S(1)}, bf16[144,1024]{1,0:T(8,128)(2,1)S(1)}, u32[]{:S(2)}, u32[]{:S(2)}) collective-permute-start(bf16[144,1024]{1,0:T(8,128)(2,1)S(1)} %shard_map.310), channel_id=1, source_target_pairs={{0,2},{2,0},{1,3},{3,1},{4,6},{6,4},{5,7},{7,5},{8,10},{10,8},{9,1... | collective-permute-start | bytes 884744 | tf_op jit(solution)/shard_map/ppermute | solution.py:20
  340.5 24.2 %collective-permute-start.86 = (bf16[1,128,1024]{2,1,0:T(8,128)(2,1)S(1)}, bf16[1,128,1024]{2,1,0:T(8,128)(2,1)S(1)}, u32[]{:S(2)}, u32[]{:S(2)}) collective-permute-start(bf16[1,128,1024]{2,1,0:T(8,128)(2,1)S(1)} %shard_map.307.refs_0_), channel_id=1, source_target_pairs={{0,0},{2,4},{4,2},{6,6},{1,1},{3,5},{5,3},{7,7},{8,8},{10,12},{12,... | collective-permute-start | bytes 786440 | tf_op jit(solution)/shard_map/ppermute | solution.py:1204
  360.7 11.9 %collective-permute-start.97 = (bf16[48,1792]{1,0:T(8,128)(2,1)S(1)}, bf16[48,1792]{1,0:T(8,128)(2,1)S(1)}, u32[]{:S(2)}, u32[]{:S(2)}) collective-permute-start(bf16[48,1792]{1,0:T(8,128)(2,1)S(1)} %get-tuple-element.357), channel_id=1, source_target_pairs={{0,4},{4,0},{1,5},{5,1},{2,6},{6,2},{3,7},{7,3},{8,12},{12,8},{9,1... | collective-permute-start | bytes 516104 | tf_op jit(solution)/shard_map/ppermute | solution.py:20
  360.7 11.9 %collective-permute-start.98 = (bf16[48,1792]{1,0:T(8,128)(2,1)S(1)}, bf16[48,1792]{1,0:T(8,128)(2,1)S(1)}, u32[]{:S(2)}, u32[]{:S(2)}) collective-permute-start(bf16[48,1792]{1,0:T(8,128)(2,1)S(1)} %get-tuple-element.358), channel_id=1, source_target_pairs={{0,1},{1,0},{2,3},{3,2},{4,5},{5,4},{6,7},{7,6},{8,9},{9,8},{10,11... | collective-permute-start | bytes 516104 | tf_op jit(solution)/shard_map/ppermute | solution.py:20
  360.7 11.9 %collective-permute-start.99 = (bf16[48,1792]{1,0:T(8,128)(2,1)S(1)}, bf16[48,1792]{1,0:T(8,128)(2,1)S(1)}, u32[]{:S(2)}, u32[]{:S(2)}) collective-permute-start(bf16[48,1792]{1,0:T(8,128)(2,1)S(1)} %get-tuple-element.359), channel_id=1, source_target_pairs={{0,5},{5,0},{1,4},{4,1},{2,7},{7,2},{3,6},{6,3},{8,13},{13,8},{9,1... | collective-permute-start | bytes 516104 | tf_op jit(solution)/shard_map/ppermute | solution.py:1212
  362.6 9.9 %collective-permute-start.100 = (bf16[64,512]{1,0:T(8,128)(2,1)S(1)}, bf16[64,512]{1,0:T(8,128)(2,1)S(1)}, u32[]{:S(2)}, u32[]{:S(2)}) collective-permute-start(bf16[64,512]{1,0:T(8,128)(2,1)S(1)} %get-tuple-element.360), channel_id=1, source_target_pairs={{0,0},{1,16},{16,1},{17,17},{2,2},{3,18},{18,3},{19,19},{4,4},{5,2... | collective-permute-start | bytes 196616 | tf_op jit(solution)/shard_map/ppermute | solution.py:1437
  (47 other events, 204.8 us)

commit v6 on v5

--- a/solution.py
+++ b/solution.py
@@ -471,10 +471,10 @@
 
 
 def mlp_1_slots(refs):
-    own, own_down, far, far_down, by_x_1, by_y_1, by_x, by_y, across_x, across_y, both = refs
+    own, own_down, far, far_down, near_x, near_y, by_x, by_y, across_x, across_y, both = refs
     own, far = Joined(View(own, 128), own_down, 128), Joined(View(far, 128), far_down, 128)
     across = Joined(across_y, across_x, 128)
-    return own, far, View(by_x_1, 192), by_x, View(by_y_1, 192), by_y, across, both
+    return own, far, near_x, by_x, near_y, by_y, across, both
 
 
 def second_message(far, near_x, near_y, to_x, to_y, rows):
@@ -495,18 +495,20 @@
     second_message(far, near_x, near_y, to_x, to_y, 256)
 
 
-def att_1_message(far, near_x, near_y, own, own_down, to_x, to_y, to_both):
+def att_1_message(far, near_x, near_y, own, own_down, to_x, to_y, to_both, mine):
     to_both[...] = far[0:128, :]
     second_message(far, View(near_x, 256), View(near_y, 256), to_x, to_y, 128)
-    for to in (to_x, to_y):
-        to[192:320, :] = own[128:256, :]
-        to[320:448, :] = own_down[...]
-
-
-def mlp_1_message(far, far_down, near_x, near_y, to_all, to_x, to_y):
+    mine[0:128, :] = own[128:256, :]
+    mine[128:256, :] = own_down[...]
+
+
+def mlp_1_message(far, far_down, to_all):
     to_all[...] = Joined(View(far, 128), far_down, 128)[0:256, :]
-    to_y[...] = near_x[192:320, :]
-    to_x[...] = near_y[320:448, :]
+
+
+def mlp_1_across(near_x, near_y, to_x, to_y):
+    to_y[...] = near_x[0:128, :]
+    to_x[...] = near_y[128:256, :]
 
 
 def slot_blocks():
@@ -1311,29 +1313,30 @@
         mlp_stage(0), mlp_outs, *with_other(h), *mlp_0, vec, after=(deep_far,), us=4
     )
     down_1_far = swap(down_1, "zh")
-    one_x, one_y, both, token = second_hops(
-        att_1_message, 448, 448, deep_far, pair_x, pair_y, deep, down_1, after=(keep,), rows=128
-    )
+    to_x, to_y, to_both, mine = run(
+        att_1_message, [shape(192, 1024)] * 2 + [shape(128, 1024), row],
+        deep_far, pair_x, pair_y, deep, down_1, after=(keep,),
+    )
+    one_x, one_y, both = swap(to_x, "x"), swap(to_y, "y"), both_ways(to_both)
     att_1 = (deep, deep_far, pair_x, pair_y, one_x, one_y, both)
     part, came = summed_core(keep, *send)
+    mine, token = gate((part, one_x, one_y), mine)
+    near_x, near_y = swap(mine, "x"), swap(mine, "y")
     x2_0, *h = run(norm_stage(5, 8), [rowf, *halves], x1_0, part, came, vec, after=(token, down_1_far), us=1)
-    to_all, to_x, to_y = run(
-        mlp_1_message, [row, shape(128, 1024), shape(128, 1024)], deep_far, down_1_far, one_x, one_y,
-        after=(both,),
-    )
+    (to_all,) = run(mlp_1_message, [row], deep_far, down_1_far, after=(both, near_x, near_y))
     by_x, by_y = swap(to_all, "x"), swap(to_all, "y")
     h1_1, qkv_1, probs_1, o_1, keep, *send = run(
         with_scratch(next_attention, *weights_scratch, dist),
         attention_outs, *with_other(h), *att_1, vec, *segments, after=(to_all,), us=9,
     )
-    by_x, by_y, to_x, to_y, *send, _ = gate((keep,), by_x, by_y, to_x, to_y, *send)
+    to_x, to_y = run(mlp_1_across, [shape(128, 1024)] * 2, near_x, near_y, after=(keep,))
     mlp_1 = (
-        deep, down_1, deep_far, down_1_far, one_x, one_y, by_x, by_y,
+        deep, down_1, deep_far, down_1_far, near_x, near_y, by_x, by_y,
         swap(to_x, "x"), swap(to_y, "y"), both_ways(to_all),
     )
     cot, _ = gate((keep,), cot)
     cot = corner(cot)
-    part, came = summed_core(keep, *send)
+    part, came = summed_core(keep, *send, after=(by_x, by_y))
     x1_1, *h = run(norm_stage(10, 11), [rowf, *halves], x2_0, part, came, vec, after=(token,), us=1)
     by_zl = swap(cot, "zl")
     cots = (cot, swap(cot, "core"), by_zl, swap(by_zl, "core"))

time: 380 us -> 378 us (level)
  waiting for transfers between devices: 207 us -> 201 us
  starting transfers between devices: 94.2 us -> 99 us
    ppermute x86 -> x88, waiting for transfers between devices: 181 us -> 176 us  [swap(): return lax.ppermute(value, axis, [(0, 1), (1, 0)])]
    ppermute x86 -> x88, starting transfers between devices: 76.3 us -> 80.4 us  [swap(): return lax.ppermute(value, axis, [(0, 1), (1, 0)])]
    pallas_call x43 -> x44, Pallas kernels: 62.6 us -> 62.8 us  [run(): pl.pallas_call(body, out_shape=tuple(outs), in_specs=[free] * skip + [sme...]
  transfers between devices with their start and end apart: 102 -> 104, of which waited for: 62 -> 61; matrix products, arithmetic and copies ran while one was open for 0% -> 0% of each run, Pallas kernels for 13% -> 14%
where the time goes in v6:
time: 378 us; the launch traced here: 373 us
  waiting for transfers between devices  201 us (53%)
  starting transfers between devices  99 us (26%)
  Pallas kernels  65.8 us (17%)
  local copies, waits for them, and re-layouts  5.63 us (1%)
    ppermute x88, waiting for transfers between devices, swap(): return lax.ppermute(value, axis, [(0, 1), (1, 0)])  176 us
    ppermute x88, starting transfers between devices, swap(): return lax.ppermute(value, axis, [(0, 1), (1, 0)])  80.4 us
    pallas_call x44, Pallas kernels, run(): pl.pallas_call(body, out_shape=tuple(outs), in_specs=[free] * skip + [sme...  62.8 us
    ppermute x4, waiting for transfers between devices, both_ways(): return lax.ppermute(value, ('y', 'x'), [(0, 3), (3, 0), (1, 2), (2, 1)])  9.16 us
    ppermute x4, waiting for transfers between devices, to_partners(): lax.ppermute(three, ('core', 'zl'), [(0, 3), (3, 0), (1, 2), (2, 1)])  8.5 us
  transfers between devices with their start and end apart: 104, of which 61 were waited for; matrix products, arithmetic and copies ran while one was open for 0% of the time, Pallas kernels for 14%

profile of v6, /device:TPU:4, one launch (start us, length us, event | category | flops | bytes accessed | tf_op | source)
XLA Modules:
  0.0 373.3 jit_solution(5697091636294739813)
XLA Ops:
  0.7 2.4 shard_map.263
  3.1 1.6 collective-permute-start.1
  5.0 3.4 collective-permute-start.3
  14.8 1.9 collective-permute-start.6
  18.3 2.6 collective-permute-start.9
  21.6 2.4 collective-permute-done.6.refs_2_
  24.9 7.3 %collective-permute-done.7.refs_3_ = bf16[32,2816]{1,0:T(8,128)(2,1)S(1)} collective-permute-done((bf16[32,2816]{1,0:T(8,128)(2,1)S(1)}, bf16[32,2816]{1,0:T(8,128)(2,1)S(1)}, u32[]{:S(2)}, u32[]{:S(2)}) %collective-permute-start.7) | collective-permute-done | bytes 180256 | tf_op jit(solution)/shard_map/ppermute | solution.py:1214
  32.4 4.8 %collective-permute-done.9.refs_2_.refs_6_.refs_7_ = bf16[144,1024]{1,0:T(8,128)(2,1)S(1)} collective-permute-done((bf16[144,1024]{1,0:T(8,128)(2,1)S(1)}, bf16[144,1024]{1,0:T(8,128)(2,1)S(1)}, u32[]{:S(2)}, u32[]{:S(2)}) %collective-permute-start.9) | collective-permute-done | bytes 294944 | tf_op jit(solution)/shard_map/ppermute | solution.py:20
  37.9 1.7 collective-permute-start.13
  42.4 6.0 %collective-permute-start.15 = (bf16[128,1024]{1,0:T(8,128)(2,1)S(1)}, bf16[128,1024]{1,0:T(8,128)(2,1)S(1)}, u32[]{:S(2)}, u32[]{:S(2)}) collective-permute-start(bf16[128,1024]{1,0:T(8,128)(2,1)S(1)} %get-tuple-element.208), channel_id=1, source_target_pairs={{0,2},{2,0},{1,3},{3,1},{4,6},{6,4},{5,7},{7,5},{8,10},{10,8},{9,1... | collective-permute-start | bytes 786440 | tf_op jit(solution)/shard_map/ppermute | solution.py:20
  48.4 1.9 collective-permute-done.16.refs_4_.refs_3_.refs_2_.refs_18_
  50.4 8.4 %collective-permute-done.15.refs_3_.refs_1_.refs_6_ = bf16[128,1024]{1,0:T(8,128)(2,1)S(1)} collective-permute-done((bf16[128,1024]{1,0:T(8,128)(2,1)S(1)}, bf16[128,1024]{1,0:T(8,128)(2,1)S(1)}, u32[]{:S(2)}, u32[]{:S(2)}) %collective-permute-start.15) | collective-permute-done | bytes 262176 | tf_op jit(solution)/shard_map/ppermute | solution.py:20
  62.3 6.3 %shard_map.271 = (f32[16,1024]{1,0:T(8,128)S(1)}, bf16[512,1024]{1,0:T(8,128)(2,1)S(1)}, bf16[512,768]{1,0:T(8,128)(2,1)S(1)}, bf16[4,512,512]{2,1,0:T(8,128)(2,...) custom-call(f32[8,128]{1,0:T(8,128)S(1)} %get-tuple-element.210.refs, ...), custom_call_target="tpu_custom_call" | custom-call | flops 100000000 | tf_op jit(solution)/shard_map/pallas_call | solution.py:531
  68.6 7.8 %collective-permute-done.20.refs_1_ = bf16[128,1024]{1,0:T(8,128)(2,1)S(1)} collective-permute-done((bf16[128,1024]{1,0:T(8,128)(2,1)S(1)}, bf16[128,1024]{1,0:T(8,128)(2,1)S(1)}, u32[]{:S(2)}, u32[]{:S(2)}) %collective-permute-start.20) | collective-permute-done | bytes 262176 | tf_op jit(solution)/shard_map/ppermute | solution.py:20
  85.2 18.9 %collective-permute-done.26.refs_4_ = bf16[256,1024]{1,0:T(8,128)(2,1)S(1)} collective-permute-done((bf16[256,1024]{1,0:T(8,128)(2,1)S(1)}, bf16[256,1024]{1,0:T(8,128)(2,1)S(1)}, u32[]{:S(2)}, u32[]{:S(2)}) %collective-permute-start.26) | collective-permute-done | bytes 524320 | tf_op jit(solution)/shard_map/ppermute | solution.py:20
  105.1 2.1 collective-permute-done.23.refs_0_.refs_1_.refs_3_.refs_6_.refs_8_.refs_7_
  107.1 6.1 %collective-permute-done.31.refs_12_ = bf16[256,1024]{1,0:T(8,128)(2,1)S(1)} collective-permute-done((bf16[256,1024]{1,0:T(8,128)(2,1)S(1)}, bf16[256,1024]{1,0:T(8,128)(2,1)S(1)}, u32[]{:S(2)}, u32[]{:S(2)}) %collective-permute-start.31) | collective-permute-done | bytes 524320 | tf_op jit(solution)/shard_map/ppermute | solution.py:695
  113.2 3.1 shard_map.276
  122.1 3.8 %collective-permute-done.34.refs_1_.refs_9_.refs_10_ = bf16[192,1024]{1,0:T(8,128)(2,1)S(1)} collective-permute-done((bf16[192,1024]{1,0:T(8,128)(2,1)S(1)}, bf16[192,1024]{1,0:T(8,128)(2,1)S(1)}, u32[]{:S(2)}, u32[]{:S(2)}) %collective-permute-start.34) | collective-permute-done | bytes 393248 | tf_op jit(solution)/shard_map/ppermute | solution.py:20
  129.2 2.6 collective-permute-start.36
  133.3 6.0 %collective-permute-done.36.refs_1_.refs_4_.refs_7_.refs_9_ = bf16[128,1024]{1,0:T(8,128)(2,1)S(1)} collective-permute-done((bf16[128,1024]{1,0:T(8,128)(2,1)S(1)}, bf16[128,1024]{1,0:T(8,128)(2,1)S(1)}, u32[]{:S(2)}, u32[]{:S(2)}) %collective-permute-start.36) | collective-permute-done | bytes 262176 | tf_op jit(solution)/shard_map/ppermute | solution.py:20
  141.8 3.1 collective-permute-done.38.refs_0_.refs_11_.refs_12_
  147.3 5.2 %shard_map.282 = (bf16[512,1024]{1,0:T(8,128)(2,1)S(1)}, bf16[512,768]{1,0:T(8,128)(2,1)S(1)}, bf16[4,512,512]{2,1,0:T(8,128)(2,1)S(1)}, bf16[512,256]{1,0:T(8,1...) custom-call(bf16[256,1024]{1,0:T(8,128)(2,1)S(1)} %shard_map.281.refs_0_, ...), custom_call_target="tpu_custom_call" | custom-call | flops 90000000 | tf_op jit(solution)/shard_map/pallas_call | solution.py:531
  154.5 1.6 collective-permute-done.42.refs_1_.refs_11_.refs_13_
  156.6 2.6 collective-permute-start.47
  164.5 7.1 %collective-permute-done.47.refs_3_ = bf16[256,1024]{1,0:T(8,128)(2,1)S(1)} collective-permute-done((bf16[256,1024]{1,0:T(8,128)(2,1)S(1)}, bf16[256,1024]{1,0:T(8,128)(2,1)S(1)}, u32[]{:S(2)}, u32[]{:S(2)}) %collective-permute-start.47) | collective-permute-done | bytes 524320 | tf_op jit(solution)/shard_map/ppermute | solution.py:20
  172.7 3.0 collective-permute-done.50.refs_12_.refs_14_
  176.5 3.1 shard_map.286
  180.3 2.8 collective-permute-done.57.refs_3_.refs_2_
  184.6 4.8 %shard_map.289 = (bf16[512,1024]{1,0:T(8,128)(2,1)S(1)}, bf16[512,1024]{1,0:T(8,128)(2,1)S(1)}, f32[256,1024]{1,0:T(8,128)S(1)}, bf16[128,1024]{1,0:T(8,128)(2,1)S(1)}, bf16[128,1024]{1,0:T(8,128)(2,1)S(1)}) custom-call(bf16[128,1024]{1,0:T(8,128)(2,1)S(1)} %get-tuple-element.256.refs_0_.refs_1_, bf16[128,1024]{1,0:T(8,128)(2,1)S(1)} %collective-permute-done.55.refs_1_, ...), custom_call_target="tpu_custom_call" | custom-call | flops 60000000 | tf_op jit(solution)/shard_map/pallas_call | solution.py:531
  189.4 2.6 collective-permute-done.59.refs_1_
  194.9 2.5 shard_map.293
  199.4 9.3 %collective-permute-done.63.refs_4_ = bf16[256,1024]{1,0:T(8,128)(2,1)S(1)} collective-permute-done((bf16[256,1024]{1,0:T(8,128)(2,1)S(1)}, bf16[256,1024]{1,0:T(8,128)(2,1)S(1)}, u32[]{:S(2)}, u32[]{:S(2)}) %collective-permute-start.63) | collective-permute-done | bytes 524320 | tf_op jit(solution)/shard_map/ppermute | solution.py:20
  211.9 5.3 %shard_map.295 = (bf16[512,1024]{1,0:T(8,128)(2,1)S(1)}, bf16[512,768]{1,0:T(8,128)(2,1)S(1)}, f32[256,1024]{1,0:T(8,128)S(1)}, bf16[128,1024]{1,0:T(8,128)(2,1)S(1)}, bf16[128,1024]{1,0:T(8,128)(2,1)S(1)}) custom-call(bf16[128,1024]{1,0:T(8,128)(2,1)S(1)} %get-tuple-element.272.refs_0_, bf16[128,1024]{1,0:T(8,128)(2,1)S(1)} %get-tuple-element.273.refs_1_, ...), custom_call_target="tpu_custom_call" | custom-call | flops 90000000 | tf_op jit(solution)/shard_map/pallas_call | solution.py:531
  219.7 2.7 collective-permute-done.68.refs_7_.refs_0_
  223.3 1.9 shard_map.297
  227.5 7.7 %collective-permute-done.70.refs_3_ = bf16[256,1024]{1,0:T(8,128)(2,1)S(1)} collective-permute-done((bf16[256,1024]{1,0:T(8,128)(2,1)S(1)}, bf16[256,1024]{1,0:T(8,128)(2,1)S(1)}, u32[]{:S(2)}, u32[]{:S(2)}) %collective-permute-start.70) | collective-permute-done | bytes 524320 | tf_op jit(solution)/shard_map/ppermute | solution.py:20
  236.3 2.0 collective-permute-start.71
  239.8 4.8 %shard_map.299 = (bf16[512,1024]{1,0:T(8,128)(2,1)S(1)}, bf16[512,1024]{1,0:T(8,128)(2,1)S(1)}, f32[256,1024]{1,0:T(8,128)S(1)}, bf16[128,1024]{1,0:T(8,128)(2,1)S(1)}, bf16[128,1024]{1,0:T(8,128)(2,1)S(1)}) custom-call(bf16[128,1024]{1,0:T(8,128)(2,1)S(1)} %get-tuple-element.288.refs_0_, bf16[128,1024]{1,0:T(8,128)(2,1)S(1)} %get-tuple-element.289.refs_1_, ...), custom_call_target="tpu_custom_call" | custom-call | flops 60000000 | tf_op jit(solution)/shard_map/pallas_call | solution.py:531
  246.8 3.0 shard_map.301
  249.8 1.7 collective-permute-start.80
  252.0 3.1 collective-permute-start.77
  255.1 10.4 %collective-permute-done.77.refs_3_ = bf16[256,1024]{1,0:T(8,128)(2,1)S(1)} collective-permute-done((bf16[256,1024]{1,0:T(8,128)(2,1)S(1)}, bf16[256,1024]{1,0:T(8,128)(2,1)S(1)}, u32[]{:S(2)}, u32[]{:S(2)}) %collective-permute-start.77) | collective-permute-done | bytes 524320 | tf_op jit(solution)/shard_map/ppermute | solution.py:20
  266.6 2.6 collective-permute-start.78
  270.7 5.3 %shard_map.303 = (bf16[512,1024]{1,0:T(8,128)(2,1)S(1)}, bf16[512,768]{1,0:T(8,128)(2,1)S(1)}, f32[256,1024]{1,0:T(8,128)S(1)}, bf16[128,1024]{1,0:T(8,128)(2,1)S(1)}, bf16[128,1024]{1,0:T(8,128)(2,1)S(1)}) custom-call(bf16[128,1024]{1,0:T(8,128)(2,1)S(1)} %get-tuple-element.304.refs_0_, bf16[128,1024]{1,0:T(8,128)(2,1)S(1)} %get-tuple-element.305.refs_1_, ...), custom_call_target="tpu_custom_call" | custom-call | flops 90000000 | tf_op jit(solution)/shard_map/pallas_call | solution.py:531
  277.3 2.4 collective-permute-done.81.refs_4_.refs_2_.refs_3_
  280.3 2.3 collective-permute-start.86
  282.6 2.9 collective-permute-start.83
  285.5 10.3 %collective-permute-done.82.refs_1_.refs_5_ = bf16[256,1024]{1,0:T(8,128)(2,1)S(1)} collective-permute-done((bf16[256,1024]{1,0:T(8,128)(2,1)S(1)}, bf16[256,1024]{1,0:T(8,128)(2,1)S(1)}, u32[]{:S(2)}, u32[]{:S(2)}) %collective-permute-start.82) | collective-permute-done | bytes 524320 | tf_op jit(solution)/shard_map/ppermute | solution.py:20
  296.0 2.6 shard_map.306
  298.6 2.0 collective-permute-start.93
  300.7 3.3 collective-permute-start.87
  304.2 7.4 %collective-permute-done.87.refs_3_ = bf16[128,1024]{1,0:T(8,128)(2,1)S(1)} collective-permute-done((bf16[128,1024]{1,0:T(8,128)(2,1)S(1)}, bf16[128,1024]{1,0:T(8,128)(2,1)S(1)}, u32[]{:S(2)}, u32[]{:S(2)}) %collective-permute-start.87) | collective-permute-done | bytes 262176 | tf_op jit(solution)/shard_map/ppermute | solution.py:20
  312.2 1.6 collective-permute-done.93.refs_2_.refs_4_
  315.9 3.2 collective-permute-done.89.refs_7_
  321.5 1.9 collective-permute-start.95
  323.4 7.2 %collective-permute-done.91.refs_1_.refs_2_ = bf16[32,1792]{1,0:T(8,128)(2,1)S(1)} collective-permute-done((bf16[32,1792]{1,0:T(8,128)(2,1)S(1)}, bf16[32,1792]{1,0:T(8,128)(2,1)S(1)}, u32[]{:S(2)}, u32[]{:S(2)}) %collective-permute-start.91) | collective-permute-done | bytes 114720 | tf_op jit(solution)/shard_map/ppermute | solution.py:20
  331.9 6.3 %collective-permute-start.98 = (bf16[144,1024]{1,0:T(8,128)(2,1)S(1)}, bf16[144,1024]{1,0:T(8,128)(2,1)S(1)}, u32[]{:S(2)}, u32[]{:S(2)}) collective-permute-start(bf16[144,1024]{1,0:T(8,128)(2,1)S(1)} %shard_map.311), channel_id=1, source_target_pairs={{0,2},{2,0},{1,3},{3,1},{4,6},{6,4},{5,7},{7,5},{8,10},{10,8},{9,1... | collective-permute-start | bytes 884744 | tf_op jit(solution)/shard_map/ppermute | solution.py:20
  338.8 13.1 %collective-permute-done.96.refs_8_ = bf16[256,1024]{1,0:T(8,128)(2,1)S(1)} collective-permute-done((bf16[256,1024]{1,0:T(8,128)(2,1)S(1)}, bf16[256,1024]{1,0:T(8,128)(2,1)S(1)}, u32[]{:S(2)}, u32[]{:S(2)}) %collective-permute-start.96) | collective-permute-done | bytes 524320 | tf_op jit(solution)/shard_map/ppermute | solution.py:20
  351.9 4.6 %collective-permute-done.98.refs_10_ = bf16[144,1024]{1,0:T(8,128)(2,1)S(1)} collective-permute-done((bf16[144,1024]{1,0:T(8,128)(2,1)S(1)}, bf16[144,1024]{1,0:T(8,128)(2,1)S(1)}, u32[]{:S(2)}, u32[]{:S(2)}) %collective-permute-start.98) | collective-permute-done | bytes 294944 | tf_op jit(solution)/shard_map/ppermute | solution.py:20
  357.9 1.9 collective-permute-start.101
  359.8 3.0 collective-permute-start.102
  363.7 6.9 %collective-permute-done.102.refs_8_ = bf16[64,512]{1,0:T(8,128)(2,1)S(1)} collective-permute-done((bf16[64,512]{1,0:T(8,128)(2,1)S(1)}, bf16[64,512]{1,0:T(8,128)(2,1)S(1)}, u32[]{:S(2)}, u32[]{:S(2)}) %collective-permute-start.102) | collective-permute-done | bytes 65568 | tf_op jit(solution)/shard_map/ppermute | solution.py:1440
  370.6 1.7 shard_map.313
  (215 shorter events, 88.2 us)
Async XLA Ops:
  3.0 11.0 %collective-permute-start = (bf16[48,768]{1,0:T(8,128)(2,1)}, bf16[48,768]{1,0:T(8,128)(2,1)S(1)}, u32[]{:S(2)}, u32[]{:S(2)}) collective-permute-start(bf16[48,768]{1,0:T(8,128)(2,1)} %get-tuple-element.192), channel_id=1, source_target_pairs={{0,4},{4,0},{1,5},{5,1},{2,6},{6,2},{3,7},{7,3},{8,12},{12,8},{9,1... | collective-permute-start | bytes 221192 | tf_op jit(solution)/shard_map/ppermute | solution.py:20
  3.1 11.0 %collective-permute-start.1 = (bf16[48,768]{1,0:T(8,128)(2,1)}, bf16[48,768]{1,0:T(8,128)(2,1)S(1)}, u32[]{:S(2)}, u32[]{:S(2)}) collective-permute-start(bf16[48,768]{1,0:T(8,128)(2,1)} %get-tuple-element.193), channel_id=1, source_target_pairs={{0,1},{1,0},{2,3},{3,2},{4,5},{5,4},{6,7},{7,6},{8,9},{9,8},{10,11... | collective-permute-start | bytes 221192 | tf_op jit(solution)/shard_map/ppermute | solution.py:20
  4.8 9.3 %collective-permute-start.2 = (bf16[48,768]{1,0:T(8,128)(2,1)}, bf16[48,768]{1,0:T(8,128)(2,1)S(1)}, u32[]{:S(2)}, u32[]{:S(2)}) collective-permute-start(bf16[48,768]{1,0:T(8,128)(2,1)} %get-tuple-element.194), channel_id=1, source_target_pairs={{0,5},{5,0},{1,4},{4,1},{2,7},{7,2},{3,6},{6,3},{8,13},{13,8},{9,1... | collective-permute-start | bytes 221192 | tf_op jit(solution)/shard_map/ppermute | solution.py:1214
  14.8 9.2 %collective-permute-start.6 = (bf16[32,2816]{1,0:T(8,128)(2,1)S(1)}, bf16[32,2816]{1,0:T(8,128)(2,1)S(1)}, u32[]{:S(2)}, u32[]{:S(2)}) collective-permute-start(bf16[32,2816]{1,0:T(8,128)(2,1)S(1)} %get-tuple-element.201), channel_id=1, source_target_pairs={{0,1},{1,0},{2,3},{3,2},{4,5},{5,4},{6,7},{7,6},{8,9},{9,8},{10,11... | collective-permute-start | bytes 540680 | tf_op jit(solution)/shard_map/ppermute | solution.py:20
  16.7 15.6 %collective-permute-start.11 = (bf16[144,1024]{1,0:T(8,128)(2,1)S(1)}, bf16[144,1024]{1,0:T(8,128)(2,1)S(1)}, u32[]{:S(2)}, u32[]{:S(2)}) collective-permute-start(bf16[144,1024]{1,0:T(8,128)(2,1)S(1)} %shard_map.265.refs_0_.refs_5_.refs_6_), channel_id=1, source_target_pairs={{0,16},{16,0},{1,17},{17,1},{2,18},{18,2},{3,19},{19,3},{4,20},{20... | collective-permute-start | bytes 884744 | tf_op jit(solution)/shard_map/ppermute | solution.py:20
  16.8 15.6 %collective-permute-start.10 = (bf16[144,1024]{1,0:T(8,128)(2,1)S(1)}, bf16[144,1024]{1,0:T(8,128)(2,1)S(1)}, u32[]{:S(2)}, u32[]{:S(2)}) collective-permute-start(bf16[144,1024]{1,0:T(8,128)(2,1)S(1)} %shard_map.265.refs_0_.refs_5_.refs_6_), channel_id=1, source_target_pairs={{0,8},{8,0},{1,9},{9,1},{2,10},{10,2},{3,11},{11,3},{4,12},{12,4},... | collective-permute-start | bytes 884744 | tf_op jit(solution)/shard_map/ppermute | solution.py:20
  18.3 18.9 %collective-permute-start.9 = (bf16[144,1024]{1,0:T(8,128)(2,1)S(1)}, bf16[144,1024]{1,0:T(8,128)(2,1)S(1)}, u32[]{:S(2)}, u32[]{:S(2)}) collective-permute-start(bf16[144,1024]{1,0:T(8,128)(2,1)S(1)} %shard_map.265.refs_0_.refs_5_.refs_6_), channel_id=1, source_target_pairs={{0,2},{2,0},{1,3},{3,1},{4,6},{6,4},{5,7},{7,5},{8,10},{10,8},{9,1... | collective-permute-start | bytes 884744 | tf_op jit(solution)/shard_map/ppermute | solution.py:20
  20.9 11.5 %collective-permute-start.8 = (bf16[1,128,1024]{2,1,0:T(8,128)(2,1)S(1)}, bf16[1,128,1024]{2,1,0:T(8,128)(2,1)S(1)}, u32[]{:S(2)}, u32[]{:S(2)}) collective-permute-start(bf16[1,128,1024]{2,1,0:T(8,128)(2,1)S(1)} %copy-done.8), channel_id=1, source_target_pairs={{0,0},{2,4},{4,2},{6,6},{1,1},{3,5},{5,3},{7,7},{8,8},{10,12},{12,... | collective-permute-start | bytes 786440 | tf_op jit(solution)/shard_map/ppermute | solution.py:1206
  37.3 21.5 %collective-permute-start.12 = (bf16[224,1024]{1,0:T(8,128)(2,1)S(1)}, bf16[224,1024]{1,0:T(8,128)(2,1)S(1)}, u32[]{:S(2)}, u32[]{:S(2)}) collective-permute-start(bf16[224,1024]{1,0:T(8,128)(2,1)S(1)} %get-tuple-element.205.refs_0_), channel_id=1, source_target_pairs={{0,8},{8,0},{1,9},{9,1},{2,10},{10,2},{3,11},{11,3},{4,12},{12,4},... | collective-permute-start | bytes 1376264 | tf_op jit(solution)/shard_map/ppermute | solution.py:20
  37.9 20.9 %collective-permute-start.13 = (bf16[208,1024]{1,0:T(8,128)(2,1)S(1)}, bf16[208,1024]{1,0:T(8,128)(2,1)S(1)}, u32[]{:S(2)}, u32[]{:S(2)}) collective-permute-start(bf16[208,1024]{1,0:T(8,128)(2,1)S(1)} %get-tuple-element.206), channel_id=1, source_target_pairs={{0,16},{16,0},{1,17},{17,1},{2,18},{18,2},{3,19},{19,3},{4,20},{20... | collective-permute-start | bytes 1277960 | tf_op jit(solution)/shard_map/ppermute | solution.py:20
  39.6 19.2 %collective-permute-start.14 = (bf16[144,1024]{1,0:T(8,128)(2,1)S(1)}, bf16[144,1024]{1,0:T(8,128)(2,1)S(1)}, u32[]{:S(2)}, u32[]{:S(2)}) collective-permute-start(bf16[144,1024]{1,0:T(8,128)(2,1)S(1)} %collective-permute-done.9.refs_2_.refs_6_.refs_7_), channel_id=1, source_target_pairs={{0,24},{24,0},{8,16},{16,8},{1,25},{25,1},{9,17},{17,9},{2,26},{26... | collective-permute-start | bytes 884744 | tf_op jit(solution)/shard_map/ppermute | solution.py:695
  40.8 9.5 %collective-permute-start.16 = (bf16[1,128,1024]{2,1,0:T(8,128)(2,1)S(1)}, bf16[1,128,1024]{2,1,0:T(8,128)(2,1)S(1)}, u32[]{:S(2)}, u32[]{:S(2)}) collective-permute-start(bf16[1,128,1024]{2,1,0:T(8,128)(2,1)S(1)} %collective-permute-done.8.refs_1_.refs_16_.refs_4_), channel_id=1, source_target_pairs={{0,1},{1,0},{2,3},{3,2},{4,5},{5,4},{6,7},{7,6},{8,9},{9,8},{10,11... | collective-permute-start | bytes 786440 | tf_op jit(solution)/shard_map/ppermute | solution.py:20
  42.4 16.4 %collective-permute-start.15 = (bf16[128,1024]{1,0:T(8,128)(2,1)S(1)}, bf16[128,1024]{1,0:T(8,128)(2,1)S(1)}, u32[]{:S(2)}, u32[]{:S(2)}) collective-permute-start(bf16[128,1024]{1,0:T(8,128)(2,1)S(1)} %get-tuple-element.208), channel_id=1, source_target_pairs={{0,2},{2,0},{1,3},{3,1},{4,6},{6,4},{5,7},{7,5},{8,10},{10,8},{9,1... | collective-permute-start | bytes 786440 | tf_op jit(solution)/shard_map/ppermute | solution.py:20
  58.8 19.0 %collective-permute-start.22 = (bf16[384,1024]{1,0:T(8,128)(2,1)S(1)}, bf16[384,1024]{1,0:T(8,128)(2,1)S(1)}, u32[]{:S(2)}, u32[]{:S(2)}) collective-permute-start(bf16[384,1024]{1,0:T(8,128)(2,1)S(1)} %get-tuple-element.213), channel_id=1, source_target_pairs={{0,16},{16,0},{1,17},{17,1},{2,18},{18,2},{3,19},{19,3},{4,20},{20... | collective-permute-start | bytes 2359304 | tf_op jit(solution)/shard_map/ppermute | solution.py:20
  59.8 18.1 %collective-permute-start.21 = (bf16[384,1024]{1,0:T(8,128)(2,1)S(1)}, bf16[384,1024]{1,0:T(8,128)(2,1)S(1)}, u32[]{:S(2)}, u32[]{:S(2)}) collective-permute-start(bf16[384,1024]{1,0:T(8,128)(2,1)S(1)} %get-tuple-element.213), channel_id=1, source_target_pairs={{0,8},{8,0},{1,9},{9,1},{2,10},{10,2},{3,11},{11,3},{4,12},{12,4},... | collective-permute-start | bytes 2359304 | tf_op jit(solution)/shard_map/ppermute | solution.py:20
  62.2 14.1 %collective-permute-start.20 = (bf16[128,1024]{1,0:T(8,128)(2,1)S(1)}, bf16[128,1024]{1,0:T(8,128)(2,1)S(1)}, u32[]{:S(2)}, u32[]{:S(2)}) collective-permute-start(bf16[128,1024]{1,0:T(8,128)(2,1)S(1)} %get-tuple-element.212), channel_id=1, source_target_pairs={{0,2},{2,0},{1,3},{3,1},{4,6},{6,4},{5,7},{7,5},{8,10},{10,8},{9,1... | collective-permute-start | bytes 786440 | tf_op jit(solution)/shard_map/ppermute | solution.py:20
  80.5 23.7 %collective-permute-start.26 = (bf16[256,1024]{1,0:T(8,128)(2,1)S(1)}, bf16[256,1024]{1,0:T(8,128)(2,1)S(1)}, u32[]{:S(2)}, u32[]{:S(2)}) collective-permute-start(bf16[256,1024]{1,0:T(8,128)(2,1)S(1)} %shard_map.273.refs_0_.refs_3_), channel_id=1, source_target_pairs={{0,1},{1,0},{2,3},{3,2},{4,5},{5,4},{6,7},{7,6},{8,9},{9,8},{10,11... | collective-permute-start | bytes 1572872 | tf_op jit(solution)/shard_map/ppermute | solution.py:20
  81.3 25.9 %collective-permute-start.23 = (bf16[256,1024]{1,0:T(8,128)(2,1)S(1)}, bf16[256,1024]{1,0:T(8,128)(2,1)S(1)}, u32[]{:S(2)}, u32[]{:S(2)}) collective-permute-start(bf16[256,1024]{1,0:T(8,128)(2,1)S(1)} %get-tuple-element.218.refs_4_.refs_5_.refs_6_), channel_id=1, source_target_pairs={{0,2},{2,0},{1,3},{3,1},{4,6},{6,4},{5,7},{7,5},{8,10},{10,8},{9,1... | collective-permute-start | bytes 1572872 | tf_op jit(solution)/shard_map/ppermute | solution.py:20
  81.7 31.5 %collective-permute-start.30 = (bf16[384,1024]{1,0:T(8,128)(2,1)S(1)}, bf16[384,1024]{1,0:T(8,128)(2,1)S(1)}, u32[]{:S(2)}, u32[]{:S(2)}) collective-permute-start(bf16[384,1024]{1,0:T(8,128)(2,1)S(1)} %get-tuple-element.229), channel_id=1, source_target_pairs={{0,16},{16,0},{1,17},{17,1},{2,18},{18,2},{3,19},{19,3},{4,20},{20... | collective-permute-start | bytes 2359304 | tf_op jit(solution)/shard_map/ppermute | solution.py:20
  83.0 30.2 %collective-permute-start.29 = (bf16[384,1024]{1,0:T(8,128)(2,1)S(1)}, bf16[384,1024]{1,0:T(8,128)(2,1)S(1)}, u32[]{:S(2)}, u32[]{:S(2)}) collective-permute-start(bf16[384,1024]{1,0:T(8,128)(2,1)S(1)} %get-tuple-element.224.refs_0_), channel_id=1, source_target_pairs={{0,8},{8,0},{1,9},{9,1},{2,10},{10,2},{3,11},{11,3},{4,12},{12,4},... | collective-permute-start | bytes 2359304 | tf_op jit(solution)/shard_map/ppermute | solution.py:20
  84.4 28.8 %collective-permute-start.31 = (bf16[256,1024]{1,0:T(8,128)(2,1)S(1)}, bf16[256,1024]{1,0:T(8,128)(2,1)S(1)}, u32[]{:S(2)}, u32[]{:S(2)}) collective-permute-start(bf16[256,1024]{1,0:T(8,128)(2,1)S(1)} %get-tuple-element.230), channel_id=1, source_target_pairs={{0,24},{24,0},{8,16},{16,8},{1,25},{25,1},{9,17},{17,9},{2,26},{26... | collective-permute-start | bytes 1572872 | tf_op jit(solution)/shard_map/ppermute | solution.py:695
  116.4 9.5 %collective-permute-start.34 = (bf16[192,1024]{1,0:T(8,128)(2,1)S(1)}, bf16[192,1024]{1,0:T(8,128)(2,1)S(1)}, u32[]{:S(2)}, u32[]{:S(2)}) collective-permute-start(bf16[192,1024]{1,0:T(8,128)(2,1)S(1)} %get-tuple-element.235), channel_id=1, source_target_pairs={{0,8},{8,0},{1,9},{9,1},{2,10},{10,2},{3,11},{11,3},{4,12},{12,4},... | collective-permute-start | bytes 1179656 | tf_op jit(solution)/shard_map/ppermute | solution.py:20
  118.0 9.3 %collective-permute-start.35 = (bf16[192,1024]{1,0:T(8,128)(2,1)S(1)}, bf16[192,1024]{1,0:T(8,128)(2,1)S(1)}, u32[]{:S(2)}, u32[]{:S(2)}) collective-permute-start(bf16[192,1024]{1,0:T(8,128)(2,1)S(1)} %get-tuple-element.236), channel_id=1, source_target_pairs={{0,16},{16,0},{1,17},{17,1},{2,18},{18,2},{3,19},{19,3},{4,20},{20... | collective-permute-start | bytes 1179656 | tf_op jit(solution)/shard_map/ppermute | solution.py:20
  121.1 19.6 %collective-permute-start.37 = (bf16[256,1024]{1,0:T(8,128)(2,1)S(1)}, bf16[256,1024]{1,0:T(8,128)(2,1)S(1)}, u32[]{:S(2)}, u32[]{:S(2)}) collective-permute-start(bf16[256,1024]{1,0:T(8,128)(2,1)S(1)} %shard_map.277.refs_0_.refs_3_), channel_id=1, source_target_pairs={{0,1},{1,0},{2,3},{3,2},{4,5},{5,4},{6,7},{7,6},{8,9},{9,8},{10,11... | collective-permute-start | bytes 1572872 | tf_op jit(solution)/shard_map/ppermute | solution.py:20
  127.3 17.7 %collective-permute-start.40 = (bf16[256,1024]{1,0:T(8,128)(2,1)S(1)}, bf16[256,1024]{1,0:T(8,128)(2,1)S(1)}, u32[]{:S(2)}, u32[]{:S(2)}) collective-permute-start(bf16[256,1024]{1,0:T(8,128)(2,1)S(1)} %get-tuple-element.242), channel_id=1, source_target_pairs={{0,16},{16,0},{1,17},{17,1},{2,18},{18,2},{3,19},{19,3},{4,20},{20... | collective-permute-start | bytes 1572872 | tf_op jit(solution)/shard_map/ppermute | solution.py:20
  128.4 16.6 %collective-permute-start.39 = (bf16[256,1024]{1,0:T(8,128)(2,1)S(1)}, bf16[256,1024]{1,0:T(8,128)(2,1)S(1)}, u32[]{:S(2)}, u32[]{:S(2)}) collective-permute-start(bf16[256,1024]{1,0:T(8,128)(2,1)S(1)} %get-tuple-element.242), channel_id=1, source_target_pairs={{0,8},{8,0},{1,9},{9,1},{2,10},{10,2},{3,11},{11,3},{4,12},{12,4},... | collective-permute-start | bytes 1572872 | tf_op jit(solution)/shard_map/ppermute | solution.py:20
  129.2 10.1 %collective-permute-start.36 = (bf16[128,1024]{1,0:T(8,128)(2,1)S(1)}, bf16[128,1024]{1,0:T(8,128)(2,1)S(1)}, u32[]{:S(2)}, u32[]{:S(2)}) collective-permute-start(bf16[128,1024]{1,0:T(8,128)(2,1)S(1)} %get-tuple-element.234.refs_5_.refs_7_), channel_id=1, source_target_pairs={{0,2},{2,0},{1,3},{3,1},{4,6},{6,4},{5,7},{7,5},{8,10},{10,8},{9,1... | collective-permute-start | bytes 786440 | tf_op jit(solution)/shard_map/ppermute | solution.py:20
  131.8 13.1 %collective-permute-start.38 = (bf16[128,1024]{1,0:T(8,128)(2,1)S(1)}, bf16[128,1024]{1,0:T(8,128)(2,1)S(1)}, u32[]{:S(2)}, u32[]{:S(2)}) collective-permute-start(bf16[128,1024]{1,0:T(8,128)(2,1)S(1)} %get-tuple-element.241), channel_id=1, source_target_pairs={{0,24},{24,0},{8,16},{16,8},{1,25},{25,1},{9,17},{17,9},{2,26},{26... | collective-permute-start | bytes 786440 | tf_op jit(solution)/shard_map/ppermute | solution.py:695
  145.0 11.2 %collective-permute-start.42 = (bf16[256,1024]{1,0:T(8,128)(2,1)S(1)}, bf16[256,1024]{1,0:T(8,128)(2,1)S(1)}, u32[]{:S(2)}, u32[]{:S(2)}) collective-permute-start(bf16[256,1024]{1,0:T(8,128)(2,1)S(1)} %shard_map.281.refs_0_), channel_id=1, source_target_pairs={{0,16},{16,0},{1,17},{17,1},{2,18},{18,2},{3,19},{19,3},{4,20},{20... | collective-permute-start | bytes 1572872 | tf_op jit(solution)/shard_map/ppermute | solution.py:20
  146.2 10.3 %collective-permute-start.41 = (bf16[256,1024]{1,0:T(8,128)(2,1)S(1)}, bf16[256,1024]{1,0:T(8,128)(2,1)S(1)}, u32[]{:S(2)}, u32[]{:S(2)}) collective-permute-start(bf16[256,1024]{1,0:T(8,128)(2,1)S(1)} %shard_map.281.refs_0_), channel_id=1, source_target_pairs={{0,8},{8,0},{1,9},{9,1},{2,10},{10,2},{3,11},{11,3},{4,12},{12,4},... | collective-permute-start | bytes 1572872 | tf_op jit(solution)/shard_map/ppermute | solution.py:20
  156.6 15.0 %collective-permute-start.47 = (bf16[256,1024]{1,0:T(8,128)(2,1)S(1)}, bf16[256,1024]{1,0:T(8,128)(2,1)S(1)}, u32[]{:S(2)}, u32[]{:S(2)}) collective-permute-start(bf16[256,1024]{1,0:T(8,128)(2,1)S(1)} %shard_map.283.refs_2_), channel_id=1, source_target_pairs={{0,1},{1,0},{2,3},{3,2},{4,5},{5,4},{6,7},{7,6},{8,9},{9,8},{10,11... | collective-permute-start | bytes 1572872 | tf_op jit(solution)/shard_map/ppermute | solution.py:20
  159.3 17.2 %collective-permute-start.52 = (bf16[256,1024]{1,0:T(8,128)(2,1)S(1)}, bf16[256,1024]{1,0:T(8,128)(2,1)S(1)}, u32[]{:S(2)}, u32[]{:S(2)}) collective-permute-start(bf16[256,1024]{1,0:T(8,128)(2,1)S(1)} %shard_map.281.refs_0_), channel_id=1, source_target_pairs={{0,24},{24,0},{8,16},{16,8},{1,25},{25,1},{9,17},{17,9},{2,26},{26... | collective-permute-start | bytes 1572872 | tf_op jit(solution)/shard_map/ppermute | solution.py:695
  161.3 10.9 %collective-permute-start.55 = (bf16[128,1024]{1,0:T(8,128)(2,1)S(1)}, bf16[128,1024]{1,0:T(8,128)(2,1)S(1)}, u32[]{:S(2)}, u32[]{:S(2)}) collective-permute-start(bf16[128,1024]{1,0:T(8,128)(2,1)S(1)} %get-tuple-element.258), channel_id=1, source_target_pairs={{0,0},{2,4},{4,2},{6,6},{1,1},{3,5},{5,3},{7,7},{8,8},{10,12},{12,... | collective-permute-start | bytes 786440 | tf_op jit(solution)/shard_map/ppermute | solution.py:1206
  162.4 13.3 %collective-permute-start.50 = (bf16[128,1024]{1,0:T(8,128)(2,1)S(1)}, bf16[128,1024]{1,0:T(8,128)(2,1)S(1)}, u32[]{:S(2)}, u32[]{:S(2)}) collective-permute-start(bf16[128,1024]{1,0:T(8,128)(2,1)S(1)} %get-tuple-element.251), channel_id=1, source_target_pairs={{0,8},{8,0},{1,9},{9,1},{2,10},{10,2},{3,11},{11,3},{4,12},{12,4},... | collective-permute-start | bytes 786440 | tf_op jit(solution)/shard_map/ppermute | solution.py:20
  163.1 13.4 %collective-permute-start.51 = (bf16[128,1024]{1,0:T(8,128)(2,1)S(1)}, bf16[128,1024]{1,0:T(8,128)(2,1)S(1)}, u32[]{:S(2)}, u32[]{:S(2)}) collective-permute-start(bf16[128,1024]{1,0:T(8,128)(2,1)S(1)} %get-tuple-element.252), channel_id=1, source_target_pairs={{0,16},{16,0},{1,17},{17,1},{2,18},{18,2},{3,19},{19,3},{4,20},{20... | collective-permute-start | bytes 786440 | tf_op jit(solution)/shard_map/ppermute | solution.py:20
  194.6 14.0 %collective-permute-start.63 = (bf16[256,1024]{1,0:T(8,128)(2,1)S(1)}, bf16[256,1024]{1,0:T(8,128)(2,1)S(1)}, u32[]{:S(2)}, u32[]{:S(2)}) collective-permute-start(bf16[256,1024]{1,0:T(8,128)(2,1)S(1)} %shard_map.292.refs_0_.refs_3_), channel_id=1, source_target_pairs={{0,1},{1,0},{2,3},{3,2},{4,5},{5,4},{6,7},{7,6},{8,9},{9,8},{10,11... | collective-permute-start | bytes 1572872 | tf_op jit(solution)/shard_map/ppermute | solution.py:20
  197.4 25.0 %collective-permute-start.68 = (bf16[512,1024]{1,0:T(8,128)(2,1)S(1)}, bf16[512,1024]{1,0:T(8,128)(2,1)S(1)}, u32[]{:S(2)}, u32[]{:S(2)}) collective-permute-start(bf16[512,1024]{1,0:T(8,128)(2,1)S(1)} %get-tuple-element.284), channel_id=1, source_target_pairs={{0,16},{16,0},{1,17},{17,1},{2,18},{18,2},{3,19},{19,3},{4,20},{20... | collective-permute-start | bytes 3145736 | tf_op jit(solution)/shard_map/ppermute | solution.py:20
  198.7 24.6 %collective-permute-start.69 = (bf16[512,1024]{1,0:T(8,128)(2,1)S(1)}, bf16[512,1024]{1,0:T(8,128)(2,1)S(1)}, u32[]{:S(2)}, u32[]{:S(2)}) collective-permute-start(bf16[512,1024]{1,0:T(8,128)(2,1)S(1)} %get-tuple-element.285), channel_id=1, source_target_pairs={{0,8},{8,0},{1,9},{9,1},{2,10},{10,2},{3,11},{11,3},{4,12},{12,4},... | collective-permute-start | bytes 3145736 | tf_op jit(solution)/shard_map/ppermute | solution.py:20
  219.4 15.9 %collective-permute-start.70 = (bf16[256,1024]{1,0:T(8,128)(2,1)S(1)}, bf16[256,1024]{1,0:T(8,128)(2,1)S(1)}, u32[]{:S(2)}, u32[]{:S(2)}) collective-permute-start(bf16[256,1024]{1,0:T(8,128)(2,1)S(1)} %shard_map.296.refs_0_.refs_2_), channel_id=1, source_target_pairs={{0,1},{1,0},{2,3},{3,2},{4,5},{5,4},{6,7},{7,6},{8,9},{9,8},{10,11... | collective-permute-start | bytes 1572872 | tf_op jit(solution)/shard_map/ppermute | solution.py:20
  225.2 21.5 %collective-permute-start.75 = (bf16[512,1024]{1,0:T(8,128)(2,1)S(1)}, bf16[512,1024]{1,0:T(8,128)(2,1)S(1)}, u32[]{:S(2)}, u32[]{:S(2)}) collective-permute-start(bf16[512,1024]{1,0:T(8,128)(2,1)S(1)} %get-tuple-element.299), channel_id=1, source_target_pairs={{0,16},{16,0},{1,17},{17,1},{2,18},{18,2},{3,19},{19,3},{4,20},{20... | collective-permute-start | bytes 3145736 | tf_op jit(solution)/shard_map/ppermute | solution.py:20
  226.1 20.7 %collective-permute-start.76 = (bf16[512,1024]{1,0:T(8,128)(2,1)S(1)}, bf16[512,1024]{1,0:T(8,128)(2,1)S(1)}, u32[]{:S(2)}, u32[]{:S(2)}) collective-permute-start(bf16[512,1024]{1,0:T(8,128)(2,1)S(1)} %get-tuple-element.300), channel_id=1, source_target_pairs={{0,8},{8,0},{1,9},{9,1},{2,10},{10,2},{3,11},{11,3},{4,12},{12,4},... | collective-permute-start | bytes 3145736 | tf_op jit(solution)/shard_map/ppermute | solution.py:20
  249.8 27.5 %collective-permute-start.80 = (bf16[640,1024]{1,0:T(8,128)(2,1)S(1)}, bf16[640,1024]{1,0:T(8,128)(2,1)S(1)}, u32[]{:S(2)}, u32[]{:S(2)}) collective-permute-start(bf16[640,1024]{1,0:T(8,128)(2,1)S(1)} %get-tuple-element.310), channel_id=1, source_target_pairs={{0,16},{16,0},{1,17},{17,1},{2,18},{18,2},{3,19},{19,3},{4,20},{20... | collective-permute-start | bytes 3932168 | tf_op jit(solution)/shard_map/ppermute | solution.py:20
  251.5 28.1 %collective-permute-start.81 = (bf16[640,1024]{1,0:T(8,128)(2,1)S(1)}, bf16[640,1024]{1,0:T(8,128)(2,1)S(1)}, u32[]{:S(2)}, u32[]{:S(2)}) collective-permute-start(bf16[640,1024]{1,0:T(8,128)(2,1)S(1)} %get-tuple-element.311), channel_id=1, source_target_pairs={{0,8},{8,0},{1,9},{9,1},{2,10},{10,2},{3,11},{11,3},{4,12},{12,4},... | collective-permute-start | bytes 3932168 | tf_op jit(solution)/shard_map/ppermute | solution.py:20
  252.0 13.5 %collective-permute-start.77 = (bf16[256,1024]{1,0:T(8,128)(2,1)S(1)}, bf16[256,1024]{1,0:T(8,128)(2,1)S(1)}, u32[]{:S(2)}, u32[]{:S(2)}) collective-permute-start(bf16[256,1024]{1,0:T(8,128)(2,1)S(1)} %shard_map.300.refs_0_.refs_2_), channel_id=1, source_target_pairs={{0,1},{1,0},{2,3},{3,2},{4,5},{5,4},{6,7},{7,6},{8,9},{9,8},{10,11... | collective-permute-start | bytes 1572872 | tf_op jit(solution)/shard_map/ppermute | solution.py:20
  269.2 26.6 %collective-permute-start.82 = (bf16[256,1024]{1,0:T(8,128)(2,1)S(1)}, bf16[256,1024]{1,0:T(8,128)(2,1)S(1)}, u32[]{:S(2)}, u32[]{:S(2)}) collective-permute-start(bf16[256,1024]{1,0:T(8,128)(2,1)S(1)} %get-tuple-element.314), channel_id=1, source_target_pairs={{0,2},{2,0},{1,3},{3,1},{4,6},{6,4},{5,7},{7,5},{8,10},{10,8},{9,1... | collective-permute-start | bytes 1572872 | tf_op jit(solution)/shard_map/ppermute | solution.py:20
  280.0 16.0 %collective-permute-start.85 = (bf16[256,1024]{1,0:T(8,128)(2,1)S(1)}, bf16[256,1024]{1,0:T(8,128)(2,1)S(1)}, u32[]{:S(2)}, u32[]{:S(2)}) collective-permute-start(bf16[256,1024]{1,0:T(8,128)(2,1)S(1)} %get-tuple-element.318), channel_id=1, source_target_pairs={{0,8},{8,0},{1,9},{9,1},{2,10},{10,2},{3,11},{11,3},{4,12},{12,4},... | collective-permute-start | bytes 1572872 | tf_op jit(solution)/shard_map/ppermute | solution.py:20
  280.3 15.6 %collective-permute-start.86 = (bf16[256,1024]{1,0:T(8,128)(2,1)S(1)}, bf16[256,1024]{1,0:T(8,128)(2,1)S(1)}, u32[]{:S(2)}, u32[]{:S(2)}) collective-permute-start(bf16[256,1024]{1,0:T(8,128)(2,1)S(1)} %get-tuple-element.319), channel_id=1, source_target_pairs={{0,16},{16,0},{1,17},{17,1},{2,18},{18,2},{3,19},{19,3},{4,20},{20... | collective-permute-start | bytes 1572872 | tf_op jit(solution)/shard_map/ppermute | solution.py:20
  282.6 13.2 %collective-permute-start.83 = (bf16[128,1024]{1,0:T(8,128)(2,1)S(1)}, bf16[128,1024]{1,0:T(8,128)(2,1)S(1)}, u32[]{:S(2)}, u32[]{:S(2)}) collective-permute-start(bf16[128,1024]{1,0:T(8,128)(2,1)S(1)} %get-tuple-element.315.refs_14_), channel_id=1, source_target_pairs={{0,4},{4,0},{1,5},{5,1},{2,6},{6,2},{3,7},{7,3},{8,12},{12,8},{9,1... | collective-permute-start | bytes 786440 | tf_op jit(solution)/shard_map/ppermute | solution.py:20
  285.5 10.3 %collective-permute-start.84 = (bf16[128,1024]{1,0:T(8,128)(2,1)S(1)}, bf16[128,1024]{1,0:T(8,128)(2,1)S(1)}, u32[]{:S(2)}, u32[]{:S(2)}) collective-permute-start(bf16[128,1024]{1,0:T(8,128)(2,1)S(1)} %get-tuple-element.316.refs_15_), channel_id=1, source_target_pairs={{0,4},{4,0},{1,5},{5,1},{2,6},{6,2},{3,7},{7,3},{8,12},{12,8},{9,1... | collective-permute-start | bytes 786440 | tf_op jit(solution)/shard_map/ppermute | solution.py:20
  298.6 15.2 %collective-permute-start.93 = (bf16[288,1024]{1,0:T(8,128)(2,1)S(1)}, bf16[288,1024]{1,0:T(8,128)(2,1)S(1)}, u32[]{:S(2)}, u32[]{:S(2)}) collective-permute-start(bf16[288,1024]{1,0:T(8,128)(2,1)S(1)} %get-tuple-element.337), channel_id=1, source_target_pairs={{0,16},{16,0},{1,17},{17,1},{2,18},{18,2},{3,19},{19,3},{4,20},{20... | collective-permute-start | bytes 1769480 | tf_op jit(solution)/shard_map/ppermute | solution.py:20
  300.6 14.6 %collective-permute-start.94 = (bf16[288,1024]{1,0:T(8,128)(2,1)S(1)}, bf16[288,1024]{1,0:T(8,128)(2,1)S(1)}, u32[]{:S(2)}, u32[]{:S(2)}) collective-permute-start(bf16[288,1024]{1,0:T(8,128)(2,1)S(1)} %get-tuple-element.339), channel_id=1, source_target_pairs={{0,8},{8,0},{1,9},{9,1},{2,10},{10,2},{3,11},{11,3},{4,12},{12,4},... | collective-permute-start | bytes 1769480 | tf_op jit(solution)/shard_map/ppermute | solution.py:20
  300.7 10.8 %collective-permute-start.87 = (bf16[128,1024]{1,0:T(8,128)(2,1)S(1)}, bf16[128,1024]{1,0:T(8,128)(2,1)S(1)}, u32[]{:S(2)}, u32[]{:S(2)}) collective-permute-start(bf16[128,1024]{1,0:T(8,128)(2,1)S(1)} %get-tuple-element.330), channel_id=1, source_target_pairs={{0,1},{1,0},{2,3},{3,2},{4,5},{5,4},{6,7},{7,6},{8,9},{9,8},{10,11... | collective-permute-start | bytes 786440 | tf_op jit(solution)/shard_map/ppermute | solution.py:20
  304.0 15.1 %collective-permute-start.89 = (bf16[128,1024]{1,0:T(8,128)(2,1)S(1)}, bf16[128,1024]{1,0:T(8,128)(2,1)S(1)}, u32[]{:S(2)}, u32[]{:S(2)}) collective-permute-start(bf16[128,1024]{1,0:T(8,128)(2,1)S(1)} %get-tuple-element.313.refs_0_), channel_id=1, source_target_pairs={{0,2},{2,0},{1,3},{3,1},{4,6},{6,4},{5,7},{7,5},{8,10},{10,8},{9,1... | collective-permute-start | bytes 786440 | tf_op jit(solution)/shard_map/ppermute | solution.py:20
  315.4 16.4 %collective-permute-start.97 = (bf16[144,1024]{1,0:T(8,128)(2,1)S(1)}, bf16[144,1024]{1,0:T(8,128)(2,1)S(1)}, u32[]{:S(2)}, u32[]{:S(2)}) collective-permute-start(bf16[144,1024]{1,0:T(8,128)(2,1)S(1)} %get-tuple-element.344), channel_id=1, source_target_pairs={{0,16},{16,0},{1,17},{17,1},{2,18},{18,2},{3,19},{19,3},{4,20},{20... | collective-permute-start | bytes 884744 | tf_op jit(solution)/shard_map/ppermute | solution.py:20
  315.8 36.1 %collective-permute-start.96 = (bf16[256,1024]{1,0:T(8,128)(2,1)S(1)}, bf16[256,1024]{1,0:T(8,128)(2,1)S(1)}, u32[]{:S(2)}, u32[]{:S(2)}) collective-permute-start(bf16[256,1024]{1,0:T(8,128)(2,1)S(1)} %shard_map.307.refs_0_), channel_id=1, source_target_pairs={{0,2},{2,0},{1,3},{3,1},{4,6},{6,4},{5,7},{7,5},{8,10},{10,8},{9,1... | collective-permute-start | bytes 1572872 | tf_op jit(solution)/shard_map/ppermute | solution.py:20
  319.6 10.9 %collective-permute-start.91 = (bf16[32,1792]{1,0:T(8,128)(2,1)S(1)}, bf16[32,1792]{1,0:T(8,128)(2,1)S(1)}, u32[]{:S(2)}, u32[]{:S(2)}) collective-permute-start(bf16[32,1792]{1,0:T(8,128)(2,1)S(1)} %get-tuple-element.335), channel_id=1, source_target_pairs={{0,1},{1,0},{2,3},{3,2},{4,5},{5,4},{6,7},{7,6},{8,9},{9,8},{10,11... | collective-permute-start | bytes 344072 | tf_op jit(solution)/shard_map/ppermute | solution.py:20
  320.6 11.1 %collective-permute-start.92 = (bf16[32,1792]{1,0:T(8,128)(2,1)S(1)}, bf16[32,1792]{1,0:T(8,128)(2,1)S(1)}, u32[]{:S(2)}, u32[]{:S(2)}) collective-permute-start(bf16[32,1792]{1,0:T(8,128)(2,1)S(1)} %get-tuple-element.336), channel_id=1, source_target_pairs={{0,5},{5,0},{1,4},{4,1},{2,7},{7,2},{3,6},{6,3},{8,13},{13,8},{9,1... | collective-permute-start | bytes 344072 | tf_op jit(solution)/shard_map/ppermute | solution.py:1214
  321.5 30.5 %collective-permute-start.95 = (bf16[144,1024]{1,0:T(8,128)(2,1)S(1)}, bf16[144,1024]{1,0:T(8,128)(2,1)S(1)}, u32[]{:S(2)}, u32[]{:S(2)}) collective-permute-start(bf16[144,1024]{1,0:T(8,128)(2,1)S(1)} %get-tuple-element.340), channel_id=1, source_target_pairs={{0,8},{8,0},{1,9},{9,1},{2,10},{10,2},{3,11},{11,3},{4,12},{12,4},... | collective-permute-start | bytes 884744 | tf_op jit(solution)/shard_map/ppermute | solution.py:20
  331.9 24.6 %collective-permute-start.98 = (bf16[144,1024]{1,0:T(8,128)(2,1)S(1)}, bf16[144,1024]{1,0:T(8,128)(2,1)S(1)}, u32[]{:S(2)}, u32[]{:S(2)}) collective-permute-start(bf16[144,1024]{1,0:T(8,128)(2,1)S(1)} %shard_map.311), channel_id=1, source_target_pairs={{0,2},{2,0},{1,3},{3,1},{4,6},{6,4},{5,7},{7,5},{8,10},{10,8},{9,1... | collective-permute-start | bytes 884744 | tf_op jit(solution)/shard_map/ppermute | solution.py:20
  338.1 24.7 %collective-permute-start.88 = (bf16[1,128,1024]{2,1,0:T(8,128)(2,1)S(1)}, bf16[1,128,1024]{2,1,0:T(8,128)(2,1)S(1)}, u32[]{:S(2)}, u32[]{:S(2)}) collective-permute-start(bf16[1,128,1024]{2,1,0:T(8,128)(2,1)S(1)} %shard_map.308.refs_0_), channel_id=1, source_target_pairs={{0,0},{2,4},{4,2},{6,6},{1,1},{3,5},{5,3},{7,7},{8,8},{10,12},{12,... | collective-permute-start | bytes 786440 | tf_op jit(solution)/shard_map/ppermute | solution.py:1206
  357.9 12.7 %collective-permute-start.99 = (bf16[48,1792]{1,0:T(8,128)(2,1)S(1)}, bf16[48,1792]{1,0:T(8,128)(2,1)S(1)}, u32[]{:S(2)}, u32[]{:S(2)}) collective-permute-start(bf16[48,1792]{1,0:T(8,128)(2,1)S(1)} %get-tuple-element.349), channel_id=1, source_target_pairs={{0,4},{4,0},{1,5},{5,1},{2,6},{6,2},{3,7},{7,3},{8,12},{12,8},{9,1... | collective-permute-start | bytes 516104 | tf_op jit(solution)/shard_map/ppermute | solution.py:20
  357.9 12.7 %collective-permute-start.100 = (bf16[48,1792]{1,0:T(8,128)(2,1)S(1)}, bf16[48,1792]{1,0:T(8,128)(2,1)S(1)}, u32[]{:S(2)}, u32[]{:S(2)}) collective-permute-start(bf16[48,1792]{1,0:T(8,128)(2,1)S(1)} %get-tuple-element.350), channel_id=1, source_target_pairs={{0,1},{1,0},{2,3},{3,2},{4,5},{5,4},{6,7},{7,6},{8,9},{9,8},{10,11... | collective-permute-start | bytes 516104 | tf_op jit(solution)/shard_map/ppermute | solution.py:20
  357.9 12.7 %collective-permute-start.101 = (bf16[48,1792]{1,0:T(8,128)(2,1)S(1)}, bf16[48,1792]{1,0:T(8,128)(2,1)S(1)}, u32[]{:S(2)}, u32[]{:S(2)}) collective-permute-start(bf16[48,1792]{1,0:T(8,128)(2,1)S(1)} %get-tuple-element.351), channel_id=1, source_target_pairs={{0,5},{5,0},{1,4},{4,1},{2,7},{7,2},{3,6},{6,3},{8,13},{13,8},{9,1... | collective-permute-start | bytes 516104 | tf_op jit(solution)/shard_map/ppermute | solution.py:1214
  359.8 10.8 %collective-permute-start.102 = (bf16[64,512]{1,0:T(8,128)(2,1)S(1)}, bf16[64,512]{1,0:T(8,128)(2,1)S(1)}, u32[]{:S(2)}, u32[]{:S(2)}) collective-permute-start(bf16[64,512]{1,0:T(8,128)(2,1)S(1)} %get-tuple-element.352), channel_id=1, source_target_pairs={{0,0},{1,16},{16,1},{17,17},{2,2},{3,18},{18,3},{19,19},{4,4},{5,2... | collective-permute-start | bytes 196616 | tf_op jit(solution)/shard_map/ppermute | solution.py:1440
  (49 other events, 235.0 us)
